TPU v7x, 32 devices: a whole 2x2x4 slice. The times are simulated.
32 devices in a mesh: dp: 2 (over y), expert: 16 (over z, x, core).
Axes of the slice: x: 2, y: 2, z: 4, core: 2. Of those that a mesh axis runs over, the one named last changes fastest.
Arguments:
- tokens: bfloat16 [3584, 1024], P(('dp', 'expert')), parts along dimension 0, may hold values from -6 to 6
- expert_ids: int32 [3584, 8], P(('dp', 'expert')), parts along dimension 0, may hold values from 0 to 15, all different within a row; in each aligned block of 112 rows (0 to 111, 112 to 223, ...) at most 112 rows name the same one
- gate_probs: float32 [3584, 8], P(('dp', 'expert')), parts along dimension 0, may hold values from 0.05 to 0.5
- w_gate: bfloat16 [16, 1024, 384], P('expert'), may hold values from -0.1875 to 0.1875
- w_up: bfloat16 [16, 1024, 384], P('expert'), may hold values from -0.1875 to 0.1875
- w_down: bfloat16 [16, 384, 1024], P('expert'), may hold values from -0.3125 to 0.3125
- placement: int32 [16], replicated, may hold values from 0 to 15, each once
- swap_flags: int32 [16], replicated, may hold values from 0 to 1, as said below
Outputs:
- mixed: bfloat16 [3584, 1024], P(('dp', 'expert')), parts along dimension 0
- stored_gate: bfloat16 [32, 1024, 384], P(('dp', 'expert')), parts along dimension 0
- stored_up: bfloat16 [32, 1024, 384], P(('dp', 'expert')), parts along dimension 0
- stored_down: bfloat16 [32, 384, 1024], P(('dp', 'expert')), parts along dimension 0
There are 2 independent parts, one for each index of `dp`. A program takes and returns all parts, laid end to end along the dimension named above; an argument that names none is the same for every part. Nothing has to cross between parts.
Inputs may be any that keep to these rules, and one draw needn't show every extreme that they name: `expert_ids`: each row names 8 different experts; the 112 rows of one device name one expert at most 112 times, a bound that some block reaches. `placement`: each expert is stored on exactly one device. swap_flags[d] equals swap_flags[d XOR (8)]; the number of devices is a power of two. The first and last pairs always trade, the second pair never does.
All inputs are finite; a program needn't handle non-finite values.
Results may differ from a plain program's by a relative error of at most 0.0057.
Values may be sent and summed in bfloat16 or wider, within the bound.
No kernel may reach another device: no remote copies, remote signals or barrier semaphores. Data moves between devices by JAX's collectives and lax.ppermute only.
A program may use at most 64 MiB of HBM per device.

v0:
```python
import functools

import jax
import jax.numpy as jnp
from jax import lax
from jax.experimental import pallas as pl
from jax.experimental.pallas import tpu as pltpu
from jax.sharding import PartitionSpec as P

LANES = 128
VMEM_LIMIT = 20 * 2**20


def split_parts(values):
    parts = []
    for _ in range(3):
        part = lax.reduce_precision(values, exponent_bits=8, mantissa_bits=7)
        parts.append(part.astype(jnp.bfloat16))
        values = values - part
    return parts


def pack_gates(tokens, expert_ids, gate_probs, count):
    experts = jnp.arange(count, dtype=jnp.int32)
    chosen = expert_ids[:, None, :] == experts[None, :, None]
    weights = jnp.sum(jnp.where(chosen, gate_probs[:, None, :], 0.0), axis=2)
    parts = jnp.concatenate(split_parts(weights), axis=1)
    parts = jnp.pad(parts, ((0, 0), (0, -parts.shape[1] % LANES)))
    return jnp.concatenate([tokens, parts], axis=1)


def dot(a, b):
    return jnp.dot(a, b, preferred_element_type=jnp.float32)


def token_weight(tail, expert, count):
    lane = lax.broadcasted_iota(jnp.int32, tail.shape, 1)
    mine = (lane % count == expert) & (lane < 3 * count)
    return jnp.sum(jnp.where(mine, tail.astype(jnp.float32), 0.0), axis=1, keepdims=True)


def activate(gate, up):
    return (gate / (1.0 + jnp.exp(-gate)) * up).astype(jnp.bfloat16)


def rounded(value):
    return value.astype(jnp.bfloat16).astype(jnp.float32)


def near_kernel(count, placement, *refs):
    rows, weights, outs, x = refs[:2], (refs[2:5], refs[5:8]), refs[8:10], refs[10]
    height, width = rows[0].shape[0], x.shape[1]
    me = lax.axis_index("expert")
    for i in range(2):
        x[i * height : (i + 1) * height, :] = rows[i][:, :width]
    totals = [0.0, 0.0]
    for flip, (g, u, d) in enumerate(weights):
        hidden = activate(dot(x[...], g[...]), dot(x[...], u[...]))
        value = rounded(dot(hidden, d[...]))
        for i in range(2):
            weight = token_weight(rows[i][:, width:], placement[me ^ flip], count)
            totals[i] = totals[i] + value[i * height : (i + 1) * height, :] * weight
    for i in range(2):
        outs[i][...] = totals[i]


def hidden_kernel(blocks, width, *refs):
    rows, weights, out, x = refs[:blocks], refs[blocks : blocks + 8], refs[blocks + 8], refs[blocks + 9]
    height = rows[0].shape[0]
    half = lax.axis_index("dp") % 2
    for first in range(0, blocks, 2):
        for i in range(2):
            x[i * height : (i + 1) * height, :] = rows[first + i][:, :width]
        for slot in range(2):
            ga, ua, gb, ub = weights[4 * slot : 4 * slot + 4]
            depth, ff = ga.shape
            at = pl.multiple_of(half * depth, depth)
            off = pl.multiple_of(depth - at, depth)
            xa, xb = x[:, pl.ds(at, depth)], x[:, pl.ds(off, depth)]
            gate = dot(xa, ga[...]) + dot(xb, gb[...])
            up = dot(xa, ua[...]) + dot(xb, ub[...])
            span = slice(first * height, (first + 2) * height)
            out[span, slot * ff : (slot + 1) * ff] = activate(gate, up)


def down_kernel(count, first, placement, *refs):
    rows, hidden, downs, base, outs = refs[:2], refs[2], refs[3:7], refs[7:9], refs[9:11]
    height, width = base[0].shape
    me = lax.axis_index("expert")
    far = lax.axis_size("expert") // 2
    half = lax.axis_index("dp") % 2
    weights = [
        [token_weight(r[:, width:], placement[me ^ far ^ slot], count) for slot in range(2)]
        for r in rows
    ]
    part, ff = downs[0].shape[1], downs[0].shape[0]
    at = pl.multiple_of(half * part, part)
    off = pl.multiple_of(part - at, part)
    for which, start in ((0, at), (1, off)):
        columns = pl.ds(start, part)
        totals = [base[i][:, columns] for i in range(2)]
        for slot in range(2):
            span = slice(first * height, (first + 2) * height)
            units = hidden[span, slot * ff : (slot + 1) * ff]
            value = rounded(dot(units, downs[2 * slot + which][...]))
            for i in range(2):
                totals[i] = totals[i] + value[i * height : (i + 1) * height, :] * weights[i][slot]
        for i in range(2):
            outs[i][:, columns] = totals[i].astype(outs[i].dtype)


def call(kernel, out_shape, args, scratch=(), scalars=0):
    vmem = pl.BlockSpec(memory_space=pltpu.VMEM)
    smem = pl.BlockSpec(memory_space=pltpu.SMEM)
    return pl.pallas_call(
        kernel,
        out_shape=out_shape,
        in_specs=[smem] * scalars + [vmem] * (len(args) - scalars),
        out_specs=jax.tree.map(lambda _: vmem, out_shape),
        scratch_shapes=list(scratch),
        compiler_params=pltpu.CompilerParams(vmem_limit_bytes=VMEM_LIMIT),
        cost_estimate=pl.CostEstimate(flops=0, bytes_accessed=2**20, transcendentals=0),
    )(*args)


def run_copies(copies, sems):
    copies = [pltpu.make_async_copy(a, b, sems.at[i]) for i, (a, b) in enumerate(copies)]
    for copy in copies:
        copy.start()
    for copy in copies:
        copy.wait()


def part_of(ref, axis, half, size):
    span = pl.ds(pl.multiple_of(half * size, size), size)
    return ref.at[span, :] if axis == 0 else ref.at[:, span]


def store_kernel(axis, flags, own, came, other, out, sems):
    half = lax.axis_index("dp") % 2
    size = came.shape[axis]
    taken = flags[lax.axis_index("expert")] == 1

    @pl.when(taken)
    def _():
        run_copies(
            [
                (came, part_of(out, axis, half, size)),
                (other, part_of(out, axis, 1 - half, size)),
            ],
            sems,
        )

    @pl.when(jnp.logical_not(taken))
    def _():
        run_copies([(own, out)], sems)


def store(axis, flags, own, came, other):
    vmem = pl.BlockSpec(memory_space=pltpu.VMEM)
    return pl.pallas_call(
        functools.partial(store_kernel, axis),
        out_shape=jax.ShapeDtypeStruct(own.shape, own.dtype),
        in_specs=[pl.BlockSpec(memory_space=pltpu.SMEM)] + [vmem] * 3,
        out_specs=pl.BlockSpec(memory_space=pl.ANY),
        scratch_shapes=[pltpu.SemaphoreType.DMA((2,))],
        compiler_params=pltpu.CompilerParams(vmem_limit_bytes=8 * 2**20),
        cost_estimate=pl.CostEstimate(flops=0, bytes_accessed=4 * own.size, transcendentals=0),
    )(flags, own, came, other)


def after(value, *others):
    return lax.optimization_barrier((value, *others))[0]


def per_device(tokens, expert_ids, gate_probs, w_gate, w_up, w_down, placement, swap_flags):
    count = lax.axis_size("expert")
    couple = lax.axis_index("dp") % 2
    half_axis = count // 2
    height, width = tokens.shape
    own = (w_gate[0], w_up[0], w_down[0])
    trades = [(d, d ^ 1) for d in range(lax.axis_size("dp"))]

    def send(value, bit, name):
        with jax.named_scope(name):
            return lax.ppermute(value, "expert", [(d, d ^ bit) for d in range(count)])

    def trade(value):
        with jax.named_scope("trade"):
            return lax.ppermute(value, "dp", trades)

    axes = (0, 0, 1)
    halves = []
    for w, axis in zip(own, axes):
        size = w.shape[axis] // 2
        halves.append(lax.dynamic_slice_in_dim(w, couple * size, size, axis=axis))
    z = [send(half, half_axis, "swap") for half in halves]
    near = [send(after(w, z[0], halves[2]), 1, "near") for w in own]

    bits = []
    bit = half_axis // 2
    while bit > 1:
        bits.append(bit)
        bit //= 2
    blocks = {0: pack_gates(tokens, expert_ids, gate_probs, count)}
    for stage, bit in enumerate(bits):
        for i in sorted(blocks):
            last = (i | 1 << stage) + 1 == 1 << len(bits)
            block = after(blocks[i], z[1]) if last else blocks[i]
            blocks[i | 1 << stage] = send(block, bit, "tokens")
    rows = [blocks[i] for i in range(len(blocks))]

    y = [trade(after(z[0], z[1], *rows[1:3])), trade(z[1])]
    z_near = [send(part, 1, "z_near") for part in z[:2]]

    scratch = [pltpu.VMEM((2 * height, width), jnp.bfloat16)]
    firsts = list(reversed(range(0, len(rows), 2)))
    base = {}
    for first in firsts:
        base[first] = call(
            functools.partial(near_kernel, count),
            [jax.ShapeDtypeStruct((height, width), jnp.float32)] * 2,
            [placement, *rows[first : first + 2], *own, *near],
            scratch,
            scalars=1,
        )
    lower = after(z[2], base)
    y.append(trade(lower))
    z_near.append(send(lower, 1, "z_near"))
    y_near = [send(after(part, lower), 1, "y_near") for part in y[:2]]
    ff = own[0].shape[1]
    hidden = call(
        functools.partial(hidden_kernel, len(rows), width),
        jax.ShapeDtypeStruct((len(rows) * height, 2 * ff), jnp.bfloat16),
        [*rows, *z[:2], *y[:2], *z_near[:2], *y_near[:2]],
        scratch,
    )
    y_near.append(send(after(y[2], hidden), 1, "y_near"))
    parts = {}
    for first in firsts:
        dtype = jnp.bfloat16 if first >= len(rows) // 2 else jnp.float32
        parts[first], parts[first + 1] = call(
            functools.partial(down_kernel, count, first),
            [jax.ShapeDtypeStruct((height, width), dtype)] * 2,
            [
                placement,
                *rows[first : first + 2],
                hidden,
                *(z[2], y[2], z_near[2], y_near[2]),
                *base[first],
            ],
            scalars=1,
        )
    for stage in reversed(range(len(bits))):
        for i in reversed(range(1 << stage)):
            part = parts[i | 1 << stage].astype(jnp.bfloat16)
            parts[i] = parts[i] + send(part, bits[stage], "sums").astype(jnp.float32)
    mixed = parts[0].astype(jnp.bfloat16)

    stored = [store(axis, swap_flags, *parts) for axis, *parts in zip(axes, own, z, y)]
    return (mixed, *(w[None] for w in stored))


def solution(mesh):
    in_specs = (
        P(("dp", "expert"), None),
        P(("dp", "expert"), None),
        P(("dp", "expert"), None),
        P("expert", None, None),
        P("expert", None, None),
        P("expert", None, None),
        P(),
        P(),
    )
    out_specs = (
        P(("dp", "expert"), None),
        P(("dp", "expert"), None, None),
        P(("dp", "expert"), None, None),
        P(("dp", "expert"), None, None),
    )
    return jax.shard_map(
        per_device, mesh=mesh, in_specs=in_specs, out_specs=out_specs, check_vma=False
    )
```

profile of v0, /device:TPU:0, one launch (start us, length us, event | category | flops | bytes accessed | tf_op | source)
XLA Modules:
  0.0 106.0 jit_solution(715553370634451176)
XLA Ops:
  0.7 1.2 %dynamic-slice_bitcast_fusion.1 = bf16[512,384]{1,0:T(8,128)(2,1)S(1)} fusion(bf16[1,1024,384]{2,1,0:T(8,128)(2,1)} %param.11, s32[]{:T(128)S(6)} %select_n.18), kind=kLoop, calls=%fused_computation.5 | loop fusion | bytes 786436 | tf_op jit(solution)/shard_map/dynamic_slice | solution.py:196
  1.8 4.1 %collective-permute-start.4 = (bf16[512,384]{1,0:T(8,128)(2,1)S(1)}, bf16[512,384]{1,0:T(8,128)(2,1)S(1)}, u32[]{:S(2)}, u32[]{:S(2)}) collective-permute-start(bf16[512,384]{1,0:T(8,128)(2,1)S(1)} %dynamic-slice_bitcast_fusion.1), channel_id=1, source_target_pairs={{0,8},{1,9},{2,10},{3,11},{4,12},{5,13},{6,14},{7,15},{8,0},{9,1},... | collective-permute-start | bytes 1179656 | tf_op jit(solution)/shard_map/swap/ppermute | solution.py:186
  6.0 1.8 %dynamic-slice_bitcast_fusion = bf16[384,512]{1,0:T(8,128)(2,1)} fusion(bf16[1,384,1024]{2,1,0:T(8,128)(2,1)} %param.13, s32[]{:T(128)S(6)} %select_n.18), kind=kLoop, calls=%fused_computation.4 | loop fusion | bytes 786436 | tf_op jit(solution)/shard_map/dynamic_slice | solution.py:196
  7.8 15.7 %collective-permute-done.4.refs_4_.came = bf16[512,384]{1,0:T(8,128)(2,1)S(1)} collective-permute-done((bf16[512,384]{1,0:T(8,128)(2,1)S(1)}, bf16[512,384]{1,0:T(8,128)(2,1)S(1)}, u32[]{:S(2)}, u32[]{:S(2)}) %collective-permute-start.4) | collective-permute-done | bytes 393248 | tf_op jit(solution)/shard_map/swap/ppermute | solution.py:186
  23.5 0.7 copy.17
  24.2 0.5 collective-permute-start.11
  24.7 1.0 fusion.1.refs_0_
  25.7 0.8 collective-permute-start
  26.5 3.4 %collective-permute-start.2 = (bf16[512,384]{1,0:T(8,128)(2,1)S(1)}, bf16[512,384]{1,0:T(8,128)(2,1)S(1)}, u32[]{:S(2)}, u32[]{:S(2)}) collective-permute-start(bf16[512,384]{1,0:T(8,128)(2,1)S(1)} %dynamic-slice_bitcast_fusion.2), channel_id=1, source_target_pairs={{0,8},{1,9},{2,10},{3,11},{4,12},{5,13},{6,14},{7,15},{8,0},{9,1},... | collective-permute-start | bytes 1179656 | tf_op jit(solution)/shard_map/swap/ppermute | solution.py:186
  30.0 8.3 %collective-permute-done.refs_1_ = bf16[112,1152]{1,0:T(8,128)(2,1)S(1)} collective-permute-done((bf16[112,1152]{1,0:T(8,128)(2,1)S(1)}, bf16[112,1152]{1,0:T(8,128)(2,1)S(1)}, u32[]{:S(2)}, u32[]{:S(2)}) %collective-permute-start) | collective-permute-done | bytes 258080 | tf_op jit(solution)/shard_map/tokens/ppermute | solution.py:186
  38.3 1.5 %collective-permute-start.1 = (bf16[112,1152]{1,0:T(8,128)(2,1)S(1)}, bf16[112,1152]{1,0:T(8,128)(2,1)S(1)}, u32[]{:S(2)}, u32[]{:S(2)}) collective-permute-start(bf16[112,1152]{1,0:T(8,128)(2,1)S(1)} %fusion.1.refs_0_), channel_id=1, source_target_pairs={{0,2},{1,3},{2,0},{3,1},{4,6},{5,7},{6,4},{7,5},{8,10},{9,11},{10,... | collective-permute-start | bytes 774152 | tf_op jit(solution)/shard_map/tokens/ppermute | solution.py:186
  39.9 5.7 %collective-permute-done.1.refs_0_.refs_2_ = bf16[112,1152]{1,0:T(8,128)(2,1)S(1)} collective-permute-done((bf16[112,1152]{1,0:T(8,128)(2,1)S(1)}, bf16[112,1152]{1,0:T(8,128)(2,1)S(1)}, u32[]{:S(2)}, u32[]{:S(2)}) %collective-permute-start.1) | collective-permute-done | bytes 258080 | tf_op jit(solution)/shard_map/tokens/ppermute | solution.py:186
  45.6 0.2 collective-permute-start.9
  45.8 11.1 %collective-permute-done.2.refs_5_.came = bf16[512,384]{1,0:T(8,128)(2,1)S(1)} collective-permute-done((bf16[512,384]{1,0:T(8,128)(2,1)S(1)}, bf16[512,384]{1,0:T(8,128)(2,1)S(1)}, u32[]{:S(2)}, u32[]{:S(2)}) %collective-permute-start.2) | collective-permute-done | bytes 393248 | tf_op jit(solution)/shard_map/swap/ppermute | solution.py:186
  56.9 1.5 %collective-permute-start.6 = (bf16[512,384]{1,0:T(8,128)(2,1)S(1)}, bf16[512,384]{1,0:T(8,128)(2,1)S(1)}, u32[]{:S(2)}, u32[]{:S(2)}) collective-permute-start(bf16[512,384]{1,0:T(8,128)(2,1)S(1)} %collective-permute-done.2.refs_5_.came), channel_id=1, source_target_pairs={{0,16},{16,0},{1,17},{17,1},{2,18},{18,2},{3,19},{19,3},{4,20},{20... | collective-permute-start | bytes 1179656 | tf_op jit(solution)/shard_map/trade/ppermute | solution.py:190
  58.4 0.5 collective-permute-start.5
  58.9 1.5 %collective-permute-start.3 = (bf16[112,1152]{1,0:T(8,128)(2,1)S(1)}, bf16[112,1152]{1,0:T(8,128)(2,1)S(1)}, u32[]{:S(2)}, u32[]{:S(2)}) collective-permute-start(bf16[112,1152]{1,0:T(8,128)(2,1)S(1)} %collective-permute-done.refs_1_), channel_id=1, source_target_pairs={{0,2},{1,3},{2,0},{3,1},{4,6},{5,7},{6,4},{7,5},{8,10},{9,11},{10,... | collective-permute-start | bytes 774152 | tf_op jit(solution)/shard_map/tokens/ppermute | solution.py:186
  60.4 0.0 collective-permute-done.12.refs_7_
  60.4 0.0 collective-permute-start.7
  60.4 2.3 %shard_map.111 = (f32[112,1024]{1,0:T(8,128)S(1)}, f32[112,1024]{1,0:T(8,128)S(1)}) custom-call(s32[16]{0:T(128)S(1)} %copy-done.3, bf16[112,1152]{1,0:T(8,128)(2,1)S(1)} %fusion.1.refs_0_, bf16[112,1152]{1,0:T(8,128)(2,1)S(1)} %collective-permute-done.refs_1_, bf16[1024,384]{1,0:T(8,128)(2,1)S(1)} %bitcast.13, bf16[1024,384]{1,0:T(8,128)(2,1)S(1)} %bitcast.17, ...), custom_call_target="tpu_custom_call" | custom-call | bytes 1048576 | tf_op jit(solution)/shard_map/pallas_call | solution.py:115
  62.8 3.5 %collective-permute-done.3.refs_1_.refs_3_ = bf16[112,1152]{1,0:T(8,128)(2,1)S(1)} collective-permute-done((bf16[112,1152]{1,0:T(8,128)(2,1)S(1)}, bf16[112,1152]{1,0:T(8,128)(2,1)S(1)}, u32[]{:S(2)}, u32[]{:S(2)}) %collective-permute-start.3) | collective-permute-done | bytes 258080 | tf_op jit(solution)/shard_map/tokens/ppermute | solution.py:186
  66.2 0.0 collective-permute-start.8
  66.2 2.3 %shard_map.112 = (f32[112,1024]{1,0:T(8,128)S(1)}, f32[112,1024]{1,0:T(8,128)S(1)}) custom-call(s32[16]{0:T(128)S(1)} %copy-done.3, bf16[112,1152]{1,0:T(8,128)(2,1)S(1)} %collective-permute-done.1.refs_0_.refs_2_, bf16[112,1152]{1,0:T(8,128)(2,1)S(1)} %collective-permute-done.3.refs_1_.refs_3_, bf16[1024,384]{1,0:T(8,128)(2,1)S(1)} %bitcast.14, ...), custom_call_target="tpu_custom_call" | custom-call | bytes 1048576 | tf_op jit(solution)/shard_map/pallas_call | solution.py:115
  68.6 0.0 collective-permute-done.9.refs_3_.came
  68.6 0.3 collective-permute-done.6.refs_7_.other
  68.9 0.3 collective-permute-start.14
  69.2 6.9 %collective-permute-done.5.refs_6_.other = bf16[512,384]{1,0:T(8,128)(2,1)S(1)} collective-permute-done((bf16[512,384]{1,0:T(8,128)(2,1)S(1)}, bf16[512,384]{1,0:T(8,128)(2,1)S(1)}, u32[]{:S(2)}, u32[]{:S(2)}) %collective-permute-start.5) | collective-permute-done | bytes 393248 | tf_op jit(solution)/shard_map/trade/ppermute | solution.py:190
  76.1 0.0 collective-permute-start.13
  76.1 1.5 %collective-permute-start.15 = (bf16[384,512]{1,0:T(8,128)(2,1)S(1)}, bf16[384,512]{1,0:T(8,128)(2,1)S(1)}, u32[]{:S(2)}, u32[]{:S(2)}) collective-permute-start(bf16[384,512]{1,0:T(8,128)(2,1)S(1)} %collective-permute-done.9.refs_3_.came), channel_id=1, source_target_pairs={{0,16},{16,0},{1,17},{17,1},{2,18},{18,2},{3,19},{19,3},{4,20},{20... | collective-permute-start | bytes 1179656 | tf_op jit(solution)/shard_map/trade/ppermute | solution.py:190
  77.6 0.2 collective-permute-start.16
  77.8 0.0 collective-permute-done.14.refs_11_
  77.8 0.0 collective-permute-done.13.refs_10_
  77.8 2.2 %shard_map.113.refs_2_ = bf16[448,768]{1,0:T(8,128)(2,1)S(1)} custom-call(bf16[112,1152]{1,0:T(8,128)(2,1)S(1)} %fusion.1.refs_0_, bf16[112,1152]{1,0:T(8,128)(2,1)S(1)} %collective-permute-done.refs_1_, bf16[112,1152]{1,0:T(8,128)(2,1)S(1)} %collective-permute-done.1.refs_0_.refs_2_, bf16[112,1152]{1,0:T(8,128)(2,1)S(1)} %collective-permute-done.3.refs_1_.refs_3_, ...), custom_call_target="tpu_custom_call" | custom-call | bytes 1048576 | tf_op jit(solution)/shard_map/pallas_call | solution.py:115
  80.0 7.6 %collective-permute-done.15.refs_4_.other = bf16[384,512]{1,0:T(8,128)(2,1)S(1)} collective-permute-done((bf16[384,512]{1,0:T(8,128)(2,1)S(1)}, bf16[384,512]{1,0:T(8,128)(2,1)S(1)}, u32[]{:S(2)}, u32[]{:S(2)}) %collective-permute-start.15) | collective-permute-done | bytes 393248 | tf_op jit(solution)/shard_map/trade/ppermute | solution.py:190
  87.6 1.7 %collective-permute-done.17.refs_6_ = bf16[384,512]{1,0:T(8,128)(2,1)S(1)} collective-permute-done((bf16[384,512]{1,0:T(8,128)(2,1)S(1)}, bf16[384,512]{1,0:T(8,128)(2,1)S(1)}, u32[]{:S(2)}, u32[]{:S(2)}) %collective-permute-start.17) | collective-permute-done | bytes 393248 | tf_op jit(solution)/shard_map/y_near/ppermute | solution.py:186
  89.3 1.2 %shard_map.115 = (bf16[112,1024]{1,0:T(8,128)(2,1)S(1)}, bf16[112,1024]{1,0:T(8,128)(2,1)S(1)}) custom-call(s32[16]{0:T(128)S(1)} %copy-done.3, bf16[112,1152]{1,0:T(8,128)(2,1)S(1)} %collective-permute-done.1.refs_0_.refs_2_, bf16[112,1152]{1,0:T(8,128)(2,1)S(1)} %collective-permute-done.3.refs_1_.refs_3_, bf16[448,768]{1,0:T(8,128)(2,1)S(1)} %shard_map.113.refs_2_, ...), custom_call_target="tpu_custom_call" | custom-call | bytes 1048576 | tf_op jit(solution)/shard_map/pallas_call | solution.py:115
  90.5 1.6 %collective-permute-start.19 = (bf16[112,1024]{1,0:T(8,128)(2,1)S(1)}, bf16[112,1024]{1,0:T(8,128)(2,1)S(1)}, u32[]{:S(2)}, u32[]{:S(2)}) collective-permute-start(bf16[112,1024]{1,0:T(8,128)(2,1)S(1)} %get-tuple-element.37), channel_id=1, source_target_pairs={{0,2},{1,3},{2,0},{3,1},{4,6},{5,7},{6,4},{7,5},{8,10},{9,11},{10,... | collective-permute-start | bytes 688136 | tf_op jit(solution)/shard_map/sums/ppermute | solution.py:186
  92.1 0.5 collective-permute-start.18
  92.6 1.2 %shard_map.114 = (f32[112,1024]{1,0:T(8,128)S(1)}, f32[112,1024]{1,0:T(8,128)S(1)}) custom-call(s32[16]{0:T(128)S(1)} %copy-done.3, bf16[112,1152]{1,0:T(8,128)(2,1)S(1)} %fusion.1.refs_0_, bf16[112,1152]{1,0:T(8,128)(2,1)S(1)} %collective-permute-done.refs_1_, bf16[448,768]{1,0:T(8,128)(2,1)S(1)} %shard_map.113.refs_2_, ...), custom_call_target="tpu_custom_call" | custom-call | bytes 1048576 | tf_op jit(solution)/shard_map/pallas_call | solution.py:115
  93.8 5.2 %collective-permute-done.19 = bf16[112,1024]{1,0:T(8,128)(2,1)S(1)} collective-permute-done((bf16[112,1024]{1,0:T(8,128)(2,1)S(1)}, bf16[112,1024]{1,0:T(8,128)(2,1)S(1)}, u32[]{:S(2)}, u32[]{:S(2)}) %collective-permute-start.19) | collective-permute-done | bytes 229408 | tf_op jit(solution)/shard_map/sums/ppermute | solution.py:186
  99.0 0.1 add_convert_fusion.1
  99.1 0.1 collective-permute-start.20
  99.2 0.5 copy-done.4
  99.7 1.4 %shard_map.116 = bf16[1024,384]{1,0:T(8,128)(2,1)} custom-call(s32[16]{0:T(128)S(1)} %copy-done.4, bf16[1024,384]{1,0:T(8,128)(2,1)S(1)} %bitcast.15, bf16[512,384]{1,0:T(8,128)(2,1)S(1)} %collective-permute-done.4.refs_4_.came, bf16[512,384]{1,0:T(8,128)(2,1)S(1)} %collective-permute-done.5.refs_6_.other), custom_call_target="tpu_custom_call" | custom-call | bytes 1572864 | tf_op jit(solution)/shard_map/pallas_call | solution.py:161
  101.1 1.4 %shard_map.117 = bf16[1024,384]{1,0:T(8,128)(2,1)} custom-call(s32[16]{0:T(128)S(1)} %copy-done.4, bf16[1024,384]{1,0:T(8,128)(2,1)S(1)} %bitcast.19, bf16[512,384]{1,0:T(8,128)(2,1)S(1)} %collective-permute-done.2.refs_5_.came, bf16[512,384]{1,0:T(8,128)(2,1)S(1)} %collective-permute-done.6.refs_7_.other), custom_call_target="tpu_custom_call" | custom-call | bytes 1572864 | tf_op jit(solution)/shard_map/pallas_call | solution.py:161
  102.6 1.4 %shard_map.118 = bf16[384,1024]{1,0:T(8,128)(2,1)} custom-call(s32[16]{0:T(128)S(1)} %copy-done.4, bf16[384,1024]{1,0:T(8,128)(2,1)S(1)} %bitcast.23, bf16[384,512]{1,0:T(8,128)(2,1)S(1)} %collective-permute-done.9.refs_3_.came, bf16[384,512]{1,0:T(8,128)(2,1)S(1)} %collective-permute-done.15.refs_4_.other), custom_call_target="tpu_custom_call" | custom-call | bytes 1572864 | tf_op jit(solution)/shard_map/pallas_call | solution.py:161
  104.1 1.1 %collective-permute-done.20 = bf16[112,1024]{1,0:T(8,128)(2,1)S(1)} collective-permute-done((bf16[112,1024]{1,0:T(8,128)(2,1)S(1)}, bf16[112,1024]{1,0:T(8,128)(2,1)S(1)}, u32[]{:S(2)}, u32[]{:S(2)}) %collective-permute-start.20) | collective-permute-done | bytes 229408 | tf_op jit(solution)/shard_map/sums/ppermute | solution.py:186
  105.2 0.8 add_convert_fusion
  (28 shorter events, 0.1 us)
Async XLA Ops:
  0.6 5.3 %copy-start.6 = (f32[112,8]{0,1:T(8,128)S(1)}, f32[112,8]{0,1:T(8,128)}, u32[]{:S(2)}) copy-start(f32[112,8]{0,1:T(8,128)} %param.10) | copy-start | bytes 10756
  0.6 5.3 %copy-start.7 = (s32[112,8]{0,1:T(8,128)S(1)}, s32[112,8]{0,1:T(8,128)}, u32[]{:S(2)}) copy-start(s32[112,8]{0,1:T(8,128)} %param.9) | copy-start | bytes 10756
  0.7 22.8 %copy-start = (bf16[1,1024,384]{2,1,0:T(8,128)(2,1)S(1)}, bf16[1,1024,384]{2,1,0:T(8,128)(2,1)}, u32[]{:S(2)}) copy-start(bf16[1,1024,384]{2,1,0:T(8,128)(2,1)} %param.11) | copy-start | bytes 2359300
  0.7 23.5 %copy-start.1 = (bf16[1,1024,384]{2,1,0:T(8,128)(2,1)S(1)}, bf16[1,1024,384]{2,1,0:T(8,128)(2,1)}, u32[]{:S(2)}) copy-start(bf16[1,1024,384]{2,1,0:T(8,128)(2,1)} %param.12) | copy-start | bytes 2359300
  1.8 21.6 %collective-permute-start.4 = (bf16[512,384]{1,0:T(8,128)(2,1)S(1)}, bf16[512,384]{1,0:T(8,128)(2,1)S(1)}, u32[]{:S(2)}, u32[]{:S(2)}) collective-permute-start(bf16[512,384]{1,0:T(8,128)(2,1)S(1)} %dynamic-slice_bitcast_fusion.1), channel_id=1, source_target_pairs={{0,8},{1,9},{2,10},{3,11},{4,12},{5,13},{6,14},{7,15},{8,0},{9,1},... | collective-permute-start | bytes 1179656 | tf_op jit(solution)/shard_map/swap/ppermute | solution.py:186
  7.8 52.6 %copy-start.2 = (bf16[1,384,1024]{2,1,0:T(8,128)(2,1)S(1)}, bf16[1,384,1024]{2,1,0:T(8,128)(2,1)}, u32[]{:S(2)}) copy-start(bf16[1,384,1024]{2,1,0:T(8,128)(2,1)} %param.13) | copy-start | bytes 2359300
  23.5 34.9 %collective-permute-start.10 = (bf16[1024,384]{1,0:T(8,128)(2,1)S(1)}, bf16[1024,384]{1,0:T(8,128)(2,1)S(1)}, u32[]{:S(2)}, u32[]{:S(2)}) collective-permute-start(bf16[1024,384]{1,0:T(8,128)(2,1)S(1)} %bitcast.12), channel_id=1, source_target_pairs={{0,1},{1,0},{2,3},{3,2},{4,5},{5,4},{6,7},{7,6},{8,9},{9,8},{10,11... | collective-permute-start | bytes 2359304 | tf_op jit(solution)/shard_map/near/ppermute | solution.py:186
  24.2 34.7 %collective-permute-start.11 = (bf16[1024,384]{1,0:T(8,128)(2,1)S(1)}, bf16[1024,384]{1,0:T(8,128)(2,1)S(1)}, u32[]{:S(2)}, u32[]{:S(2)}) collective-permute-start(bf16[1024,384]{1,0:T(8,128)(2,1)S(1)} %bitcast.16), channel_id=1, source_target_pairs={{0,1},{1,0},{2,3},{3,2},{4,5},{5,4},{6,7},{7,6},{8,9},{9,8},{10,11... | collective-permute-start | bytes 2359304 | tf_op jit(solution)/shard_map/near/ppermute | solution.py:186
  25.7 12.6 %collective-permute-start = (bf16[112,1152]{1,0:T(8,128)(2,1)S(1)}, bf16[112,1152]{1,0:T(8,128)(2,1)S(1)}, u32[]{:S(2)}, u32[]{:S(2)}) collective-permute-start(bf16[112,1152]{1,0:T(8,128)(2,1)S(1)} %fusion.1.refs_0_), channel_id=1, source_target_pairs={{0,4},{1,5},{2,6},{3,7},{4,0},{5,1},{6,2},{7,3},{8,12},{9,13},{10,... | collective-permute-start | bytes 774152 | tf_op jit(solution)/shard_map/tokens/ppermute | solution.py:186
  26.5 19.1 %copy-start.5 = (bf16[384,512]{1,0:T(8,128)(2,1)S(1)}, bf16[384,512]{1,0:T(8,128)(2,1)}, u32[]{:S(2)}) copy-start(bf16[384,512]{1,0:T(8,128)(2,1)} %dynamic-slice_bitcast_fusion) | copy-start | bytes 1179652
  26.5 33.9 %copy-start.3 = (s32[16]{0:T(128)S(1)}, s32[16]{0:T(128)}, u32[]{:S(2)}) copy-start(s32[16]{0:T(128)} %placement.7) | copy-start | bytes 196
  26.5 33.9 %collective-permute-start.12 = (bf16[384,1024]{1,0:T(8,128)(2,1)}, bf16[384,1024]{1,0:T(8,128)(2,1)S(1)}, u32[]{:S(2)}, u32[]{:S(2)}) collective-permute-start(bf16[384,1024]{1,0:T(8,128)(2,1)} %bitcast.20), channel_id=1, source_target_pairs={{0,1},{1,0},{2,3},{3,2},{4,5},{5,4},{6,7},{7,6},{8,9},{9,8},{10,11... | collective-permute-start | bytes 2359304 | tf_op jit(solution)/shard_map/near/ppermute | solution.py:186
  26.5 30.3 %collective-permute-start.2 = (bf16[512,384]{1,0:T(8,128)(2,1)S(1)}, bf16[512,384]{1,0:T(8,128)(2,1)S(1)}, u32[]{:S(2)}, u32[]{:S(2)}) collective-permute-start(bf16[512,384]{1,0:T(8,128)(2,1)S(1)} %dynamic-slice_bitcast_fusion.2), channel_id=1, source_target_pairs={{0,8},{1,9},{2,10},{3,11},{4,12},{5,13},{6,14},{7,15},{8,0},{9,1},... | collective-permute-start | bytes 1179656 | tf_op jit(solution)/shard_map/swap/ppermute | solution.py:186
  38.3 7.3 %collective-permute-start.1 = (bf16[112,1152]{1,0:T(8,128)(2,1)S(1)}, bf16[112,1152]{1,0:T(8,128)(2,1)S(1)}, u32[]{:S(2)}, u32[]{:S(2)}) collective-permute-start(bf16[112,1152]{1,0:T(8,128)(2,1)S(1)} %fusion.1.refs_0_), channel_id=1, source_target_pairs={{0,2},{1,3},{2,0},{3,1},{4,6},{5,7},{6,4},{7,5},{8,10},{9,11},{10,... | collective-permute-start | bytes 774152 | tf_op jit(solution)/shard_map/tokens/ppermute | solution.py:186
  45.6 23.0 %collective-permute-start.9 = (bf16[384,512]{1,0:T(8,128)(2,1)S(1)}, bf16[384,512]{1,0:T(8,128)(2,1)S(1)}, u32[]{:S(2)}, u32[]{:S(2)}) collective-permute-start(bf16[384,512]{1,0:T(8,128)(2,1)S(1)} %copy-done.5), channel_id=1, source_target_pairs={{0,8},{1,9},{2,10},{3,11},{4,12},{5,13},{6,14},{7,15},{8,0},{9,1},... | collective-permute-start | bytes 1179656 | tf_op jit(solution)/shard_map/swap/ppermute | solution.py:186
  56.9 12.0 %collective-permute-start.6 = (bf16[512,384]{1,0:T(8,128)(2,1)S(1)}, bf16[512,384]{1,0:T(8,128)(2,1)S(1)}, u32[]{:S(2)}, u32[]{:S(2)}) collective-permute-start(bf16[512,384]{1,0:T(8,128)(2,1)S(1)} %collective-permute-done.2.refs_5_.came), channel_id=1, source_target_pairs={{0,16},{16,0},{1,17},{17,1},{2,18},{18,2},{3,19},{19,3},{4,20},{20... | collective-permute-start | bytes 1179656 | tf_op jit(solution)/shard_map/trade/ppermute | solution.py:190
  58.4 17.7 %collective-permute-start.5 = (bf16[512,384]{1,0:T(8,128)(2,1)S(1)}, bf16[512,384]{1,0:T(8,128)(2,1)S(1)}, u32[]{:S(2)}, u32[]{:S(2)}) collective-permute-start(bf16[512,384]{1,0:T(8,128)(2,1)S(1)} %collective-permute-done.4.refs_4_.came), channel_id=1, source_target_pairs={{0,16},{16,0},{1,17},{17,1},{2,18},{18,2},{3,19},{19,3},{4,20},{20... | collective-permute-start | bytes 1179656 | tf_op jit(solution)/shard_map/trade/ppermute | solution.py:190
  58.9 7.3 %collective-permute-start.3 = (bf16[112,1152]{1,0:T(8,128)(2,1)S(1)}, bf16[112,1152]{1,0:T(8,128)(2,1)S(1)}, u32[]{:S(2)}, u32[]{:S(2)}) collective-permute-start(bf16[112,1152]{1,0:T(8,128)(2,1)S(1)} %collective-permute-done.refs_1_), channel_id=1, source_target_pairs={{0,2},{1,3},{2,0},{3,1},{4,6},{5,7},{6,4},{7,5},{8,10},{9,11},{10,... | collective-permute-start | bytes 774152 | tf_op jit(solution)/shard_map/tokens/ppermute | solution.py:186
  60.4 17.2 %collective-permute-start.7 = (bf16[512,384]{1,0:T(8,128)(2,1)S(1)}, bf16[512,384]{1,0:T(8,128)(2,1)S(1)}, u32[]{:S(2)}, u32[]{:S(2)}) collective-permute-start(bf16[512,384]{1,0:T(8,128)(2,1)S(1)} %collective-permute-done.4.refs_4_.came), channel_id=1, source_target_pairs={{0,1},{1,0},{2,3},{3,2},{4,5},{5,4},{6,7},{7,6},{8,9},{9,8},{10,11... | collective-permute-start | bytes 1179656 | tf_op jit(solution)/shard_map/z_near/ppermute | solution.py:186
  66.2 11.6 %collective-permute-start.8 = (bf16[512,384]{1,0:T(8,128)(2,1)S(1)}, bf16[512,384]{1,0:T(8,128)(2,1)S(1)}, u32[]{:S(2)}, u32[]{:S(2)}) collective-permute-start(bf16[512,384]{1,0:T(8,128)(2,1)S(1)} %collective-permute-done.2.refs_5_.came), channel_id=1, source_target_pairs={{0,1},{1,0},{2,3},{3,2},{4,5},{5,4},{6,7},{7,6},{8,9},{9,8},{10,11... | collective-permute-start | bytes 1179656 | tf_op jit(solution)/shard_map/z_near/ppermute | solution.py:186
  68.9 8.9 %collective-permute-start.14 = (bf16[512,384]{1,0:T(8,128)(2,1)S(1)}, bf16[512,384]{1,0:T(8,128)(2,1)S(1)}, u32[]{:S(2)}, u32[]{:S(2)}) collective-permute-start(bf16[512,384]{1,0:T(8,128)(2,1)S(1)} %collective-permute-done.6.refs_7_.other), channel_id=1, source_target_pairs={{0,1},{1,0},{2,3},{3,2},{4,5},{5,4},{6,7},{7,6},{8,9},{9,8},{10,11... | collective-permute-start | bytes 1179656 | tf_op jit(solution)/shard_map/y_near/ppermute | solution.py:186
  76.1 1.8 %collective-permute-start.13 = (bf16[512,384]{1,0:T(8,128)(2,1)S(1)}, bf16[512,384]{1,0:T(8,128)(2,1)S(1)}, u32[]{:S(2)}, u32[]{:S(2)}) collective-permute-start(bf16[512,384]{1,0:T(8,128)(2,1)S(1)} %collective-permute-done.5.refs_6_.other), channel_id=1, source_target_pairs={{0,1},{1,0},{2,3},{3,2},{4,5},{5,4},{6,7},{7,6},{8,9},{9,8},{10,11... | collective-permute-start | bytes 1179656 | tf_op jit(solution)/shard_map/y_near/ppermute | solution.py:186
  76.1 11.5 %collective-permute-start.15 = (bf16[384,512]{1,0:T(8,128)(2,1)S(1)}, bf16[384,512]{1,0:T(8,128)(2,1)S(1)}, u32[]{:S(2)}, u32[]{:S(2)}) collective-permute-start(bf16[384,512]{1,0:T(8,128)(2,1)S(1)} %collective-permute-done.9.refs_3_.came), channel_id=1, source_target_pairs={{0,16},{16,0},{1,17},{17,1},{2,18},{18,2},{3,19},{19,3},{4,20},{20... | collective-permute-start | bytes 1179656 | tf_op jit(solution)/shard_map/trade/ppermute | solution.py:190
  77.6 10.0 %collective-permute-start.16 = (bf16[384,512]{1,0:T(8,128)(2,1)S(1)}, bf16[384,512]{1,0:T(8,128)(2,1)S(1)}, u32[]{:S(2)}, u32[]{:S(2)}) collective-permute-start(bf16[384,512]{1,0:T(8,128)(2,1)S(1)} %collective-permute-done.9.refs_3_.came), channel_id=1, source_target_pairs={{0,1},{1,0},{2,3},{3,2},{4,5},{5,4},{6,7},{7,6},{8,9},{9,8},{10,11... | collective-permute-start | bytes 1179656 | tf_op jit(solution)/shard_map/z_near/ppermute | solution.py:186
  87.6 1.7 %collective-permute-start.17 = (bf16[384,512]{1,0:T(8,128)(2,1)S(1)}, bf16[384,512]{1,0:T(8,128)(2,1)S(1)}, u32[]{:S(2)}, u32[]{:S(2)}) collective-permute-start(bf16[384,512]{1,0:T(8,128)(2,1)S(1)} %collective-permute-done.15.refs_4_.other), channel_id=1, source_target_pairs={{0,1},{1,0},{2,3},{3,2},{4,5},{5,4},{6,7},{7,6},{8,9},{9,8},{10,11... | collective-permute-start | bytes 1179656 | tf_op jit(solution)/shard_map/y_near/ppermute | solution.py:186
  90.5 8.5 %collective-permute-start.19 = (bf16[112,1024]{1,0:T(8,128)(2,1)S(1)}, bf16[112,1024]{1,0:T(8,128)(2,1)S(1)}, u32[]{:S(2)}, u32[]{:S(2)}) collective-permute-start(bf16[112,1024]{1,0:T(8,128)(2,1)S(1)} %get-tuple-element.37), channel_id=1, source_target_pairs={{0,2},{1,3},{2,0},{3,1},{4,6},{5,7},{6,4},{7,5},{8,10},{9,11},{10,... | collective-permute-start | bytes 688136 | tf_op jit(solution)/shard_map/sums/ppermute | solution.py:186
  92.1 12.0 %collective-permute-start.18 = (bf16[112,1024]{1,0:T(8,128)(2,1)S(1)}, bf16[112,1024]{1,0:T(8,128)(2,1)S(1)}, u32[]{:S(2)}, u32[]{:S(2)}) collective-permute-start(bf16[112,1024]{1,0:T(8,128)(2,1)S(1)} %get-tuple-element.35), channel_id=1, source_target_pairs={{0,2},{1,3},{2,0},{3,1},{4,6},{5,7},{6,4},{7,5},{8,10},{9,11},{10,... | collective-permute-start | bytes 688136 | tf_op jit(solution)/shard_map/sums/ppermute | solution.py:186
  99.0 0.7 copy-start.4
  99.1 6.1 %collective-permute-start.20 = (bf16[112,1024]{1,0:T(8,128)(2,1)S(1)}, bf16[112,1024]{1,0:T(8,128)(2,1)S(1)}, u32[]{:S(2)}, u32[]{:S(2)}) collective-permute-start(bf16[112,1024]{1,0:T(8,128)(2,1)S(1)} %add_convert_fusion.1), channel_id=1, source_target_pairs={{0,4},{1,5},{2,6},{3,7},{4,0},{5,1},{6,2},{7,3},{8,12},{9,13},{10,... | collective-permute-start | bytes 688136 | tf_op jit(solution)/shard_map/sums/ppermute | solution.py:186
where the time goes:
time: 106 us
  waiting for transfers between devices  67.1 us (63%)
  starting transfers between devices  18.3 us (17%)
  Pallas kernels  13.6 us (13%)
  local copies, waits for them, and re-layouts  4.23 us (4%)
  other arithmetic  1.85 us (2%)
    ppermute x18, waiting for transfers between devices, send(): return lax.ppermute(value, 'expert', [(d, d ^ bit) for d in range(count)])  52.3 us
    ppermute x3, waiting for transfers between devices, trade(): return lax.ppermute(value, 'dp', trades)  14.8 us
    ppermute x18, starting transfers between devices, send(): return lax.ppermute(value, 'expert', [(d, d ^ bit) for d in range(count)])  14.8 us
    pallas_call x5, Pallas kernels, call(): pl.pallas_call(kernel, out_shape=out_shape, in_specs=[smem] * scalars + [...  9.29 us
    pallas_call x3, Pallas kernels, store(): pl.pallas_call(functools.partial(store_kernel, axis), out_shape=jax.Shape...  4.34 us
    ppermute x3, starting transfers between devices, trade(): return lax.ppermute(value, 'dp', trades)  3.55 us
    dynamic_slice x3, local copies, waits for them, and re-layouts, per_device(): halves.append(lax.dynamic_slice_in_dim(w, couple * size, size, axis=axis))  2.97 us
  transfers between devices with their start and end apart: 21, of which 11 were waited for; matrix products, arithmetic and copies ran while one was open for 3% of the time, Pallas kernels for 12%

commit v1 on v0

--- a/solution.py
+++ b/solution.py
@@ -195,22 +195,20 @@
         size = w.shape[axis] // 2
         halves.append(lax.dynamic_slice_in_dim(w, couple * size, size, axis=axis))
     z = [send(half, half_axis, "swap") for half in halves]
-    near = [send(after(w, z[0], halves[2]), 1, "near") for w in own]
+    near = [send(w, 1, "near") for w in own]
 
     bits = []
     bit = half_axis // 2
     while bit > 1:
         bits.append(bit)
         bit //= 2
-    blocks = {0: pack_gates(tokens, expert_ids, gate_probs, count)}
+    blocks = {0: after(pack_gates(tokens, expert_ids, gate_probs, count), *near)}
     for stage, bit in enumerate(bits):
         for i in sorted(blocks):
-            last = (i | 1 << stage) + 1 == 1 << len(bits)
-            block = after(blocks[i], z[1]) if last else blocks[i]
-            blocks[i | 1 << stage] = send(block, bit, "tokens")
+            blocks[i | 1 << stage] = send(blocks[i], bit, "tokens")
     rows = [blocks[i] for i in range(len(blocks))]
 
-    y = [trade(after(z[0], z[1], *rows[1:3])), trade(z[1])]
+    y = [trade(after(z[0], z[1])), trade(z[1])]
     z_near = [send(part, 1, "z_near") for part in z[:2]]
 
     scratch = [pltpu.VMEM((2 * height, width), jnp.bfloat16)]
@@ -227,7 +225,7 @@
     lower = after(z[2], base)
     y.append(trade(lower))
     z_near.append(send(lower, 1, "z_near"))
-    y_near = [send(after(part, lower), 1, "y_near") for part in y[:2]]
+    y_near = [send(after(part, z[2], base), 1, "y_near") for part in y[:2]]
     ff = own[0].shape[1]
     hidden = call(
         functools.partial(hidden_kernel, len(rows), width),

time: 106 us -> 99.5 us (0.939)
  waiting for transfers between devices: 67.1 us -> 56.8 us
  Pallas kernels: 13.6 us -> 16.8 us
  starting transfers between devices: 18.3 us -> 19.6 us
    ppermute x3, waiting for transfers between devices: 14.8 us -> 6.44 us  [trade(): return lax.ppermute(value, 'dp', trades)]
    pallas_call x5, Pallas kernels: 9.29 us -> 12 us  [call(): pl.pallas_call(kernel, out_shape=out_shape, in_specs=[smem] * scalars + [...]
    ppermute x18, waiting for transfers between devices: 52.3 us -> 50.4 us  [send(): return lax.ppermute(value, 'expert', [(d, d ^ bit) for d in range(count)])]
  transfers between devices with their start and end apart: 21 -> 21, of which waited for: 11 -> 10; matrix products, arithmetic and copies ran while one was open for 3% -> 4% of each run, Pallas kernels for 12% -> 16%
where the time goes in v1:
time: 99.5 us; the launch traced here: 99.2 us
  waiting for transfers between devices  56.8 us (57%)
  starting transfers between devices  19.6 us (20%)
  Pallas kernels  16.8 us (17%)
  local copies, waits for them, and re-layouts  3.36 us (3%)
  other arithmetic  1.84 us (2%)
    ppermute x18, waiting for transfers between devices, send(): return lax.ppermute(value, 'expert', [(d, d ^ bit) for d in range(count)])  50.4 us
    ppermute x18, starting transfers between devices, send(): return lax.ppermute(value, 'expert', [(d, d ^ bit) for d in range(count)])  15.4 us
    pallas_call x5, Pallas kernels, call(): pl.pallas_call(kernel, out_shape=out_shape, in_specs=[smem] * scalars + [...  12 us
    ppermute x3, waiting for transfers between devices, trade(): return lax.ppermute(value, 'dp', trades)  6.44 us
    pallas_call x3, Pallas kernels, store(): pl.pallas_call(functools.partial(store_kernel, axis), out_shape=jax.Shape...  4.81 us
    ppermute x3, starting transfers between devices, trade(): return lax.ppermute(value, 'dp', trades)  4.19 us
    dynamic_slice x3, local copies, waits for them, and re-layouts, per_device(): halves.append(lax.dynamic_slice_in_dim(w, couple * size, size, axis=axis))  2.62 us
  transfers between devices with their start and end apart: 21, of which 10 were waited for; matrix products, arithmetic and copies ran while one was open for 4% of the time, Pallas kernels for 16%

profile of v1, /device:TPU:0, one launch (start us, length us, event | category | flops | bytes accessed | tf_op | source)
XLA Modules:
  0.0 99.2 jit_solution(12220016084879979588)
XLA Ops:
  0.6 0.5 collective-permute-start
  1.2 0.1 collective-permute-start.1
  1.2 0.4 collective-permute-start.2
  1.7 1.8 %dynamic-slice_bitcast_fusion.1 = bf16[512,384]{1,0:T(8,128)(2,1)} fusion(bf16[1,1024,384]{2,1,0:T(8,128)(2,1)} %param.12, s32[]{:T(128)S(6)} %select_n.18), kind=kLoop, calls=%fused_computation.5 | loop fusion | bytes 786436 | tf_op jit(solution)/shard_map/dynamic_slice | solution.py:196
  3.5 3.7 %collective-permute-start.7 = (bf16[512,384]{1,0:T(8,128)(2,1)}, bf16[512,384]{1,0:T(8,128)(2,1)S(1)}, u32[]{:S(2)}, u32[]{:S(2)}) collective-permute-start(bf16[512,384]{1,0:T(8,128)(2,1)} %dynamic-slice_bitcast_fusion.1), channel_id=1, source_target_pairs={{0,8},{1,9},{2,10},{3,11},{4,12},{5,13},{6,14},{7,15},{8,0},{9,1},... | collective-permute-start | bytes 1179656 | tf_op jit(solution)/shard_map/swap/ppermute | solution.py:186
  7.1 0.8 dynamic-slice_bitcast_fusion.2
  7.9 0.0 collective-permute-start.6
  8.0 0.7 copy.17
  8.7 1.0 fusion.1.refs_0_
  9.7 0.0 copy-start.3
  9.7 0.0 collective-permute-done.1.refs_6_
  9.7 0.0 collective-permute-done.2.refs_7_
  9.8 2.0 %collective-permute-start.3 = (bf16[112,1152]{1,0:T(8,128)(2,1)S(1)}, bf16[112,1152]{1,0:T(8,128)(2,1)S(1)}, u32[]{:S(2)}, u32[]{:S(2)}) collective-permute-start(bf16[112,1152]{1,0:T(8,128)(2,1)S(1)} %fusion.1.refs_0_), channel_id=1, source_target_pairs={{0,4},{1,5},{2,6},{3,7},{4,0},{5,1},{6,2},{7,3},{8,12},{9,13},{10,... | collective-permute-start | bytes 774152 | tf_op jit(solution)/shard_map/tokens/ppermute | solution.py:186
  11.8 2.7 %collective-permute-start.12 = (bf16[384,512]{1,0:T(8,128)(2,1)S(1)}, bf16[384,512]{1,0:T(8,128)(2,1)S(1)}, u32[]{:S(2)}, u32[]{:S(2)}) collective-permute-start(bf16[384,512]{1,0:T(8,128)(2,1)S(1)} %dynamic-slice_bitcast_fusion), channel_id=1, source_target_pairs={{0,8},{1,9},{2,10},{3,11},{4,12},{5,13},{6,14},{7,15},{8,0},{9,1},... | collective-permute-start | bytes 1179656 | tf_op jit(solution)/shard_map/swap/ppermute | solution.py:186
  14.4 28.2 %collective-permute-done.7.refs_5_.came = bf16[512,384]{1,0:T(8,128)(2,1)S(1)} collective-permute-done((bf16[512,384]{1,0:T(8,128)(2,1)}, bf16[512,384]{1,0:T(8,128)(2,1)S(1)}, u32[]{:S(2)}, u32[]{:S(2)}) %collective-permute-start.7) | collective-permute-done | bytes 393248 | tf_op jit(solution)/shard_map/swap/ppermute | solution.py:186
  42.6 1.8 %collective-permute-start.9 = (bf16[512,384]{1,0:T(8,128)(2,1)S(1)}, bf16[512,384]{1,0:T(8,128)(2,1)S(1)}, u32[]{:S(2)}, u32[]{:S(2)}) collective-permute-start(bf16[512,384]{1,0:T(8,128)(2,1)S(1)} %collective-permute-done.7.refs_5_.came), channel_id=1, source_target_pairs={{0,16},{16,0},{1,17},{17,1},{2,18},{18,2},{3,19},{19,3},{4,20},{20... | collective-permute-start | bytes 1179656 | tf_op jit(solution)/shard_map/trade/ppermute | solution.py:190
  44.4 6.8 %collective-permute-done.6.refs_4_.came = bf16[512,384]{1,0:T(8,128)(2,1)} collective-permute-done((bf16[512,384]{1,0:T(8,128)(2,1)}, bf16[512,384]{1,0:T(8,128)(2,1)}, u32[]{:S(2)}, u32[]{:S(2)}) %collective-permute-start.6) | collective-permute-done | bytes 393248 | tf_op jit(solution)/shard_map/swap/ppermute | solution.py:186
  51.1 1.8 %collective-permute-start.8 = (bf16[512,384]{1,0:T(8,128)(2,1)}, bf16[512,384]{1,0:T(8,128)(2,1)S(1)}, u32[]{:S(2)}, u32[]{:S(2)}) collective-permute-start(bf16[512,384]{1,0:T(8,128)(2,1)} %collective-permute-done.6.refs_4_.came), channel_id=1, source_target_pairs={{0,16},{16,0},{1,17},{17,1},{2,18},{18,2},{3,19},{19,3},{4,20},{20... | collective-permute-start | bytes 1179656 | tf_op jit(solution)/shard_map/trade/ppermute | solution.py:190
  52.9 1.5 %collective-permute-start.4 = (bf16[112,1152]{1,0:T(8,128)(2,1)S(1)}, bf16[112,1152]{1,0:T(8,128)(2,1)S(1)}, u32[]{:S(2)}, u32[]{:S(2)}) collective-permute-start(bf16[112,1152]{1,0:T(8,128)(2,1)S(1)} %fusion.1.refs_0_), channel_id=1, source_target_pairs={{0,2},{1,3},{2,0},{3,1},{4,6},{5,7},{6,4},{7,5},{8,10},{9,11},{10,... | collective-permute-start | bytes 774152 | tf_op jit(solution)/shard_map/tokens/ppermute | solution.py:186
  54.4 0.5 collective-permute-start.5
  55.0 3.2 %shard_map.111 = (f32[112,1024]{1,0:T(8,128)S(1)}, f32[112,1024]{1,0:T(8,128)S(1)}) custom-call(s32[16]{0:T(128)S(1)} %copy-done.3, bf16[112,1152]{1,0:T(8,128)(2,1)S(1)} %fusion.1.refs_0_, bf16[112,1152]{1,0:T(8,128)(2,1)S(1)} %collective-permute-done.3.refs_1_, bf16[1024,384]{1,0:T(8,128)(2,1)S(1)} %bitcast.13, bf16[1024,384]{1,0:T(8,128)(2,1)S(1)} %bitcast.17, ...), custom_call_target="tpu_custom_call" | custom-call | bytes 1048576 | tf_op jit(solution)/shard_map/pallas_call | solution.py:115
  58.1 4.0 %collective-permute-done.4.refs_0_.refs_2_ = bf16[112,1152]{1,0:T(8,128)(2,1)S(1)} collective-permute-done((bf16[112,1152]{1,0:T(8,128)(2,1)S(1)}, bf16[112,1152]{1,0:T(8,128)(2,1)S(1)}, u32[]{:S(2)}, u32[]{:S(2)}) %collective-permute-start.4) | collective-permute-done | bytes 258080 | tf_op jit(solution)/shard_map/tokens/ppermute | solution.py:186
  62.1 0.0 collective-permute-start.10
  62.1 3.4 %collective-permute-done.5.refs_1_.refs_3_ = bf16[112,1152]{1,0:T(8,128)(2,1)S(1)} collective-permute-done((bf16[112,1152]{1,0:T(8,128)(2,1)S(1)}, bf16[112,1152]{1,0:T(8,128)(2,1)S(1)}, u32[]{:S(2)}, u32[]{:S(2)}) %collective-permute-start.5) | collective-permute-done | bytes 258080 | tf_op jit(solution)/shard_map/tokens/ppermute | solution.py:186
  65.5 0.0 collective-permute-start.11
  65.5 3.2 %shard_map.112 = (f32[112,1024]{1,0:T(8,128)S(1)}, f32[112,1024]{1,0:T(8,128)S(1)}) custom-call(s32[16]{0:T(128)S(1)} %copy-done.3, bf16[112,1152]{1,0:T(8,128)(2,1)S(1)} %collective-permute-done.4.refs_0_.refs_2_, bf16[112,1152]{1,0:T(8,128)(2,1)S(1)} %collective-permute-done.5.refs_1_.refs_3_, bf16[1024,384]{1,0:T(8,128)(2,1)S(1)} %bitcast.14, ...), custom_call_target="tpu_custom_call" | custom-call | bytes 1048576 | tf_op jit(solution)/shard_map/pallas_call | solution.py:115
  68.7 0.0 collective-permute-done.12.refs_3_.came
  68.7 0.0 collective-permute-done.9.refs_7_.other
  68.7 0.6 collective-permute-start.14
  69.3 0.1 collective-permute-start.13
  69.4 0.6 collective-permute-start.15
  70.0 0.2 collective-permute-start.16
  70.2 0.5 collective-permute-done.14.refs_11_
  70.6 0.6 collective-permute-done.13.refs_10_
  71.2 3.2 %shard_map.113.refs_2_ = bf16[448,768]{1,0:T(8,128)(2,1)S(1)} custom-call(bf16[112,1152]{1,0:T(8,128)(2,1)S(1)} %fusion.1.refs_0_, bf16[112,1152]{1,0:T(8,128)(2,1)S(1)} %collective-permute-done.3.refs_1_, bf16[112,1152]{1,0:T(8,128)(2,1)S(1)} %collective-permute-done.4.refs_0_.refs_2_, bf16[112,1152]{1,0:T(8,128)(2,1)S(1)} %collective-permute-done.5.refs_1_.refs_3_, ...), custom_call_target="tpu_custom_call" | custom-call | bytes 1048576 | tf_op jit(solution)/shard_map/pallas_call | solution.py:115
  74.4 6.4 %collective-permute-done.15.refs_4_.other = bf16[384,512]{1,0:T(8,128)(2,1)S(1)} collective-permute-done((bf16[384,512]{1,0:T(8,128)(2,1)S(1)}, bf16[384,512]{1,0:T(8,128)(2,1)S(1)}, u32[]{:S(2)}, u32[]{:S(2)}) %collective-permute-start.15) | collective-permute-done | bytes 393248 | tf_op jit(solution)/shard_map/trade/ppermute | solution.py:190
  80.8 1.7 %collective-permute-done.17.refs_6_ = bf16[384,512]{1,0:T(8,128)(2,1)S(1)} collective-permute-done((bf16[384,512]{1,0:T(8,128)(2,1)S(1)}, bf16[384,512]{1,0:T(8,128)(2,1)S(1)}, u32[]{:S(2)}, u32[]{:S(2)}) %collective-permute-start.17) | collective-permute-done | bytes 393248 | tf_op jit(solution)/shard_map/y_near/ppermute | solution.py:186
  82.5 1.2 %shard_map.115 = (bf16[112,1024]{1,0:T(8,128)(2,1)S(1)}, bf16[112,1024]{1,0:T(8,128)(2,1)S(1)}) custom-call(s32[16]{0:T(128)S(1)} %copy-done.3, bf16[112,1152]{1,0:T(8,128)(2,1)S(1)} %collective-permute-done.4.refs_0_.refs_2_, bf16[112,1152]{1,0:T(8,128)(2,1)S(1)} %collective-permute-done.5.refs_1_.refs_3_, bf16[448,768]{1,0:T(8,128)(2,1)S(1)} %shard_map.113.refs_2_, ...), custom_call_target="tpu_custom_call" | custom-call | bytes 1048576 | tf_op jit(solution)/shard_map/pallas_call | solution.py:115
  83.8 1.6 %collective-permute-start.19 = (bf16[112,1024]{1,0:T(8,128)(2,1)S(1)}, bf16[112,1024]{1,0:T(8,128)(2,1)S(1)}, u32[]{:S(2)}, u32[]{:S(2)}) collective-permute-start(bf16[112,1024]{1,0:T(8,128)(2,1)S(1)} %get-tuple-element.31), channel_id=1, source_target_pairs={{0,2},{1,3},{2,0},{3,1},{4,6},{5,7},{6,4},{7,5},{8,10},{9,11},{10,... | collective-permute-start | bytes 688136 | tf_op jit(solution)/shard_map/sums/ppermute | solution.py:186
  85.3 0.5 collective-permute-start.18
  85.9 1.2 %shard_map.114 = (f32[112,1024]{1,0:T(8,128)S(1)}, f32[112,1024]{1,0:T(8,128)S(1)}) custom-call(s32[16]{0:T(128)S(1)} %copy-done.3, bf16[112,1152]{1,0:T(8,128)(2,1)S(1)} %fusion.1.refs_0_, bf16[112,1152]{1,0:T(8,128)(2,1)S(1)} %collective-permute-done.3.refs_1_, bf16[448,768]{1,0:T(8,128)(2,1)S(1)} %shard_map.113.refs_2_, ...), custom_call_target="tpu_custom_call" | custom-call | bytes 1048576 | tf_op jit(solution)/shard_map/pallas_call | solution.py:115
  87.1 5.2 %collective-permute-done.19 = bf16[112,1024]{1,0:T(8,128)(2,1)S(1)} collective-permute-done((bf16[112,1024]{1,0:T(8,128)(2,1)S(1)}, bf16[112,1024]{1,0:T(8,128)(2,1)S(1)}, u32[]{:S(2)}, u32[]{:S(2)}) %collective-permute-start.19) | collective-permute-done | bytes 229408 | tf_op jit(solution)/shard_map/sums/ppermute | solution.py:186
  92.3 1.1 %collective-permute-start.20 = (bf16[112,1024]{1,0:T(8,128)(2,1)S(1)}, bf16[112,1024]{1,0:T(8,128)(2,1)S(1)}, u32[]{:S(2)}, u32[]{:S(2)}) collective-permute-start(bf16[112,1024]{1,0:T(8,128)(2,1)S(1)} %add_convert_fusion.1), channel_id=1, source_target_pairs={{0,4},{1,5},{2,6},{3,7},{4,0},{5,1},{6,2},{7,3},{8,12},{9,13},{10,... | collective-permute-start | bytes 688136 | tf_op jit(solution)/shard_map/sums/ppermute | solution.py:186
  93.5 1.9 %shard_map.116 = bf16[1024,384]{1,0:T(8,128)(2,1)} custom-call(s32[16]{0:T(128)S(1)} %copy-done.4, bf16[1024,384]{1,0:T(8,128)(2,1)S(1)} %bitcast.15, bf16[512,384]{1,0:T(8,128)(2,1)} %collective-permute-done.6.refs_4_.came, bf16[512,384]{1,0:T(8,128)(2,1)S(1)} %collective-permute-done.8.refs_6_.other), custom_call_target="tpu_custom_call" | custom-call | bytes 1572864 | tf_op jit(solution)/shard_map/pallas_call | solution.py:161
  95.4 1.4 %shard_map.117 = bf16[1024,384]{1,0:T(8,128)(2,1)} custom-call(s32[16]{0:T(128)S(1)} %copy-done.4, bf16[1024,384]{1,0:T(8,128)(2,1)S(1)} %bitcast.19, bf16[512,384]{1,0:T(8,128)(2,1)S(1)} %collective-permute-done.7.refs_5_.came, bf16[512,384]{1,0:T(8,128)(2,1)S(1)} %collective-permute-done.9.refs_7_.other), custom_call_target="tpu_custom_call" | custom-call | bytes 1572864 | tf_op jit(solution)/shard_map/pallas_call | solution.py:161
  96.9 1.4 %shard_map.118 = bf16[384,1024]{1,0:T(8,128)(2,1)} custom-call(s32[16]{0:T(128)S(1)} %copy-done.4, bf16[384,1024]{1,0:T(8,128)(2,1)S(1)} %bitcast.23, bf16[384,512]{1,0:T(8,128)(2,1)S(1)} %collective-permute-done.12.refs_3_.came, bf16[384,512]{1,0:T(8,128)(2,1)S(1)} %collective-permute-done.15.refs_4_.other), custom_call_target="tpu_custom_call" | custom-call | bytes 1572864 | tf_op jit(solution)/shard_map/pallas_call | solution.py:161
  98.3 0.1 collective-permute-done.20
  98.4 0.8 add_convert_fusion
  (26 shorter events, 0.2 us)
Async XLA Ops:
  0.6 6.5 %copy-start = (bf16[1,1024,384]{2,1,0:T(8,128)(2,1)S(1)}, bf16[1,1024,384]{2,1,0:T(8,128)(2,1)}, u32[]{:S(2)}) copy-start(bf16[1,1024,384]{2,1,0:T(8,128)(2,1)} %param.11) | copy-start | bytes 2359300
  0.6 9.1 %collective-permute-start = (bf16[1024,384]{1,0:T(8,128)(2,1)}, bf16[1024,384]{1,0:T(8,128)(2,1)S(1)}, u32[]{:S(2)}, u32[]{:S(2)}) collective-permute-start(bf16[1024,384]{1,0:T(8,128)(2,1)} %bitcast.12), channel_id=1, source_target_pairs={{0,1},{1,0},{2,3},{3,2},{4,5},{5,4},{6,7},{7,6},{8,9},{9,8},{10,11... | collective-permute-start | bytes 2359304 | tf_op jit(solution)/shard_map/near/ppermute | solution.py:186
  1.2 8.6 %collective-permute-start.1 = (bf16[1024,384]{1,0:T(8,128)(2,1)}, bf16[1024,384]{1,0:T(8,128)(2,1)}, u32[]{:S(2)}, u32[]{:S(2)}) collective-permute-start(bf16[1024,384]{1,0:T(8,128)(2,1)} %bitcast.16), channel_id=1, source_target_pairs={{0,1},{1,0},{2,3},{3,2},{4,5},{5,4},{6,7},{7,6},{8,9},{9,8},{10,11... | collective-permute-start | bytes 2359304 | tf_op jit(solution)/shard_map/near/ppermute | solution.py:186
  1.2 8.5 %collective-permute-start.2 = (bf16[384,1024]{1,0:T(8,128)(2,1)}, bf16[384,1024]{1,0:T(8,128)(2,1)}, u32[]{:S(2)}, u32[]{:S(2)}) collective-permute-start(bf16[384,1024]{1,0:T(8,128)(2,1)} %bitcast.20), channel_id=1, source_target_pairs={{0,1},{1,0},{2,3},{3,2},{4,5},{5,4},{6,7},{7,6},{8,9},{9,8},{10,11... | collective-permute-start | bytes 2359304 | tf_op jit(solution)/shard_map/near/ppermute | solution.py:186
  1.7 6.3 %copy-start.5 = (f32[112,8]{0,1:T(8,128)S(1)}, f32[112,8]{0,1:T(8,128)}, u32[]{:S(2)}) copy-start(f32[112,8]{0,1:T(8,128)} %param.10) | copy-start | bytes 10756
  1.7 6.3 %copy-start.6 = (s32[112,8]{0,1:T(8,128)S(1)}, s32[112,8]{0,1:T(8,128)}, u32[]{:S(2)}) copy-start(s32[112,8]{0,1:T(8,128)} %param.9) | copy-start | bytes 10756
  3.5 8.2 %copy-start.2 = (bf16[1,384,1024]{2,1,0:T(8,128)(2,1)S(1)}, bf16[1,384,1024]{2,1,0:T(8,128)(2,1)}, u32[]{:S(2)}) copy-start(bf16[1,384,1024]{2,1,0:T(8,128)(2,1)} %param.13) | copy-start | bytes 2359300
  3.5 39.1 %collective-permute-start.7 = (bf16[512,384]{1,0:T(8,128)(2,1)}, bf16[512,384]{1,0:T(8,128)(2,1)S(1)}, u32[]{:S(2)}, u32[]{:S(2)}) collective-permute-start(bf16[512,384]{1,0:T(8,128)(2,1)} %dynamic-slice_bitcast_fusion.1), channel_id=1, source_target_pairs={{0,8},{1,9},{2,10},{3,11},{4,12},{5,13},{6,14},{7,15},{8,0},{9,1},... | collective-permute-start | bytes 1179656 | tf_op jit(solution)/shard_map/swap/ppermute | solution.py:186
  7.9 47.0 %copy-start.1 = (bf16[1,1024,384]{2,1,0:T(8,128)(2,1)S(1)}, bf16[1,1024,384]{2,1,0:T(8,128)(2,1)}, u32[]{:S(2)}) copy-start(bf16[1,1024,384]{2,1,0:T(8,128)(2,1)} %param.12) | copy-start | bytes 2359300
  7.9 43.2 %collective-permute-start.6 = (bf16[512,384]{1,0:T(8,128)(2,1)}, bf16[512,384]{1,0:T(8,128)(2,1)}, u32[]{:S(2)}, u32[]{:S(2)}) collective-permute-start(bf16[512,384]{1,0:T(8,128)(2,1)} %dynamic-slice_bitcast_fusion.2), channel_id=1, source_target_pairs={{0,8},{1,9},{2,10},{3,11},{4,12},{5,13},{6,14},{7,15},{8,0},{9,1},... | collective-permute-start | bytes 1179656 | tf_op jit(solution)/shard_map/swap/ppermute | solution.py:186
  9.7 45.2 %copy-start.3 = (s32[16]{0:T(128)S(1)}, s32[16]{0:T(128)}, u32[]{:S(2)}) copy-start(s32[16]{0:T(128)} %placement.7) | copy-start | bytes 196
  9.8 44.7 %collective-permute-start.3 = (bf16[112,1152]{1,0:T(8,128)(2,1)S(1)}, bf16[112,1152]{1,0:T(8,128)(2,1)S(1)}, u32[]{:S(2)}, u32[]{:S(2)}) collective-permute-start(bf16[112,1152]{1,0:T(8,128)(2,1)S(1)} %fusion.1.refs_0_), channel_id=1, source_target_pairs={{0,4},{1,5},{2,6},{3,7},{4,0},{5,1},{6,2},{7,3},{8,12},{9,13},{10,... | collective-permute-start | bytes 774152 | tf_op jit(solution)/shard_map/tokens/ppermute | solution.py:186
  11.8 56.9 %collective-permute-start.12 = (bf16[384,512]{1,0:T(8,128)(2,1)S(1)}, bf16[384,512]{1,0:T(8,128)(2,1)S(1)}, u32[]{:S(2)}, u32[]{:S(2)}) collective-permute-start(bf16[384,512]{1,0:T(8,128)(2,1)S(1)} %dynamic-slice_bitcast_fusion), channel_id=1, source_target_pairs={{0,8},{1,9},{2,10},{3,11},{4,12},{5,13},{6,14},{7,15},{8,0},{9,1},... | collective-permute-start | bytes 1179656 | tf_op jit(solution)/shard_map/swap/ppermute | solution.py:186
  42.6 26.1 %collective-permute-start.9 = (bf16[512,384]{1,0:T(8,128)(2,1)S(1)}, bf16[512,384]{1,0:T(8,128)(2,1)S(1)}, u32[]{:S(2)}, u32[]{:S(2)}) collective-permute-start(bf16[512,384]{1,0:T(8,128)(2,1)S(1)} %collective-permute-done.7.refs_5_.came), channel_id=1, source_target_pairs={{0,16},{16,0},{1,17},{17,1},{2,18},{18,2},{3,19},{19,3},{4,20},{20... | collective-permute-start | bytes 1179656 | tf_op jit(solution)/shard_map/trade/ppermute | solution.py:190
  51.1 18.1 %collective-permute-start.8 = (bf16[512,384]{1,0:T(8,128)(2,1)}, bf16[512,384]{1,0:T(8,128)(2,1)S(1)}, u32[]{:S(2)}, u32[]{:S(2)}) collective-permute-start(bf16[512,384]{1,0:T(8,128)(2,1)} %collective-permute-done.6.refs_4_.came), channel_id=1, source_target_pairs={{0,16},{16,0},{1,17},{17,1},{2,18},{18,2},{3,19},{19,3},{4,20},{20... | collective-permute-start | bytes 1179656 | tf_op jit(solution)/shard_map/trade/ppermute | solution.py:190
  52.9 9.2 %collective-permute-start.4 = (bf16[112,1152]{1,0:T(8,128)(2,1)S(1)}, bf16[112,1152]{1,0:T(8,128)(2,1)S(1)}, u32[]{:S(2)}, u32[]{:S(2)}) collective-permute-start(bf16[112,1152]{1,0:T(8,128)(2,1)S(1)} %fusion.1.refs_0_), channel_id=1, source_target_pairs={{0,2},{1,3},{2,0},{3,1},{4,6},{5,7},{6,4},{7,5},{8,10},{9,11},{10,... | collective-permute-start | bytes 774152 | tf_op jit(solution)/shard_map/tokens/ppermute | solution.py:186
  54.4 11.1 %collective-permute-start.5 = (bf16[112,1152]{1,0:T(8,128)(2,1)S(1)}, bf16[112,1152]{1,0:T(8,128)(2,1)S(1)}, u32[]{:S(2)}, u32[]{:S(2)}) collective-permute-start(bf16[112,1152]{1,0:T(8,128)(2,1)S(1)} %collective-permute-done.3.refs_1_), channel_id=1, source_target_pairs={{0,2},{1,3},{2,0},{3,1},{4,6},{5,7},{6,4},{7,5},{8,10},{9,11},{10,... | collective-permute-start | bytes 774152 | tf_op jit(solution)/shard_map/tokens/ppermute | solution.py:186
  62.1 7.9 %collective-permute-start.10 = (bf16[512,384]{1,0:T(8,128)(2,1)}, bf16[512,384]{1,0:T(8,128)(2,1)S(1)}, u32[]{:S(2)}, u32[]{:S(2)}) collective-permute-start(bf16[512,384]{1,0:T(8,128)(2,1)} %collective-permute-done.6.refs_4_.came), channel_id=1, source_target_pairs={{0,1},{1,0},{2,3},{3,2},{4,5},{5,4},{6,7},{7,6},{8,9},{9,8},{10,11... | collective-permute-start | bytes 1179656 | tf_op jit(solution)/shard_map/z_near/ppermute | solution.py:186
  65.5 4.7 %collective-permute-start.11 = (bf16[512,384]{1,0:T(8,128)(2,1)S(1)}, bf16[512,384]{1,0:T(8,128)(2,1)S(1)}, u32[]{:S(2)}, u32[]{:S(2)}) collective-permute-start(bf16[512,384]{1,0:T(8,128)(2,1)S(1)} %collective-permute-done.7.refs_5_.came), channel_id=1, source_target_pairs={{0,1},{1,0},{2,3},{3,2},{4,5},{5,4},{6,7},{7,6},{8,9},{9,8},{10,11... | collective-permute-start | bytes 1179656 | tf_op jit(solution)/shard_map/z_near/ppermute | solution.py:186
  68.7 1.9 %collective-permute-start.14 = (bf16[512,384]{1,0:T(8,128)(2,1)S(1)}, bf16[512,384]{1,0:T(8,128)(2,1)S(1)}, u32[]{:S(2)}, u32[]{:S(2)}) collective-permute-start(bf16[512,384]{1,0:T(8,128)(2,1)S(1)} %collective-permute-done.9.refs_7_.other), channel_id=1, source_target_pairs={{0,1},{1,0},{2,3},{3,2},{4,5},{5,4},{6,7},{7,6},{8,9},{9,8},{10,11... | collective-permute-start | bytes 1179656 | tf_op jit(solution)/shard_map/y_near/ppermute | solution.py:186
  69.3 1.9 %collective-permute-start.13 = (bf16[512,384]{1,0:T(8,128)(2,1)S(1)}, bf16[512,384]{1,0:T(8,128)(2,1)S(1)}, u32[]{:S(2)}, u32[]{:S(2)}) collective-permute-start(bf16[512,384]{1,0:T(8,128)(2,1)S(1)} %collective-permute-done.8.refs_6_.other), channel_id=1, source_target_pairs={{0,1},{1,0},{2,3},{3,2},{4,5},{5,4},{6,7},{7,6},{8,9},{9,8},{10,11... | collective-permute-start | bytes 1179656 | tf_op jit(solution)/shard_map/y_near/ppermute | solution.py:186
  69.4 11.5 %collective-permute-start.15 = (bf16[384,512]{1,0:T(8,128)(2,1)S(1)}, bf16[384,512]{1,0:T(8,128)(2,1)S(1)}, u32[]{:S(2)}, u32[]{:S(2)}) collective-permute-start(bf16[384,512]{1,0:T(8,128)(2,1)S(1)} %collective-permute-done.12.refs_3_.came), channel_id=1, source_target_pairs={{0,16},{16,0},{1,17},{17,1},{2,18},{18,2},{3,19},{19,3},{4,20},{20... | collective-permute-start | bytes 1179656 | tf_op jit(solution)/shard_map/trade/ppermute | solution.py:190
  70.0 10.8 %collective-permute-start.16 = (bf16[384,512]{1,0:T(8,128)(2,1)S(1)}, bf16[384,512]{1,0:T(8,128)(2,1)S(1)}, u32[]{:S(2)}, u32[]{:S(2)}) collective-permute-start(bf16[384,512]{1,0:T(8,128)(2,1)S(1)} %collective-permute-done.12.refs_3_.came), channel_id=1, source_target_pairs={{0,1},{1,0},{2,3},{3,2},{4,5},{5,4},{6,7},{7,6},{8,9},{9,8},{10,11... | collective-permute-start | bytes 1179656 | tf_op jit(solution)/shard_map/z_near/ppermute | solution.py:186
  80.8 1.7 %collective-permute-start.17 = (bf16[384,512]{1,0:T(8,128)(2,1)S(1)}, bf16[384,512]{1,0:T(8,128)(2,1)S(1)}, u32[]{:S(2)}, u32[]{:S(2)}) collective-permute-start(bf16[384,512]{1,0:T(8,128)(2,1)S(1)} %collective-permute-done.15.refs_4_.other), channel_id=1, source_target_pairs={{0,1},{1,0},{2,3},{3,2},{4,5},{5,4},{6,7},{7,6},{8,9},{9,8},{10,11... | collective-permute-start | bytes 1179656 | tf_op jit(solution)/shard_map/y_near/ppermute | solution.py:186
  83.8 8.5 %collective-permute-start.19 = (bf16[112,1024]{1,0:T(8,128)(2,1)S(1)}, bf16[112,1024]{1,0:T(8,128)(2,1)S(1)}, u32[]{:S(2)}, u32[]{:S(2)}) collective-permute-start(bf16[112,1024]{1,0:T(8,128)(2,1)S(1)} %get-tuple-element.31), channel_id=1, source_target_pairs={{0,2},{1,3},{2,0},{3,1},{4,6},{5,7},{6,4},{7,5},{8,10},{9,11},{10,... | collective-permute-start | bytes 688136 | tf_op jit(solution)/shard_map/sums/ppermute | solution.py:186
  85.3 13.0 %collective-permute-start.18 = (bf16[112,1024]{1,0:T(8,128)(2,1)S(1)}, bf16[112,1024]{1,0:T(8,128)(2,1)S(1)}, u32[]{:S(2)}, u32[]{:S(2)}) collective-permute-start(bf16[112,1024]{1,0:T(8,128)(2,1)S(1)} %get-tuple-element.29), channel_id=1, source_target_pairs={{0,2},{1,3},{2,0},{3,1},{4,6},{5,7},{6,4},{7,5},{8,10},{9,11},{10,... | collective-permute-start | bytes 688136 | tf_op jit(solution)/shard_map/sums/ppermute | solution.py:186
  92.3 1.2 %copy-start.4 = (s32[16]{0:T(128)S(1)}, s32[16]{0:T(128)}, u32[]{:S(2)}) copy-start(s32[16]{0:T(128)} %flags.5) | copy-start | bytes 196
  92.3 6.1 %collective-permute-start.20 = (bf16[112,1024]{1,0:T(8,128)(2,1)S(1)}, bf16[112,1024]{1,0:T(8,128)(2,1)S(1)}, u32[]{:S(2)}, u32[]{:S(2)}) collective-permute-start(bf16[112,1024]{1,0:T(8,128)(2,1)S(1)} %add_convert_fusion.1), channel_id=1, source_target_pairs={{0,4},{1,5},{2,6},{3,7},{4,0},{5,1},{6,2},{7,3},{8,12},{9,13},{10,... | collective-permute-start | bytes 688136 | tf_op jit(solution)/shard_map/sums/ppermute | solution.py:186

commit v2 on v1

v2 whole, which is shorter than its diff:
```python
import functools

import jax
import jax.numpy as jnp
from jax import lax
from jax.experimental import pallas as pl
from jax.experimental.pallas import tpu as pltpu
from jax.sharding import PartitionSpec as P

LANES = 128
VMEM_LIMIT = 20 * 2**20


def split_parts(values):
    parts = []
    for _ in range(3):
        part = lax.reduce_precision(values, exponent_bits=8, mantissa_bits=7)
        parts.append(part.astype(jnp.bfloat16))
        values = values - part
    return parts


def pack_gates(tokens, expert_ids, gate_probs, count):
    experts = jnp.arange(count, dtype=jnp.int32)
    chosen = expert_ids[:, None, :] == experts[None, :, None]
    weights = jnp.sum(jnp.where(chosen, gate_probs[:, None, :], 0.0), axis=2)
    parts = jnp.concatenate(split_parts(weights), axis=1)
    parts = jnp.pad(parts, ((0, 0), (0, -parts.shape[1] % LANES)))
    return jnp.concatenate([tokens, parts], axis=1)


def dot(a, b):
    return jnp.dot(a, b, preferred_element_type=jnp.float32)


def token_weight(tail, expert, count):
    lane = lax.broadcasted_iota(jnp.int32, tail.shape, 1)
    mine = (lane % count == expert) & (lane < 3 * count)
    return jnp.sum(jnp.where(mine, tail.astype(jnp.float32), 0.0), axis=1, keepdims=True)


def activate(gate, up):
    return (gate / (1.0 + jnp.exp(-gate)) * up).astype(jnp.bfloat16)


def rounded(value):
    return value.astype(jnp.bfloat16).astype(jnp.float32)


def near_kernel(count, placement, *refs):
    rows, weights, outs, x = refs[:2], (refs[2:5], refs[5:8]), refs[8:10], refs[10]
    height, width = rows[0].shape[0], x.shape[1]
    me = lax.axis_index("expert")
    for i in range(2):
        x[i * height : (i + 1) * height, :] = rows[i][:, :width]
    totals = [0.0, 0.0]
    for flip, (g, u, d) in enumerate(weights):
        hidden = activate(dot(x[...], g[...]), dot(x[...], u[...]))
        value = rounded(dot(hidden, d[...]))
        for i in range(2):
            weight = token_weight(rows[i][:, width:], placement[me ^ flip], count)
            totals[i] = totals[i] + value[i * height : (i + 1) * height, :] * weight
    for i in range(2):
        outs[i][...] = totals[i]


def hidden_kernel(blocks, width, *refs):
    rows, weights, out, x = refs[:blocks], refs[blocks : blocks + 4], refs[blocks + 4], refs[blocks + 5]
    height = rows[0].shape[0]
    half = lax.axis_index("dp") % 2
    for first in range(0, blocks, 2):
        for i in range(2):
            x[i * height : (i + 1) * height, :] = rows[first + i][:, :width]
        for slot in range(2):
            own, other = weights[2 * slot : 2 * slot + 2]
            depth, ff = own.shape[0] // 2, own.shape[1]
            at = pl.multiple_of(half * depth, depth)
            off = pl.multiple_of(depth - at, depth)
            xa, xb = x[:, pl.ds(at, depth)], x[:, pl.ds(off, depth)]
            gate = dot(xa, own[:depth, :]) + dot(xb, other[:depth, :])
            up = dot(xa, own[depth:, :]) + dot(xb, other[depth:, :])
            span = slice(first * height, (first + 2) * height)
            out[span, slot * ff : (slot + 1) * ff] = activate(gate, up)


def down_kernel(count, first, flip, placement, *refs):
    rows, hidden, downs, base, outs = refs[:2], refs[2], refs[3:5], refs[5:7], refs[7:9]
    height, part = outs[0].shape
    ff = downs[0].shape[0]
    me = lax.axis_index("expert")
    far = lax.axis_size("expert") // 2
    half = (lax.axis_index("dp") + flip) % 2
    columns = pl.ds(pl.multiple_of(half * part, part), part)
    totals = [base[i][:, columns] for i in range(2)]
    for slot, down in enumerate(downs):
        span = slice(first * height, (first + 2) * height)
        value = rounded(dot(hidden[span, slot * ff : (slot + 1) * ff], down[...]))
        for i in range(2):
            weight = token_weight(rows[i][:, base[0].shape[1]:], placement[me ^ far ^ slot], count)
            totals[i] = totals[i] + value[i * height : (i + 1) * height, :] * weight
    for i in range(2):
        outs[i][...] = totals[i].astype(outs[i].dtype)


def call(kernel, out_shape, args, scratch=(), scalars=0):
    vmem = pl.BlockSpec(memory_space=pltpu.VMEM)
    smem = pl.BlockSpec(memory_space=pltpu.SMEM)
    return pl.pallas_call(
        kernel,
        out_shape=out_shape,
        in_specs=[smem] * scalars + [vmem] * (len(args) - scalars),
        out_specs=jax.tree.map(lambda _: vmem, out_shape),
        scratch_shapes=list(scratch),
        compiler_params=pltpu.CompilerParams(vmem_limit_bytes=VMEM_LIMIT),
        cost_estimate=pl.CostEstimate(flops=0, bytes_accessed=0, transcendentals=0),
    )(*args)


def run_copies(copies, sems):
    copies = [pltpu.make_async_copy(a, b, sems.at[i]) for i, (a, b) in enumerate(copies)]
    for copy in copies:
        copy.start()
    for copy in copies:
        copy.wait()


def part_of(ref, axis, half, size):
    span = pl.ds(pl.multiple_of(half * size, size), size)
    return ref.at[span, :] if axis == 0 else ref.at[:, span]


def store_kernel(axis, first, flags, own, came, other, out, sems):
    half = lax.axis_index("dp") % 2
    size = out.shape[axis] // 2
    taken = flags[lax.axis_index("expert")] == 1

    @pl.when(taken)
    def _():
        if axis == 0:
            parts = [ref.at[pl.ds(first, size), :] for ref in (came, other)]
        else:
            parts = [came, other]
        run_copies(
            [
                (parts[0], part_of(out, axis, half, size)),
                (parts[1], part_of(out, axis, 1 - half, size)),
            ],
            sems,
        )

    @pl.when(jnp.logical_not(taken))
    def _():
        run_copies([(own, out)], sems)


def store(axis, first, flags, own, came, other):
    vmem = pl.BlockSpec(memory_space=pltpu.VMEM)
    return pl.pallas_call(
        functools.partial(store_kernel, axis, first),
        out_shape=jax.ShapeDtypeStruct(own.shape, own.dtype),
        in_specs=[pl.BlockSpec(memory_space=pltpu.SMEM)] + [vmem] * 3,
        out_specs=pl.BlockSpec(memory_space=pl.ANY),
        scratch_shapes=[pltpu.SemaphoreType.DMA((2,))],
        compiler_params=pltpu.CompilerParams(vmem_limit_bytes=8 * 2**20),
        cost_estimate=pl.CostEstimate(flops=0, bytes_accessed=0, transcendentals=0),
    )(flags, own, came, other)


def after(value, *others):
    return lax.optimization_barrier((value, *others))[0]


def per_device(tokens, expert_ids, gate_probs, w_gate, w_up, w_down, placement, swap_flags):
    count = lax.axis_size("expert")
    couple = lax.axis_index("dp") % 2
    half_axis = count // 2
    height, width = tokens.shape
    own = (w_gate[0], w_up[0], w_down[0])
    ff = own[0].shape[1]
    trades = [(d, d ^ 1) for d in range(lax.axis_size("dp"))]

    def send(value, bit, name):
        with jax.named_scope(name):
            return lax.ppermute(value, "expert", [(d, d ^ bit) for d in range(count)])

    def trade(value):
        with jax.named_scope("trade"):
            return lax.ppermute(value, "dp", trades)

    depth, part = own[0].shape[0] // 2, width // 2

    def half_of(first, second):
        return jnp.where(couple == 0, first, second)

    upper = half_of(
        jnp.concatenate([own[0][:depth], own[1][:depth]], axis=0),
        jnp.concatenate([own[0][depth:], own[1][depth:]], axis=0),
    )
    lower = half_of(own[2][:, :part], own[2][:, part:])

    bits = []
    bit = half_axis // 2
    while bit > 1:
        bits.append(bit)
        bit //= 2
    blocks = {0: pack_gates(tokens, expert_ids, gate_probs, count)}
    for stage, bit in enumerate(bits):
        for i in sorted(blocks):
            blocks[i | 1 << stage] = send(blocks[i], bit, "tokens")
    rows = [blocks[i] for i in range(len(blocks))]

    z_upper = send(upper, half_axis, "swap")
    z_lower = send(after(lower, z_upper, *rows), half_axis, "swap")
    y_upper = trade(after(z_upper, *rows))
    near = [send(after(w, lower), 1, "near") for w in own]

    firsts = list(reversed(range(0, len(rows), 2)))
    scratch = [pltpu.VMEM((2 * height, width), jnp.bfloat16)]
    base = {}
    for first in firsts:
        base[first] = call(
            functools.partial(near_kernel, count),
            [jax.ShapeDtypeStruct((height, width), jnp.float32)] * 2,
            [placement, *rows[first : first + 2], *own, *near],
            scratch,
            scalars=1,
        )

    arrived = after(z_lower, base)
    y_lower = trade(arrived)
    z_near = [send(z_upper, 1, "z_near"), send(arrived, 1, "z_near")]
    y_near = [send(after(y_upper, arrived), 1, "y_near")]
    hidden = call(
        functools.partial(hidden_kernel, len(rows), width),
        jax.ShapeDtypeStruct((len(rows) * height, 2 * ff), jnp.bfloat16),
        [*rows, z_upper, y_upper, z_near[0], y_near[0]],
        scratch,
    )

    def far_sums(flip, downs):
        parts = {}
        for first in firsts:
            dtype = jnp.bfloat16 if first >= len(rows) // 2 else jnp.float32
            parts[first], parts[first + 1] = call(
                functools.partial(down_kernel, count, first, flip),
                [jax.ShapeDtypeStruct((height, downs[0].shape[1]), dtype)] * 2,
                [placement, *rows[first : first + 2], hidden, *downs, *base[first]],
                scalars=1,
            )
        return parts

    def collect(parts, stages, *others):
        for stage in stages:
            for i in reversed(range(1 << stage)):
                part = parts[i | 1 << stage].astype(jnp.bfloat16)
                came = after(send(part, bits[stage], "sums"), *others)
                parts[i] = parts[i] + came.astype(jnp.float32)
        return parts[0].astype(jnp.bfloat16)

    stages = list(reversed(range(len(bits))))
    parts = far_sums(0, [arrived, z_near[1]])
    flags = after(swap_flags, parts)
    stored = [
        store(0, 0, flags, own[0], z_upper, y_upper),
        store(0, depth, flags, own[1], z_upper, y_upper),
    ]
    landed = after(y_lower, stored)
    collect(parts, stages[:1], landed)
    y_near.append(send(after(landed, parts), 1, "y_near"))
    last_parts = far_sums(1, [landed, y_near[1]])
    stored.append(store(1, 0, after(swap_flags, last_parts), own[2], z_lower, y_lower))
    parts = after(parts, last_parts[firsts[0]])
    mixed = [collect(parts, stages[1:]), collect(last_parts, stages)]
    mixed = half_of(jnp.concatenate(mixed, axis=1), jnp.concatenate(mixed[::-1], axis=1))
    return (mixed, *(w[None] for w in stored))


def solution(mesh):
    in_specs = (
        P(("dp", "expert"), None),
        P(("dp", "expert"), None),
        P(("dp", "expert"), None),
        P("expert", None, None),
        P("expert", None, None),
        P("expert", None, None),
        P(),
        P(),
    )
    out_specs = (
        P(("dp", "expert"), None),
        P(("dp", "expert"), None, None),
        P(("dp", "expert"), None, None),
        P(("dp", "expert"), None, None),
    )
    return jax.shard_map(
        per_device, mesh=mesh, in_specs=in_specs, out_specs=out_specs, check_vma=False
    )
```

time: 99.5 us -> 89.4 us (0.90)
  waiting for transfers between devices: 56.8 us -> 53.2 us
  starting transfers between devices: 19.6 us -> 17.2 us
  Pallas kernels: 16.8 us -> 15 us
  local copies, waits for them, and re-layouts: 3.36 us -> 1.67 us
    ppermute x3 -> x2, waiting for transfers between devices: 6.44 us -> 0.14 us  [trade(): return lax.ppermute(value, 'dp', trades)]
    ppermute x18, waiting for transfers between devices: 50.4 us -> 53.1 us  [send(): return lax.ppermute(value, 'expert', [(d, d ^ bit) for d in range(count)])]
    dynamic_slice x3 -> x0, local copies, waits for them, and re-layouts: 2.62 us -> none  [per_device(): halves.append(lax.dynamic_slice_in_dim(w, couple * size, size, axis=axis))]
    ppermute x3 -> x2, starting transfers between devices: 4.19 us -> 2.32 us  [trade(): return lax.ppermute(value, 'dp', trades)]
    slice x0 -> x1, local copies, waits for them, and re-layouts: none -> 1.52 us  [per_device(): own[1][depth:]]
    pallas_call x5 -> x7, Pallas kernels: 12 us -> 10.6 us  [call(): pl.pallas_call(kernel, out_shape=out_shape, in_specs=[smem] * scalars + [...]
    select_n x0 -> x3, other arithmetic: none -> 1.02 us  [half_of(): return jnp.where(couple == 0, first, second)]
  transfers between devices with their start and end apart: 21 -> 20, of which waited for: 10 -> 11; matrix products, arithmetic and copies ran while one was open for 4% -> 0% of each run, Pallas kernels for 16% -> 16%
where the time goes in v2:
time: 89.4 us; the launch traced here: 89.2 us
  waiting for transfers between devices  53.2 us (60%)
  starting transfers between devices  17.2 us (19%)
  Pallas kernels  15 us (17%)
  local copies, waits for them, and re-layouts  1.67 us (2%)
  other arithmetic  1.24 us (1%)
  between operations  0.94 us (1%)
    ppermute x18, waiting for transfers between devices, send(): return lax.ppermute(value, 'expert', [(d, d ^ bit) for d in range(count)])  53.1 us
    ppermute x18, starting transfers between devices, send(): return lax.ppermute(value, 'expert', [(d, d ^ bit) for d in range(count)])  14.9 us
    pallas_call x7, Pallas kernels, call(): pl.pallas_call(kernel, out_shape=out_shape, in_specs=[smem] * scalars + [...  10.6 us
    pallas_call x3, Pallas kernels, store(): pl.pallas_call(functools.partial(store_kernel, axis, first), out_shape=ja...  4.35 us
    ppermute x2, starting transfers between devices, trade(): return lax.ppermute(value, 'dp', trades)  2.32 us
  transfers between devices with their start and end apart: 20, of which 11 were waited for; matrix products, arithmetic and copies ran while one was open for 0% of the time, Pallas kernels for 16%

profile of v2, /device:TPU:0, one launch (start us, length us, event | category | flops | bytes accessed | tf_op | source)
XLA Modules:
  0.0 89.2 jit_solution(4492175611060060897)
XLA Ops:
  0.6 1.5 %slice_bitcast_fusion = (bf16[512,384]{1,0:T(8,128)(2,1)S(1)}, bf16[512,384]{1,0:T(8,128)(2,1)S(1)}, bf16[512,384]{1,0:T(8,128)(2,1)S(1)}, bf16[512,384]{1,0:T(8,128)(2,1)S(1)}) fusion(bf16[1,1024,384]{2,1,0:T(8,128)(2,1)} %param.12, bf16[1,1024,384]{2,1,0:T(8,128)(2,1)} %param.11), kind=kLoop, calls=%fused_computation.4 | loop fusion | bytes 3145728 | tf_op jit(solution)/shard_map/slice | solution.py:197
  2.2 0.0 copy-start.6
  2.2 0.0 copy-start.7
  2.2 0.0 copy-start.5
  2.2 0.2 maximum_select_fusion
  2.4 4.1 %collective-permute-start.3 = (bf16[1024,384]{1,0:T(8,128)(2,1)S(1)}, bf16[1024,384]{1,0:T(8,128)(2,1)S(1)}, u32[]{:S(2)}, u32[]{:S(2)}) collective-permute-start(bf16[1024,384]{1,0:T(8,128)(2,1)S(1)} %maximum_select_fusion), channel_id=1, source_target_pairs={{0,8},{1,9},{2,10},{3,11},{4,12},{5,13},{6,14},{7,15},{8,0},{9,1},... | collective-permute-start | bytes 2359304 | tf_op jit(solution)/shard_map/swap/ppermute | solution.py:184
  6.6 0.1 copy.17
  6.7 0.0 copy-start.2
  6.7 0.0 copy-start.1
  6.8 1.6 %collective-permute-start = (bf16[112,1152]{1,0:T(8,128)(2,1)S(1)}, bf16[112,1152]{1,0:T(8,128)(2,1)S(1)}, u32[]{:S(2)}, u32[]{:S(2)}) collective-permute-start(bf16[112,1152]{1,0:T(8,128)(2,1)S(1)} %fusion.1.refs_0_), channel_id=1, source_target_pairs={{0,4},{1,5},{2,6},{3,7},{4,0},{5,1},{6,2},{7,3},{8,12},{9,13},{10,... | collective-permute-start | bytes 774152 | tf_op jit(solution)/shard_map/tokens/ppermute | solution.py:184
  8.4 1.5 %collective-permute-start.1 = (bf16[112,1152]{1,0:T(8,128)(2,1)S(1)}, bf16[112,1152]{1,0:T(8,128)(2,1)S(1)}, u32[]{:S(2)}, u32[]{:S(2)}) collective-permute-start(bf16[112,1152]{1,0:T(8,128)(2,1)S(1)} %fusion.1.refs_0_), channel_id=1, source_target_pairs={{0,2},{1,3},{2,0},{3,1},{4,6},{5,7},{6,4},{7,5},{8,10},{9,11},{10,... | collective-permute-start | bytes 774152 | tf_op jit(solution)/shard_map/tokens/ppermute | solution.py:184
  9.9 19.0 %collective-permute-done.refs_1_ = bf16[112,1152]{1,0:T(8,128)(2,1)S(1)} collective-permute-done((bf16[112,1152]{1,0:T(8,128)(2,1)S(1)}, bf16[112,1152]{1,0:T(8,128)(2,1)S(1)}, u32[]{:S(2)}, u32[]{:S(2)}) %collective-permute-start) | collective-permute-done | bytes 258080 | tf_op jit(solution)/shard_map/tokens/ppermute | solution.py:184
  28.9 1.5 %collective-permute-start.2 = (bf16[112,1152]{1,0:T(8,128)(2,1)S(1)}, bf16[112,1152]{1,0:T(8,128)(2,1)S(1)}, u32[]{:S(2)}, u32[]{:S(2)}) collective-permute-start(bf16[112,1152]{1,0:T(8,128)(2,1)S(1)} %collective-permute-done.refs_1_), channel_id=1, source_target_pairs={{0,2},{1,3},{2,0},{3,1},{4,6},{5,7},{6,4},{7,5},{8,10},{9,11},{10,... | collective-permute-start | bytes 774152 | tf_op jit(solution)/shard_map/tokens/ppermute | solution.py:184
  30.4 0.1 collective-permute-start.9
  30.5 0.5 collective-permute-start.7
  31.0 0.1 collective-permute-start.8
  31.1 4.9 %collective-permute-done.2.refs_1_.refs_3_ = bf16[112,1152]{1,0:T(8,128)(2,1)S(1)} collective-permute-done((bf16[112,1152]{1,0:T(8,128)(2,1)S(1)}, bf16[112,1152]{1,0:T(8,128)(2,1)S(1)}, u32[]{:S(2)}, u32[]{:S(2)}) %collective-permute-start.2) | collective-permute-done | bytes 258080 | tf_op jit(solution)/shard_map/tokens/ppermute | solution.py:184
  36.0 4.9 %collective-permute-done.3.refs_4_.came = bf16[1024,384]{1,0:T(8,128)(2,1)S(1)} collective-permute-done((bf16[1024,384]{1,0:T(8,128)(2,1)S(1)}, bf16[1024,384]{1,0:T(8,128)(2,1)S(1)}, u32[]{:S(2)}, u32[]{:S(2)}) %collective-permute-start.3) | collective-permute-done | bytes 786464 | tf_op jit(solution)/shard_map/swap/ppermute | solution.py:184
  40.9 1.6 %collective-permute-start.4 = (bf16[1024,384]{1,0:T(8,128)(2,1)S(1)}, bf16[1024,384]{1,0:T(8,128)(2,1)S(1)}, u32[]{:S(2)}, u32[]{:S(2)}) collective-permute-start(bf16[1024,384]{1,0:T(8,128)(2,1)S(1)} %collective-permute-done.3.refs_4_.came), channel_id=1, source_target_pairs={{0,16},{16,0},{1,17},{17,1},{2,18},{18,2},{3,19},{19,3},{4,20},{20... | collective-permute-start | bytes 2359304 | tf_op jit(solution)/shard_map/trade/ppermute | solution.py:188
  42.5 2.3 %shard_map.112 = (f32[112,1024]{1,0:T(8,128)S(1)}, f32[112,1024]{1,0:T(8,128)S(1)}) custom-call(s32[16]{0:T(128)S(1)} %copy-done.3, bf16[112,1152]{1,0:T(8,128)(2,1)S(1)} %collective-permute-done.1.refs_0_.refs_2_, bf16[112,1152]{1,0:T(8,128)(2,1)S(1)} %collective-permute-done.2.refs_1_.refs_3_, bf16[1024,384]{1,0:T(8,128)(2,1)S(1)} %bitcast.24, ...), custom_call_target="tpu_custom_call" | custom-call | tf_op jit(solution)/shard_map/pallas_call | solution.py:108
  44.9 2.3 %shard_map.111 = (f32[112,1024]{1,0:T(8,128)S(1)}, f32[112,1024]{1,0:T(8,128)S(1)}) custom-call(s32[16]{0:T(128)S(1)} %copy-done.3, bf16[112,1152]{1,0:T(8,128)(2,1)S(1)} %fusion.1.refs_0_, bf16[112,1152]{1,0:T(8,128)(2,1)S(1)} %collective-permute-done.refs_1_, bf16[1024,384]{1,0:T(8,128)(2,1)S(1)} %bitcast.25, bf16[1024,384]{1,0:T(8,128)(2,1)S(1)} %bitcast.21, ...), custom_call_target="tpu_custom_call" | custom-call | tf_op jit(solution)/shard_map/pallas_call | solution.py:108
  47.2 0.1 collective-permute-start.5
  47.3 14.3 %collective-permute-done.6.refs_3_.came = bf16[384,512]{1,0:T(8,128)(2,1)S(1)} collective-permute-done((bf16[384,512]{1,0:T(8,128)(2,1)S(1)}, bf16[384,512]{1,0:T(8,128)(2,1)S(1)}, u32[]{:S(2)}, u32[]{:S(2)}) %collective-permute-start.6) | collective-permute-done | bytes 393248 | tf_op jit(solution)/shard_map/swap/ppermute | solution.py:184
  61.5 0.5 collective-permute-start.11
  62.1 0.8 collective-permute-start.13
  62.8 1.0 %collective-permute-done.10.refs_7_ = bf16[1024,384]{1,0:T(8,128)(2,1)S(1)} collective-permute-done((bf16[1024,384]{1,0:T(8,128)(2,1)S(1)}, bf16[1024,384]{1,0:T(8,128)(2,1)S(1)}, u32[]{:S(2)}, u32[]{:S(2)}) %collective-permute-start.10) | collective-permute-done | bytes 786464 | tf_op jit(solution)/shard_map/y_near/ppermute | solution.py:184
  63.8 2.2 %shard_map.113.refs_2_ = bf16[448,768]{1,0:T(8,128)(2,1)S(1)} custom-call(bf16[112,1152]{1,0:T(8,128)(2,1)S(1)} %fusion.1.refs_0_, bf16[112,1152]{1,0:T(8,128)(2,1)S(1)} %collective-permute-done.refs_1_, bf16[112,1152]{1,0:T(8,128)(2,1)S(1)} %collective-permute-done.1.refs_0_.refs_2_, bf16[112,1152]{1,0:T(8,128)(2,1)S(1)} %collective-permute-done.2.refs_1_.refs_3_, ...), custom_call_target="tpu_custom_call" | custom-call | tf_op jit(solution)/shard_map/pallas_call | solution.py:108
  66.0 0.9 %shard_map.115 = (bf16[112,512]{1,0:T(8,128)(2,1)S(1)}, bf16[112,512]{1,0:T(8,128)(2,1)S(1)}) custom-call(s32[16]{0:T(128)S(1)} %copy-done.3, bf16[112,1152]{1,0:T(8,128)(2,1)S(1)} %collective-permute-done.1.refs_0_.refs_2_, bf16[112,1152]{1,0:T(8,128)(2,1)S(1)} %collective-permute-done.2.refs_1_.refs_3_, bf16[448,768]{1,0:T(8,128)(2,1)S(1)} %shard_map.113.refs_2_, ...), custom_call_target="tpu_custom_call" | custom-call | tf_op jit(solution)/shard_map/pallas_call | solution.py:108
  67.0 1.6 %collective-permute-start.14 = (bf16[112,512]{1,0:T(8,128)(2,1)S(1)}, bf16[112,512]{1,0:T(8,128)(2,1)S(1)}, u32[]{:S(2)}, u32[]{:S(2)}) collective-permute-start(bf16[112,512]{1,0:T(8,128)(2,1)S(1)} %get-tuple-element.45), channel_id=1, source_target_pairs={{0,2},{1,3},{2,0},{3,1},{4,6},{5,7},{6,4},{7,5},{8,10},{9,11},{10,... | collective-permute-start | bytes 344072 | tf_op jit(solution)/shard_map/sums/ppermute | solution.py:184
  68.6 0.5 collective-permute-start.12
  69.1 0.9 %shard_map.114 = (f32[112,512]{1,0:T(8,128)S(1)}, f32[112,512]{1,0:T(8,128)S(1)}) custom-call(s32[16]{0:T(128)S(1)} %copy-done.3, bf16[112,1152]{1,0:T(8,128)(2,1)S(1)} %fusion.1.refs_0_, bf16[112,1152]{1,0:T(8,128)(2,1)S(1)} %collective-permute-done.refs_1_, bf16[448,768]{1,0:T(8,128)(2,1)S(1)} %shard_map.113.refs_2_, ...), custom_call_target="tpu_custom_call" | custom-call | tf_op jit(solution)/shard_map/pallas_call | solution.py:108
  70.0 1.4 %shard_map.117 = bf16[1024,384]{1,0:T(8,128)(2,1)} custom-call(s32[16]{0:T(128)S(1)} %copy-done.4, bf16[1024,384]{1,0:T(8,128)(2,1)S(1)} %bitcast.22, bf16[1024,384]{1,0:T(8,128)(2,1)S(1)} %collective-permute-done.3.refs_4_.came, bf16[1024,384]{1,0:T(8,128)(2,1)S(1)} %collective-permute-done.4.refs_5_.other), custom_call_target="tpu_custom_call" | custom-call | tf_op jit(solution)/shard_map/pallas_call | solution.py:158
  71.5 1.4 %shard_map.116 = bf16[1024,384]{1,0:T(8,128)(2,1)} custom-call(s32[16]{0:T(128)S(1)} %copy-done.4, bf16[1024,384]{1,0:T(8,128)(2,1)S(1)} %bitcast.26, bf16[1024,384]{1,0:T(8,128)(2,1)S(1)} %collective-permute-done.3.refs_4_.came, bf16[1024,384]{1,0:T(8,128)(2,1)S(1)} %collective-permute-done.4.refs_5_.other), custom_call_target="tpu_custom_call" | custom-call | tf_op jit(solution)/shard_map/pallas_call | solution.py:158
  72.9 0.1 collective-permute-done.13.refs_3_.other
  73.1 1.6 %collective-permute-done.12 = bf16[112,512]{1,0:T(8,128)(2,1)S(1)} collective-permute-done((bf16[112,512]{1,0:T(8,128)(2,1)S(1)}, bf16[112,512]{1,0:T(8,128)(2,1)S(1)}, u32[]{:S(2)}, u32[]{:S(2)}) %collective-permute-start.12) | collective-permute-done | bytes 114720 | tf_op jit(solution)/shard_map/sums/ppermute | solution.py:184
  74.7 0.1 collective-permute-start.15
  74.8 1.7 %collective-permute-done.15.refs_4_ = bf16[384,512]{1,0:T(8,128)(2,1)S(1)} collective-permute-done((bf16[384,512]{1,0:T(8,128)(2,1)S(1)}, bf16[384,512]{1,0:T(8,128)(2,1)S(1)}, u32[]{:S(2)}, u32[]{:S(2)}) %collective-permute-start.15) | collective-permute-done | bytes 393248 | tf_op jit(solution)/shard_map/y_near/ppermute | solution.py:184
  76.5 0.9 %shard_map.118 = (bf16[112,512]{1,0:T(8,128)(2,1)S(1)}, bf16[112,512]{1,0:T(8,128)(2,1)S(1)}) custom-call(s32[16]{0:T(128)S(1)} %copy-done.3, bf16[112,1152]{1,0:T(8,128)(2,1)S(1)} %collective-permute-done.1.refs_0_.refs_2_, bf16[112,1152]{1,0:T(8,128)(2,1)S(1)} %collective-permute-done.2.refs_1_.refs_3_, bf16[448,768]{1,0:T(8,128)(2,1)S(1)} %shard_map.113.refs_2_, ...), custom_call_target="tpu_custom_call" | custom-call | tf_op jit(solution)/shard_map/pallas_call | solution.py:108
  77.5 1.6 %collective-permute-start.18 = (bf16[112,512]{1,0:T(8,128)(2,1)S(1)}, bf16[112,512]{1,0:T(8,128)(2,1)S(1)}, u32[]{:S(2)}, u32[]{:S(2)}) collective-permute-start(bf16[112,512]{1,0:T(8,128)(2,1)S(1)} %get-tuple-element.56), channel_id=1, source_target_pairs={{0,2},{1,3},{2,0},{3,1},{4,6},{5,7},{6,4},{7,5},{8,10},{9,11},{10,... | collective-permute-start | bytes 344072 | tf_op jit(solution)/shard_map/sums/ppermute | solution.py:184
  79.0 0.5 collective-permute-start.17
  79.6 0.9 %shard_map.119 = (f32[112,512]{1,0:T(8,128)S(1)}, f32[112,512]{1,0:T(8,128)S(1)}) custom-call(s32[16]{0:T(128)S(1)} %copy-done.3, bf16[112,1152]{1,0:T(8,128)(2,1)S(1)} %fusion.1.refs_0_, bf16[112,1152]{1,0:T(8,128)(2,1)S(1)} %collective-permute-done.refs_1_, bf16[448,768]{1,0:T(8,128)(2,1)S(1)} %shard_map.113.refs_2_, ...), custom_call_target="tpu_custom_call" | custom-call | tf_op jit(solution)/shard_map/pallas_call | solution.py:108
  80.5 0.1 collective-permute-start.16
  80.6 1.4 %shard_map.120 = bf16[384,1024]{1,0:T(8,128)(2,1)} custom-call(s32[16]{0:T(128)S(1)} %copy-done.4, bf16[384,1024]{1,0:T(8,128)(2,1)S(1)} %bitcast.18, bf16[384,512]{1,0:T(8,128)(2,1)S(1)} %collective-permute-done.6.refs_3_.came, bf16[384,512]{1,0:T(8,128)(2,1)S(1)} %collective-permute-done.13.refs_3_.other), custom_call_target="tpu_custom_call" | custom-call | tf_op jit(solution)/shard_map/pallas_call | solution.py:158
  82.0 1.5 %collective-permute-done.18 = bf16[112,512]{1,0:T(8,128)(2,1)S(1)} collective-permute-done((bf16[112,512]{1,0:T(8,128)(2,1)S(1)}, bf16[112,512]{1,0:T(8,128)(2,1)S(1)}, u32[]{:S(2)}, u32[]{:S(2)}) %collective-permute-start.18) | collective-permute-done | bytes 114720 | tf_op jit(solution)/shard_map/sums/ppermute | solution.py:184
  83.6 0.6 collective-permute-start.19
  84.2 1.9 %collective-permute-done.16 = bf16[112,512]{1,0:T(8,128)(2,1)S(1)} collective-permute-done((bf16[112,512]{1,0:T(8,128)(2,1)S(1)}, bf16[112,512]{1,0:T(8,128)(2,1)S(1)}, u32[]{:S(2)}, u32[]{:S(2)}) %collective-permute-start.16) | collective-permute-done | bytes 114720 | tf_op jit(solution)/shard_map/sums/ppermute | solution.py:184
  86.1 2.3 %collective-permute-done.19 = bf16[112,512]{1,0:T(8,128)(2,1)S(1)} collective-permute-done((bf16[112,512]{1,0:T(8,128)(2,1)S(1)}, bf16[112,512]{1,0:T(8,128)(2,1)S(1)}, u32[]{:S(2)}, u32[]{:S(2)}) %collective-permute-start.19) | collective-permute-done | bytes 114720 | tf_op jit(solution)/shard_map/sums/ppermute | solution.py:184
  88.5 0.8 maximum_select_fusion.1
  (32 shorter events, 0.3 us)
Async XLA Ops:
  2.2 4.4 %copy-start.6 = (f32[112,8]{0,1:T(8,128)S(1)}, f32[112,8]{0,1:T(8,128)}, u32[]{:S(2)}) copy-start(f32[112,8]{0,1:T(8,128)} %param.10) | copy-start | bytes 10756
  2.2 4.4 %copy-start.7 = (s32[112,8]{0,1:T(8,128)S(1)}, s32[112,8]{0,1:T(8,128)}, u32[]{:S(2)}) copy-start(s32[112,8]{0,1:T(8,128)} %param.9) | copy-start | bytes 10756
  2.2 4.5 %copy-start.5 = (bf16[112,1024]{1,0:T(8,128)(2,1)S(1)}, bf16[112,1024]{1,0:T(8,128)(2,1)}, u32[]{:S(2)}) copy-start(bf16[112,1024]{1,0:T(8,128)(2,1)} %param.8) | copy-start | bytes 688132
  2.2 28.2 %copy-start = (bf16[1,384,1024]{2,1,0:T(8,128)(2,1)S(1)}, bf16[1,384,1024]{2,1,0:T(8,128)(2,1)}, u32[]{:S(2)}) copy-start(bf16[1,384,1024]{2,1,0:T(8,128)(2,1)} %param.13) | copy-start | bytes 2359300
  2.4 38.5 %collective-permute-start.3 = (bf16[1024,384]{1,0:T(8,128)(2,1)S(1)}, bf16[1024,384]{1,0:T(8,128)(2,1)S(1)}, u32[]{:S(2)}, u32[]{:S(2)}) collective-permute-start(bf16[1024,384]{1,0:T(8,128)(2,1)S(1)} %maximum_select_fusion), channel_id=1, source_target_pairs={{0,8},{1,9},{2,10},{3,11},{4,12},{5,13},{6,14},{7,15},{8,0},{9,1},... | collective-permute-start | bytes 2359304 | tf_op jit(solution)/shard_map/swap/ppermute | solution.py:184
  6.7 23.8 %copy-start.2 = (bf16[1,1024,384]{2,1,0:T(8,128)(2,1)S(1)}, bf16[1,1024,384]{2,1,0:T(8,128)(2,1)}, u32[]{:S(2)}) copy-start(bf16[1,1024,384]{2,1,0:T(8,128)(2,1)} %param.11) | copy-start | bytes 2359300
  6.7 24.3 %copy-start.1 = (bf16[1,1024,384]{2,1,0:T(8,128)(2,1)S(1)}, bf16[1,1024,384]{2,1,0:T(8,128)(2,1)}, u32[]{:S(2)}) copy-start(bf16[1,1024,384]{2,1,0:T(8,128)(2,1)} %param.12) | copy-start | bytes 2359300
  6.7 35.8 %copy-start.3 = (s32[16]{0:T(128)S(1)}, s32[16]{0:T(128)}, u32[]{:S(2)}) copy-start(s32[16]{0:T(128)} %placement.11) | copy-start | bytes 196
  6.8 22.1 %collective-permute-start = (bf16[112,1152]{1,0:T(8,128)(2,1)S(1)}, bf16[112,1152]{1,0:T(8,128)(2,1)S(1)}, u32[]{:S(2)}, u32[]{:S(2)}) collective-permute-start(bf16[112,1152]{1,0:T(8,128)(2,1)S(1)} %fusion.1.refs_0_), channel_id=1, source_target_pairs={{0,4},{1,5},{2,6},{3,7},{4,0},{5,1},{6,2},{7,3},{8,12},{9,13},{10,... | collective-permute-start | bytes 774152 | tf_op jit(solution)/shard_map/tokens/ppermute | solution.py:184
  8.4 22.6 %collective-permute-start.1 = (bf16[112,1152]{1,0:T(8,128)(2,1)S(1)}, bf16[112,1152]{1,0:T(8,128)(2,1)S(1)}, u32[]{:S(2)}, u32[]{:S(2)}) collective-permute-start(bf16[112,1152]{1,0:T(8,128)(2,1)S(1)} %fusion.1.refs_0_), channel_id=1, source_target_pairs={{0,2},{1,3},{2,0},{3,1},{4,6},{5,7},{6,4},{7,5},{8,10},{9,11},{10,... | collective-permute-start | bytes 774152 | tf_op jit(solution)/shard_map/tokens/ppermute | solution.py:184
  28.9 7.1 %collective-permute-start.2 = (bf16[112,1152]{1,0:T(8,128)(2,1)S(1)}, bf16[112,1152]{1,0:T(8,128)(2,1)S(1)}, u32[]{:S(2)}, u32[]{:S(2)}) collective-permute-start(bf16[112,1152]{1,0:T(8,128)(2,1)S(1)} %collective-permute-done.refs_1_), channel_id=1, source_target_pairs={{0,2},{1,3},{2,0},{3,1},{4,6},{5,7},{6,4},{7,5},{8,10},{9,11},{10,... | collective-permute-start | bytes 774152 | tf_op jit(solution)/shard_map/tokens/ppermute | solution.py:184
  30.4 12.1 %collective-permute-start.9 = (bf16[384,1024]{1,0:T(8,128)(2,1)S(1)}, bf16[384,1024]{1,0:T(8,128)(2,1)S(1)}, u32[]{:S(2)}, u32[]{:S(2)}) collective-permute-start(bf16[384,1024]{1,0:T(8,128)(2,1)S(1)} %bitcast.15), channel_id=1, source_target_pairs={{0,1},{1,0},{2,3},{3,2},{4,5},{5,4},{6,7},{7,6},{8,9},{9,8},{10,11... | collective-permute-start | bytes 2359304 | tf_op jit(solution)/shard_map/near/ppermute | solution.py:184
  30.5 12.0 %collective-permute-start.7 = (bf16[1024,384]{1,0:T(8,128)(2,1)S(1)}, bf16[1024,384]{1,0:T(8,128)(2,1)S(1)}, u32[]{:S(2)}, u32[]{:S(2)}) collective-permute-start(bf16[1024,384]{1,0:T(8,128)(2,1)S(1)} %bitcast.23), channel_id=1, source_target_pairs={{0,1},{1,0},{2,3},{3,2},{4,5},{5,4},{6,7},{7,6},{8,9},{9,8},{10,11... | collective-permute-start | bytes 2359304 | tf_op jit(solution)/shard_map/near/ppermute | solution.py:184
  31.0 11.5 %collective-permute-start.8 = (bf16[1024,384]{1,0:T(8,128)(2,1)S(1)}, bf16[1024,384]{1,0:T(8,128)(2,1)S(1)}, u32[]{:S(2)}, u32[]{:S(2)}) collective-permute-start(bf16[1024,384]{1,0:T(8,128)(2,1)S(1)} %bitcast.19), channel_id=1, source_target_pairs={{0,1},{1,0},{2,3},{3,2},{4,5},{5,4},{6,7},{7,6},{8,9},{9,8},{10,11... | collective-permute-start | bytes 2359304 | tf_op jit(solution)/shard_map/near/ppermute | solution.py:184
  40.9 20.6 %collective-permute-start.4 = (bf16[1024,384]{1,0:T(8,128)(2,1)S(1)}, bf16[1024,384]{1,0:T(8,128)(2,1)S(1)}, u32[]{:S(2)}, u32[]{:S(2)}) collective-permute-start(bf16[1024,384]{1,0:T(8,128)(2,1)S(1)} %collective-permute-done.3.refs_4_.came), channel_id=1, source_target_pairs={{0,16},{16,0},{1,17},{17,1},{2,18},{18,2},{3,19},{19,3},{4,20},{20... | collective-permute-start | bytes 2359304 | tf_op jit(solution)/shard_map/trade/ppermute | solution.py:188
  42.5 19.1 %collective-permute-start.6 = (bf16[384,512]{1,0:T(8,128)(2,1)S(1)}, bf16[384,512]{1,0:T(8,128)(2,1)S(1)}, u32[]{:S(2)}, u32[]{:S(2)}) collective-permute-start(bf16[384,512]{1,0:T(8,128)(2,1)S(1)} %slice_select_fusion), channel_id=1, source_target_pairs={{0,8},{1,9},{2,10},{3,11},{4,12},{5,13},{6,14},{7,15},{8,0},{9,1},... | collective-permute-start | bytes 1179656 | tf_op jit(solution)/shard_map/swap/ppermute | solution.py:184
  47.2 15.6 %collective-permute-start.5 = (bf16[1024,384]{1,0:T(8,128)(2,1)S(1)}, bf16[1024,384]{1,0:T(8,128)(2,1)S(1)}, u32[]{:S(2)}, u32[]{:S(2)}) collective-permute-start(bf16[1024,384]{1,0:T(8,128)(2,1)S(1)} %collective-permute-done.3.refs_4_.came), channel_id=1, source_target_pairs={{0,1},{1,0},{2,3},{3,2},{4,5},{5,4},{6,7},{7,6},{8,9},{9,8},{10,11... | collective-permute-start | bytes 2359304 | tf_op jit(solution)/shard_map/z_near/ppermute | solution.py:184
  61.5 2.3 %collective-permute-start.10 = (bf16[1024,384]{1,0:T(8,128)(2,1)S(1)}, bf16[1024,384]{1,0:T(8,128)(2,1)S(1)}, u32[]{:S(2)}, u32[]{:S(2)}) collective-permute-start(bf16[1024,384]{1,0:T(8,128)(2,1)S(1)} %collective-permute-done.4.refs_5_.other), channel_id=1, source_target_pairs={{0,1},{1,0},{2,3},{3,2},{4,5},{5,4},{6,7},{7,6},{8,9},{9,8},{10,11... | collective-permute-start | bytes 2359304 | tf_op jit(solution)/shard_map/y_near/ppermute | solution.py:184
  61.5 4.5 %collective-permute-start.11 = (bf16[384,512]{1,0:T(8,128)(2,1)S(1)}, bf16[384,512]{1,0:T(8,128)(2,1)S(1)}, u32[]{:S(2)}, u32[]{:S(2)}) collective-permute-start(bf16[384,512]{1,0:T(8,128)(2,1)S(1)} %collective-permute-done.6.refs_3_.came), channel_id=1, source_target_pairs={{0,1},{1,0},{2,3},{3,2},{4,5},{5,4},{6,7},{7,6},{8,9},{9,8},{10,11... | collective-permute-start | bytes 1179656 | tf_op jit(solution)/shard_map/z_near/ppermute | solution.py:184
  62.1 11.0 %collective-permute-start.13 = (bf16[384,512]{1,0:T(8,128)(2,1)S(1)}, bf16[384,512]{1,0:T(8,128)(2,1)S(1)}, u32[]{:S(2)}, u32[]{:S(2)}) collective-permute-start(bf16[384,512]{1,0:T(8,128)(2,1)S(1)} %collective-permute-done.6.refs_3_.came), channel_id=1, source_target_pairs={{0,16},{16,0},{1,17},{17,1},{2,18},{18,2},{3,19},{19,3},{4,20},{20... | collective-permute-start | bytes 1179656 | tf_op jit(solution)/shard_map/trade/ppermute | solution.py:188
  67.0 6.1 %collective-permute-start.14 = (bf16[112,512]{1,0:T(8,128)(2,1)S(1)}, bf16[112,512]{1,0:T(8,128)(2,1)S(1)}, u32[]{:S(2)}, u32[]{:S(2)}) collective-permute-start(bf16[112,512]{1,0:T(8,128)(2,1)S(1)} %get-tuple-element.45), channel_id=1, source_target_pairs={{0,2},{1,3},{2,0},{3,1},{4,6},{5,7},{6,4},{7,5},{8,10},{9,11},{10,... | collective-permute-start | bytes 344072 | tf_op jit(solution)/shard_map/sums/ppermute | solution.py:184
  68.6 1.4 %copy-start.4 = (s32[16]{0:T(128)S(1)}, s32[16]{0:T(128)}, u32[]{:S(2)}) copy-start(s32[16]{0:T(128)} %flags.2) | copy-start | bytes 196
  68.6 6.1 %collective-permute-start.12 = (bf16[112,512]{1,0:T(8,128)(2,1)S(1)}, bf16[112,512]{1,0:T(8,128)(2,1)S(1)}, u32[]{:S(2)}, u32[]{:S(2)}) collective-permute-start(bf16[112,512]{1,0:T(8,128)(2,1)S(1)} %get-tuple-element.43), channel_id=1, source_target_pairs={{0,2},{1,3},{2,0},{3,1},{4,6},{5,7},{6,4},{7,5},{8,10},{9,11},{10,... | collective-permute-start | bytes 344072 | tf_op jit(solution)/shard_map/sums/ppermute | solution.py:184
  74.7 1.8 %collective-permute-start.15 = (bf16[384,512]{1,0:T(8,128)(2,1)S(1)}, bf16[384,512]{1,0:T(8,128)(2,1)S(1)}, u32[]{:S(2)}, u32[]{:S(2)}) collective-permute-start(bf16[384,512]{1,0:T(8,128)(2,1)S(1)} %collective-permute-done.13.refs_3_.other), channel_id=1, source_target_pairs={{0,1},{1,0},{2,3},{3,2},{4,5},{5,4},{6,7},{7,6},{8,9},{9,8},{10,11... | collective-permute-start | bytes 1179656 | tf_op jit(solution)/shard_map/y_near/ppermute | solution.py:184
  77.5 6.1 %collective-permute-start.18 = (bf16[112,512]{1,0:T(8,128)(2,1)S(1)}, bf16[112,512]{1,0:T(8,128)(2,1)S(1)}, u32[]{:S(2)}, u32[]{:S(2)}) collective-permute-start(bf16[112,512]{1,0:T(8,128)(2,1)S(1)} %get-tuple-element.56), channel_id=1, source_target_pairs={{0,2},{1,3},{2,0},{3,1},{4,6},{5,7},{6,4},{7,5},{8,10},{9,11},{10,... | collective-permute-start | bytes 344072 | tf_op jit(solution)/shard_map/sums/ppermute | solution.py:184
  79.0 7.1 %collective-permute-start.17 = (bf16[112,512]{1,0:T(8,128)(2,1)S(1)}, bf16[112,512]{1,0:T(8,128)(2,1)S(1)}, u32[]{:S(2)}, u32[]{:S(2)}) collective-permute-start(bf16[112,512]{1,0:T(8,128)(2,1)S(1)} %get-tuple-element.51), channel_id=1, source_target_pairs={{0,2},{1,3},{2,0},{3,1},{4,6},{5,7},{6,4},{7,5},{8,10},{9,11},{10,... | collective-permute-start | bytes 344072 | tf_op jit(solution)/shard_map/sums/ppermute | solution.py:184
  80.5 5.6 %collective-permute-start.16 = (bf16[112,512]{1,0:T(8,128)(2,1)S(1)}, bf16[112,512]{1,0:T(8,128)(2,1)S(1)}, u32[]{:S(2)}, u32[]{:S(2)}) collective-permute-start(bf16[112,512]{1,0:T(8,128)(2,1)S(1)} %convert_add_fusion), channel_id=1, source_target_pairs={{0,4},{1,5},{2,6},{3,7},{4,0},{5,1},{6,2},{7,3},{8,12},{9,13},{10,... | collective-permute-start | bytes 344072 | tf_op jit(solution)/shard_map/sums/ppermute | solution.py:184
  83.6 4.9 %collective-permute-start.19 = (bf16[112,512]{1,0:T(8,128)(2,1)S(1)}, bf16[112,512]{1,0:T(8,128)(2,1)S(1)}, u32[]{:S(2)}, u32[]{:S(2)}) collective-permute-start(bf16[112,512]{1,0:T(8,128)(2,1)S(1)} %add_convert_fusion.1), channel_id=1, source_target_pairs={{0,4},{1,5},{2,6},{3,7},{4,0},{5,1},{6,2},{7,3},{8,12},{9,13},{10,... | collective-permute-start | bytes 344072 | tf_op jit(solution)/shard_map/sums/ppermute | solution.py:184

commit v3 on v2

--- a/solution.py
+++ b/solution.py
@@ -102,6 +102,17 @@
         outs[i][...] = totals[i].astype(outs[i].dtype)
 
 
+def finish_kernel(ours, *refs):
+    out = refs[-1]
+    for flip, parts in ((0, refs[:ours]), (1, refs[ours:-1])):
+        width = parts[0].shape[1]
+        half = (lax.axis_index("dp") + flip) % 2
+        total = parts[0][...]
+        for part in parts[1:]:
+            total = total + part[...].astype(jnp.float32)
+        out[:, pl.ds(pl.multiple_of(half * width, width), width)] = total.astype(out.dtype)
+
+
 def call(kernel, out_shape, args, scratch=(), scalars=0):
     vmem = pl.BlockSpec(memory_space=pltpu.VMEM)
     smem = pl.BlockSpec(memory_space=pltpu.SMEM)
@@ -204,9 +215,11 @@
         bits.append(bit)
         bit //= 2
     blocks = {0: pack_gates(tokens, expert_ids, gate_probs, count)}
+    masks = {0: 0}
     for stage, bit in enumerate(bits):
         for i in sorted(blocks):
             blocks[i | 1 << stage] = send(blocks[i], bit, "tokens")
+            masks[i | 1 << stage] = masks[i] ^ bit
     rows = [blocks[i] for i in range(len(blocks))]
 
     z_upper = send(upper, half_axis, "swap")
@@ -240,38 +253,37 @@
     def far_sums(flip, downs):
         parts = {}
         for first in firsts:
-            dtype = jnp.bfloat16 if first >= len(rows) // 2 else jnp.float32
+            for i in (0, 1):
+                parts[first + i] = jnp.bfloat16 if first + i > 0 else jnp.float32
+            shape = (height, downs[0].shape[1])
             parts[first], parts[first + 1] = call(
                 functools.partial(down_kernel, count, first, flip),
-                [jax.ShapeDtypeStruct((height, downs[0].shape[1]), dtype)] * 2,
+                [jax.ShapeDtypeStruct(shape, parts[first + i]) for i in (0, 1)],
                 [placement, *rows[first : first + 2], hidden, *downs, *base[first]],
                 scalars=1,
             )
         return parts
 
-    def collect(parts, stages, *others):
-        for stage in stages:
-            for i in reversed(range(1 << stage)):
-                part = parts[i | 1 << stage].astype(jnp.bfloat16)
-                came = after(send(part, bits[stage], "sums"), *others)
-                parts[i] = parts[i] + came.astype(jnp.float32)
-        return parts[0].astype(jnp.bfloat16)
-
-    stages = list(reversed(range(len(bits))))
+    def collect(parts):
+        return [parts[0]] + [send(parts[i], masks[i], "sums") for i in reversed(range(1, len(parts)))]
+
     parts = far_sums(0, [arrived, z_near[1]])
     flags = after(swap_flags, parts)
     stored = [
         store(0, 0, flags, own[0], z_upper, y_upper),
         store(0, depth, flags, own[1], z_upper, y_upper),
     ]
-    landed = after(y_lower, stored)
-    collect(parts, stages[:1], landed)
-    y_near.append(send(after(landed, parts), 1, "y_near"))
+    ours = collect(parts)
+    landed = after(y_lower, stored, ours[1:-1])
+    y_near.append(send(landed, 1, "y_near"))
     last_parts = far_sums(1, [landed, y_near[1]])
     stored.append(store(1, 0, after(swap_flags, last_parts), own[2], z_lower, y_lower))
-    parts = after(parts, last_parts[firsts[0]])
-    mixed = [collect(parts, stages[1:]), collect(last_parts, stages)]
-    mixed = half_of(jnp.concatenate(mixed, axis=1), jnp.concatenate(mixed[::-1], axis=1))
+    others = collect(last_parts)
+    mixed = call(
+        functools.partial(finish_kernel, len(ours)),
+        jax.ShapeDtypeStruct((height, width), tokens.dtype),
+        [*ours, *others],
+    )
     return (mixed, *(w[None] for w in stored))
 
 

time: 89.4 us -> 87.2 us (0.975)
  waiting for transfers between devices: 53.2 us -> 49.8 us
  starting transfers between devices: 17.2 us -> 18.5 us
  other arithmetic: 1.24 us -> 0.32 us
    ppermute x18, waiting for transfers between devices: 53.1 us -> 49.2 us  [send(): return lax.ppermute(value, 'expert', [(d, d ^ bit) for d in range(count)])]
    ppermute x18, starting transfers between devices: 14.9 us -> 16.2 us  [send(): return lax.ppermute(value, 'expert', [(d, d ^ bit) for d in range(count)])]
    pallas_call x7 -> x8, Pallas kernels: 10.6 us -> 11.4 us  [call(): pl.pallas_call(kernel, out_shape=out_shape, in_specs=[smem] * scalars + [...]
  transfers between devices with their start and end apart: 20 -> 20, of which waited for: 11 -> 11; matrix products, arithmetic and copies ran while one was open for 0% -> 0% of each run, Pallas kernels for 16% -> 17%
where the time goes in v3:
time: 87.2 us; the launch traced here: 87 us
  waiting for transfers between devices  49.8 us (57%)
  starting transfers between devices  18.5 us (21%)
  Pallas kernels  15.8 us (18%)
  local copies, waits for them, and re-layouts  1.67 us (2%)
  between operations  0.9 us (1%)
    ppermute x18, waiting for transfers between devices, send(): return lax.ppermute(value, 'expert', [(d, d ^ bit) for d in range(count)])  49.2 us
    ppermute x18, starting transfers between devices, send(): return lax.ppermute(value, 'expert', [(d, d ^ bit) for d in range(count)])  16.2 us
    pallas_call x8, Pallas kernels, call(): pl.pallas_call(kernel, out_shape=out_shape, in_specs=[smem] * scalars + [...  11.4 us
    pallas_call x3, Pallas kernels, store(): pl.pallas_call(functools.partial(store_kernel, axis, first), out_shape=ja...  4.34 us
    ppermute x2, starting transfers between devices, trade(): return lax.ppermute(value, 'dp', trades)  2.32 us
  transfers between devices with their start and end apart: 20, of which 11 were waited for; matrix products, arithmetic and copies ran while one was open for 0% of the time, Pallas kernels for 17%

profile of v3, /device:TPU:0, one launch (start us, length us, event | category | flops | bytes accessed | tf_op | source)
XLA Modules:
  0.0 87.0 jit_solution(15698741325303230502)
XLA Ops:
  0.6 1.5 %slice_bitcast_fusion = (bf16[512,384]{1,0:T(8,128)(2,1)S(1)}, bf16[512,384]{1,0:T(8,128)(2,1)S(1)}, bf16[512,384]{1,0:T(8,128)(2,1)S(1)}, bf16[512,384]{1,0:T(8,128)(2,1)S(1)}) fusion(bf16[1,1024,384]{2,1,0:T(8,128)(2,1)} %param.12, bf16[1,1024,384]{2,1,0:T(8,128)(2,1)} %param.11), kind=kLoop, calls=%fused_computation.4 | loop fusion | bytes 3145728 | tf_op jit(solution)/shard_map/slice | solution.py:208
  2.2 0.0 copy-start.6
  2.2 0.0 copy-start.7
  2.2 0.0 copy-start.5
  2.2 0.0 copy-start
  2.2 0.2 maximum_select_fusion
  2.4 4.1 %collective-permute-start.3 = (bf16[1024,384]{1,0:T(8,128)(2,1)S(1)}, bf16[1024,384]{1,0:T(8,128)(2,1)S(1)}, u32[]{:S(2)}, u32[]{:S(2)}) collective-permute-start(bf16[1024,384]{1,0:T(8,128)(2,1)S(1)} %maximum_select_fusion), channel_id=1, source_target_pairs={{0,8},{1,9},{2,10},{3,11},{4,12},{5,13},{6,14},{7,15},{8,0},{9,1},... | collective-permute-start | bytes 2359304 | tf_op jit(solution)/shard_map/swap/ppermute | solution.py:195
  6.6 0.1 copy.17
  6.7 0.0 copy-start.2
  6.7 0.0 copy-start.1
  6.8 1.6 %collective-permute-start = (bf16[112,1152]{1,0:T(8,128)(2,1)S(1)}, bf16[112,1152]{1,0:T(8,128)(2,1)S(1)}, u32[]{:S(2)}, u32[]{:S(2)}) collective-permute-start(bf16[112,1152]{1,0:T(8,128)(2,1)S(1)} %fusion.1.refs_0_), channel_id=1, source_target_pairs={{0,4},{1,5},{2,6},{3,7},{4,0},{5,1},{6,2},{7,3},{8,12},{9,13},{10,... | collective-permute-start | bytes 774152 | tf_op jit(solution)/shard_map/tokens/ppermute | solution.py:195
  8.4 1.5 %collective-permute-start.1 = (bf16[112,1152]{1,0:T(8,128)(2,1)S(1)}, bf16[112,1152]{1,0:T(8,128)(2,1)S(1)}, u32[]{:S(2)}, u32[]{:S(2)}) collective-permute-start(bf16[112,1152]{1,0:T(8,128)(2,1)S(1)} %fusion.1.refs_0_), channel_id=1, source_target_pairs={{0,2},{1,3},{2,0},{3,1},{4,6},{5,7},{6,4},{7,5},{8,10},{9,11},{10,... | collective-permute-start | bytes 774152 | tf_op jit(solution)/shard_map/tokens/ppermute | solution.py:195
  9.9 19.0 %collective-permute-done.refs_1_ = bf16[112,1152]{1,0:T(8,128)(2,1)S(1)} collective-permute-done((bf16[112,1152]{1,0:T(8,128)(2,1)S(1)}, bf16[112,1152]{1,0:T(8,128)(2,1)S(1)}, u32[]{:S(2)}, u32[]{:S(2)}) %collective-permute-start) | collective-permute-done | bytes 258080 | tf_op jit(solution)/shard_map/tokens/ppermute | solution.py:195
  28.9 1.5 %collective-permute-start.2 = (bf16[112,1152]{1,0:T(8,128)(2,1)S(1)}, bf16[112,1152]{1,0:T(8,128)(2,1)S(1)}, u32[]{:S(2)}, u32[]{:S(2)}) collective-permute-start(bf16[112,1152]{1,0:T(8,128)(2,1)S(1)} %collective-permute-done.refs_1_), channel_id=1, source_target_pairs={{0,2},{1,3},{2,0},{3,1},{4,6},{5,7},{6,4},{7,5},{8,10},{9,11},{10,... | collective-permute-start | bytes 774152 | tf_op jit(solution)/shard_map/tokens/ppermute | solution.py:195
  30.4 0.1 collective-permute-start.9
  30.5 0.5 collective-permute-start.7
  31.0 0.1 collective-permute-start.8
  31.1 4.9 %collective-permute-done.2.refs_1_.refs_3_ = bf16[112,1152]{1,0:T(8,128)(2,1)S(1)} collective-permute-done((bf16[112,1152]{1,0:T(8,128)(2,1)S(1)}, bf16[112,1152]{1,0:T(8,128)(2,1)S(1)}, u32[]{:S(2)}, u32[]{:S(2)}) %collective-permute-start.2) | collective-permute-done | bytes 258080 | tf_op jit(solution)/shard_map/tokens/ppermute | solution.py:195
  36.0 4.9 %collective-permute-done.3.refs_4_.came = bf16[1024,384]{1,0:T(8,128)(2,1)S(1)} collective-permute-done((bf16[1024,384]{1,0:T(8,128)(2,1)S(1)}, bf16[1024,384]{1,0:T(8,128)(2,1)S(1)}, u32[]{:S(2)}, u32[]{:S(2)}) %collective-permute-start.3) | collective-permute-done | bytes 786464 | tf_op jit(solution)/shard_map/swap/ppermute | solution.py:195
  40.9 1.6 %collective-permute-start.4 = (bf16[1024,384]{1,0:T(8,128)(2,1)S(1)}, bf16[1024,384]{1,0:T(8,128)(2,1)S(1)}, u32[]{:S(2)}, u32[]{:S(2)}) collective-permute-start(bf16[1024,384]{1,0:T(8,128)(2,1)S(1)} %collective-permute-done.3.refs_4_.came), channel_id=1, source_target_pairs={{0,16},{16,0},{1,17},{17,1},{2,18},{18,2},{3,19},{19,3},{4,20},{20... | collective-permute-start | bytes 2359304 | tf_op jit(solution)/shard_map/trade/ppermute | solution.py:199
  42.5 2.3 %shard_map.112 = (f32[112,1024]{1,0:T(8,128)S(1)}, f32[112,1024]{1,0:T(8,128)S(1)}) custom-call(s32[16]{0:T(128)S(1)} %copy-done.3, bf16[112,1152]{1,0:T(8,128)(2,1)S(1)} %collective-permute-done.1.refs_0_.refs_2_, bf16[112,1152]{1,0:T(8,128)(2,1)S(1)} %collective-permute-done.2.refs_1_.refs_3_, bf16[1024,384]{1,0:T(8,128)(2,1)S(1)} %bitcast.24, ...), custom_call_target="tpu_custom_call" | custom-call | tf_op jit(solution)/shard_map/pallas_call | solution.py:119
  44.9 2.3 %shard_map.111 = (f32[112,1024]{1,0:T(8,128)S(1)}, f32[112,1024]{1,0:T(8,128)S(1)}) custom-call(s32[16]{0:T(128)S(1)} %copy-done.3, bf16[112,1152]{1,0:T(8,128)(2,1)S(1)} %fusion.1.refs_0_, bf16[112,1152]{1,0:T(8,128)(2,1)S(1)} %collective-permute-done.refs_1_, bf16[1024,384]{1,0:T(8,128)(2,1)S(1)} %bitcast.25, bf16[1024,384]{1,0:T(8,128)(2,1)S(1)} %bitcast.21, ...), custom_call_target="tpu_custom_call" | custom-call | tf_op jit(solution)/shard_map/pallas_call | solution.py:119
  47.2 0.1 collective-permute-start.5
  47.3 14.3 %collective-permute-done.6.refs_3_.came = bf16[384,512]{1,0:T(8,128)(2,1)S(1)} collective-permute-done((bf16[384,512]{1,0:T(8,128)(2,1)S(1)}, bf16[384,512]{1,0:T(8,128)(2,1)S(1)}, u32[]{:S(2)}, u32[]{:S(2)}) %collective-permute-start.6) | collective-permute-done | bytes 393248 | tf_op jit(solution)/shard_map/swap/ppermute | solution.py:195
  61.5 0.5 collective-permute-start.11
  62.1 0.8 collective-permute-start.15
  62.8 1.0 %collective-permute-done.10.refs_7_ = bf16[1024,384]{1,0:T(8,128)(2,1)S(1)} collective-permute-done((bf16[1024,384]{1,0:T(8,128)(2,1)S(1)}, bf16[1024,384]{1,0:T(8,128)(2,1)S(1)}, u32[]{:S(2)}, u32[]{:S(2)}) %collective-permute-start.10) | collective-permute-done | bytes 786464 | tf_op jit(solution)/shard_map/y_near/ppermute | solution.py:195
  63.8 2.2 %shard_map.113.refs_2_ = bf16[448,768]{1,0:T(8,128)(2,1)S(1)} custom-call(bf16[112,1152]{1,0:T(8,128)(2,1)S(1)} %fusion.1.refs_0_, bf16[112,1152]{1,0:T(8,128)(2,1)S(1)} %collective-permute-done.refs_1_, bf16[112,1152]{1,0:T(8,128)(2,1)S(1)} %collective-permute-done.1.refs_0_.refs_2_, bf16[112,1152]{1,0:T(8,128)(2,1)S(1)} %collective-permute-done.2.refs_1_.refs_3_, ...), custom_call_target="tpu_custom_call" | custom-call | tf_op jit(solution)/shard_map/pallas_call | solution.py:119
  66.0 0.9 %shard_map.115 = (bf16[112,512]{1,0:T(8,128)(2,1)S(1)}, bf16[112,512]{1,0:T(8,128)(2,1)S(1)}) custom-call(s32[16]{0:T(128)S(1)} %copy-done.3, bf16[112,1152]{1,0:T(8,128)(2,1)S(1)} %collective-permute-done.1.refs_0_.refs_2_, bf16[112,1152]{1,0:T(8,128)(2,1)S(1)} %collective-permute-done.2.refs_1_.refs_3_, bf16[448,768]{1,0:T(8,128)(2,1)S(1)} %shard_map.113.refs_2_, ...), custom_call_target="tpu_custom_call" | custom-call | tf_op jit(solution)/shard_map/pallas_call | solution.py:119
  67.0 0.6 collective-permute-start.12
  67.5 1.1 %collective-permute-start.13 = (bf16[112,512]{1,0:T(8,128)(2,1)S(1)}, bf16[112,512]{1,0:T(8,128)(2,1)S(1)}, u32[]{:S(2)}, u32[]{:S(2)}) collective-permute-start(bf16[112,512]{1,0:T(8,128)(2,1)S(1)} %get-tuple-element.39), channel_id=1, source_target_pairs={{0,2},{1,3},{2,0},{3,1},{4,6},{5,7},{6,4},{7,5},{8,10},{9,11},{10,... | collective-permute-start | bytes 344072 | tf_op jit(solution)/shard_map/sums/ppermute | solution.py:195
  68.6 0.9 %shard_map.114 = (f32[112,512]{1,0:T(8,128)S(1)}, bf16[112,512]{1,0:T(8,128)(2,1)S(1)}) custom-call(s32[16]{0:T(128)S(1)} %copy-done.3, bf16[112,1152]{1,0:T(8,128)(2,1)S(1)} %fusion.1.refs_0_, bf16[112,1152]{1,0:T(8,128)(2,1)S(1)} %collective-permute-done.refs_1_, bf16[448,768]{1,0:T(8,128)(2,1)S(1)} %shard_map.113.refs_2_, ...), custom_call_target="tpu_custom_call" | custom-call | tf_op jit(solution)/shard_map/pallas_call | solution.py:119
  69.6 1.4 %shard_map.117 = bf16[1024,384]{1,0:T(8,128)(2,1)} custom-call(s32[16]{0:T(128)S(1)} %copy-done.4, bf16[1024,384]{1,0:T(8,128)(2,1)S(1)} %bitcast.22, bf16[1024,384]{1,0:T(8,128)(2,1)S(1)} %collective-permute-done.3.refs_4_.came, bf16[1024,384]{1,0:T(8,128)(2,1)S(1)} %collective-permute-done.4.refs_5_.other), custom_call_target="tpu_custom_call" | custom-call | tf_op jit(solution)/shard_map/pallas_call | solution.py:169
  71.1 1.4 %shard_map.116 = bf16[1024,384]{1,0:T(8,128)(2,1)} custom-call(s32[16]{0:T(128)S(1)} %copy-done.4, bf16[1024,384]{1,0:T(8,128)(2,1)S(1)} %bitcast.26, bf16[1024,384]{1,0:T(8,128)(2,1)S(1)} %collective-permute-done.3.refs_4_.came, bf16[1024,384]{1,0:T(8,128)(2,1)S(1)} %collective-permute-done.4.refs_5_.other), custom_call_target="tpu_custom_call" | custom-call | tf_op jit(solution)/shard_map/pallas_call | solution.py:169
  72.5 0.6 collective-permute-done.15.refs_3_.other
  73.1 0.2 collective-permute-done.12.refs_1_
  73.2 1.7 %collective-permute-done.13.refs_2_ = bf16[112,512]{1,0:T(8,128)(2,1)S(1)} collective-permute-done((bf16[112,512]{1,0:T(8,128)(2,1)S(1)}, bf16[112,512]{1,0:T(8,128)(2,1)S(1)}, u32[]{:S(2)}, u32[]{:S(2)}) %collective-permute-start.13) | collective-permute-done | bytes 114720 | tf_op jit(solution)/shard_map/sums/ppermute | solution.py:195
  74.9 1.0 %collective-permute-start.14 = (bf16[112,512]{1,0:T(8,128)(2,1)S(1)}, bf16[112,512]{1,0:T(8,128)(2,1)S(1)}, u32[]{:S(2)}, u32[]{:S(2)}) collective-permute-start(bf16[112,512]{1,0:T(8,128)(2,1)S(1)} %get-tuple-element.40), channel_id=1, source_target_pairs={{0,4},{1,5},{2,6},{3,7},{4,0},{5,1},{6,2},{7,3},{8,12},{9,13},{10,... | collective-permute-start | bytes 344072 | tf_op jit(solution)/shard_map/sums/ppermute | solution.py:195
  75.9 0.7 collective-permute-done.16.refs_4_
  76.6 0.9 %shard_map.119 = (bf16[112,512]{1,0:T(8,128)(2,1)S(1)}, bf16[112,512]{1,0:T(8,128)(2,1)S(1)}) custom-call(s32[16]{0:T(128)S(1)} %copy-done.3, bf16[112,1152]{1,0:T(8,128)(2,1)S(1)} %collective-permute-done.1.refs_0_.refs_2_, bf16[112,1152]{1,0:T(8,128)(2,1)S(1)} %collective-permute-done.2.refs_1_.refs_3_, bf16[448,768]{1,0:T(8,128)(2,1)S(1)} %shard_map.113.refs_2_, ...), custom_call_target="tpu_custom_call" | custom-call | tf_op jit(solution)/shard_map/pallas_call | solution.py:119
  77.6 1.2 %collective-permute-start.17 = (bf16[112,512]{1,0:T(8,128)(2,1)S(1)}, bf16[112,512]{1,0:T(8,128)(2,1)S(1)}, u32[]{:S(2)}, u32[]{:S(2)}) collective-permute-start(bf16[112,512]{1,0:T(8,128)(2,1)S(1)} %get-tuple-element.44), channel_id=1, source_target_pairs={{0,6},{1,7},{2,4},{3,5},{4,2},{5,3},{6,0},{7,1},{8,14},{9,15},{10,... | collective-permute-start | bytes 344072 | tf_op jit(solution)/shard_map/sums/ppermute | solution.py:195
  78.8 1.3 %collective-permute-start.18 = (bf16[112,512]{1,0:T(8,128)(2,1)S(1)}, bf16[112,512]{1,0:T(8,128)(2,1)S(1)}, u32[]{:S(2)}, u32[]{:S(2)}) collective-permute-start(bf16[112,512]{1,0:T(8,128)(2,1)S(1)} %get-tuple-element.45), channel_id=1, source_target_pairs={{0,2},{1,3},{2,0},{3,1},{4,6},{5,7},{6,4},{7,5},{8,10},{9,11},{10,... | collective-permute-start | bytes 344072 | tf_op jit(solution)/shard_map/sums/ppermute | solution.py:195
  80.1 0.9 %shard_map.118 = (f32[112,512]{1,0:T(8,128)S(1)}, bf16[112,512]{1,0:T(8,128)(2,1)S(1)}) custom-call(s32[16]{0:T(128)S(1)} %copy-done.3, bf16[112,1152]{1,0:T(8,128)(2,1)S(1)} %fusion.1.refs_0_, bf16[112,1152]{1,0:T(8,128)(2,1)S(1)} %collective-permute-done.refs_1_, bf16[448,768]{1,0:T(8,128)(2,1)S(1)} %shard_map.113.refs_2_, ...), custom_call_target="tpu_custom_call" | custom-call | tf_op jit(solution)/shard_map/pallas_call | solution.py:119
  81.1 1.1 %collective-permute-start.19 = (bf16[112,512]{1,0:T(8,128)(2,1)S(1)}, bf16[112,512]{1,0:T(8,128)(2,1)S(1)}, u32[]{:S(2)}, u32[]{:S(2)}) collective-permute-start(bf16[112,512]{1,0:T(8,128)(2,1)S(1)} %get-tuple-element.46), channel_id=1, source_target_pairs={{0,4},{1,5},{2,6},{3,7},{4,0},{5,1},{6,2},{7,3},{8,12},{9,13},{10,... | collective-permute-start | bytes 344072 | tf_op jit(solution)/shard_map/sums/ppermute | solution.py:195
  82.2 1.4 %shard_map.121 = bf16[384,1024]{1,0:T(8,128)(2,1)} custom-call(s32[16]{0:T(128)S(1)} %copy-done.4, bf16[384,1024]{1,0:T(8,128)(2,1)S(1)} %bitcast.18, bf16[384,512]{1,0:T(8,128)(2,1)S(1)} %collective-permute-done.6.refs_3_.came, bf16[384,512]{1,0:T(8,128)(2,1)S(1)} %collective-permute-done.15.refs_3_.other), custom_call_target="tpu_custom_call" | custom-call | tf_op jit(solution)/shard_map/pallas_call | solution.py:169
  83.6 0.4 collective-permute-done.17.refs_5_
  84.0 2.2 %collective-permute-done.18.refs_6_ = bf16[112,512]{1,0:T(8,128)(2,1)S(1)} collective-permute-done((bf16[112,512]{1,0:T(8,128)(2,1)S(1)}, bf16[112,512]{1,0:T(8,128)(2,1)S(1)}, u32[]{:S(2)}, u32[]{:S(2)}) %collective-permute-start.18) | collective-permute-done | bytes 114720 | tf_op jit(solution)/shard_map/sums/ppermute | solution.py:195
  86.2 0.8 shard_map.120
  (27 shorter events, 0.2 us)
Async XLA Ops:
  2.2 4.4 %copy-start.6 = (f32[112,8]{0,1:T(8,128)S(1)}, f32[112,8]{0,1:T(8,128)}, u32[]{:S(2)}) copy-start(f32[112,8]{0,1:T(8,128)} %param.10) | copy-start | bytes 10756
  2.2 4.4 %copy-start.7 = (s32[112,8]{0,1:T(8,128)S(1)}, s32[112,8]{0,1:T(8,128)}, u32[]{:S(2)}) copy-start(s32[112,8]{0,1:T(8,128)} %param.9) | copy-start | bytes 10756
  2.2 4.5 %copy-start.5 = (bf16[112,1024]{1,0:T(8,128)(2,1)S(1)}, bf16[112,1024]{1,0:T(8,128)(2,1)}, u32[]{:S(2)}) copy-start(bf16[112,1024]{1,0:T(8,128)(2,1)} %param.8) | copy-start | bytes 688132
  2.2 28.2 %copy-start = (bf16[1,384,1024]{2,1,0:T(8,128)(2,1)S(1)}, bf16[1,384,1024]{2,1,0:T(8,128)(2,1)}, u32[]{:S(2)}) copy-start(bf16[1,384,1024]{2,1,0:T(8,128)(2,1)} %param.13) | copy-start | bytes 2359300
  2.4 38.5 %collective-permute-start.3 = (bf16[1024,384]{1,0:T(8,128)(2,1)S(1)}, bf16[1024,384]{1,0:T(8,128)(2,1)S(1)}, u32[]{:S(2)}, u32[]{:S(2)}) collective-permute-start(bf16[1024,384]{1,0:T(8,128)(2,1)S(1)} %maximum_select_fusion), channel_id=1, source_target_pairs={{0,8},{1,9},{2,10},{3,11},{4,12},{5,13},{6,14},{7,15},{8,0},{9,1},... | collective-permute-start | bytes 2359304 | tf_op jit(solution)/shard_map/swap/ppermute | solution.py:195
  6.7 23.8 %copy-start.2 = (bf16[1,1024,384]{2,1,0:T(8,128)(2,1)S(1)}, bf16[1,1024,384]{2,1,0:T(8,128)(2,1)}, u32[]{:S(2)}) copy-start(bf16[1,1024,384]{2,1,0:T(8,128)(2,1)} %param.11) | copy-start | bytes 2359300
  6.7 24.3 %copy-start.1 = (bf16[1,1024,384]{2,1,0:T(8,128)(2,1)S(1)}, bf16[1,1024,384]{2,1,0:T(8,128)(2,1)}, u32[]{:S(2)}) copy-start(bf16[1,1024,384]{2,1,0:T(8,128)(2,1)} %param.12) | copy-start | bytes 2359300
  6.7 35.8 %copy-start.3 = (s32[16]{0:T(128)S(1)}, s32[16]{0:T(128)}, u32[]{:S(2)}) copy-start(s32[16]{0:T(128)} %placement.11) | copy-start | bytes 196
  6.8 22.1 %collective-permute-start = (bf16[112,1152]{1,0:T(8,128)(2,1)S(1)}, bf16[112,1152]{1,0:T(8,128)(2,1)S(1)}, u32[]{:S(2)}, u32[]{:S(2)}) collective-permute-start(bf16[112,1152]{1,0:T(8,128)(2,1)S(1)} %fusion.1.refs_0_), channel_id=1, source_target_pairs={{0,4},{1,5},{2,6},{3,7},{4,0},{5,1},{6,2},{7,3},{8,12},{9,13},{10,... | collective-permute-start | bytes 774152 | tf_op jit(solution)/shard_map/tokens/ppermute | solution.py:195
  8.4 22.6 %collective-permute-start.1 = (bf16[112,1152]{1,0:T(8,128)(2,1)S(1)}, bf16[112,1152]{1,0:T(8,128)(2,1)S(1)}, u32[]{:S(2)}, u32[]{:S(2)}) collective-permute-start(bf16[112,1152]{1,0:T(8,128)(2,1)S(1)} %fusion.1.refs_0_), channel_id=1, source_target_pairs={{0,2},{1,3},{2,0},{3,1},{4,6},{5,7},{6,4},{7,5},{8,10},{9,11},{10,... | collective-permute-start | bytes 774152 | tf_op jit(solution)/shard_map/tokens/ppermute | solution.py:195
  28.9 7.1 %collective-permute-start.2 = (bf16[112,1152]{1,0:T(8,128)(2,1)S(1)}, bf16[112,1152]{1,0:T(8,128)(2,1)S(1)}, u32[]{:S(2)}, u32[]{:S(2)}) collective-permute-start(bf16[112,1152]{1,0:T(8,128)(2,1)S(1)} %collective-permute-done.refs_1_), channel_id=1, source_target_pairs={{0,2},{1,3},{2,0},{3,1},{4,6},{5,7},{6,4},{7,5},{8,10},{9,11},{10,... | collective-permute-start | bytes 774152 | tf_op jit(solution)/shard_map/tokens/ppermute | solution.py:195
  30.4 12.1 %collective-permute-start.9 = (bf16[384,1024]{1,0:T(8,128)(2,1)S(1)}, bf16[384,1024]{1,0:T(8,128)(2,1)S(1)}, u32[]{:S(2)}, u32[]{:S(2)}) collective-permute-start(bf16[384,1024]{1,0:T(8,128)(2,1)S(1)} %bitcast.15), channel_id=1, source_target_pairs={{0,1},{1,0},{2,3},{3,2},{4,5},{5,4},{6,7},{7,6},{8,9},{9,8},{10,11... | collective-permute-start | bytes 2359304 | tf_op jit(solution)/shard_map/near/ppermute | solution.py:195
  30.5 12.0 %collective-permute-start.7 = (bf16[1024,384]{1,0:T(8,128)(2,1)S(1)}, bf16[1024,384]{1,0:T(8,128)(2,1)S(1)}, u32[]{:S(2)}, u32[]{:S(2)}) collective-permute-start(bf16[1024,384]{1,0:T(8,128)(2,1)S(1)} %bitcast.23), channel_id=1, source_target_pairs={{0,1},{1,0},{2,3},{3,2},{4,5},{5,4},{6,7},{7,6},{8,9},{9,8},{10,11... | collective-permute-start | bytes 2359304 | tf_op jit(solution)/shard_map/near/ppermute | solution.py:195
  31.0 11.5 %collective-permute-start.8 = (bf16[1024,384]{1,0:T(8,128)(2,1)S(1)}, bf16[1024,384]{1,0:T(8,128)(2,1)S(1)}, u32[]{:S(2)}, u32[]{:S(2)}) collective-permute-start(bf16[1024,384]{1,0:T(8,128)(2,1)S(1)} %bitcast.19), channel_id=1, source_target_pairs={{0,1},{1,0},{2,3},{3,2},{4,5},{5,4},{6,7},{7,6},{8,9},{9,8},{10,11... | collective-permute-start | bytes 2359304 | tf_op jit(solution)/shard_map/near/ppermute | solution.py:195
  40.9 20.6 %collective-permute-start.4 = (bf16[1024,384]{1,0:T(8,128)(2,1)S(1)}, bf16[1024,384]{1,0:T(8,128)(2,1)S(1)}, u32[]{:S(2)}, u32[]{:S(2)}) collective-permute-start(bf16[1024,384]{1,0:T(8,128)(2,1)S(1)} %collective-permute-done.3.refs_4_.came), channel_id=1, source_target_pairs={{0,16},{16,0},{1,17},{17,1},{2,18},{18,2},{3,19},{19,3},{4,20},{20... | collective-permute-start | bytes 2359304 | tf_op jit(solution)/shard_map/trade/ppermute | solution.py:199
  42.5 19.1 %collective-permute-start.6 = (bf16[384,512]{1,0:T(8,128)(2,1)S(1)}, bf16[384,512]{1,0:T(8,128)(2,1)S(1)}, u32[]{:S(2)}, u32[]{:S(2)}) collective-permute-start(bf16[384,512]{1,0:T(8,128)(2,1)S(1)} %slice_select_fusion), channel_id=1, source_target_pairs={{0,8},{1,9},{2,10},{3,11},{4,12},{5,13},{6,14},{7,15},{8,0},{9,1},... | collective-permute-start | bytes 1179656 | tf_op jit(solution)/shard_map/swap/ppermute | solution.py:195
  47.2 15.6 %collective-permute-start.5 = (bf16[1024,384]{1,0:T(8,128)(2,1)S(1)}, bf16[1024,384]{1,0:T(8,128)(2,1)S(1)}, u32[]{:S(2)}, u32[]{:S(2)}) collective-permute-start(bf16[1024,384]{1,0:T(8,128)(2,1)S(1)} %collective-permute-done.3.refs_4_.came), channel_id=1, source_target_pairs={{0,1},{1,0},{2,3},{3,2},{4,5},{5,4},{6,7},{7,6},{8,9},{9,8},{10,11... | collective-permute-start | bytes 2359304 | tf_op jit(solution)/shard_map/z_near/ppermute | solution.py:195
  61.5 2.3 %collective-permute-start.10 = (bf16[1024,384]{1,0:T(8,128)(2,1)S(1)}, bf16[1024,384]{1,0:T(8,128)(2,1)S(1)}, u32[]{:S(2)}, u32[]{:S(2)}) collective-permute-start(bf16[1024,384]{1,0:T(8,128)(2,1)S(1)} %collective-permute-done.4.refs_5_.other), channel_id=1, source_target_pairs={{0,1},{1,0},{2,3},{3,2},{4,5},{5,4},{6,7},{7,6},{8,9},{9,8},{10,11... | collective-permute-start | bytes 2359304 | tf_op jit(solution)/shard_map/y_near/ppermute | solution.py:195
  61.5 4.5 %collective-permute-start.11 = (bf16[384,512]{1,0:T(8,128)(2,1)S(1)}, bf16[384,512]{1,0:T(8,128)(2,1)S(1)}, u32[]{:S(2)}, u32[]{:S(2)}) collective-permute-start(bf16[384,512]{1,0:T(8,128)(2,1)S(1)} %collective-permute-done.6.refs_3_.came), channel_id=1, source_target_pairs={{0,1},{1,0},{2,3},{3,2},{4,5},{5,4},{6,7},{7,6},{8,9},{9,8},{10,11... | collective-permute-start | bytes 1179656 | tf_op jit(solution)/shard_map/z_near/ppermute | solution.py:195
  62.1 11.0 %collective-permute-start.15 = (bf16[384,512]{1,0:T(8,128)(2,1)S(1)}, bf16[384,512]{1,0:T(8,128)(2,1)S(1)}, u32[]{:S(2)}, u32[]{:S(2)}) collective-permute-start(bf16[384,512]{1,0:T(8,128)(2,1)S(1)} %collective-permute-done.6.refs_3_.came), channel_id=1, source_target_pairs={{0,16},{16,0},{1,17},{17,1},{2,18},{18,2},{3,19},{19,3},{4,20},{20... | collective-permute-start | bytes 1179656 | tf_op jit(solution)/shard_map/trade/ppermute | solution.py:199
  67.0 6.3 %collective-permute-start.12 = (bf16[112,512]{1,0:T(8,128)(2,1)S(1)}, bf16[112,512]{1,0:T(8,128)(2,1)S(1)}, u32[]{:S(2)}, u32[]{:S(2)}) collective-permute-start(bf16[112,512]{1,0:T(8,128)(2,1)S(1)} %get-tuple-element.38), channel_id=1, source_target_pairs={{0,6},{1,7},{2,4},{3,5},{4,2},{5,3},{6,0},{7,1},{8,14},{9,15},{10,... | collective-permute-start | bytes 344072 | tf_op jit(solution)/shard_map/sums/ppermute | solution.py:195
  67.5 2.1 %copy-start.4 = (s32[16]{0:T(128)S(1)}, s32[16]{0:T(128)}, u32[]{:S(2)}) copy-start(s32[16]{0:T(128)} %flags.2) | copy-start | bytes 196
  67.5 7.4 %collective-permute-start.13 = (bf16[112,512]{1,0:T(8,128)(2,1)S(1)}, bf16[112,512]{1,0:T(8,128)(2,1)S(1)}, u32[]{:S(2)}, u32[]{:S(2)}) collective-permute-start(bf16[112,512]{1,0:T(8,128)(2,1)S(1)} %get-tuple-element.39), channel_id=1, source_target_pairs={{0,2},{1,3},{2,0},{3,1},{4,6},{5,7},{6,4},{7,5},{8,10},{9,11},{10,... | collective-permute-start | bytes 344072 | tf_op jit(solution)/shard_map/sums/ppermute | solution.py:195
  74.9 1.7 %collective-permute-start.16 = (bf16[384,512]{1,0:T(8,128)(2,1)S(1)}, bf16[384,512]{1,0:T(8,128)(2,1)S(1)}, u32[]{:S(2)}, u32[]{:S(2)}) collective-permute-start(bf16[384,512]{1,0:T(8,128)(2,1)S(1)} %collective-permute-done.15.refs_3_.other), channel_id=1, source_target_pairs={{0,1},{1,0},{2,3},{3,2},{4,5},{5,4},{6,7},{7,6},{8,9},{9,8},{10,11... | collective-permute-start | bytes 1179656 | tf_op jit(solution)/shard_map/y_near/ppermute | solution.py:195
  74.9 8.7 %collective-permute-start.14 = (bf16[112,512]{1,0:T(8,128)(2,1)S(1)}, bf16[112,512]{1,0:T(8,128)(2,1)S(1)}, u32[]{:S(2)}, u32[]{:S(2)}) collective-permute-start(bf16[112,512]{1,0:T(8,128)(2,1)S(1)} %get-tuple-element.40), channel_id=1, source_target_pairs={{0,4},{1,5},{2,6},{3,7},{4,0},{5,1},{6,2},{7,3},{8,12},{9,13},{10,... | collective-permute-start | bytes 344072 | tf_op jit(solution)/shard_map/sums/ppermute | solution.py:195
  77.6 6.4 %collective-permute-start.17 = (bf16[112,512]{1,0:T(8,128)(2,1)S(1)}, bf16[112,512]{1,0:T(8,128)(2,1)S(1)}, u32[]{:S(2)}, u32[]{:S(2)}) collective-permute-start(bf16[112,512]{1,0:T(8,128)(2,1)S(1)} %get-tuple-element.44), channel_id=1, source_target_pairs={{0,6},{1,7},{2,4},{3,5},{4,2},{5,3},{6,0},{7,1},{8,14},{9,15},{10,... | collective-permute-start | bytes 344072 | tf_op jit(solution)/shard_map/sums/ppermute | solution.py:195
  78.8 7.4 %collective-permute-start.18 = (bf16[112,512]{1,0:T(8,128)(2,1)S(1)}, bf16[112,512]{1,0:T(8,128)(2,1)S(1)}, u32[]{:S(2)}, u32[]{:S(2)}) collective-permute-start(bf16[112,512]{1,0:T(8,128)(2,1)S(1)} %get-tuple-element.45), channel_id=1, source_target_pairs={{0,2},{1,3},{2,0},{3,1},{4,6},{5,7},{6,4},{7,5},{8,10},{9,11},{10,... | collective-permute-start | bytes 344072 | tf_op jit(solution)/shard_map/sums/ppermute | solution.py:195
  81.1 5.1 %collective-permute-start.19 = (bf16[112,512]{1,0:T(8,128)(2,1)S(1)}, bf16[112,512]{1,0:T(8,128)(2,1)S(1)}, u32[]{:S(2)}, u32[]{:S(2)}) collective-permute-start(bf16[112,512]{1,0:T(8,128)(2,1)S(1)} %get-tuple-element.46), channel_id=1, source_target_pairs={{0,4},{1,5},{2,6},{3,7},{4,0},{5,1},{6,2},{7,3},{8,12},{9,13},{10,... | collective-permute-start | bytes 344072 | tf_op jit(solution)/shard_map/sums/ppermute | solution.py:195

commit v4 on v3

--- a/solution.py
+++ b/solution.py
@@ -265,7 +265,7 @@
         return parts
 
     def collect(parts):
-        return [parts[0]] + [send(parts[i], masks[i], "sums") for i in reversed(range(1, len(parts)))]
+        return [parts[0]] + [send(parts[i], masks[i], "sums") for i in range(1, len(parts))]
 
     parts = far_sums(0, [arrived, z_near[1]])
     flags = after(swap_flags, parts)
@@ -274,7 +274,7 @@
         store(0, depth, flags, own[1], z_upper, y_upper),
     ]
     ours = collect(parts)
-    landed = after(y_lower, stored, ours[1:-1])
+    landed = after(y_lower, stored, ours[1::2])
     y_near.append(send(landed, 1, "y_near"))
     last_parts = far_sums(1, [landed, y_near[1]])
     stored.append(store(1, 0, after(swap_flags, last_parts), own[2], z_lower, y_lower))

time: 87.2 us -> 88.2 us (1.011)
  starting transfers between devices: 18.5 us -> 19.5 us
    ppermute x18, starting transfers between devices: 16.2 us -> 17.2 us  [send(): return lax.ppermute(value, 'expert', [(d, d ^ bit) for d in range(count)])]
  transfers between devices with their start and end apart: 20 -> 20, of which waited for: 11 -> 9; matrix products, arithmetic and copies ran while one was open for 0% -> 0% of each run, Pallas kernels for 17% -> 17%
where the time goes in v4:
time: 88.2 us; the launch traced here: 88 us
  waiting for transfers between devices  49.8 us (56%)
  starting transfers between devices  19.5 us (22%)
  Pallas kernels  15.8 us (18%)
  local copies, waits for them, and re-layouts  1.68 us (2%)
  between operations  0.92 us (1%)
    ppermute x18, waiting for transfers between devices, send(): return lax.ppermute(value, 'expert', [(d, d ^ bit) for d in range(count)])  49.8 us
    ppermute x18, starting transfers between devices, send(): return lax.ppermute(value, 'expert', [(d, d ^ bit) for d in range(count)])  17.2 us
    pallas_call x8, Pallas kernels, call(): pl.pallas_call(kernel, out_shape=out_shape, in_specs=[smem] * scalars + [...  11.4 us
    pallas_call x3, Pallas kernels, store(): pl.pallas_call(functools.partial(store_kernel, axis, first), out_shape=ja...  4.34 us
    ppermute x2, starting transfers between devices, trade(): return lax.ppermute(value, 'dp', trades)  2.32 us
  transfers between devices with their start and end apart: 20, of which 9 were waited for; matrix products, arithmetic and copies ran while one was open for 0% of the time, Pallas kernels for 17%

profile of v4, /device:TPU:0, one launch (start us, length us, event | category | flops | bytes accessed | tf_op | source)
XLA Modules:
  0.0 88.0 jit_solution(16956257245615621607)
XLA Ops:
  0.6 1.5 %slice_bitcast_fusion = (bf16[512,384]{1,0:T(8,128)(2,1)S(1)}, bf16[512,384]{1,0:T(8,128)(2,1)S(1)}, bf16[512,384]{1,0:T(8,128)(2,1)S(1)}, bf16[512,384]{1,0:T(8,128)(2,1)S(1)}) fusion(bf16[1,1024,384]{2,1,0:T(8,128)(2,1)} %param.12, bf16[1,1024,384]{2,1,0:T(8,128)(2,1)} %param.11), kind=kLoop, calls=%fused_computation.4 | loop fusion | bytes 3145728 | tf_op jit(solution)/shard_map/slice | solution.py:208
  2.2 0.0 copy-start.6
  2.2 0.0 copy-start.7
  2.2 0.0 copy-start.5
  2.2 0.0 copy-start
  2.2 0.2 maximum_select_fusion
  2.4 4.1 %collective-permute-start.3 = (bf16[1024,384]{1,0:T(8,128)(2,1)S(1)}, bf16[1024,384]{1,0:T(8,128)(2,1)S(1)}, u32[]{:S(2)}, u32[]{:S(2)}) collective-permute-start(bf16[1024,384]{1,0:T(8,128)(2,1)S(1)} %maximum_select_fusion), channel_id=1, source_target_pairs={{0,8},{1,9},{2,10},{3,11},{4,12},{5,13},{6,14},{7,15},{8,0},{9,1},... | collective-permute-start | bytes 2359304 | tf_op jit(solution)/shard_map/swap/ppermute | solution.py:195
  6.6 0.1 copy.17
  6.7 0.0 copy-start.2
  6.7 0.0 copy-start.1
  6.7 0.0 copy-start.3
  6.8 1.6 %collective-permute-start = (bf16[112,1152]{1,0:T(8,128)(2,1)S(1)}, bf16[112,1152]{1,0:T(8,128)(2,1)S(1)}, u32[]{:S(2)}, u32[]{:S(2)}) collective-permute-start(bf16[112,1152]{1,0:T(8,128)(2,1)S(1)} %fusion.1.refs_0_), channel_id=1, source_target_pairs={{0,4},{1,5},{2,6},{3,7},{4,0},{5,1},{6,2},{7,3},{8,12},{9,13},{10,... | collective-permute-start | bytes 774152 | tf_op jit(solution)/shard_map/tokens/ppermute | solution.py:195
  8.4 1.5 %collective-permute-start.1 = (bf16[112,1152]{1,0:T(8,128)(2,1)S(1)}, bf16[112,1152]{1,0:T(8,128)(2,1)S(1)}, u32[]{:S(2)}, u32[]{:S(2)}) collective-permute-start(bf16[112,1152]{1,0:T(8,128)(2,1)S(1)} %fusion.1.refs_0_), channel_id=1, source_target_pairs={{0,2},{1,3},{2,0},{3,1},{4,6},{5,7},{6,4},{7,5},{8,10},{9,11},{10,... | collective-permute-start | bytes 774152 | tf_op jit(solution)/shard_map/tokens/ppermute | solution.py:195
  9.9 19.0 %collective-permute-done.refs_1_ = bf16[112,1152]{1,0:T(8,128)(2,1)S(1)} collective-permute-done((bf16[112,1152]{1,0:T(8,128)(2,1)S(1)}, bf16[112,1152]{1,0:T(8,128)(2,1)S(1)}, u32[]{:S(2)}, u32[]{:S(2)}) %collective-permute-start) | collective-permute-done | bytes 258080 | tf_op jit(solution)/shard_map/tokens/ppermute | solution.py:195
  28.9 1.5 %collective-permute-start.2 = (bf16[112,1152]{1,0:T(8,128)(2,1)S(1)}, bf16[112,1152]{1,0:T(8,128)(2,1)S(1)}, u32[]{:S(2)}, u32[]{:S(2)}) collective-permute-start(bf16[112,1152]{1,0:T(8,128)(2,1)S(1)} %collective-permute-done.refs_1_), channel_id=1, source_target_pairs={{0,2},{1,3},{2,0},{3,1},{4,6},{5,7},{6,4},{7,5},{8,10},{9,11},{10,... | collective-permute-start | bytes 774152 | tf_op jit(solution)/shard_map/tokens/ppermute | solution.py:195
  30.4 0.1 collective-permute-start.9
  30.5 0.5 collective-permute-start.7
  31.0 0.1 collective-permute-start.8
  31.1 4.9 %collective-permute-done.2.refs_1_.refs_3_ = bf16[112,1152]{1,0:T(8,128)(2,1)S(1)} collective-permute-done((bf16[112,1152]{1,0:T(8,128)(2,1)S(1)}, bf16[112,1152]{1,0:T(8,128)(2,1)S(1)}, u32[]{:S(2)}, u32[]{:S(2)}) %collective-permute-start.2) | collective-permute-done | bytes 258080 | tf_op jit(solution)/shard_map/tokens/ppermute | solution.py:195
  36.0 4.9 %collective-permute-done.3.refs_4_.came = bf16[1024,384]{1,0:T(8,128)(2,1)S(1)} collective-permute-done((bf16[1024,384]{1,0:T(8,128)(2,1)S(1)}, bf16[1024,384]{1,0:T(8,128)(2,1)S(1)}, u32[]{:S(2)}, u32[]{:S(2)}) %collective-permute-start.3) | collective-permute-done | bytes 786464 | tf_op jit(solution)/shard_map/swap/ppermute | solution.py:195
  40.9 1.6 %collective-permute-start.4 = (bf16[1024,384]{1,0:T(8,128)(2,1)S(1)}, bf16[1024,384]{1,0:T(8,128)(2,1)S(1)}, u32[]{:S(2)}, u32[]{:S(2)}) collective-permute-start(bf16[1024,384]{1,0:T(8,128)(2,1)S(1)} %collective-permute-done.3.refs_4_.came), channel_id=1, source_target_pairs={{0,16},{16,0},{1,17},{17,1},{2,18},{18,2},{3,19},{19,3},{4,20},{20... | collective-permute-start | bytes 2359304 | tf_op jit(solution)/shard_map/trade/ppermute | solution.py:199
  42.5 2.3 %shard_map.112 = (f32[112,1024]{1,0:T(8,128)S(1)}, f32[112,1024]{1,0:T(8,128)S(1)}) custom-call(s32[16]{0:T(128)S(1)} %copy-done.3, bf16[112,1152]{1,0:T(8,128)(2,1)S(1)} %collective-permute-done.1.refs_0_.refs_2_, bf16[112,1152]{1,0:T(8,128)(2,1)S(1)} %collective-permute-done.2.refs_1_.refs_3_, bf16[1024,384]{1,0:T(8,128)(2,1)S(1)} %bitcast.24, ...), custom_call_target="tpu_custom_call" | custom-call | tf_op jit(solution)/shard_map/pallas_call | solution.py:119
  44.9 2.3 %shard_map.111 = (f32[112,1024]{1,0:T(8,128)S(1)}, f32[112,1024]{1,0:T(8,128)S(1)}) custom-call(s32[16]{0:T(128)S(1)} %copy-done.3, bf16[112,1152]{1,0:T(8,128)(2,1)S(1)} %fusion.1.refs_0_, bf16[112,1152]{1,0:T(8,128)(2,1)S(1)} %collective-permute-done.refs_1_, bf16[1024,384]{1,0:T(8,128)(2,1)S(1)} %bitcast.25, bf16[1024,384]{1,0:T(8,128)(2,1)S(1)} %bitcast.21, ...), custom_call_target="tpu_custom_call" | custom-call | tf_op jit(solution)/shard_map/pallas_call | solution.py:119
  47.2 0.1 collective-permute-start.5
  47.3 14.3 %collective-permute-done.6.refs_3_.came = bf16[384,512]{1,0:T(8,128)(2,1)S(1)} collective-permute-done((bf16[384,512]{1,0:T(8,128)(2,1)S(1)}, bf16[384,512]{1,0:T(8,128)(2,1)S(1)}, u32[]{:S(2)}, u32[]{:S(2)}) %collective-permute-start.6) | collective-permute-done | bytes 393248 | tf_op jit(solution)/shard_map/swap/ppermute | solution.py:195
  61.5 0.5 collective-permute-start.11
  62.1 0.8 collective-permute-start.15
  62.8 1.0 %collective-permute-done.10.refs_7_ = bf16[1024,384]{1,0:T(8,128)(2,1)S(1)} collective-permute-done((bf16[1024,384]{1,0:T(8,128)(2,1)S(1)}, bf16[1024,384]{1,0:T(8,128)(2,1)S(1)}, u32[]{:S(2)}, u32[]{:S(2)}) %collective-permute-start.10) | collective-permute-done | bytes 786464 | tf_op jit(solution)/shard_map/y_near/ppermute | solution.py:195
  63.8 2.2 %shard_map.113.refs_2_ = bf16[448,768]{1,0:T(8,128)(2,1)S(1)} custom-call(bf16[112,1152]{1,0:T(8,128)(2,1)S(1)} %fusion.1.refs_0_, bf16[112,1152]{1,0:T(8,128)(2,1)S(1)} %collective-permute-done.refs_1_, bf16[112,1152]{1,0:T(8,128)(2,1)S(1)} %collective-permute-done.1.refs_0_.refs_2_, bf16[112,1152]{1,0:T(8,128)(2,1)S(1)} %collective-permute-done.2.refs_1_.refs_3_, ...), custom_call_target="tpu_custom_call" | custom-call | tf_op jit(solution)/shard_map/pallas_call | solution.py:119
  66.0 0.9 %shard_map.115 = (bf16[112,512]{1,0:T(8,128)(2,1)S(1)}, bf16[112,512]{1,0:T(8,128)(2,1)S(1)}) custom-call(s32[16]{0:T(128)S(1)} %copy-done.3, bf16[112,1152]{1,0:T(8,128)(2,1)S(1)} %collective-permute-done.1.refs_0_.refs_2_, bf16[112,1152]{1,0:T(8,128)(2,1)S(1)} %collective-permute-done.2.refs_1_.refs_3_, bf16[448,768]{1,0:T(8,128)(2,1)S(1)} %shard_map.113.refs_2_, ...), custom_call_target="tpu_custom_call" | custom-call | tf_op jit(solution)/shard_map/pallas_call | solution.py:119
  67.0 0.0 copy-start.4
  67.0 0.6 collective-permute-start.14
  67.5 0.9 %shard_map.114 = (f32[112,512]{1,0:T(8,128)S(1)}, bf16[112,512]{1,0:T(8,128)(2,1)S(1)}) custom-call(s32[16]{0:T(128)S(1)} %copy-done.3, bf16[112,1152]{1,0:T(8,128)(2,1)S(1)} %fusion.1.refs_0_, bf16[112,1152]{1,0:T(8,128)(2,1)S(1)} %collective-permute-done.refs_1_, bf16[448,768]{1,0:T(8,128)(2,1)S(1)} %shard_map.113.refs_2_, ...), custom_call_target="tpu_custom_call" | custom-call | tf_op jit(solution)/shard_map/pallas_call | solution.py:119
  68.5 2.5 %collective-permute-start.12 = (bf16[112,512]{1,0:T(8,128)(2,1)S(1)}, bf16[112,512]{1,0:T(8,128)(2,1)S(1)}, u32[]{:S(2)}, u32[]{:S(2)}) collective-permute-start(bf16[112,512]{1,0:T(8,128)(2,1)S(1)} %get-tuple-element.38), channel_id=1, source_target_pairs={{0,4},{1,5},{2,6},{3,7},{4,0},{5,1},{6,2},{7,3},{8,12},{9,13},{10,... | collective-permute-start | bytes 344072 | tf_op jit(solution)/shard_map/sums/ppermute | solution.py:195
  71.0 1.4 %shard_map.117 = bf16[1024,384]{1,0:T(8,128)(2,1)} custom-call(s32[16]{0:T(128)S(1)} %copy-done.4, bf16[1024,384]{1,0:T(8,128)(2,1)S(1)} %bitcast.22, bf16[1024,384]{1,0:T(8,128)(2,1)S(1)} %collective-permute-done.3.refs_4_.came, bf16[1024,384]{1,0:T(8,128)(2,1)S(1)} %collective-permute-done.4.refs_5_.other), custom_call_target="tpu_custom_call" | custom-call | tf_op jit(solution)/shard_map/pallas_call | solution.py:169
  72.5 1.4 %shard_map.116 = bf16[1024,384]{1,0:T(8,128)(2,1)} custom-call(s32[16]{0:T(128)S(1)} %copy-done.4, bf16[1024,384]{1,0:T(8,128)(2,1)S(1)} %bitcast.26, bf16[1024,384]{1,0:T(8,128)(2,1)S(1)} %collective-permute-done.3.refs_4_.came, bf16[1024,384]{1,0:T(8,128)(2,1)S(1)} %collective-permute-done.4.refs_5_.other), custom_call_target="tpu_custom_call" | custom-call | tf_op jit(solution)/shard_map/pallas_call | solution.py:169
  74.0 1.7 %collective-permute-done.12.refs_1_ = bf16[112,512]{1,0:T(8,128)(2,1)S(1)} collective-permute-done((bf16[112,512]{1,0:T(8,128)(2,1)S(1)}, bf16[112,512]{1,0:T(8,128)(2,1)S(1)}, u32[]{:S(2)}, u32[]{:S(2)}) %collective-permute-start.12) | collective-permute-done | bytes 114720 | tf_op jit(solution)/shard_map/sums/ppermute | solution.py:195
  75.6 0.5 collective-permute-start.13
  76.2 1.2 %collective-permute-done.16.refs_4_ = bf16[384,512]{1,0:T(8,128)(2,1)S(1)} collective-permute-done((bf16[384,512]{1,0:T(8,128)(2,1)S(1)}, bf16[384,512]{1,0:T(8,128)(2,1)S(1)}, u32[]{:S(2)}, u32[]{:S(2)}) %collective-permute-start.16) | collective-permute-done | bytes 393248 | tf_op jit(solution)/shard_map/y_near/ppermute | solution.py:195
  77.4 0.9 %shard_map.119 = (bf16[112,512]{1,0:T(8,128)(2,1)S(1)}, bf16[112,512]{1,0:T(8,128)(2,1)S(1)}) custom-call(s32[16]{0:T(128)S(1)} %copy-done.3, bf16[112,1152]{1,0:T(8,128)(2,1)S(1)} %collective-permute-done.1.refs_0_.refs_2_, bf16[112,1152]{1,0:T(8,128)(2,1)S(1)} %collective-permute-done.2.refs_1_.refs_3_, bf16[448,768]{1,0:T(8,128)(2,1)S(1)} %shard_map.113.refs_2_, ...), custom_call_target="tpu_custom_call" | custom-call | tf_op jit(solution)/shard_map/pallas_call | solution.py:119
  78.3 0.6 collective-permute-start.18
  78.9 1.2 %collective-permute-start.19 = (bf16[112,512]{1,0:T(8,128)(2,1)S(1)}, bf16[112,512]{1,0:T(8,128)(2,1)S(1)}, u32[]{:S(2)}, u32[]{:S(2)}) collective-permute-start(bf16[112,512]{1,0:T(8,128)(2,1)S(1)} %get-tuple-element.46), channel_id=1, source_target_pairs={{0,6},{1,7},{2,4},{3,5},{4,2},{5,3},{6,0},{7,1},{8,14},{9,15},{10,... | collective-permute-start | bytes 344072 | tf_op jit(solution)/shard_map/sums/ppermute | solution.py:195
  80.1 0.9 %shard_map.118 = (f32[112,512]{1,0:T(8,128)S(1)}, bf16[112,512]{1,0:T(8,128)(2,1)S(1)}) custom-call(s32[16]{0:T(128)S(1)} %copy-done.3, bf16[112,1152]{1,0:T(8,128)(2,1)S(1)} %fusion.1.refs_0_, bf16[112,1152]{1,0:T(8,128)(2,1)S(1)} %collective-permute-done.refs_1_, bf16[448,768]{1,0:T(8,128)(2,1)S(1)} %shard_map.113.refs_2_, ...), custom_call_target="tpu_custom_call" | custom-call | tf_op jit(solution)/shard_map/pallas_call | solution.py:119
  81.1 1.8 %collective-permute-start.17 = (bf16[112,512]{1,0:T(8,128)(2,1)S(1)}, bf16[112,512]{1,0:T(8,128)(2,1)S(1)}, u32[]{:S(2)}, u32[]{:S(2)}) collective-permute-start(bf16[112,512]{1,0:T(8,128)(2,1)S(1)} %get-tuple-element.44), channel_id=1, source_target_pairs={{0,4},{1,5},{2,6},{3,7},{4,0},{5,1},{6,2},{7,3},{8,12},{9,13},{10,... | collective-permute-start | bytes 344072 | tf_op jit(solution)/shard_map/sums/ppermute | solution.py:195
  82.9 1.4 %shard_map.121 = bf16[384,1024]{1,0:T(8,128)(2,1)} custom-call(s32[16]{0:T(128)S(1)} %copy-done.4, bf16[384,1024]{1,0:T(8,128)(2,1)S(1)} %bitcast.18, bf16[384,512]{1,0:T(8,128)(2,1)S(1)} %collective-permute-done.6.refs_3_.came, bf16[384,512]{1,0:T(8,128)(2,1)S(1)} %collective-permute-done.15.refs_3_.other), custom_call_target="tpu_custom_call" | custom-call | tf_op jit(solution)/shard_map/pallas_call | solution.py:169
  84.4 1.8 %collective-permute-done.18.refs_6_ = bf16[112,512]{1,0:T(8,128)(2,1)S(1)} collective-permute-done((bf16[112,512]{1,0:T(8,128)(2,1)S(1)}, bf16[112,512]{1,0:T(8,128)(2,1)S(1)}, u32[]{:S(2)}, u32[]{:S(2)}) %collective-permute-start.18) | collective-permute-done | bytes 114720 | tf_op jit(solution)/shard_map/sums/ppermute | solution.py:195
  86.1 1.1 %collective-permute-done.17.refs_5_ = bf16[112,512]{1,0:T(8,128)(2,1)S(1)} collective-permute-done((bf16[112,512]{1,0:T(8,128)(2,1)S(1)}, bf16[112,512]{1,0:T(8,128)(2,1)S(1)}, u32[]{:S(2)}, u32[]{:S(2)}) %collective-permute-start.17) | collective-permute-done | bytes 114720 | tf_op jit(solution)/shard_map/sums/ppermute | solution.py:195
  87.2 0.8 shard_map.120
  (27 shorter events, 0.2 us)
Async XLA Ops:
  2.2 4.4 %copy-start.6 = (f32[112,8]{0,1:T(8,128)S(1)}, f32[112,8]{0,1:T(8,128)}, u32[]{:S(2)}) copy-start(f32[112,8]{0,1:T(8,128)} %param.10) | copy-start | bytes 10756
  2.2 4.4 %copy-start.7 = (s32[112,8]{0,1:T(8,128)S(1)}, s32[112,8]{0,1:T(8,128)}, u32[]{:S(2)}) copy-start(s32[112,8]{0,1:T(8,128)} %param.9) | copy-start | bytes 10756
  2.2 4.5 %copy-start.5 = (bf16[112,1024]{1,0:T(8,128)(2,1)S(1)}, bf16[112,1024]{1,0:T(8,128)(2,1)}, u32[]{:S(2)}) copy-start(bf16[112,1024]{1,0:T(8,128)(2,1)} %param.8) | copy-start | bytes 688132
  2.2 28.2 %copy-start = (bf16[1,384,1024]{2,1,0:T(8,128)(2,1)S(1)}, bf16[1,384,1024]{2,1,0:T(8,128)(2,1)}, u32[]{:S(2)}) copy-start(bf16[1,384,1024]{2,1,0:T(8,128)(2,1)} %param.13) | copy-start | bytes 2359300
  2.4 38.5 %collective-permute-start.3 = (bf16[1024,384]{1,0:T(8,128)(2,1)S(1)}, bf16[1024,384]{1,0:T(8,128)(2,1)S(1)}, u32[]{:S(2)}, u32[]{:S(2)}) collective-permute-start(bf16[1024,384]{1,0:T(8,128)(2,1)S(1)} %maximum_select_fusion), channel_id=1, source_target_pairs={{0,8},{1,9},{2,10},{3,11},{4,12},{5,13},{6,14},{7,15},{8,0},{9,1},... | collective-permute-start | bytes 2359304 | tf_op jit(solution)/shard_map/swap/ppermute | solution.py:195
  6.7 23.8 %copy-start.2 = (bf16[1,1024,384]{2,1,0:T(8,128)(2,1)S(1)}, bf16[1,1024,384]{2,1,0:T(8,128)(2,1)}, u32[]{:S(2)}) copy-start(bf16[1,1024,384]{2,1,0:T(8,128)(2,1)} %param.11) | copy-start | bytes 2359300
  6.7 24.3 %copy-start.1 = (bf16[1,1024,384]{2,1,0:T(8,128)(2,1)S(1)}, bf16[1,1024,384]{2,1,0:T(8,128)(2,1)}, u32[]{:S(2)}) copy-start(bf16[1,1024,384]{2,1,0:T(8,128)(2,1)} %param.12) | copy-start | bytes 2359300
  6.7 35.8 %copy-start.3 = (s32[16]{0:T(128)S(1)}, s32[16]{0:T(128)}, u32[]{:S(2)}) copy-start(s32[16]{0:T(128)} %placement.11) | copy-start | bytes 196
  6.8 22.1 %collective-permute-start = (bf16[112,1152]{1,0:T(8,128)(2,1)S(1)}, bf16[112,1152]{1,0:T(8,128)(2,1)S(1)}, u32[]{:S(2)}, u32[]{:S(2)}) collective-permute-start(bf16[112,1152]{1,0:T(8,128)(2,1)S(1)} %fusion.1.refs_0_), channel_id=1, source_target_pairs={{0,4},{1,5},{2,6},{3,7},{4,0},{5,1},{6,2},{7,3},{8,12},{9,13},{10,... | collective-permute-start | bytes 774152 | tf_op jit(solution)/shard_map/tokens/ppermute | solution.py:195
  8.4 22.6 %collective-permute-start.1 = (bf16[112,1152]{1,0:T(8,128)(2,1)S(1)}, bf16[112,1152]{1,0:T(8,128)(2,1)S(1)}, u32[]{:S(2)}, u32[]{:S(2)}) collective-permute-start(bf16[112,1152]{1,0:T(8,128)(2,1)S(1)} %fusion.1.refs_0_), channel_id=1, source_target_pairs={{0,2},{1,3},{2,0},{3,1},{4,6},{5,7},{6,4},{7,5},{8,10},{9,11},{10,... | collective-permute-start | bytes 774152 | tf_op jit(solution)/shard_map/tokens/ppermute | solution.py:195
  28.9 7.1 %collective-permute-start.2 = (bf16[112,1152]{1,0:T(8,128)(2,1)S(1)}, bf16[112,1152]{1,0:T(8,128)(2,1)S(1)}, u32[]{:S(2)}, u32[]{:S(2)}) collective-permute-start(bf16[112,1152]{1,0:T(8,128)(2,1)S(1)} %collective-permute-done.refs_1_), channel_id=1, source_target_pairs={{0,2},{1,3},{2,0},{3,1},{4,6},{5,7},{6,4},{7,5},{8,10},{9,11},{10,... | collective-permute-start | bytes 774152 | tf_op jit(solution)/shard_map/tokens/ppermute | solution.py:195
  30.4 12.1 %collective-permute-start.9 = (bf16[384,1024]{1,0:T(8,128)(2,1)S(1)}, bf16[384,1024]{1,0:T(8,128)(2,1)S(1)}, u32[]{:S(2)}, u32[]{:S(2)}) collective-permute-start(bf16[384,1024]{1,0:T(8,128)(2,1)S(1)} %bitcast.15), channel_id=1, source_target_pairs={{0,1},{1,0},{2,3},{3,2},{4,5},{5,4},{6,7},{7,6},{8,9},{9,8},{10,11... | collective-permute-start | bytes 2359304 | tf_op jit(solution)/shard_map/near/ppermute | solution.py:195
  30.5 12.0 %collective-permute-start.7 = (bf16[1024,384]{1,0:T(8,128)(2,1)S(1)}, bf16[1024,384]{1,0:T(8,128)(2,1)S(1)}, u32[]{:S(2)}, u32[]{:S(2)}) collective-permute-start(bf16[1024,384]{1,0:T(8,128)(2,1)S(1)} %bitcast.23), channel_id=1, source_target_pairs={{0,1},{1,0},{2,3},{3,2},{4,5},{5,4},{6,7},{7,6},{8,9},{9,8},{10,11... | collective-permute-start | bytes 2359304 | tf_op jit(solution)/shard_map/near/ppermute | solution.py:195
  31.0 11.5 %collective-permute-start.8 = (bf16[1024,384]{1,0:T(8,128)(2,1)S(1)}, bf16[1024,384]{1,0:T(8,128)(2,1)S(1)}, u32[]{:S(2)}, u32[]{:S(2)}) collective-permute-start(bf16[1024,384]{1,0:T(8,128)(2,1)S(1)} %bitcast.19), channel_id=1, source_target_pairs={{0,1},{1,0},{2,3},{3,2},{4,5},{5,4},{6,7},{7,6},{8,9},{9,8},{10,11... | collective-permute-start | bytes 2359304 | tf_op jit(solution)/shard_map/near/ppermute | solution.py:195
  40.9 20.6 %collective-permute-start.4 = (bf16[1024,384]{1,0:T(8,128)(2,1)S(1)}, bf16[1024,384]{1,0:T(8,128)(2,1)S(1)}, u32[]{:S(2)}, u32[]{:S(2)}) collective-permute-start(bf16[1024,384]{1,0:T(8,128)(2,1)S(1)} %collective-permute-done.3.refs_4_.came), channel_id=1, source_target_pairs={{0,16},{16,0},{1,17},{17,1},{2,18},{18,2},{3,19},{19,3},{4,20},{20... | collective-permute-start | bytes 2359304 | tf_op jit(solution)/shard_map/trade/ppermute | solution.py:199
  42.5 19.1 %collective-permute-start.6 = (bf16[384,512]{1,0:T(8,128)(2,1)S(1)}, bf16[384,512]{1,0:T(8,128)(2,1)S(1)}, u32[]{:S(2)}, u32[]{:S(2)}) collective-permute-start(bf16[384,512]{1,0:T(8,128)(2,1)S(1)} %slice_select_fusion), channel_id=1, source_target_pairs={{0,8},{1,9},{2,10},{3,11},{4,12},{5,13},{6,14},{7,15},{8,0},{9,1},... | collective-permute-start | bytes 1179656 | tf_op jit(solution)/shard_map/swap/ppermute | solution.py:195
  47.2 15.6 %collective-permute-start.5 = (bf16[1024,384]{1,0:T(8,128)(2,1)S(1)}, bf16[1024,384]{1,0:T(8,128)(2,1)S(1)}, u32[]{:S(2)}, u32[]{:S(2)}) collective-permute-start(bf16[1024,384]{1,0:T(8,128)(2,1)S(1)} %collective-permute-done.3.refs_4_.came), channel_id=1, source_target_pairs={{0,1},{1,0},{2,3},{3,2},{4,5},{5,4},{6,7},{7,6},{8,9},{9,8},{10,11... | collective-permute-start | bytes 2359304 | tf_op jit(solution)/shard_map/z_near/ppermute | solution.py:195
  61.5 2.3 %collective-permute-start.10 = (bf16[1024,384]{1,0:T(8,128)(2,1)S(1)}, bf16[1024,384]{1,0:T(8,128)(2,1)S(1)}, u32[]{:S(2)}, u32[]{:S(2)}) collective-permute-start(bf16[1024,384]{1,0:T(8,128)(2,1)S(1)} %collective-permute-done.4.refs_5_.other), channel_id=1, source_target_pairs={{0,1},{1,0},{2,3},{3,2},{4,5},{5,4},{6,7},{7,6},{8,9},{9,8},{10,11... | collective-permute-start | bytes 2359304 | tf_op jit(solution)/shard_map/y_near/ppermute | solution.py:195
  61.5 4.5 %collective-permute-start.11 = (bf16[384,512]{1,0:T(8,128)(2,1)S(1)}, bf16[384,512]{1,0:T(8,128)(2,1)S(1)}, u32[]{:S(2)}, u32[]{:S(2)}) collective-permute-start(bf16[384,512]{1,0:T(8,128)(2,1)S(1)} %collective-permute-done.6.refs_3_.came), channel_id=1, source_target_pairs={{0,1},{1,0},{2,3},{3,2},{4,5},{5,4},{6,7},{7,6},{8,9},{9,8},{10,11... | collective-permute-start | bytes 1179656 | tf_op jit(solution)/shard_map/z_near/ppermute | solution.py:195
  62.1 11.9 %collective-permute-start.15 = (bf16[384,512]{1,0:T(8,128)(2,1)S(1)}, bf16[384,512]{1,0:T(8,128)(2,1)S(1)}, u32[]{:S(2)}, u32[]{:S(2)}) collective-permute-start(bf16[384,512]{1,0:T(8,128)(2,1)S(1)} %collective-permute-done.6.refs_3_.came), channel_id=1, source_target_pairs={{0,16},{16,0},{1,17},{17,1},{2,18},{18,2},{3,19},{19,3},{4,20},{20... | collective-permute-start | bytes 1179656 | tf_op jit(solution)/shard_map/trade/ppermute | solution.py:199
  67.0 4.1 %copy-start.4 = (s32[16]{0:T(128)S(1)}, s32[16]{0:T(128)}, u32[]{:S(2)}) copy-start(s32[16]{0:T(128)} %flags.2) | copy-start | bytes 196
  67.0 7.0 %collective-permute-start.14 = (bf16[112,512]{1,0:T(8,128)(2,1)S(1)}, bf16[112,512]{1,0:T(8,128)(2,1)S(1)}, u32[]{:S(2)}, u32[]{:S(2)}) collective-permute-start(bf16[112,512]{1,0:T(8,128)(2,1)S(1)} %get-tuple-element.40), channel_id=1, source_target_pairs={{0,6},{1,7},{2,4},{3,5},{4,2},{5,3},{6,0},{7,1},{8,14},{9,15},{10,... | collective-permute-start | bytes 344072 | tf_op jit(solution)/shard_map/sums/ppermute | solution.py:195
  68.5 7.1 %collective-permute-start.12 = (bf16[112,512]{1,0:T(8,128)(2,1)S(1)}, bf16[112,512]{1,0:T(8,128)(2,1)S(1)}, u32[]{:S(2)}, u32[]{:S(2)}) collective-permute-start(bf16[112,512]{1,0:T(8,128)(2,1)S(1)} %get-tuple-element.38), channel_id=1, source_target_pairs={{0,4},{1,5},{2,6},{3,7},{4,0},{5,1},{6,2},{7,3},{8,12},{9,13},{10,... | collective-permute-start | bytes 344072 | tf_op jit(solution)/shard_map/sums/ppermute | solution.py:195
  75.6 1.7 %collective-permute-start.16 = (bf16[384,512]{1,0:T(8,128)(2,1)S(1)}, bf16[384,512]{1,0:T(8,128)(2,1)S(1)}, u32[]{:S(2)}, u32[]{:S(2)}) collective-permute-start(bf16[384,512]{1,0:T(8,128)(2,1)S(1)} %collective-permute-done.15.refs_3_.other), channel_id=1, source_target_pairs={{0,1},{1,0},{2,3},{3,2},{4,5},{5,4},{6,7},{7,6},{8,9},{9,8},{10,11... | collective-permute-start | bytes 1179656 | tf_op jit(solution)/shard_map/y_near/ppermute | solution.py:195
  75.6 8.7 %collective-permute-start.13 = (bf16[112,512]{1,0:T(8,128)(2,1)S(1)}, bf16[112,512]{1,0:T(8,128)(2,1)S(1)}, u32[]{:S(2)}, u32[]{:S(2)}) collective-permute-start(bf16[112,512]{1,0:T(8,128)(2,1)S(1)} %get-tuple-element.39), channel_id=1, source_target_pairs={{0,2},{1,3},{2,0},{3,1},{4,6},{5,7},{6,4},{7,5},{8,10},{9,11},{10,... | collective-permute-start | bytes 344072 | tf_op jit(solution)/shard_map/sums/ppermute | solution.py:195
  78.3 7.8 %collective-permute-start.18 = (bf16[112,512]{1,0:T(8,128)(2,1)S(1)}, bf16[112,512]{1,0:T(8,128)(2,1)S(1)}, u32[]{:S(2)}, u32[]{:S(2)}) collective-permute-start(bf16[112,512]{1,0:T(8,128)(2,1)S(1)} %get-tuple-element.45), channel_id=1, source_target_pairs={{0,2},{1,3},{2,0},{3,1},{4,6},{5,7},{6,4},{7,5},{8,10},{9,11},{10,... | collective-permute-start | bytes 344072 | tf_op jit(solution)/shard_map/sums/ppermute | solution.py:195
  78.9 7.2 %collective-permute-start.19 = (bf16[112,512]{1,0:T(8,128)(2,1)S(1)}, bf16[112,512]{1,0:T(8,128)(2,1)S(1)}, u32[]{:S(2)}, u32[]{:S(2)}) collective-permute-start(bf16[112,512]{1,0:T(8,128)(2,1)S(1)} %get-tuple-element.46), channel_id=1, source_target_pairs={{0,6},{1,7},{2,4},{3,5},{4,2},{5,3},{6,0},{7,1},{8,14},{9,15},{10,... | collective-permute-start | bytes 344072 | tf_op jit(solution)/shard_map/sums/ppermute | solution.py:195
  81.1 6.1 %collective-permute-start.17 = (bf16[112,512]{1,0:T(8,128)(2,1)S(1)}, bf16[112,512]{1,0:T(8,128)(2,1)S(1)}, u32[]{:S(2)}, u32[]{:S(2)}) collective-permute-start(bf16[112,512]{1,0:T(8,128)(2,1)S(1)} %get-tuple-element.44), channel_id=1, source_target_pairs={{0,4},{1,5},{2,6},{3,7},{4,0},{5,1},{6,2},{7,3},{8,12},{9,13},{10,... | collective-permute-start | bytes 344072 | tf_op jit(solution)/shard_map/sums/ppermute | solution.py:195

commit v5 on v3

--- a/solution.py
+++ b/solution.py
@@ -65,41 +65,44 @@
 
 
 def hidden_kernel(blocks, width, *refs):
-    rows, weights, out, x = refs[:blocks], refs[blocks : blocks + 4], refs[blocks + 4], refs[blocks + 5]
+    rows, own, other, out, x = refs[:blocks], refs[blocks], refs[blocks + 1], refs[blocks + 2], refs[blocks + 3]
     height = rows[0].shape[0]
     half = lax.axis_index("dp") % 2
+    depth = own.shape[0] // 2
+    at = pl.multiple_of(half * depth, depth)
+    off = pl.multiple_of(depth - at, depth)
     for first in range(0, blocks, 2):
         for i in range(2):
             x[i * height : (i + 1) * height, :] = rows[first + i][:, :width]
-        for slot in range(2):
-            own, other = weights[2 * slot : 2 * slot + 2]
-            depth, ff = own.shape[0] // 2, own.shape[1]
-            at = pl.multiple_of(half * depth, depth)
-            off = pl.multiple_of(depth - at, depth)
-            xa, xb = x[:, pl.ds(at, depth)], x[:, pl.ds(off, depth)]
-            gate = dot(xa, own[:depth, :]) + dot(xb, other[:depth, :])
-            up = dot(xa, own[depth:, :]) + dot(xb, other[depth:, :])
-            span = slice(first * height, (first + 2) * height)
-            out[span, slot * ff : (slot + 1) * ff] = activate(gate, up)
-
-
-def down_kernel(count, first, flip, placement, *refs):
-    rows, hidden, downs, base, outs = refs[:2], refs[2], refs[3:5], refs[5:7], refs[7:9]
+        xa, xb = x[:, pl.ds(at, depth)], x[:, pl.ds(off, depth)]
+        gate = dot(xa, own[:depth, :]) + dot(xb, other[:depth, :])
+        up = dot(xa, own[depth:, :]) + dot(xb, other[depth:, :])
+        out[first * height : (first + 2) * height, :] = activate(gate, up)
+
+
+def down_kernel(count, flips, blocks, half_flip, placement, *refs):
+    number = len(blocks)
+    rows, refs = refs[:number], refs[number:]
+    experts, refs = refs[: 2 * len(flips)], refs[2 * len(flips) :]
+    base, outs = refs[:number], refs[number:]
     height, part = outs[0].shape
-    ff = downs[0].shape[0]
+    width = 2 * part
     me = lax.axis_index("expert")
     far = lax.axis_size("expert") // 2
-    half = (lax.axis_index("dp") + flip) % 2
+    half = (lax.axis_index("dp") + half_flip) % 2
     columns = pl.ds(pl.multiple_of(half * part, part), part)
-    totals = [base[i][:, columns] for i in range(2)]
-    for slot, down in enumerate(downs):
-        span = slice(first * height, (first + 2) * height)
-        value = rounded(dot(hidden[span, slot * ff : (slot + 1) * ff], down[...]))
-        for i in range(2):
-            weight = token_weight(rows[i][:, base[0].shape[1]:], placement[me ^ far ^ slot], count)
-            totals[i] = totals[i] + value[i * height : (i + 1) * height, :] * weight
-    for i in range(2):
-        outs[i][...] = totals[i].astype(outs[i].dtype)
+    for first in range(0, number, 2):
+        pair = range(first, first + 2)
+        totals = {i: base[i][...] if base[i].shape[1] == part else base[i][:, columns] for i in pair}
+        for flip, hidden, down in zip(flips, experts[::2], experts[1::2]):
+            span = slice(blocks[first] * height, (blocks[first] + 2) * height)
+            value = rounded(dot(hidden[span, :], down[...]))
+            for i in pair:
+                weight = token_weight(rows[i][:, width:], placement[me ^ far ^ flip], count)
+                at = (i - first) * height
+                totals[i] = totals[i] + value[at : at + height, :] * weight
+        for i in pair:
+            outs[i][...] = totals[i].astype(outs[i].dtype)
 
 
 def finish_kernel(ours, *refs):
@@ -243,31 +246,34 @@
     y_lower = trade(arrived)
     z_near = [send(z_upper, 1, "z_near"), send(arrived, 1, "z_near")]
     y_near = [send(after(y_upper, arrived), 1, "y_near")]
-    hidden = call(
-        functools.partial(hidden_kernel, len(rows), width),
-        jax.ShapeDtypeStruct((len(rows) * height, 2 * ff), jnp.bfloat16),
-        [*rows, z_upper, y_upper, z_near[0], y_near[0]],
-        scratch,
-    )
-
-    def far_sums(flip, downs):
-        parts = {}
-        for first in firsts:
-            for i in (0, 1):
-                parts[first + i] = jnp.bfloat16 if first + i > 0 else jnp.float32
-            shape = (height, downs[0].shape[1])
-            parts[first], parts[first + 1] = call(
-                functools.partial(down_kernel, count, first, flip),
-                [jax.ShapeDtypeStruct(shape, parts[first + i]) for i in (0, 1)],
-                [placement, *rows[first : first + 2], hidden, *downs, *base[first]],
-                scalars=1,
-            )
-        return parts
+    hidden = [
+        call(
+            functools.partial(hidden_kernel, len(rows), width),
+            jax.ShapeDtypeStruct((len(rows) * height, ff), jnp.bfloat16),
+            [*rows, own_part, other_part],
+            scratch,
+        )
+        for own_part, other_part in ((z_upper, y_upper), (z_near[0], y_near[0]))
+    ]
+
+    def far_sums(flips, downs, half_flip, blocks, sums, last):
+        kinds = [jnp.bfloat16 if last and i > 0 else jnp.float32 for i in blocks]
+        experts = [x for flip, down in zip(flips, downs) for x in (hidden[flip], down)]
+        out = call(
+            functools.partial(down_kernel, count, flips, blocks, half_flip),
+            [jax.ShapeDtypeStruct((height, part), kind) for kind in kinds],
+            [placement, *(rows[i] for i in blocks), *experts, *(sums[i] for i in blocks)],
+            scalars=1,
+        )
+        return dict(zip(blocks, out))
 
     def collect(parts):
         return [parts[0]] + [send(parts[i], masks[i], "sums") for i in reversed(range(1, len(parts)))]
 
-    parts = far_sums(0, [arrived, z_near[1]])
+    near_sums = [x for first in reversed(firsts) for x in base[first]]
+    parts = {}
+    for first in firsts:
+        parts |= far_sums((0, 1), [arrived, z_near[1]], 0, (first, first + 1), near_sums, True)
     flags = after(swap_flags, parts)
     stored = [
         store(0, 0, flags, own[0], z_upper, y_upper),
@@ -276,7 +282,11 @@
     ours = collect(parts)
     landed = after(y_lower, stored, ours[1:-1])
     y_near.append(send(landed, 1, "y_near"))
-    last_parts = far_sums(1, [landed, y_near[1]])
+    everyone = tuple(range(len(rows)))
+    last_sums = far_sums((0,), [landed], 1, everyone, near_sums, False)
+    last_parts = {}
+    for first in firsts:
+        last_parts |= far_sums((1,), [y_near[1]], 1, (first, first + 1), last_sums, True)
     stored.append(store(1, 0, after(swap_flags, last_parts), own[2], z_lower, y_lower))
     others = collect(last_parts)
     mixed = call(

time: 87.2 us -> 86.6 us (level)
  waiting for transfers between devices: 49.8 us -> 48.6 us
  Pallas kernels: 15.8 us -> 16.7 us
    ppermute x18, waiting for transfers between devices: 49.2 us -> 47.5 us  [send(): return lax.ppermute(value, 'expert', [(d, d ^ bit) for d in range(count)])]
    pallas_call x8 -> x10, Pallas kernels: 11.4 us -> 12.4 us  [call(): pl.pallas_call(kernel, out_shape=out_shape, in_specs=[smem] * scalars + [...]
  transfers between devices with their start and end apart: 20 -> 20, of which waited for: 11 -> 9; matrix products, arithmetic and copies ran while one was open for 0% -> 0% of each run, Pallas kernels for 17% -> 18%
where the time goes in v5:
time: 86.6 us; the launch traced here: 86.5 us
  waiting for transfers between devices  48.6 us (56%)
  starting transfers between devices  18.2 us (21%)
  Pallas kernels  16.7 us (19%)
  local copies, waits for them, and re-layouts  1.67 us (2%)
  between operations  0.93 us (1%)
    ppermute x18, waiting for transfers between devices, send(): return lax.ppermute(value, 'expert', [(d, d ^ bit) for d in range(count)])  47.5 us
    ppermute x18, starting transfers between devices, send(): return lax.ppermute(value, 'expert', [(d, d ^ bit) for d in range(count)])  15.9 us
    pallas_call x10, Pallas kernels, call(): pl.pallas_call(kernel, out_shape=out_shape, in_specs=[smem] * scalars + [...  12.4 us
    pallas_call x3, Pallas kernels, store(): pl.pallas_call(functools.partial(store_kernel, axis, first), out_shape=ja...  4.34 us
    ppermute x2, starting transfers between devices, trade(): return lax.ppermute(value, 'dp', trades)  2.32 us
  transfers between devices with their start and end apart: 20, of which 9 were waited for; matrix products, arithmetic and copies ran while one was open for 0% of the time, Pallas kernels for 18%

profile of v5, /device:TPU:0, one launch (start us, length us, event | category | flops | bytes accessed | tf_op | source)
XLA Modules:
  0.0 86.5 jit_solution(17499038249268593204)
XLA Ops:
  0.6 1.5 %slice_bitcast_fusion = (bf16[512,384]{1,0:T(8,128)(2,1)S(1)}, bf16[512,384]{1,0:T(8,128)(2,1)S(1)}, bf16[512,384]{1,0:T(8,128)(2,1)S(1)}, bf16[512,384]{1,0:T(8,128)(2,1)S(1)}) fusion(bf16[1,1024,384]{2,1,0:T(8,128)(2,1)} %param.12, bf16[1,1024,384]{2,1,0:T(8,128)(2,1)} %param.11), kind=kLoop, calls=%fused_computation.4 | loop fusion | bytes 3145728 | tf_op jit(solution)/shard_map/slice | solution.py:211
  2.2 0.0 copy-start.6
  2.2 0.0 copy-start.7
  2.2 0.0 copy-start.5
  2.2 0.0 copy-start
  2.2 0.2 maximum_select_fusion
  2.4 4.1 %collective-permute-start.3 = (bf16[1024,384]{1,0:T(8,128)(2,1)S(1)}, bf16[1024,384]{1,0:T(8,128)(2,1)S(1)}, u32[]{:S(2)}, u32[]{:S(2)}) collective-permute-start(bf16[1024,384]{1,0:T(8,128)(2,1)S(1)} %maximum_select_fusion), channel_id=1, source_target_pairs={{0,8},{1,9},{2,10},{3,11},{4,12},{5,13},{6,14},{7,15},{8,0},{9,1},... | collective-permute-start | bytes 2359304 | tf_op jit(solution)/shard_map/swap/ppermute | solution.py:198
  6.6 0.1 copy.17
  6.7 0.0 copy-start.1
  6.7 0.0 copy-start.3
  6.8 1.6 %collective-permute-start = (bf16[112,1152]{1,0:T(8,128)(2,1)S(1)}, bf16[112,1152]{1,0:T(8,128)(2,1)S(1)}, u32[]{:S(2)}, u32[]{:S(2)}) collective-permute-start(bf16[112,1152]{1,0:T(8,128)(2,1)S(1)} %fusion.1.refs_0_), channel_id=1, source_target_pairs={{0,4},{1,5},{2,6},{3,7},{4,0},{5,1},{6,2},{7,3},{8,12},{9,13},{10,... | collective-permute-start | bytes 774152 | tf_op jit(solution)/shard_map/tokens/ppermute | solution.py:198
  8.4 1.5 %collective-permute-start.1 = (bf16[112,1152]{1,0:T(8,128)(2,1)S(1)}, bf16[112,1152]{1,0:T(8,128)(2,1)S(1)}, u32[]{:S(2)}, u32[]{:S(2)}) collective-permute-start(bf16[112,1152]{1,0:T(8,128)(2,1)S(1)} %fusion.1.refs_0_), channel_id=1, source_target_pairs={{0,2},{1,3},{2,0},{3,1},{4,6},{5,7},{6,4},{7,5},{8,10},{9,11},{10,... | collective-permute-start | bytes 774152 | tf_op jit(solution)/shard_map/tokens/ppermute | solution.py:198
  9.9 19.0 %collective-permute-done.refs_1_ = bf16[112,1152]{1,0:T(8,128)(2,1)S(1)} collective-permute-done((bf16[112,1152]{1,0:T(8,128)(2,1)S(1)}, bf16[112,1152]{1,0:T(8,128)(2,1)S(1)}, u32[]{:S(2)}, u32[]{:S(2)}) %collective-permute-start) | collective-permute-done | bytes 258080 | tf_op jit(solution)/shard_map/tokens/ppermute | solution.py:198
  28.9 1.5 %collective-permute-start.2 = (bf16[112,1152]{1,0:T(8,128)(2,1)S(1)}, bf16[112,1152]{1,0:T(8,128)(2,1)S(1)}, u32[]{:S(2)}, u32[]{:S(2)}) collective-permute-start(bf16[112,1152]{1,0:T(8,128)(2,1)S(1)} %collective-permute-done.refs_1_), channel_id=1, source_target_pairs={{0,2},{1,3},{2,0},{3,1},{4,6},{5,7},{6,4},{7,5},{8,10},{9,11},{10,... | collective-permute-start | bytes 774152 | tf_op jit(solution)/shard_map/tokens/ppermute | solution.py:198
  30.4 0.1 collective-permute-start.8
  30.5 0.5 collective-permute-start.6
  31.0 0.1 collective-permute-start.7
  31.1 4.9 %collective-permute-done.2.refs_3_.refs_1_ = bf16[112,1152]{1,0:T(8,128)(2,1)S(1)} collective-permute-done((bf16[112,1152]{1,0:T(8,128)(2,1)S(1)}, bf16[112,1152]{1,0:T(8,128)(2,1)S(1)}, u32[]{:S(2)}, u32[]{:S(2)}) %collective-permute-start.2) | collective-permute-done | bytes 258080 | tf_op jit(solution)/shard_map/tokens/ppermute | solution.py:198
  36.0 4.9 %collective-permute-done.3.refs_4_.came = bf16[1024,384]{1,0:T(8,128)(2,1)S(1)} collective-permute-done((bf16[1024,384]{1,0:T(8,128)(2,1)S(1)}, bf16[1024,384]{1,0:T(8,128)(2,1)S(1)}, u32[]{:S(2)}, u32[]{:S(2)}) %collective-permute-start.3) | collective-permute-done | bytes 786464 | tf_op jit(solution)/shard_map/swap/ppermute | solution.py:198
  40.9 1.6 %collective-permute-start.4 = (bf16[1024,384]{1,0:T(8,128)(2,1)S(1)}, bf16[1024,384]{1,0:T(8,128)(2,1)S(1)}, u32[]{:S(2)}, u32[]{:S(2)}) collective-permute-start(bf16[1024,384]{1,0:T(8,128)(2,1)S(1)} %collective-permute-done.3.refs_4_.came), channel_id=1, source_target_pairs={{0,16},{16,0},{1,17},{17,1},{2,18},{18,2},{3,19},{19,3},{4,20},{20... | collective-permute-start | bytes 2359304 | tf_op jit(solution)/shard_map/trade/ppermute | solution.py:202
  42.5 2.3 %shard_map.113 = (f32[112,1024]{1,0:T(8,128)S(1)}, f32[112,1024]{1,0:T(8,128)S(1)}) custom-call(s32[16]{0:T(128)S(1)} %copy-done.3, bf16[112,1152]{1,0:T(8,128)(2,1)S(1)} %collective-permute-done.1.refs_2_.refs_0_, bf16[112,1152]{1,0:T(8,128)(2,1)S(1)} %collective-permute-done.2.refs_3_.refs_1_, bf16[1024,384]{1,0:T(8,128)(2,1)S(1)} %bitcast.24, ...), custom_call_target="tpu_custom_call" | custom-call | tf_op jit(solution)/shard_map/pallas_call | solution.py:122
  44.9 2.3 %shard_map.112 = (f32[112,1024]{1,0:T(8,128)S(1)}, f32[112,1024]{1,0:T(8,128)S(1)}) custom-call(s32[16]{0:T(128)S(1)} %copy-done.3, bf16[112,1152]{1,0:T(8,128)(2,1)S(1)} %fusion.1.refs_0_, bf16[112,1152]{1,0:T(8,128)(2,1)S(1)} %collective-permute-done.refs_1_, bf16[1024,384]{1,0:T(8,128)(2,1)S(1)} %bitcast.25, bf16[1024,384]{1,0:T(8,128)(2,1)S(1)} %bitcast.21, ...), custom_call_target="tpu_custom_call" | custom-call | tf_op jit(solution)/shard_map/pallas_call | solution.py:122
  47.2 0.1 collective-permute-start.9
  47.3 14.3 %collective-permute-done.5.refs_3_.came = bf16[384,512]{1,0:T(8,128)(2,1)S(1)} collective-permute-done((bf16[384,512]{1,0:T(8,128)(2,1)S(1)}, bf16[384,512]{1,0:T(8,128)(2,1)S(1)}, u32[]{:S(2)}, u32[]{:S(2)}) %collective-permute-start.5) | collective-permute-done | bytes 393248 | tf_op jit(solution)/shard_map/swap/ppermute | solution.py:198
  61.5 0.5 collective-permute-start.11
  62.1 0.8 collective-permute-start.15
  62.8 1.2 %shard_map.111.refs_2_.refs_4_ = bf16[448,384]{1,0:T(8,128)(2,1)S(1)} custom-call(bf16[112,1152]{1,0:T(8,128)(2,1)S(1)} %fusion.1.refs_0_, bf16[112,1152]{1,0:T(8,128)(2,1)S(1)} %collective-permute-done.refs_1_, bf16[112,1152]{1,0:T(8,128)(2,1)S(1)} %collective-permute-done.1.refs_2_.refs_0_, bf16[112,1152]{1,0:T(8,128)(2,1)S(1)} %collective-permute-done.2.refs_3_.refs_1_, ...), custom_call_target="tpu_custom_call" | custom-call | tf_op jit(solution)/shard_map/pallas_call | solution.py:122
  64.0 1.2 %shard_map.114.refs_4_.refs_2_ = bf16[448,384]{1,0:T(8,128)(2,1)S(1)} custom-call(bf16[112,1152]{1,0:T(8,128)(2,1)S(1)} %fusion.1.refs_0_, bf16[112,1152]{1,0:T(8,128)(2,1)S(1)} %collective-permute-done.refs_1_, bf16[112,1152]{1,0:T(8,128)(2,1)S(1)} %collective-permute-done.1.refs_2_.refs_0_, bf16[112,1152]{1,0:T(8,128)(2,1)S(1)} %collective-permute-done.2.refs_3_.refs_1_, ...), custom_call_target="tpu_custom_call" | custom-call | tf_op jit(solution)/shard_map/pallas_call | solution.py:122
  65.2 1.0 %shard_map.116 = (bf16[112,512]{1,0:T(8,128)(2,1)S(1)}, bf16[112,512]{1,0:T(8,128)(2,1)S(1)}) custom-call(s32[16]{0:T(128)S(1)} %copy-done.3, bf16[112,1152]{1,0:T(8,128)(2,1)S(1)} %collective-permute-done.1.refs_2_.refs_0_, bf16[112,1152]{1,0:T(8,128)(2,1)S(1)} %collective-permute-done.2.refs_3_.refs_1_, bf16[448,384]{1,0:T(8,128)(2,1)S(1)} %shard_map.111.refs_2_.refs_4_, ...), custom_call_target="tpu_custom_call" | custom-call | tf_op jit(solution)/shard_map/pallas_call | solution.py:122
  66.2 1.3 %collective-permute-start.12 = (bf16[112,512]{1,0:T(8,128)(2,1)S(1)}, bf16[112,512]{1,0:T(8,128)(2,1)S(1)}, u32[]{:S(2)}, u32[]{:S(2)}) collective-permute-start(bf16[112,512]{1,0:T(8,128)(2,1)S(1)} %get-tuple-element.42), channel_id=1, source_target_pairs={{0,6},{1,7},{2,4},{3,5},{4,2},{5,3},{6,0},{7,1},{8,14},{9,15},{10,... | collective-permute-start | bytes 344072 | tf_op jit(solution)/shard_map/sums/ppermute | solution.py:198
  67.5 0.5 collective-permute-start.13
  68.1 0.9 %shard_map.115 = (f32[112,512]{1,0:T(8,128)S(1)}, bf16[112,512]{1,0:T(8,128)(2,1)S(1)}) custom-call(s32[16]{0:T(128)S(1)} %copy-done.3, bf16[112,1152]{1,0:T(8,128)(2,1)S(1)} %fusion.1.refs_0_, bf16[112,1152]{1,0:T(8,128)(2,1)S(1)} %collective-permute-done.refs_1_, bf16[448,384]{1,0:T(8,128)(2,1)S(1)} %shard_map.111.refs_2_.refs_4_, ...), custom_call_target="tpu_custom_call" | custom-call | tf_op jit(solution)/shard_map/pallas_call | solution.py:122
  69.0 1.4 %shard_map.118 = bf16[1024,384]{1,0:T(8,128)(2,1)} custom-call(s32[16]{0:T(128)S(1)} %copy-done.4, bf16[1024,384]{1,0:T(8,128)(2,1)S(1)} %bitcast.22, bf16[1024,384]{1,0:T(8,128)(2,1)S(1)} %collective-permute-done.3.refs_4_.came, bf16[1024,384]{1,0:T(8,128)(2,1)S(1)} %collective-permute-done.4.refs_5_.other), custom_call_target="tpu_custom_call" | custom-call | tf_op jit(solution)/shard_map/pallas_call | solution.py:172
  70.5 1.4 %shard_map.117 = bf16[1024,384]{1,0:T(8,128)(2,1)} custom-call(s32[16]{0:T(128)S(1)} %copy-done.4, bf16[1024,384]{1,0:T(8,128)(2,1)S(1)} %bitcast.26, bf16[1024,384]{1,0:T(8,128)(2,1)S(1)} %collective-permute-done.3.refs_4_.came, bf16[1024,384]{1,0:T(8,128)(2,1)S(1)} %collective-permute-done.4.refs_5_.other), custom_call_target="tpu_custom_call" | custom-call | tf_op jit(solution)/shard_map/pallas_call | solution.py:172
  71.9 1.1 %collective-permute-done.15.refs_5_.other = bf16[384,512]{1,0:T(8,128)(2,1)S(1)} collective-permute-done((bf16[384,512]{1,0:T(8,128)(2,1)S(1)}, bf16[384,512]{1,0:T(8,128)(2,1)S(1)}, u32[]{:S(2)}, u32[]{:S(2)}) %collective-permute-start.15) | collective-permute-done | bytes 393248 | tf_op jit(solution)/shard_map/trade/ppermute | solution.py:202
  73.1 1.4 %collective-permute-done.13.refs_2_ = bf16[112,512]{1,0:T(8,128)(2,1)S(1)} collective-permute-done((bf16[112,512]{1,0:T(8,128)(2,1)S(1)}, bf16[112,512]{1,0:T(8,128)(2,1)S(1)}, u32[]{:S(2)}, u32[]{:S(2)}) %collective-permute-start.13) | collective-permute-done | bytes 114720 | tf_op jit(solution)/shard_map/sums/ppermute | solution.py:198
  74.5 0.4 collective-permute-start.14
  74.9 0.9 %shard_map.119 = (f32[112,512]{1,0:T(8,128)S(1)}, f32[112,512]{1,0:T(8,128)S(1)}, f32[112,512]{1,0:T(8,128)S(1)}, f32[112,512]{1,0:T(8,128)S(1)}) custom-call(s32[16]{0:T(128)S(1)} %copy-done.3, bf16[112,1152]{1,0:T(8,128)(2,1)S(1)} %fusion.1.refs_0_, bf16[112,1152]{1,0:T(8,128)(2,1)S(1)} %collective-permute-done.refs_1_, ...), custom_call_target="tpu_custom_call" | custom-call | tf_op jit(solution)/shard_map/pallas_call | solution.py:122
  75.9 0.3 collective-permute-done.16.refs_3_
  76.2 0.8 shard_map.121
  77.0 1.6 %collective-permute-start.17 = (bf16[112,512]{1,0:T(8,128)(2,1)S(1)}, bf16[112,512]{1,0:T(8,128)(2,1)S(1)}, u32[]{:S(2)}, u32[]{:S(2)}) collective-permute-start(bf16[112,512]{1,0:T(8,128)(2,1)S(1)} %get-tuple-element.52), channel_id=1, source_target_pairs={{0,6},{1,7},{2,4},{3,5},{4,2},{5,3},{6,0},{7,1},{8,14},{9,15},{10,... | collective-permute-start | bytes 344072 | tf_op jit(solution)/shard_map/sums/ppermute | solution.py:198
  78.6 1.2 %collective-permute-start.18 = (bf16[112,512]{1,0:T(8,128)(2,1)S(1)}, bf16[112,512]{1,0:T(8,128)(2,1)S(1)}, u32[]{:S(2)}, u32[]{:S(2)}) collective-permute-start(bf16[112,512]{1,0:T(8,128)(2,1)S(1)} %get-tuple-element.53), channel_id=1, source_target_pairs={{0,2},{1,3},{2,0},{3,1},{4,6},{5,7},{6,4},{7,5},{8,10},{9,11},{10,... | collective-permute-start | bytes 344072 | tf_op jit(solution)/shard_map/sums/ppermute | solution.py:198
  79.9 0.8 shard_map.120
  80.7 0.8 collective-permute-start.19
  81.5 1.4 %shard_map.123 = bf16[384,1024]{1,0:T(8,128)(2,1)} custom-call(s32[16]{0:T(128)S(1)} %copy-done.4, bf16[384,1024]{1,0:T(8,128)(2,1)S(1)} %bitcast.18, bf16[384,512]{1,0:T(8,128)(2,1)S(1)} %collective-permute-done.5.refs_3_.came, bf16[384,512]{1,0:T(8,128)(2,1)S(1)} %collective-permute-done.15.refs_5_.other), custom_call_target="tpu_custom_call" | custom-call | tf_op jit(solution)/shard_map/pallas_call | solution.py:172
  83.0 0.3 collective-permute-done.17.refs_5_
  83.3 2.4 %collective-permute-done.18.refs_6_ = bf16[112,512]{1,0:T(8,128)(2,1)S(1)} collective-permute-done((bf16[112,512]{1,0:T(8,128)(2,1)S(1)}, bf16[112,512]{1,0:T(8,128)(2,1)S(1)}, u32[]{:S(2)}, u32[]{:S(2)}) %collective-permute-start.18) | collective-permute-done | bytes 114720 | tf_op jit(solution)/shard_map/sums/ppermute | solution.py:198
  85.7 0.8 shard_map.122
  (29 shorter events, 0.2 us)
Async XLA Ops:
  2.2 4.4 %copy-start.6 = (f32[112,8]{0,1:T(8,128)S(1)}, f32[112,8]{0,1:T(8,128)}, u32[]{:S(2)}) copy-start(f32[112,8]{0,1:T(8,128)} %param.10) | copy-start | bytes 10756
  2.2 4.4 %copy-start.7 = (s32[112,8]{0,1:T(8,128)S(1)}, s32[112,8]{0,1:T(8,128)}, u32[]{:S(2)}) copy-start(s32[112,8]{0,1:T(8,128)} %param.9) | copy-start | bytes 10756
  2.2 4.5 %copy-start.5 = (bf16[112,1024]{1,0:T(8,128)(2,1)S(1)}, bf16[112,1024]{1,0:T(8,128)(2,1)}, u32[]{:S(2)}) copy-start(bf16[112,1024]{1,0:T(8,128)(2,1)} %param.8) | copy-start | bytes 688132
  2.2 28.2 %copy-start = (bf16[1,384,1024]{2,1,0:T(8,128)(2,1)S(1)}, bf16[1,384,1024]{2,1,0:T(8,128)(2,1)}, u32[]{:S(2)}) copy-start(bf16[1,384,1024]{2,1,0:T(8,128)(2,1)} %param.13) | copy-start | bytes 2359300
  2.4 38.5 %collective-permute-start.3 = (bf16[1024,384]{1,0:T(8,128)(2,1)S(1)}, bf16[1024,384]{1,0:T(8,128)(2,1)S(1)}, u32[]{:S(2)}, u32[]{:S(2)}) collective-permute-start(bf16[1024,384]{1,0:T(8,128)(2,1)S(1)} %maximum_select_fusion), channel_id=1, source_target_pairs={{0,8},{1,9},{2,10},{3,11},{4,12},{5,13},{6,14},{7,15},{8,0},{9,1},... | collective-permute-start | bytes 2359304 | tf_op jit(solution)/shard_map/swap/ppermute | solution.py:198
  6.7 23.8 %copy-start.2 = (bf16[1,1024,384]{2,1,0:T(8,128)(2,1)S(1)}, bf16[1,1024,384]{2,1,0:T(8,128)(2,1)}, u32[]{:S(2)}) copy-start(bf16[1,1024,384]{2,1,0:T(8,128)(2,1)} %param.11) | copy-start | bytes 2359300
  6.7 24.3 %copy-start.1 = (bf16[1,1024,384]{2,1,0:T(8,128)(2,1)S(1)}, bf16[1,1024,384]{2,1,0:T(8,128)(2,1)}, u32[]{:S(2)}) copy-start(bf16[1,1024,384]{2,1,0:T(8,128)(2,1)} %param.12) | copy-start | bytes 2359300
  6.7 35.8 %copy-start.3 = (s32[16]{0:T(128)S(1)}, s32[16]{0:T(128)}, u32[]{:S(2)}) copy-start(s32[16]{0:T(128)} %placement.13) | copy-start | bytes 196
  6.8 22.1 %collective-permute-start = (bf16[112,1152]{1,0:T(8,128)(2,1)S(1)}, bf16[112,1152]{1,0:T(8,128)(2,1)S(1)}, u32[]{:S(2)}, u32[]{:S(2)}) collective-permute-start(bf16[112,1152]{1,0:T(8,128)(2,1)S(1)} %fusion.1.refs_0_), channel_id=1, source_target_pairs={{0,4},{1,5},{2,6},{3,7},{4,0},{5,1},{6,2},{7,3},{8,12},{9,13},{10,... | collective-permute-start | bytes 774152 | tf_op jit(solution)/shard_map/tokens/ppermute | solution.py:198
  8.4 22.6 %collective-permute-start.1 = (bf16[112,1152]{1,0:T(8,128)(2,1)S(1)}, bf16[112,1152]{1,0:T(8,128)(2,1)S(1)}, u32[]{:S(2)}, u32[]{:S(2)}) collective-permute-start(bf16[112,1152]{1,0:T(8,128)(2,1)S(1)} %fusion.1.refs_0_), channel_id=1, source_target_pairs={{0,2},{1,3},{2,0},{3,1},{4,6},{5,7},{6,4},{7,5},{8,10},{9,11},{10,... | collective-permute-start | bytes 774152 | tf_op jit(solution)/shard_map/tokens/ppermute | solution.py:198
  28.9 7.1 %collective-permute-start.2 = (bf16[112,1152]{1,0:T(8,128)(2,1)S(1)}, bf16[112,1152]{1,0:T(8,128)(2,1)S(1)}, u32[]{:S(2)}, u32[]{:S(2)}) collective-permute-start(bf16[112,1152]{1,0:T(8,128)(2,1)S(1)} %collective-permute-done.refs_1_), channel_id=1, source_target_pairs={{0,2},{1,3},{2,0},{3,1},{4,6},{5,7},{6,4},{7,5},{8,10},{9,11},{10,... | collective-permute-start | bytes 774152 | tf_op jit(solution)/shard_map/tokens/ppermute | solution.py:198
  30.4 12.1 %collective-permute-start.8 = (bf16[384,1024]{1,0:T(8,128)(2,1)S(1)}, bf16[384,1024]{1,0:T(8,128)(2,1)S(1)}, u32[]{:S(2)}, u32[]{:S(2)}) collective-permute-start(bf16[384,1024]{1,0:T(8,128)(2,1)S(1)} %bitcast.15), channel_id=1, source_target_pairs={{0,1},{1,0},{2,3},{3,2},{4,5},{5,4},{6,7},{7,6},{8,9},{9,8},{10,11... | collective-permute-start | bytes 2359304 | tf_op jit(solution)/shard_map/near/ppermute | solution.py:198
  30.5 12.0 %collective-permute-start.6 = (bf16[1024,384]{1,0:T(8,128)(2,1)S(1)}, bf16[1024,384]{1,0:T(8,128)(2,1)S(1)}, u32[]{:S(2)}, u32[]{:S(2)}) collective-permute-start(bf16[1024,384]{1,0:T(8,128)(2,1)S(1)} %bitcast.23), channel_id=1, source_target_pairs={{0,1},{1,0},{2,3},{3,2},{4,5},{5,4},{6,7},{7,6},{8,9},{9,8},{10,11... | collective-permute-start | bytes 2359304 | tf_op jit(solution)/shard_map/near/ppermute | solution.py:198
  31.0 11.5 %collective-permute-start.7 = (bf16[1024,384]{1,0:T(8,128)(2,1)S(1)}, bf16[1024,384]{1,0:T(8,128)(2,1)S(1)}, u32[]{:S(2)}, u32[]{:S(2)}) collective-permute-start(bf16[1024,384]{1,0:T(8,128)(2,1)S(1)} %bitcast.19), channel_id=1, source_target_pairs={{0,1},{1,0},{2,3},{3,2},{4,5},{5,4},{6,7},{7,6},{8,9},{9,8},{10,11... | collective-permute-start | bytes 2359304 | tf_op jit(solution)/shard_map/near/ppermute | solution.py:198
  40.9 20.6 %collective-permute-start.4 = (bf16[1024,384]{1,0:T(8,128)(2,1)S(1)}, bf16[1024,384]{1,0:T(8,128)(2,1)S(1)}, u32[]{:S(2)}, u32[]{:S(2)}) collective-permute-start(bf16[1024,384]{1,0:T(8,128)(2,1)S(1)} %collective-permute-done.3.refs_4_.came), channel_id=1, source_target_pairs={{0,16},{16,0},{1,17},{17,1},{2,18},{18,2},{3,19},{19,3},{4,20},{20... | collective-permute-start | bytes 2359304 | tf_op jit(solution)/shard_map/trade/ppermute | solution.py:202
  42.5 19.1 %collective-permute-start.5 = (bf16[384,512]{1,0:T(8,128)(2,1)S(1)}, bf16[384,512]{1,0:T(8,128)(2,1)S(1)}, u32[]{:S(2)}, u32[]{:S(2)}) collective-permute-start(bf16[384,512]{1,0:T(8,128)(2,1)S(1)} %slice_select_fusion), channel_id=1, source_target_pairs={{0,8},{1,9},{2,10},{3,11},{4,12},{5,13},{6,14},{7,15},{8,0},{9,1},... | collective-permute-start | bytes 1179656 | tf_op jit(solution)/shard_map/swap/ppermute | solution.py:198
  47.2 16.8 %collective-permute-start.9 = (bf16[1024,384]{1,0:T(8,128)(2,1)S(1)}, bf16[1024,384]{1,0:T(8,128)(2,1)S(1)}, u32[]{:S(2)}, u32[]{:S(2)}) collective-permute-start(bf16[1024,384]{1,0:T(8,128)(2,1)S(1)} %collective-permute-done.3.refs_4_.came), channel_id=1, source_target_pairs={{0,1},{1,0},{2,3},{3,2},{4,5},{5,4},{6,7},{7,6},{8,9},{9,8},{10,11... | collective-permute-start | bytes 2359304 | tf_op jit(solution)/shard_map/z_near/ppermute | solution.py:198
  61.5 2.5 %collective-permute-start.10 = (bf16[1024,384]{1,0:T(8,128)(2,1)S(1)}, bf16[1024,384]{1,0:T(8,128)(2,1)S(1)}, u32[]{:S(2)}, u32[]{:S(2)}) collective-permute-start(bf16[1024,384]{1,0:T(8,128)(2,1)S(1)} %collective-permute-done.4.refs_5_.other), channel_id=1, source_target_pairs={{0,1},{1,0},{2,3},{3,2},{4,5},{5,4},{6,7},{7,6},{8,9},{9,8},{10,11... | collective-permute-start | bytes 2359304 | tf_op jit(solution)/shard_map/y_near/ppermute | solution.py:198
  61.5 3.7 %collective-permute-start.11 = (bf16[384,512]{1,0:T(8,128)(2,1)S(1)}, bf16[384,512]{1,0:T(8,128)(2,1)S(1)}, u32[]{:S(2)}, u32[]{:S(2)}) collective-permute-start(bf16[384,512]{1,0:T(8,128)(2,1)S(1)} %collective-permute-done.5.refs_3_.came), channel_id=1, source_target_pairs={{0,1},{1,0},{2,3},{3,2},{4,5},{5,4},{6,7},{7,6},{8,9},{9,8},{10,11... | collective-permute-start | bytes 1179656 | tf_op jit(solution)/shard_map/z_near/ppermute | solution.py:198
  62.1 11.0 %collective-permute-start.15 = (bf16[384,512]{1,0:T(8,128)(2,1)S(1)}, bf16[384,512]{1,0:T(8,128)(2,1)S(1)}, u32[]{:S(2)}, u32[]{:S(2)}) collective-permute-start(bf16[384,512]{1,0:T(8,128)(2,1)S(1)} %collective-permute-done.5.refs_3_.came), channel_id=1, source_target_pairs={{0,16},{16,0},{1,17},{17,1},{2,18},{18,2},{3,19},{19,3},{4,20},{20... | collective-permute-start | bytes 1179656 | tf_op jit(solution)/shard_map/trade/ppermute | solution.py:202
  66.2 6.9 %collective-permute-start.12 = (bf16[112,512]{1,0:T(8,128)(2,1)S(1)}, bf16[112,512]{1,0:T(8,128)(2,1)S(1)}, u32[]{:S(2)}, u32[]{:S(2)}) collective-permute-start(bf16[112,512]{1,0:T(8,128)(2,1)S(1)} %get-tuple-element.42), channel_id=1, source_target_pairs={{0,6},{1,7},{2,4},{3,5},{4,2},{5,3},{6,0},{7,1},{8,14},{9,15},{10,... | collective-permute-start | bytes 344072 | tf_op jit(solution)/shard_map/sums/ppermute | solution.py:198
  67.5 1.5 %copy-start.4 = (s32[16]{0:T(128)S(1)}, s32[16]{0:T(128)}, u32[]{:S(2)}) copy-start(s32[16]{0:T(128)} %flags.2) | copy-start | bytes 196
  67.5 7.0 %collective-permute-start.13 = (bf16[112,512]{1,0:T(8,128)(2,1)S(1)}, bf16[112,512]{1,0:T(8,128)(2,1)S(1)}, u32[]{:S(2)}, u32[]{:S(2)}) collective-permute-start(bf16[112,512]{1,0:T(8,128)(2,1)S(1)} %get-tuple-element.43), channel_id=1, source_target_pairs={{0,2},{1,3},{2,0},{3,1},{4,6},{5,7},{6,4},{7,5},{8,10},{9,11},{10,... | collective-permute-start | bytes 344072 | tf_op jit(solution)/shard_map/sums/ppermute | solution.py:198
  74.5 1.7 %collective-permute-start.16 = (bf16[384,512]{1,0:T(8,128)(2,1)S(1)}, bf16[384,512]{1,0:T(8,128)(2,1)S(1)}, u32[]{:S(2)}, u32[]{:S(2)}) collective-permute-start(bf16[384,512]{1,0:T(8,128)(2,1)S(1)} %collective-permute-done.15.refs_5_.other), channel_id=1, source_target_pairs={{0,1},{1,0},{2,3},{3,2},{4,5},{5,4},{6,7},{7,6},{8,9},{9,8},{10,11... | collective-permute-start | bytes 1179656 | tf_op jit(solution)/shard_map/y_near/ppermute | solution.py:198
  74.5 8.5 %collective-permute-start.14 = (bf16[112,512]{1,0:T(8,128)(2,1)S(1)}, bf16[112,512]{1,0:T(8,128)(2,1)S(1)}, u32[]{:S(2)}, u32[]{:S(2)}) collective-permute-start(bf16[112,512]{1,0:T(8,128)(2,1)S(1)} %get-tuple-element.44), channel_id=1, source_target_pairs={{0,4},{1,5},{2,6},{3,7},{4,0},{5,1},{6,2},{7,3},{8,12},{9,13},{10,... | collective-permute-start | bytes 344072 | tf_op jit(solution)/shard_map/sums/ppermute | solution.py:198
  77.0 6.3 %collective-permute-start.17 = (bf16[112,512]{1,0:T(8,128)(2,1)S(1)}, bf16[112,512]{1,0:T(8,128)(2,1)S(1)}, u32[]{:S(2)}, u32[]{:S(2)}) collective-permute-start(bf16[112,512]{1,0:T(8,128)(2,1)S(1)} %get-tuple-element.52), channel_id=1, source_target_pairs={{0,6},{1,7},{2,4},{3,5},{4,2},{5,3},{6,0},{7,1},{8,14},{9,15},{10,... | collective-permute-start | bytes 344072 | tf_op jit(solution)/shard_map/sums/ppermute | solution.py:198
  78.6 7.0 %collective-permute-start.18 = (bf16[112,512]{1,0:T(8,128)(2,1)S(1)}, bf16[112,512]{1,0:T(8,128)(2,1)S(1)}, u32[]{:S(2)}, u32[]{:S(2)}) collective-permute-start(bf16[112,512]{1,0:T(8,128)(2,1)S(1)} %get-tuple-element.53), channel_id=1, source_target_pairs={{0,2},{1,3},{2,0},{3,1},{4,6},{5,7},{6,4},{7,5},{8,10},{9,11},{10,... | collective-permute-start | bytes 344072 | tf_op jit(solution)/shard_map/sums/ppermute | solution.py:198
  80.7 5.0 %collective-permute-start.19 = (bf16[112,512]{1,0:T(8,128)(2,1)S(1)}, bf16[112,512]{1,0:T(8,128)(2,1)S(1)}, u32[]{:S(2)}, u32[]{:S(2)}) collective-permute-start(bf16[112,512]{1,0:T(8,128)(2,1)S(1)} %get-tuple-element.54), channel_id=1, source_target_pairs={{0,4},{1,5},{2,6},{3,7},{4,0},{5,1},{6,2},{7,3},{8,12},{9,13},{10,... | collective-permute-start | bytes 344072 | tf_op jit(solution)/shard_map/sums/ppermute | solution.py:198

commit v6 on v5

--- a/solution.py
+++ b/solution.py
@@ -143,6 +143,31 @@
     return ref.at[span, :] if axis == 0 else ref.at[:, span]
 
 
+def upper_kernel(gate, up, out, sems):
+    half = lax.axis_index("dp") % 2
+    depth = out.shape[0] // 2
+    run_copies(
+        [
+            (part_of(gate, 0, half, depth), out.at[pl.ds(0, depth), :]),
+            (part_of(up, 0, half, depth), out.at[pl.ds(depth, depth), :]),
+        ],
+        sems,
+    )
+
+
+def take_upper(gate, up):
+    hbm = pl.BlockSpec(memory_space=pl.ANY)
+    return pl.pallas_call(
+        upper_kernel,
+        out_shape=jax.ShapeDtypeStruct(gate.shape, gate.dtype),
+        in_specs=[hbm] * 2,
+        out_specs=pl.BlockSpec(memory_space=pltpu.VMEM),
+        scratch_shapes=[pltpu.SemaphoreType.DMA((2,))],
+        compiler_params=pltpu.CompilerParams(vmem_limit_bytes=58 * 2**20),
+        cost_estimate=pl.CostEstimate(flops=0, bytes_accessed=0, transcendentals=0),
+    )(gate, up)
+
+
 def store_kernel(axis, first, flags, own, came, other, out, sems):
     half = lax.axis_index("dp") % 2
     size = out.shape[axis] // 2
@@ -206,10 +231,7 @@
     def half_of(first, second):
         return jnp.where(couple == 0, first, second)
 
-    upper = half_of(
-        jnp.concatenate([own[0][:depth], own[1][:depth]], axis=0),
-        jnp.concatenate([own[0][depth:], own[1][depth:]], axis=0),
-    )
+    upper = take_upper(own[0], own[1])
     lower = half_of(own[2][:, :part], own[2][:, part:])
 
     bits = []

time: 86.6 us -> 89 us (1.028)
  Pallas kernels: 16.7 us -> 21.2 us
  waiting for transfers between devices: 48.6 us -> 46.5 us
  starting transfers between devices: 18.2 us -> 19.2 us
    pallas_call x0 -> x1, Pallas kernels: none -> 2.11 us  [take_upper(): pl.pallas_call(upper_kernel, out_shape=jax.ShapeDtypeStruct(gate.shape, g...]
    slice x1 -> x0, local copies, waits for them, and re-layouts: 1.52 us -> none  [per_device(): own[1][depth:]]
    pallas_call x3, Pallas kernels: 4.34 us -> 5.55 us  [store(): pl.pallas_call(functools.partial(store_kernel, axis, first), out_shape=ja...]
    pallas_call x10, Pallas kernels: 12.4 us -> 13.5 us  [call(): pl.pallas_call(kernel, out_shape=out_shape, in_specs=[smem] * scalars + [...]
    ppermute x2, waiting for transfers between devices: 1.15 us -> 0.01 us  [trade(): return lax.ppermute(value, 'dp', trades)]
    ppermute x18, starting transfers between devices: 15.9 us -> 16.9 us  [send(): return lax.ppermute(value, 'expert', [(d, d ^ bit) for d in range(count)])]
    ppermute x18, waiting for transfers between devices: 47.5 us -> 46.5 us  [send(): return lax.ppermute(value, 'expert', [(d, d ^ bit) for d in range(count)])]
  transfers between devices with their start and end apart: 20 -> 20, of which waited for: 9 -> 7; matrix products, arithmetic and copies ran while one was open for 0% -> 0% of each run, Pallas kernels for 18% -> 21%
where the time goes in v6:
time: 89 us; the launch traced here: 88.8 us
  waiting for transfers between devices  46.5 us (52%)
  Pallas kernels  21.2 us (24%)
  starting transfers between devices  19.2 us (22%)
  between operations  0.94 us (1%)
    ppermute x18, waiting for transfers between devices, send(): return lax.ppermute(value, 'expert', [(d, d ^ bit) for d in range(count)])  46.5 us
    ppermute x18, starting transfers between devices, send(): return lax.ppermute(value, 'expert', [(d, d ^ bit) for d in range(count)])  16.9 us
    pallas_call x10, Pallas kernels, call(): pl.pallas_call(kernel, out_shape=out_shape, in_specs=[smem] * scalars + [...  13.5 us
    pallas_call x3, Pallas kernels, store(): pl.pallas_call(functools.partial(store_kernel, axis, first), out_shape=ja...  5.55 us
    ppermute x2, starting transfers between devices, trade(): return lax.ppermute(value, 'dp', trades)  2.32 us
    pallas_call x1, Pallas kernels, take_upper(): pl.pallas_call(upper_kernel, out_shape=jax.ShapeDtypeStruct(gate.shape, g...  2.11 us
  transfers between devices with their start and end apart: 20, of which 7 were waited for; matrix products, arithmetic and copies ran while one was open for 0% of the time, Pallas kernels for 21%

profile of v6, /device:TPU:0, one launch (start us, length us, event | category | flops | bytes accessed | tf_op | source)
XLA Modules:
  0.0 88.8 jit_solution(6727762406243186276)
XLA Ops:
  0.7 2.1 %shard_map.111 = bf16[1024,384]{1,0:T(8,128)(2,1)} custom-call(bf16[1024,384]{1,0:T(8,128)(2,1)} %bitcast.16, bf16[1024,384]{1,0:T(8,128)(2,1)} %bitcast.11), custom_call_target="tpu_custom_call" | custom-call | tf_op jit(solution)/shard_map/pallas_call | solution.py:160
  2.8 4.1 %collective-permute-start.3 = (bf16[1024,384]{1,0:T(8,128)(2,1)}, bf16[1024,384]{1,0:T(8,128)(2,1)}, u32[]{:S(2)}, u32[]{:S(2)}) collective-permute-start(bf16[1024,384]{1,0:T(8,128)(2,1)} %shard_map.111), channel_id=1, source_target_pairs={{0,8},{1,9},{2,10},{3,11},{4,12},{5,13},{6,14},{7,15},{8,0},{9,1},... | collective-permute-start | bytes 2359304 | tf_op jit(solution)/shard_map/swap/ppermute | solution.py:223
  7.0 0.1 copy.17
  7.1 0.0 copy-start.2
  7.1 0.0 copy-start.1
  7.1 1.6 %collective-permute-start = (bf16[112,1152]{1,0:T(8,128)(2,1)S(1)}, bf16[112,1152]{1,0:T(8,128)(2,1)S(1)}, u32[]{:S(2)}, u32[]{:S(2)}) collective-permute-start(bf16[112,1152]{1,0:T(8,128)(2,1)S(1)} %fusion.1.refs_0_), channel_id=1, source_target_pairs={{0,4},{1,5},{2,6},{3,7},{4,0},{5,1},{6,2},{7,3},{8,12},{9,13},{10,... | collective-permute-start | bytes 774152 | tf_op jit(solution)/shard_map/tokens/ppermute | solution.py:223
  8.8 1.5 %collective-permute-start.1 = (bf16[112,1152]{1,0:T(8,128)(2,1)S(1)}, bf16[112,1152]{1,0:T(8,128)(2,1)S(1)}, u32[]{:S(2)}, u32[]{:S(2)}) collective-permute-start(bf16[112,1152]{1,0:T(8,128)(2,1)S(1)} %fusion.1.refs_0_), channel_id=1, source_target_pairs={{0,2},{1,3},{2,0},{3,1},{4,6},{5,7},{6,4},{7,5},{8,10},{9,11},{10,... | collective-permute-start | bytes 774152 | tf_op jit(solution)/shard_map/tokens/ppermute | solution.py:223
  10.3 19.2 %collective-permute-done.refs_1_ = bf16[112,1152]{1,0:T(8,128)(2,1)S(1)} collective-permute-done((bf16[112,1152]{1,0:T(8,128)(2,1)S(1)}, bf16[112,1152]{1,0:T(8,128)(2,1)S(1)}, u32[]{:S(2)}, u32[]{:S(2)}) %collective-permute-start) | collective-permute-done | bytes 258080 | tf_op jit(solution)/shard_map/tokens/ppermute | solution.py:223
  29.5 1.5 %collective-permute-start.2 = (bf16[112,1152]{1,0:T(8,128)(2,1)S(1)}, bf16[112,1152]{1,0:T(8,128)(2,1)S(1)}, u32[]{:S(2)}, u32[]{:S(2)}) collective-permute-start(bf16[112,1152]{1,0:T(8,128)(2,1)S(1)} %collective-permute-done.refs_1_), channel_id=1, source_target_pairs={{0,2},{1,3},{2,0},{3,1},{4,6},{5,7},{6,4},{7,5},{8,10},{9,11},{10,... | collective-permute-start | bytes 774152 | tf_op jit(solution)/shard_map/tokens/ppermute | solution.py:223
  31.0 0.1 collective-permute-start.6
  31.1 0.5 collective-permute-start.7
  31.6 0.0 collective-permute-done.1.refs_2_.refs_0_
  31.6 0.1 collective-permute-start.8
  31.7 4.9 %collective-permute-done.2.refs_3_.refs_1_ = bf16[112,1152]{1,0:T(8,128)(2,1)S(1)} collective-permute-done((bf16[112,1152]{1,0:T(8,128)(2,1)S(1)}, bf16[112,1152]{1,0:T(8,128)(2,1)S(1)}, u32[]{:S(2)}, u32[]{:S(2)}) %collective-permute-start.2) | collective-permute-done | bytes 258080 | tf_op jit(solution)/shard_map/tokens/ppermute | solution.py:223
  36.6 5.0 %collective-permute-done.3.refs_4_.came = bf16[1024,384]{1,0:T(8,128)(2,1)} collective-permute-done((bf16[1024,384]{1,0:T(8,128)(2,1)}, bf16[1024,384]{1,0:T(8,128)(2,1)}, u32[]{:S(2)}, u32[]{:S(2)}) %collective-permute-start.3) | collective-permute-done | bytes 786464 | tf_op jit(solution)/shard_map/swap/ppermute | solution.py:223
  41.6 1.6 %collective-permute-start.4 = (bf16[1024,384]{1,0:T(8,128)(2,1)}, bf16[1024,384]{1,0:T(8,128)(2,1)S(1)}, u32[]{:S(2)}, u32[]{:S(2)}) collective-permute-start(bf16[1024,384]{1,0:T(8,128)(2,1)} %collective-permute-done.3.refs_4_.came), channel_id=1, source_target_pairs={{0,16},{16,0},{1,17},{17,1},{2,18},{18,2},{3,19},{19,3},{4,20},{20... | collective-permute-start | bytes 2359304 | tf_op jit(solution)/shard_map/trade/ppermute | solution.py:227
  43.2 0.0 collective-permute-start.5
  43.2 0.0 collective-permute-done.6.refs_5_
  43.2 0.0 collective-permute-done.8.refs_7_
  43.2 2.3 %shard_map.114 = (f32[112,1024]{1,0:T(8,128)S(1)}, f32[112,1024]{1,0:T(8,128)S(1)}) custom-call(s32[16]{0:T(128)S(1)} %copy-done.3, bf16[112,1152]{1,0:T(8,128)(2,1)S(1)} %collective-permute-done.1.refs_2_.refs_0_, bf16[112,1152]{1,0:T(8,128)(2,1)S(1)} %collective-permute-done.2.refs_3_.refs_1_, bf16[1024,384]{1,0:T(8,128)(2,1)S(1)} %bitcast.18, ...), custom_call_target="tpu_custom_call" | custom-call | tf_op jit(solution)/shard_map/pallas_call | solution.py:122
  45.6 2.3 %shard_map.113 = (f32[112,1024]{1,0:T(8,128)S(1)}, f32[112,1024]{1,0:T(8,128)S(1)}) custom-call(s32[16]{0:T(128)S(1)} %copy-done.3, bf16[112,1152]{1,0:T(8,128)(2,1)S(1)} %fusion.1.refs_0_, bf16[112,1152]{1,0:T(8,128)(2,1)S(1)} %collective-permute-done.refs_1_, bf16[1024,384]{1,0:T(8,128)(2,1)S(1)} %bitcast.19, bf16[1024,384]{1,0:T(8,128)(2,1)S(1)} %bitcast.14, ...), custom_call_target="tpu_custom_call" | custom-call | tf_op jit(solution)/shard_map/pallas_call | solution.py:122
  47.9 0.1 collective-permute-start.9
  48.0 14.2 %collective-permute-done.5.refs_3_.came = bf16[384,512]{1,0:T(8,128)(2,1)S(1)} collective-permute-done((bf16[384,512]{1,0:T(8,128)(2,1)S(1)}, bf16[384,512]{1,0:T(8,128)(2,1)S(1)}, u32[]{:S(2)}, u32[]{:S(2)}) %collective-permute-start.5) | collective-permute-done | bytes 393248 | tf_op jit(solution)/shard_map/swap/ppermute | solution.py:223
  62.2 0.5 collective-permute-start.11
  62.7 0.8 collective-permute-start.15
  63.5 2.3 %shard_map.112.refs_2_.refs_4_ = bf16[448,384]{1,0:T(8,128)(2,1)S(1)} custom-call(bf16[112,1152]{1,0:T(8,128)(2,1)S(1)} %fusion.1.refs_0_, bf16[112,1152]{1,0:T(8,128)(2,1)S(1)} %collective-permute-done.refs_1_, bf16[112,1152]{1,0:T(8,128)(2,1)S(1)} %collective-permute-done.1.refs_2_.refs_0_, bf16[112,1152]{1,0:T(8,128)(2,1)S(1)} %collective-permute-done.2.refs_3_.refs_1_, ...), custom_call_target="tpu_custom_call" | custom-call | tf_op jit(solution)/shard_map/pallas_call | solution.py:122
  65.8 1.2 %shard_map.115.refs_4_.refs_2_ = bf16[448,384]{1,0:T(8,128)(2,1)S(1)} custom-call(bf16[112,1152]{1,0:T(8,128)(2,1)S(1)} %fusion.1.refs_0_, bf16[112,1152]{1,0:T(8,128)(2,1)S(1)} %collective-permute-done.refs_1_, bf16[112,1152]{1,0:T(8,128)(2,1)S(1)} %collective-permute-done.1.refs_2_.refs_0_, bf16[112,1152]{1,0:T(8,128)(2,1)S(1)} %collective-permute-done.2.refs_3_.refs_1_, ...), custom_call_target="tpu_custom_call" | custom-call | tf_op jit(solution)/shard_map/pallas_call | solution.py:122
  67.1 0.9 %shard_map.117 = (bf16[112,512]{1,0:T(8,128)(2,1)S(1)}, bf16[112,512]{1,0:T(8,128)(2,1)S(1)}) custom-call(s32[16]{0:T(128)S(1)} %copy-done.3, bf16[112,1152]{1,0:T(8,128)(2,1)S(1)} %collective-permute-done.1.refs_2_.refs_0_, bf16[112,1152]{1,0:T(8,128)(2,1)S(1)} %collective-permute-done.2.refs_3_.refs_1_, bf16[448,384]{1,0:T(8,128)(2,1)S(1)} %shard_map.112.refs_2_.refs_4_, ...), custom_call_target="tpu_custom_call" | custom-call | tf_op jit(solution)/shard_map/pallas_call | solution.py:122
  68.0 1.5 %collective-permute-start.12 = (bf16[112,512]{1,0:T(8,128)(2,1)S(1)}, bf16[112,512]{1,0:T(8,128)(2,1)S(1)}, u32[]{:S(2)}, u32[]{:S(2)}) collective-permute-start(bf16[112,512]{1,0:T(8,128)(2,1)S(1)} %get-tuple-element.42), channel_id=1, source_target_pairs={{0,6},{1,7},{2,4},{3,5},{4,2},{5,3},{6,0},{7,1},{8,14},{9,15},{10,... | collective-permute-start | bytes 344072 | tf_op jit(solution)/shard_map/sums/ppermute | solution.py:223
  69.6 0.5 collective-permute-start.13
  70.1 0.9 %shard_map.116 = (f32[112,512]{1,0:T(8,128)S(1)}, bf16[112,512]{1,0:T(8,128)(2,1)S(1)}) custom-call(s32[16]{0:T(128)S(1)} %copy-done.3, bf16[112,1152]{1,0:T(8,128)(2,1)S(1)} %fusion.1.refs_0_, bf16[112,1152]{1,0:T(8,128)(2,1)S(1)} %collective-permute-done.refs_1_, bf16[448,384]{1,0:T(8,128)(2,1)S(1)} %shard_map.112.refs_2_.refs_4_, ...), custom_call_target="tpu_custom_call" | custom-call | tf_op jit(solution)/shard_map/pallas_call | solution.py:122
  71.1 0.0 copy-start.4
  71.1 0.6 copy-done.4
  71.7 2.0 %shard_map.119 = bf16[1024,384]{1,0:T(8,128)(2,1)} custom-call(s32[16]{0:T(128)S(1)} %copy-done.4, bf16[1024,384]{1,0:T(8,128)(2,1)S(1)} %bitcast.15, bf16[1024,384]{1,0:T(8,128)(2,1)} %collective-permute-done.3.refs_4_.came, bf16[1024,384]{1,0:T(8,128)(2,1)S(1)} %collective-permute-done.4.refs_5_.other), custom_call_target="tpu_custom_call" | custom-call | tf_op jit(solution)/shard_map/pallas_call | solution.py:197
  73.8 2.1 %shard_map.118 = bf16[1024,384]{1,0:T(8,128)(2,1)} custom-call(s32[16]{0:T(128)S(1)} %copy-done.4, bf16[1024,384]{1,0:T(8,128)(2,1)S(1)} %bitcast.20, bf16[1024,384]{1,0:T(8,128)(2,1)} %collective-permute-done.3.refs_4_.came, bf16[1024,384]{1,0:T(8,128)(2,1)S(1)} %collective-permute-done.4.refs_5_.other), custom_call_target="tpu_custom_call" | custom-call | tf_op jit(solution)/shard_map/pallas_call | solution.py:197
  75.8 0.4 collective-permute-done.13.refs_2_
  76.2 0.0 collective-permute-start.16
  76.3 1.3 %collective-permute-start.14 = (bf16[112,512]{1,0:T(8,128)(2,1)S(1)}, bf16[112,512]{1,0:T(8,128)(2,1)S(1)}, u32[]{:S(2)}, u32[]{:S(2)}) collective-permute-start(bf16[112,512]{1,0:T(8,128)(2,1)S(1)} %get-tuple-element.44), channel_id=1, source_target_pairs={{0,4},{1,5},{2,6},{3,7},{4,0},{5,1},{6,2},{7,3},{8,12},{9,13},{10,... | collective-permute-start | bytes 344072 | tf_op jit(solution)/shard_map/sums/ppermute | solution.py:223
  77.5 0.9 %shard_map.120 = (f32[112,512]{1,0:T(8,128)S(1)}, f32[112,512]{1,0:T(8,128)S(1)}, f32[112,512]{1,0:T(8,128)S(1)}, f32[112,512]{1,0:T(8,128)S(1)}) custom-call(s32[16]{0:T(128)S(1)} %copy-done.3, bf16[112,1152]{1,0:T(8,128)(2,1)S(1)} %fusion.1.refs_0_, bf16[112,1152]{1,0:T(8,128)(2,1)S(1)} %collective-permute-done.refs_1_, ...), custom_call_target="tpu_custom_call" | custom-call | tf_op jit(solution)/shard_map/pallas_call | solution.py:122
  78.5 0.8 shard_map.122
  79.3 1.5 %collective-permute-start.17 = (bf16[112,512]{1,0:T(8,128)(2,1)S(1)}, bf16[112,512]{1,0:T(8,128)(2,1)S(1)}, u32[]{:S(2)}, u32[]{:S(2)}) collective-permute-start(bf16[112,512]{1,0:T(8,128)(2,1)S(1)} %get-tuple-element.52), channel_id=1, source_target_pairs={{0,6},{1,7},{2,4},{3,5},{4,2},{5,3},{6,0},{7,1},{8,14},{9,15},{10,... | collective-permute-start | bytes 344072 | tf_op jit(solution)/shard_map/sums/ppermute | solution.py:223
  80.8 0.8 collective-permute-start.18
  81.6 0.8 shard_map.121
  82.5 1.3 %collective-permute-start.19 = (bf16[112,512]{1,0:T(8,128)(2,1)S(1)}, bf16[112,512]{1,0:T(8,128)(2,1)S(1)}, u32[]{:S(2)}, u32[]{:S(2)}) collective-permute-start(bf16[112,512]{1,0:T(8,128)(2,1)S(1)} %get-tuple-element.54), channel_id=1, source_target_pairs={{0,4},{1,5},{2,6},{3,7},{4,0},{5,1},{6,2},{7,3},{8,12},{9,13},{10,... | collective-permute-start | bytes 344072 | tf_op jit(solution)/shard_map/sums/ppermute | solution.py:223
  83.8 1.4 %shard_map.124 = bf16[384,1024]{1,0:T(8,128)(2,1)} custom-call(s32[16]{0:T(128)S(1)} %copy-done.4, bf16[384,1024]{1,0:T(8,128)(2,1)S(1)} %bitcast.10, bf16[384,512]{1,0:T(8,128)(2,1)S(1)} %collective-permute-done.5.refs_3_.came, bf16[384,512]{1,0:T(8,128)(2,1)S(1)} %collective-permute-done.15.refs_5_.other), custom_call_target="tpu_custom_call" | custom-call | tf_op jit(solution)/shard_map/pallas_call | solution.py:197
  85.2 0.4 collective-permute-done.17.refs_5_
  85.6 2.3 %collective-permute-done.18.refs_6_ = bf16[112,512]{1,0:T(8,128)(2,1)S(1)} collective-permute-done((bf16[112,512]{1,0:T(8,128)(2,1)S(1)}, bf16[112,512]{1,0:T(8,128)(2,1)S(1)}, u32[]{:S(2)}, u32[]{:S(2)}) %collective-permute-start.18) | collective-permute-done | bytes 114720 | tf_op jit(solution)/shard_map/sums/ppermute | solution.py:223
  88.0 0.8 shard_map.123
  (28 shorter events, 0.2 us)
Async XLA Ops:
  0.6 6.3 %copy-start.6 = (f32[112,8]{0,1:T(8,128)S(1)}, f32[112,8]{0,1:T(8,128)}, u32[]{:S(2)}) copy-start(f32[112,8]{0,1:T(8,128)} %param.10) | copy-start | bytes 10756
  0.6 6.3 %copy-start.7 = (s32[112,8]{0,1:T(8,128)S(1)}, s32[112,8]{0,1:T(8,128)}, u32[]{:S(2)}) copy-start(s32[112,8]{0,1:T(8,128)} %param.9) | copy-start | bytes 10756
  0.7 6.4 %copy-start.5 = (bf16[112,1024]{1,0:T(8,128)(2,1)S(1)}, bf16[112,1024]{1,0:T(8,128)(2,1)}, u32[]{:S(2)}) copy-start(bf16[112,1024]{1,0:T(8,128)(2,1)} %param.8) | copy-start | bytes 688132
  0.7 30.3 %copy-start = (bf16[1,384,1024]{2,1,0:T(8,128)(2,1)S(1)}, bf16[1,384,1024]{2,1,0:T(8,128)(2,1)}, u32[]{:S(2)}) copy-start(bf16[1,384,1024]{2,1,0:T(8,128)(2,1)} %param.13) | copy-start | bytes 2359300
  2.8 38.8 %collective-permute-start.3 = (bf16[1024,384]{1,0:T(8,128)(2,1)}, bf16[1024,384]{1,0:T(8,128)(2,1)}, u32[]{:S(2)}, u32[]{:S(2)}) collective-permute-start(bf16[1024,384]{1,0:T(8,128)(2,1)} %shard_map.111), channel_id=1, source_target_pairs={{0,8},{1,9},{2,10},{3,11},{4,12},{5,13},{6,14},{7,15},{8,0},{9,1},... | collective-permute-start | bytes 2359304 | tf_op jit(solution)/shard_map/swap/ppermute | solution.py:223
  7.1 23.9 %copy-start.2 = (bf16[1,1024,384]{2,1,0:T(8,128)(2,1)S(1)}, bf16[1,1024,384]{2,1,0:T(8,128)(2,1)}, u32[]{:S(2)}) copy-start(bf16[1,1024,384]{2,1,0:T(8,128)(2,1)} %param.11) | copy-start | bytes 2359300
  7.1 24.0 %copy-start.1 = (bf16[1,1024,384]{2,1,0:T(8,128)(2,1)S(1)}, bf16[1,1024,384]{2,1,0:T(8,128)(2,1)}, u32[]{:S(2)}) copy-start(bf16[1,1024,384]{2,1,0:T(8,128)(2,1)} %param.12) | copy-start | bytes 2359300
  7.1 22.3 %collective-permute-start = (bf16[112,1152]{1,0:T(8,128)(2,1)S(1)}, bf16[112,1152]{1,0:T(8,128)(2,1)S(1)}, u32[]{:S(2)}, u32[]{:S(2)}) collective-permute-start(bf16[112,1152]{1,0:T(8,128)(2,1)S(1)} %fusion.1.refs_0_), channel_id=1, source_target_pairs={{0,4},{1,5},{2,6},{3,7},{4,0},{5,1},{6,2},{7,3},{8,12},{9,13},{10,... | collective-permute-start | bytes 774152 | tf_op jit(solution)/shard_map/tokens/ppermute | solution.py:223
  8.8 22.8 %collective-permute-start.1 = (bf16[112,1152]{1,0:T(8,128)(2,1)S(1)}, bf16[112,1152]{1,0:T(8,128)(2,1)S(1)}, u32[]{:S(2)}, u32[]{:S(2)}) collective-permute-start(bf16[112,1152]{1,0:T(8,128)(2,1)S(1)} %fusion.1.refs_0_), channel_id=1, source_target_pairs={{0,2},{1,3},{2,0},{3,1},{4,6},{5,7},{6,4},{7,5},{8,10},{9,11},{10,... | collective-permute-start | bytes 774152 | tf_op jit(solution)/shard_map/tokens/ppermute | solution.py:223
  29.5 7.1 %collective-permute-start.2 = (bf16[112,1152]{1,0:T(8,128)(2,1)S(1)}, bf16[112,1152]{1,0:T(8,128)(2,1)S(1)}, u32[]{:S(2)}, u32[]{:S(2)}) collective-permute-start(bf16[112,1152]{1,0:T(8,128)(2,1)S(1)} %collective-permute-done.refs_1_), channel_id=1, source_target_pairs={{0,2},{1,3},{2,0},{3,1},{4,6},{5,7},{6,4},{7,5},{8,10},{9,11},{10,... | collective-permute-start | bytes 774152 | tf_op jit(solution)/shard_map/tokens/ppermute | solution.py:223
  31.0 12.2 %copy-start.3 = (s32[16]{0:T(128)S(1)}, s32[16]{0:T(128)}, u32[]{:S(2)}) copy-start(s32[16]{0:T(128)} %placement.13) | copy-start | bytes 196
  31.0 12.2 %collective-permute-start.6 = (bf16[1024,384]{1,0:T(8,128)(2,1)S(1)}, bf16[1024,384]{1,0:T(8,128)(2,1)S(1)}, u32[]{:S(2)}, u32[]{:S(2)}) collective-permute-start(bf16[1024,384]{1,0:T(8,128)(2,1)S(1)} %bitcast.17), channel_id=1, source_target_pairs={{0,1},{1,0},{2,3},{3,2},{4,5},{5,4},{6,7},{7,6},{8,9},{9,8},{10,11... | collective-permute-start | bytes 2359304 | tf_op jit(solution)/shard_map/near/ppermute | solution.py:223
  31.1 12.1 %collective-permute-start.7 = (bf16[1024,384]{1,0:T(8,128)(2,1)S(1)}, bf16[1024,384]{1,0:T(8,128)(2,1)S(1)}, u32[]{:S(2)}, u32[]{:S(2)}) collective-permute-start(bf16[1024,384]{1,0:T(8,128)(2,1)S(1)} %bitcast.12), channel_id=1, source_target_pairs={{0,1},{1,0},{2,3},{3,2},{4,5},{5,4},{6,7},{7,6},{8,9},{9,8},{10,11... | collective-permute-start | bytes 2359304 | tf_op jit(solution)/shard_map/near/ppermute | solution.py:223
  31.6 11.6 %collective-permute-start.8 = (bf16[384,1024]{1,0:T(8,128)(2,1)S(1)}, bf16[384,1024]{1,0:T(8,128)(2,1)S(1)}, u32[]{:S(2)}, u32[]{:S(2)}) collective-permute-start(bf16[384,1024]{1,0:T(8,128)(2,1)S(1)} %bitcast.7), channel_id=1, source_target_pairs={{0,1},{1,0},{2,3},{3,2},{4,5},{5,4},{6,7},{7,6},{8,9},{9,8},{10,11... | collective-permute-start | bytes 2359304 | tf_op jit(solution)/shard_map/near/ppermute | solution.py:223
  41.6 20.6 %collective-permute-start.4 = (bf16[1024,384]{1,0:T(8,128)(2,1)}, bf16[1024,384]{1,0:T(8,128)(2,1)S(1)}, u32[]{:S(2)}, u32[]{:S(2)}) collective-permute-start(bf16[1024,384]{1,0:T(8,128)(2,1)} %collective-permute-done.3.refs_4_.came), channel_id=1, source_target_pairs={{0,16},{16,0},{1,17},{17,1},{2,18},{18,2},{3,19},{19,3},{4,20},{20... | collective-permute-start | bytes 2359304 | tf_op jit(solution)/shard_map/trade/ppermute | solution.py:227
  43.2 19.1 %collective-permute-start.5 = (bf16[384,512]{1,0:T(8,128)(2,1)S(1)}, bf16[384,512]{1,0:T(8,128)(2,1)S(1)}, u32[]{:S(2)}, u32[]{:S(2)}) collective-permute-start(bf16[384,512]{1,0:T(8,128)(2,1)S(1)} %slice_select_fusion), channel_id=1, source_target_pairs={{0,8},{1,9},{2,10},{3,11},{4,12},{5,13},{6,14},{7,15},{8,0},{9,1},... | collective-permute-start | bytes 1179656 | tf_op jit(solution)/shard_map/swap/ppermute | solution.py:223
  47.9 17.9 %collective-permute-start.9 = (bf16[1024,384]{1,0:T(8,128)(2,1)}, bf16[1024,384]{1,0:T(8,128)(2,1)S(1)}, u32[]{:S(2)}, u32[]{:S(2)}) collective-permute-start(bf16[1024,384]{1,0:T(8,128)(2,1)} %collective-permute-done.3.refs_4_.came), channel_id=1, source_target_pairs={{0,1},{1,0},{2,3},{3,2},{4,5},{5,4},{6,7},{7,6},{8,9},{9,8},{10,11... | collective-permute-start | bytes 2359304 | tf_op jit(solution)/shard_map/z_near/ppermute | solution.py:223
  62.2 3.6 %collective-permute-start.10 = (bf16[1024,384]{1,0:T(8,128)(2,1)S(1)}, bf16[1024,384]{1,0:T(8,128)(2,1)S(1)}, u32[]{:S(2)}, u32[]{:S(2)}) collective-permute-start(bf16[1024,384]{1,0:T(8,128)(2,1)S(1)} %collective-permute-done.4.refs_5_.other), channel_id=1, source_target_pairs={{0,1},{1,0},{2,3},{3,2},{4,5},{5,4},{6,7},{7,6},{8,9},{9,8},{10,11... | collective-permute-start | bytes 2359304 | tf_op jit(solution)/shard_map/y_near/ppermute | solution.py:223
  62.2 4.9 %collective-permute-start.11 = (bf16[384,512]{1,0:T(8,128)(2,1)S(1)}, bf16[384,512]{1,0:T(8,128)(2,1)S(1)}, u32[]{:S(2)}, u32[]{:S(2)}) collective-permute-start(bf16[384,512]{1,0:T(8,128)(2,1)S(1)} %collective-permute-done.5.refs_3_.came), channel_id=1, source_target_pairs={{0,1},{1,0},{2,3},{3,2},{4,5},{5,4},{6,7},{7,6},{8,9},{9,8},{10,11... | collective-permute-start | bytes 1179656 | tf_op jit(solution)/shard_map/z_near/ppermute | solution.py:223
  62.7 13.1 %collective-permute-start.15 = (bf16[384,512]{1,0:T(8,128)(2,1)S(1)}, bf16[384,512]{1,0:T(8,128)(2,1)S(1)}, u32[]{:S(2)}, u32[]{:S(2)}) collective-permute-start(bf16[384,512]{1,0:T(8,128)(2,1)S(1)} %collective-permute-done.5.refs_3_.came), channel_id=1, source_target_pairs={{0,16},{16,0},{1,17},{17,1},{2,18},{18,2},{3,19},{19,3},{4,20},{20... | collective-permute-start | bytes 1179656 | tf_op jit(solution)/shard_map/trade/ppermute | solution.py:227
  68.0 7.8 %collective-permute-start.12 = (bf16[112,512]{1,0:T(8,128)(2,1)S(1)}, bf16[112,512]{1,0:T(8,128)(2,1)S(1)}, u32[]{:S(2)}, u32[]{:S(2)}) collective-permute-start(bf16[112,512]{1,0:T(8,128)(2,1)S(1)} %get-tuple-element.42), channel_id=1, source_target_pairs={{0,6},{1,7},{2,4},{3,5},{4,2},{5,3},{6,0},{7,1},{8,14},{9,15},{10,... | collective-permute-start | bytes 344072 | tf_op jit(solution)/shard_map/sums/ppermute | solution.py:223
  69.6 6.7 %collective-permute-start.13 = (bf16[112,512]{1,0:T(8,128)(2,1)S(1)}, bf16[112,512]{1,0:T(8,128)(2,1)S(1)}, u32[]{:S(2)}, u32[]{:S(2)}) collective-permute-start(bf16[112,512]{1,0:T(8,128)(2,1)S(1)} %get-tuple-element.43), channel_id=1, source_target_pairs={{0,2},{1,3},{2,0},{3,1},{4,6},{5,7},{6,4},{7,5},{8,10},{9,11},{10,... | collective-permute-start | bytes 344072 | tf_op jit(solution)/shard_map/sums/ppermute | solution.py:223
  71.1 0.7 copy-start.4
  76.2 2.2 %collective-permute-start.16 = (bf16[384,512]{1,0:T(8,128)(2,1)S(1)}, bf16[384,512]{1,0:T(8,128)(2,1)S(1)}, u32[]{:S(2)}, u32[]{:S(2)}) collective-permute-start(bf16[384,512]{1,0:T(8,128)(2,1)S(1)} %collective-permute-done.15.refs_5_.other), channel_id=1, source_target_pairs={{0,1},{1,0},{2,3},{3,2},{4,5},{5,4},{6,7},{7,6},{8,9},{9,8},{10,11... | collective-permute-start | bytes 1179656 | tf_op jit(solution)/shard_map/y_near/ppermute | solution.py:223
  76.3 9.0 %collective-permute-start.14 = (bf16[112,512]{1,0:T(8,128)(2,1)S(1)}, bf16[112,512]{1,0:T(8,128)(2,1)S(1)}, u32[]{:S(2)}, u32[]{:S(2)}) collective-permute-start(bf16[112,512]{1,0:T(8,128)(2,1)S(1)} %get-tuple-element.44), channel_id=1, source_target_pairs={{0,4},{1,5},{2,6},{3,7},{4,0},{5,1},{6,2},{7,3},{8,12},{9,13},{10,... | collective-permute-start | bytes 344072 | tf_op jit(solution)/shard_map/sums/ppermute | solution.py:223
  79.3 6.3 %collective-permute-start.17 = (bf16[112,512]{1,0:T(8,128)(2,1)S(1)}, bf16[112,512]{1,0:T(8,128)(2,1)S(1)}, u32[]{:S(2)}, u32[]{:S(2)}) collective-permute-start(bf16[112,512]{1,0:T(8,128)(2,1)S(1)} %get-tuple-element.52), channel_id=1, source_target_pairs={{0,6},{1,7},{2,4},{3,5},{4,2},{5,3},{6,0},{7,1},{8,14},{9,15},{10,... | collective-permute-start | bytes 344072 | tf_op jit(solution)/shard_map/sums/ppermute | solution.py:223
  80.8 7.1 %collective-permute-start.18 = (bf16[112,512]{1,0:T(8,128)(2,1)S(1)}, bf16[112,512]{1,0:T(8,128)(2,1)S(1)}, u32[]{:S(2)}, u32[]{:S(2)}) collective-permute-start(bf16[112,512]{1,0:T(8,128)(2,1)S(1)} %get-tuple-element.53), channel_id=1, source_target_pairs={{0,2},{1,3},{2,0},{3,1},{4,6},{5,7},{6,4},{7,5},{8,10},{9,11},{10,... | collective-permute-start | bytes 344072 | tf_op jit(solution)/shard_map/sums/ppermute | solution.py:223
  82.5 5.5 %collective-permute-start.19 = (bf16[112,512]{1,0:T(8,128)(2,1)S(1)}, bf16[112,512]{1,0:T(8,128)(2,1)S(1)}, u32[]{:S(2)}, u32[]{:S(2)}) collective-permute-start(bf16[112,512]{1,0:T(8,128)(2,1)S(1)} %get-tuple-element.54), channel_id=1, source_target_pairs={{0,4},{1,5},{2,6},{3,7},{4,0},{5,1},{6,2},{7,3},{8,12},{9,13},{10,... | collective-permute-start | bytes 344072 | tf_op jit(solution)/shard_map/sums/ppermute | solution.py:223

commit v7 on v5

--- a/solution.py
+++ b/solution.py
@@ -80,12 +80,12 @@
         out[first * height : (first + 2) * height, :] = activate(gate, up)
 
 
-def down_kernel(count, flips, blocks, half_flip, placement, *refs):
-    number = len(blocks)
+def down_kernel(count, flips, places, half_flip, placement, *refs):
+    number = count // 4
     rows, refs = refs[:number], refs[number:]
     experts, refs = refs[: 2 * len(flips)], refs[2 * len(flips) :]
     base, outs = refs[:number], refs[number:]
-    height, part = outs[0].shape
+    height, part = outs[0].shape[-2:]
     width = 2 * part
     me = lax.axis_index("expert")
     far = lax.axis_size("expert") // 2
@@ -95,24 +95,26 @@
         pair = range(first, first + 2)
         totals = {i: base[i][...] if base[i].shape[1] == part else base[i][:, columns] for i in pair}
         for flip, hidden, down in zip(flips, experts[::2], experts[1::2]):
-            span = slice(blocks[first] * height, (blocks[first] + 2) * height)
-            value = rounded(dot(hidden[span, :], down[...]))
+            value = rounded(dot(hidden[first * height : (first + 2) * height, :], down[...]))
             for i in pair:
                 weight = token_weight(rows[i][:, width:], placement[me ^ far ^ flip], count)
                 at = (i - first) * height
                 totals[i] = totals[i] + value[at : at + height, :] * weight
         for i in pair:
-            outs[i][...] = totals[i].astype(outs[i].dtype)
-
-
-def finish_kernel(ours, *refs):
-    out = refs[-1]
-    for flip, parts in ((0, refs[:ours]), (1, refs[ours:-1])):
-        width = parts[0].shape[1]
+            if places is None:
+                outs[i][...] = totals[i]
+            else:
+                owner = (me // 2) % number ^ places[i]
+                outs[0][owner] = totals[i].astype(outs[0].dtype)
+
+
+def finish_kernel(ours, others, out):
+    for flip, parts in ((0, ours), (1, others)):
+        width = parts.shape[2]
         half = (lax.axis_index("dp") + flip) % 2
-        total = parts[0][...]
-        for part in parts[1:]:
-            total = total + part[...].astype(jnp.float32)
+        total = parts[0].astype(jnp.float32)
+        for i in range(1, parts.shape[0]):
+            total = total + parts[i].astype(jnp.float32)
         out[:, pl.ds(pl.multiple_of(half * width, width), width)] = total.astype(out.dtype)
 
 
@@ -256,43 +258,46 @@
         for own_part, other_part in ((z_upper, y_upper), (z_near[0], y_near[0]))
     ]
 
-    def far_sums(flips, downs, half_flip, blocks, sums, last):
-        kinds = [jnp.bfloat16 if last and i > 0 else jnp.float32 for i in blocks]
+    near_sums = [x for first in reversed(firsts) for x in base[first]]
+    places = tuple(masks[i] // 2 for i in range(len(rows)))
+
+    def far_sums(flips, downs, half_flip, sums, last):
         experts = [x for flip, down in zip(flips, downs) for x in (hidden[flip], down)]
-        out = call(
-            functools.partial(down_kernel, count, flips, blocks, half_flip),
-            [jax.ShapeDtypeStruct((height, part), kind) for kind in kinds],
-            [placement, *(rows[i] for i in blocks), *experts, *(sums[i] for i in blocks)],
+        if last:
+            shapes = [jax.ShapeDtypeStruct((len(rows), height, part), jnp.bfloat16)]
+        else:
+            shapes = [jax.ShapeDtypeStruct((height, part), jnp.float32)] * len(rows)
+        return call(
+            functools.partial(down_kernel, count, flips, places if last else None, half_flip),
+            shapes,
+            [placement, *rows, *experts, *sums],
             scalars=1,
         )
-        return dict(zip(blocks, out))
+
+    members = [range(d, d + half_axis, 2) for d in (0, 1, half_axis, half_axis + 1)]
 
     def collect(parts):
-        return [parts[0]] + [send(parts[i], masks[i], "sums") for i in reversed(range(1, len(parts)))]
-
-    near_sums = [x for first in reversed(firsts) for x in base[first]]
-    parts = {}
-    for first in firsts:
-        parts |= far_sums((0, 1), [arrived, z_near[1]], 0, (first, first + 1), near_sums, True)
+        with jax.named_scope("sums"):
+            return lax.all_to_all(
+                parts, "expert", 0, 0, axis_index_groups=[list(m) for m in members], tiled=True
+            )
+
+    (parts,) = far_sums((0, 1), [arrived, z_near[1]], 0, near_sums, True)
     flags = after(swap_flags, parts)
     stored = [
         store(0, 0, flags, own[0], z_upper, y_upper),
         store(0, depth, flags, own[1], z_upper, y_upper),
     ]
     ours = collect(parts)
-    landed = after(y_lower, stored, ours[1:-1])
+    landed = after(y_lower, stored, ours)
     y_near.append(send(landed, 1, "y_near"))
-    everyone = tuple(range(len(rows)))
-    last_sums = far_sums((0,), [landed], 1, everyone, near_sums, False)
-    last_parts = {}
-    for first in firsts:
-        last_parts |= far_sums((1,), [y_near[1]], 1, (first, first + 1), last_sums, True)
+    last_sums = far_sums((0,), [landed], 1, near_sums, False)
+    (last_parts,) = far_sums((1,), [y_near[1]], 1, last_sums, True)
     stored.append(store(1, 0, after(swap_flags, last_parts), own[2], z_lower, y_lower))
-    others = collect(last_parts)
     mixed = call(
-        functools.partial(finish_kernel, len(ours)),
+        finish_kernel,
         jax.ShapeDtypeStruct((height, width), tokens.dtype),
-        [*ours, *others],
+        [ours, collect(last_parts)],
     )
     return (mixed, *(w[None] for w in stored))
 

time: 86.6 us -> 106 us (1.22)
  waiting for transfers between devices: 48.6 us -> 54.7 us
  local copies, waits for them, and re-layouts: 1.67 us -> 7.39 us
  Pallas kernels: 16.7 us -> 20.4 us
  starting transfers between devices: 18.2 us -> 20.5 us
    all_to_all x0 -> x2, starting transfers between devices: none -> 8.21 us  [collect(): lax.all_to_all(parts, 'expert', 0, 0, axis_index_groups=[list(m) for m in...]
    all_to_all x0 -> x2, waiting for transfers between devices: none -> 6.04 us  [collect(): lax.all_to_all(parts, 'expert', 0, 0, axis_index_groups=[list(m) for m in...]
    ppermute x18 -> x12, starting transfers between devices: 15.9 us -> 9.95 us  [send(): return lax.ppermute(value, 'expert', [(d, d ^ bit) for d in range(count)])]
    unnamed x16 -> x50, local copies, waits for them, and re-layouts: 0.05 us -> 5.77 us
    ppermute x2, waiting for transfers between devices: 1.15 us -> 5.32 us  [trade(): return lax.ppermute(value, 'dp', trades)]
    ppermute x18 -> x12, waiting for transfers between devices: 47.5 us -> 43.4 us  [send(): return lax.ppermute(value, 'expert', [(d, d ^ bit) for d in range(count)])]
    pallas_call x10 -> x8, Pallas kernels: 12.4 us -> 14.4 us  [call(): pl.pallas_call(kernel, out_shape=out_shape, in_specs=[smem] * scalars + [...]
    pallas_call x3, Pallas kernels: 4.34 us -> 6.08 us  [store(): pl.pallas_call(functools.partial(store_kernel, axis, first), out_shape=ja...]
  transfers between devices with their start and end apart: 20 -> 16, of which waited for: 9 -> 6; matrix products, arithmetic and copies ran while one was open for 0% -> 0% of each run, Pallas kernels for 18% -> 15%
where the time goes in v7:
time: 106 us; the launch traced here: 105 us
  waiting for transfers between devices  54.7 us (52%)
  starting transfers between devices  20.5 us (19%)
  Pallas kernels  20.4 us (19%)
  local copies, waits for them, and re-layouts  7.39 us (7%)
  other arithmetic  1.2 us (1%)
  between operations  1.07 us (1%)
    ppermute x12, waiting for transfers between devices, send(): return lax.ppermute(value, 'expert', [(d, d ^ bit) for d in range(count)])  43.4 us
    pallas_call x8, Pallas kernels, call(): pl.pallas_call(kernel, out_shape=out_shape, in_specs=[smem] * scalars + [...  14.4 us
    ppermute x12, starting transfers between devices, send(): return lax.ppermute(value, 'expert', [(d, d ^ bit) for d in range(count)])  9.95 us
    all_to_all x2, starting transfers between devices, collect(): lax.all_to_all(parts, 'expert', 0, 0, axis_index_groups=[list(m) for m in...  8.21 us
    pallas_call x3, Pallas kernels, store(): pl.pallas_call(functools.partial(store_kernel, axis, first), out_shape=ja...  6.08 us
    all_to_all x2, waiting for transfers between devices, collect(): lax.all_to_all(parts, 'expert', 0, 0, axis_index_groups=[list(m) for m in...  6.04 us
    unnamed x50, local copies, waits for them, and re-layouts  5.77 us
    ppermute x2, waiting for transfers between devices, trade(): return lax.ppermute(value, 'dp', trades)  5.32 us
  transfers between devices with their start and end apart: 16, of which 6 were waited for; matrix products, arithmetic and copies ran while one was open for 0% of the time, Pallas kernels for 15%

profile of v7, /device:TPU:0, one launch (start us, length us, event | category | flops | bytes accessed | tf_op | source)
XLA Modules:
  0.0 105.4 jit_solution(787506922171948739)
XLA Ops:
  0.6 1.5 %slice_bitcast_fusion = (bf16[512,384]{1,0:T(8,128)(2,1)S(1)}, bf16[512,384]{1,0:T(8,128)(2,1)S(1)}, bf16[512,384]{1,0:T(8,128)(2,1)S(1)}, bf16[512,384]{1,0:T(8,128)(2,1)S(1)}) fusion(bf16[1,1024,384]{2,1,0:T(8,128)(2,1)} %param.12, bf16[1,1024,384]{2,1,0:T(8,128)(2,1)} %param.11), kind=kLoop, calls=%fused_computation.4 | loop fusion | bytes 3145728 | tf_op jit(solution)/shard_map/slice | solution.py:213
  2.2 0.0 copy-start.23
  2.2 0.0 copy-start.24
  2.2 0.0 copy-start.22
  2.2 0.0 copy-start
  2.2 1.1 %maximum_select_fusion = bf16[1024,384]{1,0:T(8,128)(2,1)} fusion(bf16[512,384]{1,0:T(8,128)(2,1)S(1)} %get-tuple-element.43, bf16[512,384]{1,0:T(8,128)(2,1)S(1)} %get-tuple-element.47, bf16[512,384]{1,0:T(8,128)(2,1)S(1)} %get-tuple-element.42, bf16[512,384]{1,0:T(8,128)(2,1)S(1)} %get-tuple-element.48, pred[]{:T(512)S(6)} %eq.22), kind=kLoop, calls=%fused_computation | loop fusion | flops 3538944 | bytes 2359297 | tf_op jit(solution)/shard_map/jit(_where)/select_n | solution.py:209
  3.3 4.0 %collective-permute-start.3 = (bf16[1024,384]{1,0:T(8,128)(2,1)}, bf16[1024,384]{1,0:T(8,128)(2,1)}, u32[]{:S(2)}, u32[]{:S(2)}) collective-permute-start(bf16[1024,384]{1,0:T(8,128)(2,1)} %maximum_select_fusion), channel_id=1, source_target_pairs={{0,8},{1,9},{2,10},{3,11},{4,12},{5,13},{6,14},{7,15},{8,0},{9,1},... | collective-permute-start | bytes 2359304 | tf_op jit(solution)/shard_map/swap/ppermute | solution.py:200
  7.4 0.1 copy.17
  7.5 0.0 copy-start.2
  7.5 0.0 copy-start.1
  7.5 0.0 copy-start.20
  7.6 1.6 %collective-permute-start = (bf16[112,1152]{1,0:T(8,128)(2,1)S(1)}, bf16[112,1152]{1,0:T(8,128)(2,1)S(1)}, u32[]{:S(2)}, u32[]{:S(2)}) collective-permute-start(bf16[112,1152]{1,0:T(8,128)(2,1)S(1)} %fusion.1.refs_0_), channel_id=1, source_target_pairs={{0,4},{1,5},{2,6},{3,7},{4,0},{5,1},{6,2},{7,3},{8,12},{9,13},{10,... | collective-permute-start | bytes 774152 | tf_op jit(solution)/shard_map/tokens/ppermute | solution.py:200
  9.2 1.5 %collective-permute-start.1 = (bf16[112,1152]{1,0:T(8,128)(2,1)S(1)}, bf16[112,1152]{1,0:T(8,128)(2,1)S(1)}, u32[]{:S(2)}, u32[]{:S(2)}) collective-permute-start(bf16[112,1152]{1,0:T(8,128)(2,1)S(1)} %fusion.1.refs_0_), channel_id=1, source_target_pairs={{0,2},{1,3},{2,0},{3,1},{4,6},{5,7},{6,4},{7,5},{8,10},{9,11},{10,... | collective-permute-start | bytes 774152 | tf_op jit(solution)/shard_map/tokens/ppermute | solution.py:200
  10.7 19.2 %collective-permute-done.refs_1_ = bf16[112,1152]{1,0:T(8,128)(2,1)S(1)} collective-permute-done((bf16[112,1152]{1,0:T(8,128)(2,1)S(1)}, bf16[112,1152]{1,0:T(8,128)(2,1)S(1)}, u32[]{:S(2)}, u32[]{:S(2)}) %collective-permute-start) | collective-permute-done | bytes 258080 | tf_op jit(solution)/shard_map/tokens/ppermute | solution.py:200
  29.9 1.5 %collective-permute-start.2 = (bf16[112,1152]{1,0:T(8,128)(2,1)S(1)}, bf16[112,1152]{1,0:T(8,128)(2,1)S(1)}, u32[]{:S(2)}, u32[]{:S(2)}) collective-permute-start(bf16[112,1152]{1,0:T(8,128)(2,1)S(1)} %collective-permute-done.refs_1_), channel_id=1, source_target_pairs={{0,2},{1,3},{2,0},{3,1},{4,6},{5,7},{6,4},{7,5},{8,10},{9,11},{10,... | collective-permute-start | bytes 774152 | tf_op jit(solution)/shard_map/tokens/ppermute | solution.py:200
  31.5 0.1 collective-permute-start.8
  31.5 0.5 collective-permute-start.6
  32.0 0.1 collective-permute-start.7
  32.1 4.9 %collective-permute-done.2.refs_3_.refs_1_ = bf16[112,1152]{1,0:T(8,128)(2,1)S(1)} collective-permute-done((bf16[112,1152]{1,0:T(8,128)(2,1)S(1)}, bf16[112,1152]{1,0:T(8,128)(2,1)S(1)}, u32[]{:S(2)}, u32[]{:S(2)}) %collective-permute-start.2) | collective-permute-done | bytes 258080 | tf_op jit(solution)/shard_map/tokens/ppermute | solution.py:200
  37.0 5.0 %collective-permute-done.3.refs_4_.came = bf16[1024,384]{1,0:T(8,128)(2,1)} collective-permute-done((bf16[1024,384]{1,0:T(8,128)(2,1)}, bf16[1024,384]{1,0:T(8,128)(2,1)}, u32[]{:S(2)}, u32[]{:S(2)}) %collective-permute-start.3) | collective-permute-done | bytes 786464 | tf_op jit(solution)/shard_map/swap/ppermute | solution.py:200
  42.0 1.6 %collective-permute-start.4 = (bf16[1024,384]{1,0:T(8,128)(2,1)}, bf16[1024,384]{1,0:T(8,128)(2,1)S(1)}, u32[]{:S(2)}, u32[]{:S(2)}) collective-permute-start(bf16[1024,384]{1,0:T(8,128)(2,1)} %collective-permute-done.3.refs_4_.came), channel_id=1, source_target_pairs={{0,16},{16,0},{1,17},{17,1},{2,18},{18,2},{3,19},{19,3},{4,20},{20... | collective-permute-start | bytes 2359304 | tf_op jit(solution)/shard_map/trade/ppermute | solution.py:204
  43.6 0.0 collective-permute-start.5
  43.6 2.3 %shard_map.113 = (f32[112,1024]{1,0:T(8,128)S(1)}, f32[112,1024]{1,0:T(8,128)S(1)}) custom-call(s32[16]{0:T(128)S(1)} %copy-done.20, bf16[112,1152]{1,0:T(8,128)(2,1)S(1)} %collective-permute-done.1.refs_2_.refs_0_, bf16[112,1152]{1,0:T(8,128)(2,1)S(1)} %collective-permute-done.2.refs_3_.refs_1_, bf16[1024,384]{1,0:T(8,128)(2,1)S(1)} %bitcast.24, ...), custom_call_target="tpu_custom_call" | custom-call | tf_op jit(solution)/shard_map/pallas_call | solution.py:124
  46.0 2.3 %shard_map.112 = (f32[112,1024]{1,0:T(8,128)S(1)}, f32[112,1024]{1,0:T(8,128)S(1)}) custom-call(s32[16]{0:T(128)S(1)} %copy-done.20, bf16[112,1152]{1,0:T(8,128)(2,1)S(1)} %fusion.1.refs_0_, bf16[112,1152]{1,0:T(8,128)(2,1)S(1)} %collective-permute-done.refs_1_, bf16[1024,384]{1,0:T(8,128)(2,1)S(1)} %bitcast.25, bf16[1024,384]{1,0:T(8,128)(2,1)S(1)} %bitcast.21, ...), custom_call_target="tpu_custom_call" | custom-call | tf_op jit(solution)/shard_map/pallas_call | solution.py:124
  48.4 0.1 collective-permute-start.9
  48.4 14.2 %collective-permute-done.5.refs_5_.came = bf16[384,512]{1,0:T(8,128)(2,1)S(1)} collective-permute-done((bf16[384,512]{1,0:T(8,128)(2,1)S(1)}, bf16[384,512]{1,0:T(8,128)(2,1)S(1)}, u32[]{:S(2)}, u32[]{:S(2)}) %collective-permute-start.5) | collective-permute-done | bytes 393248 | tf_op jit(solution)/shard_map/swap/ppermute | solution.py:200
  62.7 0.1 collective-permute-start.10
  62.7 0.5 collective-permute-start.11
  63.2 2.3 %shard_map.111.refs_4_ = bf16[448,384]{1,0:T(8,128)(2,1)S(1)} custom-call(bf16[112,1152]{1,0:T(8,128)(2,1)S(1)} %fusion.1.refs_0_, bf16[112,1152]{1,0:T(8,128)(2,1)S(1)} %collective-permute-done.refs_1_, bf16[112,1152]{1,0:T(8,128)(2,1)S(1)} %collective-permute-done.1.refs_2_.refs_0_, bf16[112,1152]{1,0:T(8,128)(2,1)S(1)} %collective-permute-done.2.refs_3_.refs_1_, ...), custom_call_target="tpu_custom_call" | custom-call | tf_op jit(solution)/shard_map/pallas_call | solution.py:124
  65.6 1.2 %shard_map.114.refs_6_.refs_4_ = bf16[448,384]{1,0:T(8,128)(2,1)S(1)} custom-call(bf16[112,1152]{1,0:T(8,128)(2,1)S(1)} %fusion.1.refs_0_, bf16[112,1152]{1,0:T(8,128)(2,1)S(1)} %collective-permute-done.refs_1_, bf16[112,1152]{1,0:T(8,128)(2,1)S(1)} %collective-permute-done.1.refs_2_.refs_0_, bf16[112,1152]{1,0:T(8,128)(2,1)S(1)} %collective-permute-done.2.refs_3_.refs_1_, ...), custom_call_target="tpu_custom_call" | custom-call | tf_op jit(solution)/shard_map/pallas_call | solution.py:124
  66.9 1.2 %shard_map.115 = bf16[4,112,512]{2,1,0:T(8,128)(2,1)S(1)} custom-call(s32[16]{0:T(128)S(1)} %copy-done.20, bf16[112,1152]{1,0:T(8,128)(2,1)S(1)} %fusion.1.refs_0_, bf16[112,1152]{1,0:T(8,128)(2,1)S(1)} %collective-permute-done.refs_1_, bf16[112,1152]{1,0:T(8,128)(2,1)S(1)} %collective-permute-done.1.refs_2_.refs_0_, ...), custom_call_target="tpu_custom_call" | custom-call | tf_op jit(solution)/shard_map/pallas_call | solution.py:124
  68.1 0.7 copy-done.5
  68.9 0.8 copy-done.9
  69.6 4.3 %all-to-all-start = ((bf16[4,112,512]{2,1,0:T(8,128)(2,1)}), bf16[4,112,512]{2,1,0:T(8,128)(2,1)}, u32[]{:S(2)}, u32[]{:S(2)}) async-start(bf16[4,112,512]{2,1,0:T(8,128)(2,1)} %copy-done.9), calls=%async_computation | async-start | bytes 917504 | tf_op jit(solution)/shard_map/sums/all_to_all | solution.py:281
  73.9 0.8 collective-permute-start.12
  74.7 1.1 %copy-done.4 = bf16[1024,384]{1,0:T(8,128)(2,1)S(1)} copy-done((bf16[1024,384]{1,0:T(8,128)(2,1)S(1)}, bf16[1024,384]{1,0:T(8,128)(2,1)}, u32[]{:S(2)}) %copy-start.4) | copy-done | bytes 786456
  75.8 2.0 %shard_map.117 = bf16[1024,384]{1,0:T(8,128)(2,1)} custom-call(s32[16]{0:T(128)S(1)} %copy-done.21, bf16[1024,384]{1,0:T(8,128)(2,1)S(1)} %bitcast.22, bf16[1024,384]{1,0:T(8,128)(2,1)} %collective-permute-done.3.refs_4_.came, bf16[1024,384]{1,0:T(8,128)(2,1)S(1)} %copy-done.4), custom_call_target="tpu_custom_call" | custom-call | tf_op jit(solution)/shard_map/pallas_call | solution.py:174
  77.9 2.1 %shard_map.116 = bf16[1024,384]{1,0:T(8,128)(2,1)} custom-call(s32[16]{0:T(128)S(1)} %copy-done.21, bf16[1024,384]{1,0:T(8,128)(2,1)S(1)} %bitcast.26, bf16[1024,384]{1,0:T(8,128)(2,1)} %collective-permute-done.3.refs_4_.came, bf16[1024,384]{1,0:T(8,128)(2,1)S(1)} %copy-done.4), custom_call_target="tpu_custom_call" | custom-call | tf_op jit(solution)/shard_map/pallas_call | solution.py:174
  80.1 5.3 %collective-permute-done.12.refs_5_.other = bf16[384,512]{1,0:T(8,128)(2,1)} collective-permute-done((bf16[384,512]{1,0:T(8,128)(2,1)}, bf16[384,512]{1,0:T(8,128)(2,1)}, u32[]{:S(2)}, u32[]{:S(2)}) %collective-permute-start.12) | collective-permute-done | bytes 393248 | tf_op jit(solution)/shard_map/trade/ppermute | solution.py:204
  85.4 1.0 copy-done.13
  86.4 1.0 copy-done.15
  87.4 1.0 copy-done.17
  88.5 1.4 %shard_map.118 = (f32[112,512]{1,0:T(8,128)S(1)}, f32[112,512]{1,0:T(8,128)S(1)}, f32[112,512]{1,0:T(8,128)S(1)}, f32[112,512]{1,0:T(8,128)S(1)}) custom-call(s32[16]{0:T(128)S(1)} %copy-done.20, bf16[112,1152]{1,0:T(8,128)(2,1)S(1)} %fusion.1.refs_0_, bf16[112,1152]{1,0:T(8,128)(2,1)S(1)} %collective-permute-done.refs_1_, ...), custom_call_target="tpu_custom_call" | custom-call | tf_op jit(solution)/shard_map/pallas_call | solution.py:124
  89.9 1.7 %shard_map.119 = bf16[4,112,512]{2,1,0:T(8,128)(2,1)} custom-call(s32[16]{0:T(128)S(1)} %copy-done.20, bf16[112,1152]{1,0:T(8,128)(2,1)S(1)} %fusion.1.refs_0_, bf16[112,1152]{1,0:T(8,128)(2,1)S(1)} %collective-permute-done.refs_1_, bf16[112,1152]{1,0:T(8,128)(2,1)S(1)} %collective-permute-done.1.refs_2_.refs_0_, ...), custom_call_target="tpu_custom_call" | custom-call | tf_op jit(solution)/shard_map/pallas_call | solution.py:124
  91.6 4.0 %all-to-all-start.1 = ((bf16[4,112,512]{2,1,0:T(8,128)(2,1)}), bf16[4,112,512]{2,1,0:T(8,128)(2,1)S(1)}, u32[]{:S(2)}, u32[]{:S(2)}) async-start(bf16[4,112,512]{2,1,0:T(8,128)(2,1)} %shard_map.119), calls=%async_computation.1 | async-start | bytes 917504 | tf_op jit(solution)/shard_map/sums/all_to_all | solution.py:281
  95.6 1.9 %shard_map.121 = bf16[384,1024]{1,0:T(8,128)(2,1)} custom-call(s32[16]{0:T(128)S(1)} %copy-done.21, bf16[384,1024]{1,0:T(8,128)(2,1)S(1)} %bitcast.18, bf16[384,512]{1,0:T(8,128)(2,1)S(1)} %copy-done.19, bf16[384,512]{1,0:T(8,128)(2,1)} %collective-permute-done.12.refs_5_.other), custom_call_target="tpu_custom_call" | custom-call | tf_op jit(solution)/shard_map/pallas_call | solution.py:174
  97.5 6.0 %all-to-all-done.1.others = bf16[4,112,512]{2,1,0:T(8,128)(2,1)S(1)} async-done(((bf16[4,112,512]{2,1,0:T(8,128)(2,1)}), bf16[4,112,512]{2,1,0:T(8,128)(2,1)S(1)}, u32[]{:S(2)}, u32[]{:S(2)}) %all-to-all-start.1) | async-done | bytes 458784 | tf_op jit(solution)/shard_map/sums/all_to_all | solution.py:281
  103.5 1.8 %shard_map.120 = bf16[112,1024]{1,0:T(8,128)(2,1)} custom-call(bf16[4,112,512]{2,1,0:T(8,128)(2,1)} %all-to-all-done.ours, bf16[4,112,512]{2,1,0:T(8,128)(2,1)S(1)} %all-to-all-done.1.others), custom_call_target="tpu_custom_call" | custom-call | tf_op jit(solution)/shard_map/pallas_call | solution.py:124
  (53 shorter events, 0.2 us)
Async XLA Ops:
  2.2 5.2 %copy-start.23 = (f32[112,8]{0,1:T(8,128)S(1)}, f32[112,8]{0,1:T(8,128)}, u32[]{:S(2)}) copy-start(f32[112,8]{0,1:T(8,128)} %param.10) | copy-start | bytes 10756
  2.2 5.2 %copy-start.24 = (s32[112,8]{0,1:T(8,128)S(1)}, s32[112,8]{0,1:T(8,128)}, u32[]{:S(2)}) copy-start(s32[112,8]{0,1:T(8,128)} %param.9) | copy-start | bytes 10756
  2.2 5.3 %copy-start.22 = (bf16[112,1024]{1,0:T(8,128)(2,1)S(1)}, bf16[112,1024]{1,0:T(8,128)(2,1)}, u32[]{:S(2)}) copy-start(bf16[112,1024]{1,0:T(8,128)(2,1)} %param.8) | copy-start | bytes 688132
  2.2 29.2 %copy-start = (bf16[1,384,1024]{2,1,0:T(8,128)(2,1)S(1)}, bf16[1,384,1024]{2,1,0:T(8,128)(2,1)}, u32[]{:S(2)}) copy-start(bf16[1,384,1024]{2,1,0:T(8,128)(2,1)} %param.13) | copy-start | bytes 2359300
  3.3 38.7 %collective-permute-start.3 = (bf16[1024,384]{1,0:T(8,128)(2,1)}, bf16[1024,384]{1,0:T(8,128)(2,1)}, u32[]{:S(2)}, u32[]{:S(2)}) collective-permute-start(bf16[1024,384]{1,0:T(8,128)(2,1)} %maximum_select_fusion), channel_id=1, source_target_pairs={{0,8},{1,9},{2,10},{3,11},{4,12},{5,13},{6,14},{7,15},{8,0},{9,1},... | collective-permute-start | bytes 2359304 | tf_op jit(solution)/shard_map/swap/ppermute | solution.py:200
  7.5 24.0 %copy-start.2 = (bf16[1,1024,384]{2,1,0:T(8,128)(2,1)S(1)}, bf16[1,1024,384]{2,1,0:T(8,128)(2,1)}, u32[]{:S(2)}) copy-start(bf16[1,1024,384]{2,1,0:T(8,128)(2,1)} %param.11) | copy-start | bytes 2359300
  7.5 24.5 %copy-start.1 = (bf16[1,1024,384]{2,1,0:T(8,128)(2,1)S(1)}, bf16[1,1024,384]{2,1,0:T(8,128)(2,1)}, u32[]{:S(2)}) copy-start(bf16[1,1024,384]{2,1,0:T(8,128)(2,1)} %param.12) | copy-start | bytes 2359300
  7.5 36.1 %copy-start.20 = (s32[16]{0:T(128)S(1)}, s32[16]{0:T(128)}, u32[]{:S(2)}) copy-start(s32[16]{0:T(128)} %placement.9) | copy-start | bytes 196
  7.6 22.3 %collective-permute-start = (bf16[112,1152]{1,0:T(8,128)(2,1)S(1)}, bf16[112,1152]{1,0:T(8,128)(2,1)S(1)}, u32[]{:S(2)}, u32[]{:S(2)}) collective-permute-start(bf16[112,1152]{1,0:T(8,128)(2,1)S(1)} %fusion.1.refs_0_), channel_id=1, source_target_pairs={{0,4},{1,5},{2,6},{3,7},{4,0},{5,1},{6,2},{7,3},{8,12},{9,13},{10,... | collective-permute-start | bytes 774152 | tf_op jit(solution)/shard_map/tokens/ppermute | solution.py:200
  9.2 22.8 %collective-permute-start.1 = (bf16[112,1152]{1,0:T(8,128)(2,1)S(1)}, bf16[112,1152]{1,0:T(8,128)(2,1)S(1)}, u32[]{:S(2)}, u32[]{:S(2)}) collective-permute-start(bf16[112,1152]{1,0:T(8,128)(2,1)S(1)} %fusion.1.refs_0_), channel_id=1, source_target_pairs={{0,2},{1,3},{2,0},{3,1},{4,6},{5,7},{6,4},{7,5},{8,10},{9,11},{10,... | collective-permute-start | bytes 774152 | tf_op jit(solution)/shard_map/tokens/ppermute | solution.py:200
  29.9 7.1 %collective-permute-start.2 = (bf16[112,1152]{1,0:T(8,128)(2,1)S(1)}, bf16[112,1152]{1,0:T(8,128)(2,1)S(1)}, u32[]{:S(2)}, u32[]{:S(2)}) collective-permute-start(bf16[112,1152]{1,0:T(8,128)(2,1)S(1)} %collective-permute-done.refs_1_), channel_id=1, source_target_pairs={{0,2},{1,3},{2,0},{3,1},{4,6},{5,7},{6,4},{7,5},{8,10},{9,11},{10,... | collective-permute-start | bytes 774152 | tf_op jit(solution)/shard_map/tokens/ppermute | solution.py:200
  31.5 12.2 %collective-permute-start.8 = (bf16[384,1024]{1,0:T(8,128)(2,1)S(1)}, bf16[384,1024]{1,0:T(8,128)(2,1)S(1)}, u32[]{:S(2)}, u32[]{:S(2)}) collective-permute-start(bf16[384,1024]{1,0:T(8,128)(2,1)S(1)} %bitcast.15), channel_id=1, source_target_pairs={{0,1},{1,0},{2,3},{3,2},{4,5},{5,4},{6,7},{7,6},{8,9},{9,8},{10,11... | collective-permute-start | bytes 2359304 | tf_op jit(solution)/shard_map/near/ppermute | solution.py:200
  31.5 12.1 %collective-permute-start.6 = (bf16[1024,384]{1,0:T(8,128)(2,1)S(1)}, bf16[1024,384]{1,0:T(8,128)(2,1)S(1)}, u32[]{:S(2)}, u32[]{:S(2)}) collective-permute-start(bf16[1024,384]{1,0:T(8,128)(2,1)S(1)} %bitcast.23), channel_id=1, source_target_pairs={{0,1},{1,0},{2,3},{3,2},{4,5},{5,4},{6,7},{7,6},{8,9},{9,8},{10,11... | collective-permute-start | bytes 2359304 | tf_op jit(solution)/shard_map/near/ppermute | solution.py:200
  32.0 11.6 %collective-permute-start.7 = (bf16[1024,384]{1,0:T(8,128)(2,1)S(1)}, bf16[1024,384]{1,0:T(8,128)(2,1)S(1)}, u32[]{:S(2)}, u32[]{:S(2)}) collective-permute-start(bf16[1024,384]{1,0:T(8,128)(2,1)S(1)} %bitcast.19), channel_id=1, source_target_pairs={{0,1},{1,0},{2,3},{3,2},{4,5},{5,4},{6,7},{7,6},{8,9},{9,8},{10,11... | collective-permute-start | bytes 2359304 | tf_op jit(solution)/shard_map/near/ppermute | solution.py:200
  42.0 20.6 %collective-permute-start.4 = (bf16[1024,384]{1,0:T(8,128)(2,1)}, bf16[1024,384]{1,0:T(8,128)(2,1)S(1)}, u32[]{:S(2)}, u32[]{:S(2)}) collective-permute-start(bf16[1024,384]{1,0:T(8,128)(2,1)} %collective-permute-done.3.refs_4_.came), channel_id=1, source_target_pairs={{0,16},{16,0},{1,17},{17,1},{2,18},{18,2},{3,19},{19,3},{4,20},{20... | collective-permute-start | bytes 2359304 | tf_op jit(solution)/shard_map/trade/ppermute | solution.py:204
  43.6 19.1 %collective-permute-start.5 = (bf16[384,512]{1,0:T(8,128)(2,1)S(1)}, bf16[384,512]{1,0:T(8,128)(2,1)S(1)}, u32[]{:S(2)}, u32[]{:S(2)}) collective-permute-start(bf16[384,512]{1,0:T(8,128)(2,1)S(1)} %slice_select_fusion), channel_id=1, source_target_pairs={{0,8},{1,9},{2,10},{3,11},{4,12},{5,13},{6,14},{7,15},{8,0},{9,1},... | collective-permute-start | bytes 1179656 | tf_op jit(solution)/shard_map/swap/ppermute | solution.py:200
  46.0 20.9 %copy-start.10 = (f32[112,1024]{1,0:T(8,128)}, f32[112,1024]{1,0:T(8,128)S(1)}, u32[]{:S(2)}) copy-start(f32[112,1024]{1,0:T(8,128)S(1)} %get-tuple-element.29.refs_10_.refs_8_) | copy-start | bytes 1376260
  46.0 20.9 %copy-start.12 = (f32[112,1024]{1,0:T(8,128)}, f32[112,1024]{1,0:T(8,128)S(1)}, u32[]{:S(2)}) copy-start(f32[112,1024]{1,0:T(8,128)S(1)} %get-tuple-element.30.refs_11_.refs_9_) | copy-start | bytes 1376260
  48.3 18.5 %copy-start.14 = (f32[112,1024]{1,0:T(8,128)}, f32[112,1024]{1,0:T(8,128)S(1)}, u32[]{:S(2)}) copy-start(f32[112,1024]{1,0:T(8,128)S(1)} %get-tuple-element.27.refs_8_.refs_6_) | copy-start | bytes 1376260
  48.3 18.5 %copy-start.16 = (f32[112,1024]{1,0:T(8,128)}, f32[112,1024]{1,0:T(8,128)S(1)}, u32[]{:S(2)}) copy-start(f32[112,1024]{1,0:T(8,128)S(1)} %get-tuple-element.28.refs_9_.refs_7_) | copy-start | bytes 1376260
  48.4 17.3 %collective-permute-start.9 = (bf16[1024,384]{1,0:T(8,128)(2,1)}, bf16[1024,384]{1,0:T(8,128)(2,1)S(1)}, u32[]{:S(2)}, u32[]{:S(2)}) collective-permute-start(bf16[1024,384]{1,0:T(8,128)(2,1)} %collective-permute-done.3.refs_4_.came), channel_id=1, source_target_pairs={{0,1},{1,0},{2,3},{3,2},{4,5},{5,4},{6,7},{7,6},{8,9},{9,8},{10,11... | collective-permute-start | bytes 2359304 | tf_op jit(solution)/shard_map/z_near/ppermute | solution.py:200
  62.7 4.2 %copy-start.18 = (bf16[384,512]{1,0:T(8,128)(2,1)}, bf16[384,512]{1,0:T(8,128)(2,1)S(1)}, u32[]{:S(2)}) copy-start(bf16[384,512]{1,0:T(8,128)(2,1)S(1)} %collective-permute-done.5.refs_5_.came) | copy-start | bytes 1179652
  62.7 2.9 %copy-start.3 = (bf16[1024,384]{1,0:T(8,128)(2,1)}, bf16[1024,384]{1,0:T(8,128)(2,1)S(1)}, u32[]{:S(2)}) copy-start(bf16[1024,384]{1,0:T(8,128)(2,1)S(1)} %collective-permute-done.4.refs_5_.other) | copy-start | bytes 2359300
  62.7 2.9 %collective-permute-start.10 = (bf16[1024,384]{1,0:T(8,128)(2,1)S(1)}, bf16[1024,384]{1,0:T(8,128)(2,1)S(1)}, u32[]{:S(2)}, u32[]{:S(2)}) collective-permute-start(bf16[1024,384]{1,0:T(8,128)(2,1)S(1)} %collective-permute-done.4.refs_5_.other), channel_id=1, source_target_pairs={{0,1},{1,0},{2,3},{3,2},{4,5},{5,4},{6,7},{7,6},{8,9},{9,8},{10,11... | collective-permute-start | bytes 2359304 | tf_op jit(solution)/shard_map/y_near/ppermute | solution.py:200
  62.7 4.1 %collective-permute-start.11 = (bf16[384,512]{1,0:T(8,128)(2,1)S(1)}, bf16[384,512]{1,0:T(8,128)(2,1)S(1)}, u32[]{:S(2)}, u32[]{:S(2)}) collective-permute-start(bf16[384,512]{1,0:T(8,128)(2,1)S(1)} %collective-permute-done.5.refs_5_.came), channel_id=1, source_target_pairs={{0,1},{1,0},{2,3},{3,2},{4,5},{5,4},{6,7},{7,6},{8,9},{9,8},{10,11... | collective-permute-start | bytes 1179656 | tf_op jit(solution)/shard_map/z_near/ppermute | solution.py:200
  65.6 1.3 %copy-start.7 = (bf16[448,384]{1,0:T(8,128)(2,1)}, bf16[448,384]{1,0:T(8,128)(2,1)S(1)}, u32[]{:S(2)}) copy-start(bf16[448,384]{1,0:T(8,128)(2,1)S(1)} %shard_map.111.refs_4_) | copy-start | bytes 1032196
  68.1 0.7 copy-start.5
  68.9 0.8 copy-start.9
  69.6 5.1 %copy-start.21 = (s32[16]{0:T(128)S(1)}, s32[16]{0:T(128)}, u32[]{:S(2)}) copy-start(s32[16]{0:T(128)} %flags.2) | copy-start | bytes 196
  69.6 15.7 %all-to-all-start = ((bf16[4,112,512]{2,1,0:T(8,128)(2,1)}), bf16[4,112,512]{2,1,0:T(8,128)(2,1)}, u32[]{:S(2)}, u32[]{:S(2)}) async-start(bf16[4,112,512]{2,1,0:T(8,128)(2,1)} %copy-done.9), calls=%async_computation | async-start | bytes 917504 | tf_op jit(solution)/shard_map/sums/all_to_all | solution.py:281
  73.9 11.5 %collective-permute-start.12 = (bf16[384,512]{1,0:T(8,128)(2,1)}, bf16[384,512]{1,0:T(8,128)(2,1)}, u32[]{:S(2)}, u32[]{:S(2)}) collective-permute-start(bf16[384,512]{1,0:T(8,128)(2,1)} %copy-done.18), channel_id=1, source_target_pairs={{0,16},{16,0},{1,17},{17,1},{2,18},{18,2},{3,19},{19,3},{4,20},{20... | collective-permute-start | bytes 1179656 | tf_op jit(solution)/shard_map/trade/ppermute | solution.py:204
  74.7 1.1 %copy-start.4 = (bf16[1024,384]{1,0:T(8,128)(2,1)S(1)}, bf16[1024,384]{1,0:T(8,128)(2,1)}, u32[]{:S(2)}) copy-start(bf16[1024,384]{1,0:T(8,128)(2,1)} %copy-done.3) | copy-start | bytes 2359300
  77.9 7.5 %copy-start.8 = (bf16[448,384]{1,0:T(8,128)(2,1)S(1)}, bf16[448,384]{1,0:T(8,128)(2,1)}, u32[]{:S(2)}) copy-start(bf16[448,384]{1,0:T(8,128)(2,1)} %copy-done.7) | copy-start | bytes 1032196
  77.9 7.5 %copy-start.11 = (f32[112,1024]{1,0:T(8,128)S(1)}, f32[112,1024]{1,0:T(8,128)}, u32[]{:S(2)}) copy-start(f32[112,1024]{1,0:T(8,128)} %copy-done.10) | copy-start | bytes 1376260
  80.1 9.8 %copy-start.6 = (bf16[448,384]{1,0:T(8,128)(2,1)S(1)}, bf16[448,384]{1,0:T(8,128)(2,1)}, u32[]{:S(2)}) copy-start(bf16[448,384]{1,0:T(8,128)(2,1)} %copy-done.5) | copy-start | bytes 1032196
  85.4 4.5 %collective-permute-start.13 = (bf16[384,512]{1,0:T(8,128)(2,1)}, bf16[384,512]{1,0:T(8,128)(2,1)S(1)}, u32[]{:S(2)}, u32[]{:S(2)}) collective-permute-start(bf16[384,512]{1,0:T(8,128)(2,1)} %collective-permute-done.12.refs_5_.other), channel_id=1, source_target_pairs={{0,1},{1,0},{2,3},{3,2},{4,5},{5,4},{6,7},{7,6},{8,9},{9,8},{10,11... | collective-permute-start | bytes 1179656 | tf_op jit(solution)/shard_map/y_near/ppermute | solution.py:200
  85.4 1.0 copy-start.13
  86.4 1.0 copy-start.15
  87.4 1.0 copy-start.17
  91.6 4.0 %copy-start.19 = (bf16[384,512]{1,0:T(8,128)(2,1)S(1)}, bf16[384,512]{1,0:T(8,128)(2,1)}, u32[]{:S(2)}) copy-start(bf16[384,512]{1,0:T(8,128)(2,1)} %copy-done.18) | copy-start | bytes 1179652
  91.6 11.9 %all-to-all-start.1 = ((bf16[4,112,512]{2,1,0:T(8,128)(2,1)}), bf16[4,112,512]{2,1,0:T(8,128)(2,1)S(1)}, u32[]{:S(2)}, u32[]{:S(2)}) async-start(bf16[4,112,512]{2,1,0:T(8,128)(2,1)} %shard_map.119), calls=%async_computation.1 | async-start | bytes 917504 | tf_op jit(solution)/shard_map/sums/all_to_all | solution.py:281

commit v8 on v5

--- a/solution.py
+++ b/solution.py
@@ -65,18 +65,18 @@
 
 
 def hidden_kernel(blocks, width, *refs):
-    rows, own, other, out, x = refs[:blocks], refs[blocks], refs[blocks + 1], refs[blocks + 2], refs[blocks + 3]
+    rows, (ga, ua, gb, ub), out, x = refs[:blocks], refs[blocks : blocks + 4], refs[blocks + 4], refs[blocks + 5]
     height = rows[0].shape[0]
     half = lax.axis_index("dp") % 2
-    depth = own.shape[0] // 2
+    depth = ga.shape[0]
     at = pl.multiple_of(half * depth, depth)
     off = pl.multiple_of(depth - at, depth)
     for first in range(0, blocks, 2):
         for i in range(2):
             x[i * height : (i + 1) * height, :] = rows[first + i][:, :width]
         xa, xb = x[:, pl.ds(at, depth)], x[:, pl.ds(off, depth)]
-        gate = dot(xa, own[:depth, :]) + dot(xb, other[:depth, :])
-        up = dot(xa, own[depth:, :]) + dot(xb, other[depth:, :])
+        gate = dot(xa, ga[...]) + dot(xb, gb[...])
+        up = dot(xa, ua[...]) + dot(xb, ub[...])
         out[first * height : (first + 2) * height, :] = activate(gate, up)
 
 
@@ -206,10 +206,7 @@
     def half_of(first, second):
         return jnp.where(couple == 0, first, second)
 
-    upper = half_of(
-        jnp.concatenate([own[0][:depth], own[1][:depth]], axis=0),
-        jnp.concatenate([own[0][depth:], own[1][depth:]], axis=0),
-    )
+    upper = [half_of(w[:depth], w[depth:]) for w in own[:2]]
     lower = half_of(own[2][:, :part], own[2][:, part:])
 
     bits = []
@@ -219,16 +216,19 @@
         bit //= 2
     blocks = {0: pack_gates(tokens, expert_ids, gate_probs, count)}
     masks = {0: 0}
+    z_upper = [send(w, half_axis, "swap") for w in upper]
     for stage, bit in enumerate(bits):
         for i in sorted(blocks):
-            blocks[i | 1 << stage] = send(blocks[i], bit, "tokens")
+            last = (i | 1 << stage) + 1 == 1 << len(bits)
+            block = after(blocks[i], z_upper[0]) if last else blocks[i]
+            blocks[i | 1 << stage] = send(block, bit, "tokens")
             masks[i | 1 << stage] = masks[i] ^ bit
     rows = [blocks[i] for i in range(len(blocks))]
 
-    z_upper = send(upper, half_axis, "swap")
-    z_lower = send(after(lower, z_upper, *rows), half_axis, "swap")
-    y_upper = trade(after(z_upper, *rows))
-    near = [send(after(w, lower), 1, "near") for w in own]
+    y_upper = [trade(z_upper[0])]
+    y_upper.append(trade(after(z_upper[1], y_upper[0])))
+    near = [send(after(w, z_upper[0], lower, upper[1], *rows[1:-1]), 1, "near") for w in own]
+    z_lower = send(after(lower, z_upper[1]), half_axis, "swap")
 
     firsts = list(reversed(range(0, len(rows), 2)))
     scratch = [pltpu.VMEM((2 * height, width), jnp.bfloat16)]
@@ -244,16 +244,16 @@
 
     arrived = after(z_lower, base)
     y_lower = trade(arrived)
-    z_near = [send(z_upper, 1, "z_near"), send(arrived, 1, "z_near")]
-    y_near = [send(after(y_upper, arrived), 1, "y_near")]
+    z_near = [send(w, 1, "z_near") for w in (*z_upper, arrived)]
+    y_near = [send(y_upper[0], 1, "y_near"), send(after(y_upper[1], arrived), 1, "y_near")]
     hidden = [
         call(
             functools.partial(hidden_kernel, len(rows), width),
             jax.ShapeDtypeStruct((len(rows) * height, ff), jnp.bfloat16),
-            [*rows, own_part, other_part],
+            [*rows, *own_part, *other_part],
             scratch,
         )
-        for own_part, other_part in ((z_upper, y_upper), (z_near[0], y_near[0]))
+        for own_part, other_part in ((z_upper, y_upper), (z_near[:2], y_near[:2]))
     ]
 
     def far_sums(flips, downs, half_flip, blocks, sums, last):
@@ -273,11 +273,11 @@
     near_sums = [x for first in reversed(firsts) for x in base[first]]
     parts = {}
     for first in firsts:
-        parts |= far_sums((0, 1), [arrived, z_near[1]], 0, (first, first + 1), near_sums, True)
+        parts |= far_sums((0, 1), [arrived, z_near[2]], 0, (first, first + 1), near_sums, True)
     flags = after(swap_flags, parts)
     stored = [
-        store(0, 0, flags, own[0], z_upper, y_upper),
-        store(0, depth, flags, own[1], z_upper, y_upper),
+        store(0, 0, flags, own[0], z_upper[0], y_upper[0]),
+        store(0, 0, flags, own[1], z_upper[1], y_upper[1]),
     ]
     ours = collect(parts)
     landed = after(y_lower, stored, ours[1:-1])
@@ -286,7 +286,7 @@
     last_sums = far_sums((0,), [landed], 1, everyone, near_sums, False)
     last_parts = {}
     for first in firsts:
-        last_parts |= far_sums((1,), [y_near[1]], 1, (first, first + 1), last_sums, True)
+        last_parts |= far_sums((1,), [y_near[2]], 1, (first, first + 1), last_sums, True)
     stored.append(store(1, 0, after(swap_flags, last_parts), own[2], z_lower, y_lower))
     others = collect(last_parts)
     mixed = call(

time: 86.6 us -> 93.6 us (1.081)
  waiting for transfers between devices: 48.6 us -> 52.6 us
  other arithmetic: 0.32 us -> 3.04 us
  starting transfers between devices: 18.2 us -> 19.3 us
    ppermute x18 -> x21, waiting for transfers between devices: 47.5 us -> 52.2 us  [send(): return lax.ppermute(value, 'expert', [(d, d ^ bit) for d in range(count)])]
    ppermute x2 -> x3, starting transfers between devices: 2.32 us -> 4.56 us  [trade(): return lax.ppermute(value, 'dp', trades)]
    slice x1 -> x0, local copies, waits for them, and re-layouts: 1.52 us -> none  [per_device(): own[1][depth:]]
    ppermute x18 -> x21, starting transfers between devices: 15.9 us -> 14.8 us  [send(): return lax.ppermute(value, 'expert', [(d, d ^ bit) for d in range(count)])]
    concatenate x1, other arithmetic: 0.02 us -> 1.04 us  [pack_gates(): return jnp.concatenate([tokens, parts], axis=1)]
    select_n x2 -> x3, other arithmetic: 0.25 us -> 1.25 us  [half_of(): return jnp.where(couple == 0, first, second)]
  transfers between devices with their start and end apart: 20 -> 24, of which waited for: 9 -> 9; matrix products, arithmetic and copies ran while one was open for 0% -> 1% of each run, Pallas kernels for 18% -> 17%
where the time goes in v8:
time: 93.6 us; the launch traced here: 93.4 us
  waiting for transfers between devices  52.6 us (56%)
  starting transfers between devices  19.3 us (21%)
  Pallas kernels  16.7 us (18%)
  other arithmetic  3.04 us (3%)
    ppermute x21, waiting for transfers between devices, send(): return lax.ppermute(value, 'expert', [(d, d ^ bit) for d in range(count)])  52.2 us
    ppermute x21, starting transfers between devices, send(): return lax.ppermute(value, 'expert', [(d, d ^ bit) for d in range(count)])  14.8 us
    pallas_call x10, Pallas kernels, call(): pl.pallas_call(kernel, out_shape=out_shape, in_specs=[smem] * scalars + [...  12.4 us
    ppermute x3, starting transfers between devices, trade(): return lax.ppermute(value, 'dp', trades)  4.56 us
    pallas_call x3, Pallas kernels, store(): pl.pallas_call(functools.partial(store_kernel, axis, first), out_shape=ja...  4.34 us
  transfers between devices with their start and end apart: 24, of which 9 were waited for; matrix products, arithmetic and copies ran while one was open for 1% of the time, Pallas kernels for 17%

profile of v8, /device:TPU:0, one launch (start us, length us, event | category | flops | bytes accessed | tf_op | source)
XLA Modules:
  0.0 93.4 jit_solution(1261772523823374818)
XLA Ops:
  0.6 0.7 select_reduce_fusion
  1.4 0.1 copy.17
  1.5 1.0 %fusion.1.refs_0_ = bf16[112,1152]{1,0:T(8,128)(2,1)S(1)} fusion(bf16[112,48]{1,0:T(8,128)(2,1)S(1)} %copy.17, bf16[112,1024]{1,0:T(8,128)(2,1)} %param.8), kind=kLoop, calls=%fused_computation.5 | loop fusion | flops 774144 | bytes 498176 | tf_op jit(solution)/shard_map/concatenate | solution.py:29
  2.6 3.1 %collective-permute-start = (bf16[112,1152]{1,0:T(8,128)(2,1)S(1)}, bf16[112,1152]{1,0:T(8,128)(2,1)S(1)}, u32[]{:S(2)}, u32[]{:S(2)}) collective-permute-start(bf16[112,1152]{1,0:T(8,128)(2,1)S(1)} %fusion.1.refs_0_), channel_id=1, source_target_pairs={{0,4},{1,5},{2,6},{3,7},{4,0},{5,1},{6,2},{7,3},{8,12},{9,13},{10,... | collective-permute-start | bytes 774152 | tf_op jit(solution)/shard_map/tokens/ppermute | solution.py:198
  5.6 1.5 %collective-permute-start.1 = (bf16[112,1152]{1,0:T(8,128)(2,1)S(1)}, bf16[112,1152]{1,0:T(8,128)(2,1)S(1)}, u32[]{:S(2)}, u32[]{:S(2)}) collective-permute-start(bf16[112,1152]{1,0:T(8,128)(2,1)S(1)} %fusion.1.refs_0_), channel_id=1, source_target_pairs={{0,2},{1,3},{2,0},{3,1},{4,6},{5,7},{6,4},{7,5},{8,10},{9,11},{10,... | collective-permute-start | bytes 774152 | tf_op jit(solution)/shard_map/tokens/ppermute | solution.py:198
  7.1 1.2 %select_bitcast_fusion.1 = bf16[512,384]{1,0:T(8,128)(2,1)S(1)} fusion(bf16[1,1024,384]{2,1,0:T(8,128)(2,1)} %param.11, pred[]{:T(512)S(6)} %eq.23), kind=kLoop, calls=%fused_computation.4 | loop fusion | flops 196608 | bytes 1179649 | tf_op jit(solution)/shard_map/jit(_where)/select_n | solution.py:207
  8.3 0.0 copy-start
  8.3 2.7 %collective-permute-start.2 = (bf16[512,384]{1,0:T(8,128)(2,1)S(1)}, bf16[512,384]{1,0:T(8,128)(2,1)S(1)}, u32[]{:S(2)}, u32[]{:S(2)}) collective-permute-start(bf16[512,384]{1,0:T(8,128)(2,1)S(1)} %select_bitcast_fusion.1), channel_id=1, source_target_pairs={{0,8},{1,9},{2,10},{3,11},{4,12},{5,13},{6,14},{7,15},{8,0},{9,1},... | collective-permute-start | bytes 1179656 | tf_op jit(solution)/shard_map/swap/ppermute | solution.py:198
  11.0 0.0 copy-start.1
  11.0 0.1 select_bitcast_fusion
  11.1 3.1 %collective-permute-done.refs_1_ = bf16[112,1152]{1,0:T(8,128)(2,1)S(1)} collective-permute-done((bf16[112,1152]{1,0:T(8,128)(2,1)S(1)}, bf16[112,1152]{1,0:T(8,128)(2,1)S(1)}, u32[]{:S(2)}, u32[]{:S(2)}) %collective-permute-start) | collective-permute-done | bytes 258080 | tf_op jit(solution)/shard_map/tokens/ppermute | solution.py:198
  14.2 13.8 %collective-permute-done.2.refs_4_.came = bf16[512,384]{1,0:T(8,128)(2,1)S(1)} collective-permute-done((bf16[512,384]{1,0:T(8,128)(2,1)S(1)}, bf16[512,384]{1,0:T(8,128)(2,1)S(1)}, u32[]{:S(2)}, u32[]{:S(2)}) %collective-permute-start.2) | collective-permute-done | bytes 393248 | tf_op jit(solution)/shard_map/swap/ppermute | solution.py:198
  28.1 0.5 collective-permute-start.8
  28.6 0.1 collective-permute-start.9
  28.6 1.5 %collective-permute-start.5 = (bf16[512,384]{1,0:T(8,128)(2,1)S(1)}, bf16[512,384]{1,0:T(8,128)(2,1)S(1)}, u32[]{:S(2)}, u32[]{:S(2)}) collective-permute-start(bf16[512,384]{1,0:T(8,128)(2,1)S(1)} %collective-permute-done.2.refs_4_.came), channel_id=1, source_target_pairs={{0,16},{16,0},{1,17},{17,1},{2,18},{18,2},{3,19},{19,3},{4,20},{20... | collective-permute-start | bytes 1179656 | tf_op jit(solution)/shard_map/trade/ppermute | solution.py:202
  30.2 19.1 %collective-permute-done.4.refs_5_.came = bf16[512,384]{1,0:T(8,128)(2,1)S(1)} collective-permute-done((bf16[512,384]{1,0:T(8,128)(2,1)S(1)}, bf16[512,384]{1,0:T(8,128)(2,1)S(1)}, u32[]{:S(2)}, u32[]{:S(2)}) %collective-permute-start.4) | collective-permute-done | bytes 393248 | tf_op jit(solution)/shard_map/swap/ppermute | solution.py:198
  49.3 1.5 %collective-permute-start.6 = (bf16[512,384]{1,0:T(8,128)(2,1)S(1)}, bf16[512,384]{1,0:T(8,128)(2,1)S(1)}, u32[]{:S(2)}, u32[]{:S(2)}) collective-permute-start(bf16[512,384]{1,0:T(8,128)(2,1)S(1)} %collective-permute-done.4.refs_5_.came), channel_id=1, source_target_pairs={{0,16},{16,0},{1,17},{17,1},{2,18},{18,2},{3,19},{19,3},{4,20},{20... | collective-permute-start | bytes 1179656 | tf_op jit(solution)/shard_map/trade/ppermute | solution.py:202
  50.8 0.6 collective-permute-start.3
  51.4 0.2 collective-permute-start.12
  51.6 2.3 %shard_map.112 = (f32[112,1024]{1,0:T(8,128)S(1)}, f32[112,1024]{1,0:T(8,128)S(1)}) custom-call(s32[16]{0:T(128)S(1)} %copy-done.3, bf16[112,1152]{1,0:T(8,128)(2,1)S(1)} %fusion.1.refs_0_, bf16[112,1152]{1,0:T(8,128)(2,1)S(1)} %collective-permute-done.refs_1_, bf16[1024,384]{1,0:T(8,128)(2,1)S(1)} %bitcast.15, bf16[1024,384]{1,0:T(8,128)(2,1)S(1)} %bitcast.11, ...), custom_call_target="tpu_custom_call" | custom-call | tf_op jit(solution)/shard_map/pallas_call | solution.py:122
  53.9 5.5 %collective-permute-done.3.refs_3_.refs_1_ = bf16[112,1152]{1,0:T(8,128)(2,1)S(1)} collective-permute-done((bf16[112,1152]{1,0:T(8,128)(2,1)S(1)}, bf16[112,1152]{1,0:T(8,128)(2,1)S(1)}, u32[]{:S(2)}, u32[]{:S(2)}) %collective-permute-start.3) | collective-permute-done | bytes 258080 | tf_op jit(solution)/shard_map/tokens/ppermute | solution.py:198
  59.4 2.3 %shard_map.113 = (f32[112,1024]{1,0:T(8,128)S(1)}, f32[112,1024]{1,0:T(8,128)S(1)}) custom-call(s32[16]{0:T(128)S(1)} %copy-done.3, bf16[112,1152]{1,0:T(8,128)(2,1)S(1)} %collective-permute-done.1.refs_2_.refs_0_, bf16[112,1152]{1,0:T(8,128)(2,1)S(1)} %collective-permute-done.3.refs_3_.refs_1_, bf16[1024,384]{1,0:T(8,128)(2,1)S(1)} %bitcast.16, ...), custom_call_target="tpu_custom_call" | custom-call | tf_op jit(solution)/shard_map/pallas_call | solution.py:122
  61.8 6.6 %collective-permute-done.7.refs_3_.came = bf16[384,512]{1,0:T(8,128)(2,1)S(1)} collective-permute-done((bf16[384,512]{1,0:T(8,128)(2,1)S(1)}, bf16[384,512]{1,0:T(8,128)(2,1)S(1)}, u32[]{:S(2)}, u32[]{:S(2)}) %collective-permute-start.7) | collective-permute-done | bytes 393248 | tf_op jit(solution)/shard_map/swap/ppermute | solution.py:198
  68.4 0.0 collective-permute-start.14
  68.4 0.5 collective-permute-start.15
  68.9 1.5 %collective-permute-start.19 = (bf16[384,512]{1,0:T(8,128)(2,1)S(1)}, bf16[384,512]{1,0:T(8,128)(2,1)S(1)}, u32[]{:S(2)}, u32[]{:S(2)}) collective-permute-start(bf16[384,512]{1,0:T(8,128)(2,1)S(1)} %collective-permute-done.7.refs_3_.came), channel_id=1, source_target_pairs={{0,16},{16,0},{1,17},{17,1},{2,18},{18,2},{3,19},{19,3},{4,20},{20... | collective-permute-start | bytes 1179656 | tf_op jit(solution)/shard_map/trade/ppermute | solution.py:202
  70.4 1.2 %shard_map.111.refs_2_.refs_4_ = bf16[448,384]{1,0:T(8,128)(2,1)S(1)} custom-call(bf16[112,1152]{1,0:T(8,128)(2,1)S(1)} %fusion.1.refs_0_, bf16[112,1152]{1,0:T(8,128)(2,1)S(1)} %collective-permute-done.refs_1_, bf16[112,1152]{1,0:T(8,128)(2,1)S(1)} %collective-permute-done.1.refs_2_.refs_0_, bf16[112,1152]{1,0:T(8,128)(2,1)S(1)} %collective-permute-done.3.refs_3_.refs_1_, ...), custom_call_target="tpu_custom_call" | custom-call | tf_op jit(solution)/shard_map/pallas_call | solution.py:122
  71.7 1.2 %shard_map.114.refs_4_.refs_2_ = bf16[448,384]{1,0:T(8,128)(2,1)S(1)} custom-call(bf16[112,1152]{1,0:T(8,128)(2,1)S(1)} %fusion.1.refs_0_, bf16[112,1152]{1,0:T(8,128)(2,1)S(1)} %collective-permute-done.refs_1_, bf16[112,1152]{1,0:T(8,128)(2,1)S(1)} %collective-permute-done.1.refs_2_.refs_0_, bf16[112,1152]{1,0:T(8,128)(2,1)S(1)} %collective-permute-done.3.refs_3_.refs_1_, ...), custom_call_target="tpu_custom_call" | custom-call | tf_op jit(solution)/shard_map/pallas_call | solution.py:122
  72.9 0.9 %shard_map.116 = (bf16[112,512]{1,0:T(8,128)(2,1)S(1)}, bf16[112,512]{1,0:T(8,128)(2,1)S(1)}) custom-call(s32[16]{0:T(128)S(1)} %copy-done.3, bf16[112,1152]{1,0:T(8,128)(2,1)S(1)} %collective-permute-done.1.refs_2_.refs_0_, bf16[112,1152]{1,0:T(8,128)(2,1)S(1)} %collective-permute-done.3.refs_3_.refs_1_, bf16[448,384]{1,0:T(8,128)(2,1)S(1)} %shard_map.111.refs_2_.refs_4_, ...), custom_call_target="tpu_custom_call" | custom-call | tf_op jit(solution)/shard_map/pallas_call | solution.py:122
  73.8 0.1 collective-permute-start.16
  73.9 1.1 %collective-permute-start.17 = (bf16[112,512]{1,0:T(8,128)(2,1)S(1)}, bf16[112,512]{1,0:T(8,128)(2,1)S(1)}, u32[]{:S(2)}, u32[]{:S(2)}) collective-permute-start(bf16[112,512]{1,0:T(8,128)(2,1)S(1)} %get-tuple-element.45), channel_id=1, source_target_pairs={{0,2},{1,3},{2,0},{3,1},{4,6},{5,7},{6,4},{7,5},{8,10},{9,11},{10,... | collective-permute-start | bytes 344072 | tf_op jit(solution)/shard_map/sums/ppermute | solution.py:198
  75.0 0.9 %shard_map.115 = (f32[112,512]{1,0:T(8,128)S(1)}, bf16[112,512]{1,0:T(8,128)(2,1)S(1)}) custom-call(s32[16]{0:T(128)S(1)} %copy-done.3, bf16[112,1152]{1,0:T(8,128)(2,1)S(1)} %fusion.1.refs_0_, bf16[112,1152]{1,0:T(8,128)(2,1)S(1)} %collective-permute-done.refs_1_, bf16[448,384]{1,0:T(8,128)(2,1)S(1)} %shard_map.111.refs_2_.refs_4_, ...), custom_call_target="tpu_custom_call" | custom-call | tf_op jit(solution)/shard_map/pallas_call | solution.py:122
  76.0 0.6 copy-done.4
  76.7 1.4 %shard_map.118 = bf16[1024,384]{1,0:T(8,128)(2,1)} custom-call(s32[16]{0:T(128)S(1)} %copy-done.4, bf16[1024,384]{1,0:T(8,128)(2,1)S(1)} %bitcast.13, bf16[512,384]{1,0:T(8,128)(2,1)S(1)} %collective-permute-done.4.refs_5_.came, bf16[512,384]{1,0:T(8,128)(2,1)S(1)} %collective-permute-done.6.refs_7_.other), custom_call_target="tpu_custom_call" | custom-call | tf_op jit(solution)/shard_map/pallas_call | solution.py:172
  78.1 1.4 %shard_map.117 = bf16[1024,384]{1,0:T(8,128)(2,1)} custom-call(s32[16]{0:T(128)S(1)} %copy-done.4, bf16[1024,384]{1,0:T(8,128)(2,1)S(1)} %bitcast.17, bf16[512,384]{1,0:T(8,128)(2,1)S(1)} %collective-permute-done.2.refs_4_.came, bf16[512,384]{1,0:T(8,128)(2,1)S(1)} %collective-permute-done.5.refs_6_.other), custom_call_target="tpu_custom_call" | custom-call | tf_op jit(solution)/shard_map/pallas_call | solution.py:172
  79.6 0.4 collective-permute-done.19.refs_5_.other
  79.9 1.3 %collective-permute-done.17.refs_2_ = bf16[112,512]{1,0:T(8,128)(2,1)S(1)} collective-permute-done((bf16[112,512]{1,0:T(8,128)(2,1)S(1)}, bf16[112,512]{1,0:T(8,128)(2,1)S(1)}, u32[]{:S(2)}, u32[]{:S(2)}) %collective-permute-start.17) | collective-permute-done | bytes 114720 | tf_op jit(solution)/shard_map/sums/ppermute | solution.py:198
  81.2 0.9 collective-permute-start.18
  82.1 1.0 %shard_map.119 = (f32[112,512]{1,0:T(8,128)S(1)}, f32[112,512]{1,0:T(8,128)S(1)}, f32[112,512]{1,0:T(8,128)S(1)}, f32[112,512]{1,0:T(8,128)S(1)}) custom-call(s32[16]{0:T(128)S(1)} %copy-done.3, bf16[112,1152]{1,0:T(8,128)(2,1)S(1)} %fusion.1.refs_0_, bf16[112,1152]{1,0:T(8,128)(2,1)S(1)} %collective-permute-done.refs_1_, ...), custom_call_target="tpu_custom_call" | custom-call | tf_op jit(solution)/shard_map/pallas_call | solution.py:122
  83.1 0.8 shard_map.121
  83.9 1.4 %collective-permute-start.21 = (bf16[112,512]{1,0:T(8,128)(2,1)S(1)}, bf16[112,512]{1,0:T(8,128)(2,1)S(1)}, u32[]{:S(2)}, u32[]{:S(2)}) collective-permute-start(bf16[112,512]{1,0:T(8,128)(2,1)S(1)} %get-tuple-element.54), channel_id=1, source_target_pairs={{0,6},{1,7},{2,4},{3,5},{4,2},{5,3},{6,0},{7,1},{8,14},{9,15},{10,... | collective-permute-start | bytes 344072 | tf_op jit(solution)/shard_map/sums/ppermute | solution.py:198
  85.3 1.3 %collective-permute-start.22 = (bf16[112,512]{1,0:T(8,128)(2,1)S(1)}, bf16[112,512]{1,0:T(8,128)(2,1)S(1)}, u32[]{:S(2)}, u32[]{:S(2)}) collective-permute-start(bf16[112,512]{1,0:T(8,128)(2,1)S(1)} %get-tuple-element.55), channel_id=1, source_target_pairs={{0,2},{1,3},{2,0},{3,1},{4,6},{5,7},{6,4},{7,5},{8,10},{9,11},{10,... | collective-permute-start | bytes 344072 | tf_op jit(solution)/shard_map/sums/ppermute | solution.py:198
  86.6 0.8 shard_map.120
  87.5 0.9 collective-permute-start.23
  88.4 1.4 %shard_map.123 = bf16[384,1024]{1,0:T(8,128)(2,1)} custom-call(s32[16]{0:T(128)S(1)} %copy-done.4, bf16[384,1024]{1,0:T(8,128)(2,1)S(1)} %bitcast.22, bf16[384,512]{1,0:T(8,128)(2,1)S(1)} %collective-permute-done.7.refs_3_.came, bf16[384,512]{1,0:T(8,128)(2,1)S(1)} %collective-permute-done.19.refs_5_.other), custom_call_target="tpu_custom_call" | custom-call | tf_op jit(solution)/shard_map/pallas_call | solution.py:172
  89.8 0.4 collective-permute-done.21.refs_5_
  90.3 2.3 %collective-permute-done.22.refs_6_ = bf16[112,512]{1,0:T(8,128)(2,1)S(1)} collective-permute-done((bf16[112,512]{1,0:T(8,128)(2,1)S(1)}, bf16[112,512]{1,0:T(8,128)(2,1)S(1)}, u32[]{:S(2)}, u32[]{:S(2)}) %collective-permute-start.22) | collective-permute-done | bytes 114720 | tf_op jit(solution)/shard_map/sums/ppermute | solution.py:198
  92.6 0.8 shard_map.122
  (31 shorter events, 0.1 us)
Async XLA Ops:
  1.5 9.5 %copy-start.2 = (bf16[1,384,1024]{2,1,0:T(8,128)(2,1)S(1)}, bf16[1,384,1024]{2,1,0:T(8,128)(2,1)}, u32[]{:S(2)}) copy-start(bf16[1,384,1024]{2,1,0:T(8,128)(2,1)} %param.13) | copy-start | bytes 2359300
  2.6 11.7 %collective-permute-start = (bf16[112,1152]{1,0:T(8,128)(2,1)S(1)}, bf16[112,1152]{1,0:T(8,128)(2,1)S(1)}, u32[]{:S(2)}, u32[]{:S(2)}) collective-permute-start(bf16[112,1152]{1,0:T(8,128)(2,1)S(1)} %fusion.1.refs_0_), channel_id=1, source_target_pairs={{0,4},{1,5},{2,6},{3,7},{4,0},{5,1},{6,2},{7,3},{8,12},{9,13},{10,... | collective-permute-start | bytes 774152 | tf_op jit(solution)/shard_map/tokens/ppermute | solution.py:198
  5.6 8.6 %collective-permute-start.1 = (bf16[112,1152]{1,0:T(8,128)(2,1)S(1)}, bf16[112,1152]{1,0:T(8,128)(2,1)S(1)}, u32[]{:S(2)}, u32[]{:S(2)}) collective-permute-start(bf16[112,1152]{1,0:T(8,128)(2,1)S(1)} %fusion.1.refs_0_), channel_id=1, source_target_pairs={{0,2},{1,3},{2,0},{3,1},{4,6},{5,7},{6,4},{7,5},{8,10},{9,11},{10,... | collective-permute-start | bytes 774152 | tf_op jit(solution)/shard_map/tokens/ppermute | solution.py:198
  8.3 2.7 %copy-start = (bf16[1,1024,384]{2,1,0:T(8,128)(2,1)S(1)}, bf16[1,1024,384]{2,1,0:T(8,128)(2,1)}, u32[]{:S(2)}) copy-start(bf16[1,1024,384]{2,1,0:T(8,128)(2,1)} %param.12) | copy-start | bytes 2359300
  8.3 19.7 %collective-permute-start.2 = (bf16[512,384]{1,0:T(8,128)(2,1)S(1)}, bf16[512,384]{1,0:T(8,128)(2,1)S(1)}, u32[]{:S(2)}, u32[]{:S(2)}) collective-permute-start(bf16[512,384]{1,0:T(8,128)(2,1)S(1)} %select_bitcast_fusion.1), channel_id=1, source_target_pairs={{0,8},{1,9},{2,10},{3,11},{4,12},{5,13},{6,14},{7,15},{8,0},{9,1},... | collective-permute-start | bytes 1179656 | tf_op jit(solution)/shard_map/swap/ppermute | solution.py:198
  11.0 17.0 %copy-start.1 = (bf16[1,1024,384]{2,1,0:T(8,128)(2,1)S(1)}, bf16[1,1024,384]{2,1,0:T(8,128)(2,1)}, u32[]{:S(2)}) copy-start(bf16[1,1024,384]{2,1,0:T(8,128)(2,1)} %param.11) | copy-start | bytes 2359300
  28.0 22.7 %collective-permute-start.10 = (bf16[384,1024]{1,0:T(8,128)(2,1)S(1)}, bf16[384,1024]{1,0:T(8,128)(2,1)S(1)}, u32[]{:S(2)}, u32[]{:S(2)}) collective-permute-start(bf16[384,1024]{1,0:T(8,128)(2,1)S(1)} %bitcast.19), channel_id=1, source_target_pairs={{0,1},{1,0},{2,3},{3,2},{4,5},{5,4},{6,7},{7,6},{8,9},{9,8},{10,11... | collective-permute-start | bytes 2359304 | tf_op jit(solution)/shard_map/near/ppermute | solution.py:198
  28.1 23.5 %copy-start.3 = (s32[16]{0:T(128)S(1)}, s32[16]{0:T(128)}, u32[]{:S(2)}) copy-start(s32[16]{0:T(128)} %placement.13) | copy-start | bytes 196
  28.1 22.7 %collective-permute-start.8 = (bf16[1024,384]{1,0:T(8,128)(2,1)S(1)}, bf16[1024,384]{1,0:T(8,128)(2,1)S(1)}, u32[]{:S(2)}, u32[]{:S(2)}) collective-permute-start(bf16[1024,384]{1,0:T(8,128)(2,1)S(1)} %bitcast.14), channel_id=1, source_target_pairs={{0,1},{1,0},{2,3},{3,2},{4,5},{5,4},{6,7},{7,6},{8,9},{9,8},{10,11... | collective-permute-start | bytes 2359304 | tf_op jit(solution)/shard_map/near/ppermute | solution.py:198
  28.6 22.8 %collective-permute-start.9 = (bf16[1024,384]{1,0:T(8,128)(2,1)S(1)}, bf16[1024,384]{1,0:T(8,128)(2,1)S(1)}, u32[]{:S(2)}, u32[]{:S(2)}) collective-permute-start(bf16[1024,384]{1,0:T(8,128)(2,1)S(1)} %bitcast.10), channel_id=1, source_target_pairs={{0,1},{1,0},{2,3},{3,2},{4,5},{5,4},{6,7},{7,6},{8,9},{9,8},{10,11... | collective-permute-start | bytes 2359304 | tf_op jit(solution)/shard_map/near/ppermute | solution.py:198
  28.6 20.6 %collective-permute-start.4 = (bf16[512,384]{1,0:T(8,128)(2,1)S(1)}, bf16[512,384]{1,0:T(8,128)(2,1)S(1)}, u32[]{:S(2)}, u32[]{:S(2)}) collective-permute-start(bf16[512,384]{1,0:T(8,128)(2,1)S(1)} %select_bitcast_fusion), channel_id=1, source_target_pairs={{0,8},{1,9},{2,10},{3,11},{4,12},{5,13},{6,14},{7,15},{8,0},{9,1},... | collective-permute-start | bytes 1179656 | tf_op jit(solution)/shard_map/swap/ppermute | solution.py:198
  28.6 20.6 %collective-permute-start.5 = (bf16[512,384]{1,0:T(8,128)(2,1)S(1)}, bf16[512,384]{1,0:T(8,128)(2,1)S(1)}, u32[]{:S(2)}, u32[]{:S(2)}) collective-permute-start(bf16[512,384]{1,0:T(8,128)(2,1)S(1)} %collective-permute-done.2.refs_4_.came), channel_id=1, source_target_pairs={{0,16},{16,0},{1,17},{17,1},{2,18},{18,2},{3,19},{19,3},{4,20},{20... | collective-permute-start | bytes 1179656 | tf_op jit(solution)/shard_map/trade/ppermute | solution.py:202
  49.3 19.1 %collective-permute-start.7 = (bf16[384,512]{1,0:T(8,128)(2,1)S(1)}, bf16[384,512]{1,0:T(8,128)(2,1)S(1)}, u32[]{:S(2)}, u32[]{:S(2)}) collective-permute-start(bf16[384,512]{1,0:T(8,128)(2,1)S(1)} %slice_select_fusion), channel_id=1, source_target_pairs={{0,8},{1,9},{2,10},{3,11},{4,12},{5,13},{6,14},{7,15},{8,0},{9,1},... | collective-permute-start | bytes 1179656 | tf_op jit(solution)/shard_map/swap/ppermute | solution.py:198
  49.3 19.1 %collective-permute-start.6 = (bf16[512,384]{1,0:T(8,128)(2,1)S(1)}, bf16[512,384]{1,0:T(8,128)(2,1)S(1)}, u32[]{:S(2)}, u32[]{:S(2)}) collective-permute-start(bf16[512,384]{1,0:T(8,128)(2,1)S(1)} %collective-permute-done.4.refs_5_.came), channel_id=1, source_target_pairs={{0,16},{16,0},{1,17},{17,1},{2,18},{18,2},{3,19},{19,3},{4,20},{20... | collective-permute-start | bytes 1179656 | tf_op jit(solution)/shard_map/trade/ppermute | solution.py:202
  50.8 18.1 %collective-permute-start.11 = (bf16[512,384]{1,0:T(8,128)(2,1)S(1)}, bf16[512,384]{1,0:T(8,128)(2,1)S(1)}, u32[]{:S(2)}, u32[]{:S(2)}) collective-permute-start(bf16[512,384]{1,0:T(8,128)(2,1)S(1)} %collective-permute-done.2.refs_4_.came), channel_id=1, source_target_pairs={{0,1},{1,0},{2,3},{3,2},{4,5},{5,4},{6,7},{7,6},{8,9},{9,8},{10,11... | collective-permute-start | bytes 1179656 | tf_op jit(solution)/shard_map/z_near/ppermute | solution.py:198
  50.8 8.6 %collective-permute-start.3 = (bf16[112,1152]{1,0:T(8,128)(2,1)S(1)}, bf16[112,1152]{1,0:T(8,128)(2,1)S(1)}, u32[]{:S(2)}, u32[]{:S(2)}) collective-permute-start(bf16[112,1152]{1,0:T(8,128)(2,1)S(1)} %collective-permute-done.refs_1_), channel_id=1, source_target_pairs={{0,2},{1,3},{2,0},{3,1},{4,6},{5,7},{6,4},{7,5},{8,10},{9,11},{10,... | collective-permute-start | bytes 774152 | tf_op jit(solution)/shard_map/tokens/ppermute | solution.py:198
  51.4 20.2 %collective-permute-start.12 = (bf16[512,384]{1,0:T(8,128)(2,1)S(1)}, bf16[512,384]{1,0:T(8,128)(2,1)S(1)}, u32[]{:S(2)}, u32[]{:S(2)}) collective-permute-start(bf16[512,384]{1,0:T(8,128)(2,1)S(1)} %collective-permute-done.4.refs_5_.came), channel_id=1, source_target_pairs={{0,1},{1,0},{2,3},{3,2},{4,5},{5,4},{6,7},{7,6},{8,9},{9,8},{10,11... | collective-permute-start | bytes 1179656 | tf_op jit(solution)/shard_map/z_near/ppermute | solution.py:198
  59.4 12.2 %collective-permute-start.13 = (bf16[512,384]{1,0:T(8,128)(2,1)S(1)}, bf16[512,384]{1,0:T(8,128)(2,1)S(1)}, u32[]{:S(2)}, u32[]{:S(2)}) collective-permute-start(bf16[512,384]{1,0:T(8,128)(2,1)S(1)} %collective-permute-done.5.refs_6_.other), channel_id=1, source_target_pairs={{0,1},{1,0},{2,3},{3,2},{4,5},{5,4},{6,7},{7,6},{8,9},{9,8},{10,11... | collective-permute-start | bytes 1179656 | tf_op jit(solution)/shard_map/y_near/ppermute | solution.py:198
  68.4 3.3 %collective-permute-start.14 = (bf16[512,384]{1,0:T(8,128)(2,1)S(1)}, bf16[512,384]{1,0:T(8,128)(2,1)S(1)}, u32[]{:S(2)}, u32[]{:S(2)}) collective-permute-start(bf16[512,384]{1,0:T(8,128)(2,1)S(1)} %collective-permute-done.6.refs_7_.other), channel_id=1, source_target_pairs={{0,1},{1,0},{2,3},{3,2},{4,5},{5,4},{6,7},{7,6},{8,9},{9,8},{10,11... | collective-permute-start | bytes 1179656 | tf_op jit(solution)/shard_map/y_near/ppermute | solution.py:198
  68.4 4.5 %collective-permute-start.15 = (bf16[384,512]{1,0:T(8,128)(2,1)S(1)}, bf16[384,512]{1,0:T(8,128)(2,1)S(1)}, u32[]{:S(2)}, u32[]{:S(2)}) collective-permute-start(bf16[384,512]{1,0:T(8,128)(2,1)S(1)} %collective-permute-done.7.refs_3_.came), channel_id=1, source_target_pairs={{0,1},{1,0},{2,3},{3,2},{4,5},{5,4},{6,7},{7,6},{8,9},{9,8},{10,11... | collective-permute-start | bytes 1179656 | tf_op jit(solution)/shard_map/z_near/ppermute | solution.py:198
  68.9 11.0 %collective-permute-start.19 = (bf16[384,512]{1,0:T(8,128)(2,1)S(1)}, bf16[384,512]{1,0:T(8,128)(2,1)S(1)}, u32[]{:S(2)}, u32[]{:S(2)}) collective-permute-start(bf16[384,512]{1,0:T(8,128)(2,1)S(1)} %collective-permute-done.7.refs_3_.came), channel_id=1, source_target_pairs={{0,16},{16,0},{1,17},{17,1},{2,18},{18,2},{3,19},{19,3},{4,20},{20... | collective-permute-start | bytes 1179656 | tf_op jit(solution)/shard_map/trade/ppermute | solution.py:202
  73.8 6.1 %collective-permute-start.16 = (bf16[112,512]{1,0:T(8,128)(2,1)S(1)}, bf16[112,512]{1,0:T(8,128)(2,1)S(1)}, u32[]{:S(2)}, u32[]{:S(2)}) collective-permute-start(bf16[112,512]{1,0:T(8,128)(2,1)S(1)} %get-tuple-element.44), channel_id=1, source_target_pairs={{0,6},{1,7},{2,4},{3,5},{4,2},{5,3},{6,0},{7,1},{8,14},{9,15},{10,... | collective-permute-start | bytes 344072 | tf_op jit(solution)/shard_map/sums/ppermute | solution.py:198
  73.9 7.3 %collective-permute-start.17 = (bf16[112,512]{1,0:T(8,128)(2,1)S(1)}, bf16[112,512]{1,0:T(8,128)(2,1)S(1)}, u32[]{:S(2)}, u32[]{:S(2)}) collective-permute-start(bf16[112,512]{1,0:T(8,128)(2,1)S(1)} %get-tuple-element.45), channel_id=1, source_target_pairs={{0,2},{1,3},{2,0},{3,1},{4,6},{5,7},{6,4},{7,5},{8,10},{9,11},{10,... | collective-permute-start | bytes 344072 | tf_op jit(solution)/shard_map/sums/ppermute | solution.py:198
  76.0 0.7 copy-start.4
  81.2 1.8 %collective-permute-start.20 = (bf16[384,512]{1,0:T(8,128)(2,1)S(1)}, bf16[384,512]{1,0:T(8,128)(2,1)S(1)}, u32[]{:S(2)}, u32[]{:S(2)}) collective-permute-start(bf16[384,512]{1,0:T(8,128)(2,1)S(1)} %collective-permute-done.19.refs_5_.other), channel_id=1, source_target_pairs={{0,1},{1,0},{2,3},{3,2},{4,5},{5,4},{6,7},{7,6},{8,9},{9,8},{10,11... | collective-permute-start | bytes 1179656 | tf_op jit(solution)/shard_map/y_near/ppermute | solution.py:198
  81.2 8.6 %collective-permute-start.18 = (bf16[112,512]{1,0:T(8,128)(2,1)S(1)}, bf16[112,512]{1,0:T(8,128)(2,1)S(1)}, u32[]{:S(2)}, u32[]{:S(2)}) collective-permute-start(bf16[112,512]{1,0:T(8,128)(2,1)S(1)} %get-tuple-element.46), channel_id=1, source_target_pairs={{0,4},{1,5},{2,6},{3,7},{4,0},{5,1},{6,2},{7,3},{8,12},{9,13},{10,... | collective-permute-start | bytes 344072 | tf_op jit(solution)/shard_map/sums/ppermute | solution.py:198
  83.9 6.3 %collective-permute-start.21 = (bf16[112,512]{1,0:T(8,128)(2,1)S(1)}, bf16[112,512]{1,0:T(8,128)(2,1)S(1)}, u32[]{:S(2)}, u32[]{:S(2)}) collective-permute-start(bf16[112,512]{1,0:T(8,128)(2,1)S(1)} %get-tuple-element.54), channel_id=1, source_target_pairs={{0,6},{1,7},{2,4},{3,5},{4,2},{5,3},{6,0},{7,1},{8,14},{9,15},{10,... | collective-permute-start | bytes 344072 | tf_op jit(solution)/shard_map/sums/ppermute | solution.py:198
  85.3 7.2 %collective-permute-start.22 = (bf16[112,512]{1,0:T(8,128)(2,1)S(1)}, bf16[112,512]{1,0:T(8,128)(2,1)S(1)}, u32[]{:S(2)}, u32[]{:S(2)}) collective-permute-start(bf16[112,512]{1,0:T(8,128)(2,1)S(1)} %get-tuple-element.55), channel_id=1, source_target_pairs={{0,2},{1,3},{2,0},{3,1},{4,6},{5,7},{6,4},{7,5},{8,10},{9,11},{10,... | collective-permute-start | bytes 344072 | tf_op jit(solution)/shard_map/sums/ppermute | solution.py:198
  87.5 5.1 %collective-permute-start.23 = (bf16[112,512]{1,0:T(8,128)(2,1)S(1)}, bf16[112,512]{1,0:T(8,128)(2,1)S(1)}, u32[]{:S(2)}, u32[]{:S(2)}) collective-permute-start(bf16[112,512]{1,0:T(8,128)(2,1)S(1)} %get-tuple-element.56), channel_id=1, source_target_pairs={{0,4},{1,5},{2,6},{3,7},{4,0},{5,1},{6,2},{7,3},{8,12},{9,13},{10,... | collective-permute-start | bytes 344072 | tf_op jit(solution)/shard_map/sums/ppermute | solution.py:198

commit v9 on v5

--- a/solution.py
+++ b/solution.py
@@ -280,7 +280,7 @@
         store(0, depth, flags, own[1], z_upper, y_upper),
     ]
     ours = collect(parts)
-    landed = after(y_lower, stored, ours[1:-1])
+    landed = after(y_lower, stored, ours[1 : len(ours) // 2])
     y_near.append(send(landed, 1, "y_near"))
     everyone = tuple(range(len(rows)))
     last_sums = far_sums((0,), [landed], 1, everyone, near_sums, False)

time: 86.6 us -> 86.6 us (level)
    ppermute x18, waiting for transfers between devices: 47.5 us -> 46.4 us  [send(): return lax.ppermute(value, 'expert', [(d, d ^ bit) for d in range(count)])]
  transfers between devices with their start and end apart: 20 -> 20, of which waited for: 9 -> 8; matrix products, arithmetic and copies ran while one was open for 0% -> 0% of each run, Pallas kernels for 18% -> 18%
where the time goes in v9:
time: 86.6 us; the launch traced here: 86.4 us
  waiting for transfers between devices  48.1 us (56%)
  starting transfers between devices  18.7 us (22%)
  Pallas kernels  16.7 us (19%)
  local copies, waits for them, and re-layouts  1.68 us (2%)
  between operations  0.96 us (1%)
    ppermute x18, waiting for transfers between devices, send(): return lax.ppermute(value, 'expert', [(d, d ^ bit) for d in range(count)])  46.4 us
    ppermute x18, starting transfers between devices, send(): return lax.ppermute(value, 'expert', [(d, d ^ bit) for d in range(count)])  16.4 us
    pallas_call x10, Pallas kernels, call(): pl.pallas_call(kernel, out_shape=out_shape, in_specs=[smem] * scalars + [...  12.4 us
    pallas_call x3, Pallas kernels, store(): pl.pallas_call(functools.partial(store_kernel, axis, first), out_shape=ja...  4.35 us
    ppermute x2, starting transfers between devices, trade(): return lax.ppermute(value, 'dp', trades)  2.32 us
  transfers between devices with their start and end apart: 20, of which 8 were waited for; matrix products, arithmetic and copies ran while one was open for 0% of the time, Pallas kernels for 18%

profile of v9, /device:TPU:0, one launch (start us, length us, event | category | flops | bytes accessed | tf_op | source)
XLA Modules:
  0.0 86.4 jit_solution(13487010130374715140)
XLA Ops:
  0.6 1.5 %slice_bitcast_fusion = (bf16[512,384]{1,0:T(8,128)(2,1)S(1)}, bf16[512,384]{1,0:T(8,128)(2,1)S(1)}, bf16[512,384]{1,0:T(8,128)(2,1)S(1)}, bf16[512,384]{1,0:T(8,128)(2,1)S(1)}) fusion(bf16[1,1024,384]{2,1,0:T(8,128)(2,1)} %param.12, bf16[1,1024,384]{2,1,0:T(8,128)(2,1)} %param.11), kind=kLoop, calls=%fused_computation.4 | loop fusion | bytes 3145728 | tf_op jit(solution)/shard_map/slice | solution.py:211
  2.2 0.0 copy-start.6
  2.2 0.0 copy-start.7
  2.2 0.0 copy-start.5
  2.2 0.0 copy-start
  2.2 0.2 maximum_select_fusion
  2.4 4.1 %collective-permute-start.3 = (bf16[1024,384]{1,0:T(8,128)(2,1)S(1)}, bf16[1024,384]{1,0:T(8,128)(2,1)S(1)}, u32[]{:S(2)}, u32[]{:S(2)}) collective-permute-start(bf16[1024,384]{1,0:T(8,128)(2,1)S(1)} %maximum_select_fusion), channel_id=1, source_target_pairs={{0,8},{1,9},{2,10},{3,11},{4,12},{5,13},{6,14},{7,15},{8,0},{9,1},... | collective-permute-start | bytes 2359304 | tf_op jit(solution)/shard_map/swap/ppermute | solution.py:198
  6.6 0.1 copy.17
  6.7 0.0 copy-start.2
  6.7 0.0 copy-start.1
  6.7 0.0 copy-start.3
  6.8 1.6 %collective-permute-start = (bf16[112,1152]{1,0:T(8,128)(2,1)S(1)}, bf16[112,1152]{1,0:T(8,128)(2,1)S(1)}, u32[]{:S(2)}, u32[]{:S(2)}) collective-permute-start(bf16[112,1152]{1,0:T(8,128)(2,1)S(1)} %fusion.1.refs_0_), channel_id=1, source_target_pairs={{0,4},{1,5},{2,6},{3,7},{4,0},{5,1},{6,2},{7,3},{8,12},{9,13},{10,... | collective-permute-start | bytes 774152 | tf_op jit(solution)/shard_map/tokens/ppermute | solution.py:198
  8.4 1.5 %collective-permute-start.1 = (bf16[112,1152]{1,0:T(8,128)(2,1)S(1)}, bf16[112,1152]{1,0:T(8,128)(2,1)S(1)}, u32[]{:S(2)}, u32[]{:S(2)}) collective-permute-start(bf16[112,1152]{1,0:T(8,128)(2,1)S(1)} %fusion.1.refs_0_), channel_id=1, source_target_pairs={{0,2},{1,3},{2,0},{3,1},{4,6},{5,7},{6,4},{7,5},{8,10},{9,11},{10,... | collective-permute-start | bytes 774152 | tf_op jit(solution)/shard_map/tokens/ppermute | solution.py:198
  9.9 19.0 %collective-permute-done.refs_1_ = bf16[112,1152]{1,0:T(8,128)(2,1)S(1)} collective-permute-done((bf16[112,1152]{1,0:T(8,128)(2,1)S(1)}, bf16[112,1152]{1,0:T(8,128)(2,1)S(1)}, u32[]{:S(2)}, u32[]{:S(2)}) %collective-permute-start) | collective-permute-done | bytes 258080 | tf_op jit(solution)/shard_map/tokens/ppermute | solution.py:198
  28.9 1.5 %collective-permute-start.2 = (bf16[112,1152]{1,0:T(8,128)(2,1)S(1)}, bf16[112,1152]{1,0:T(8,128)(2,1)S(1)}, u32[]{:S(2)}, u32[]{:S(2)}) collective-permute-start(bf16[112,1152]{1,0:T(8,128)(2,1)S(1)} %collective-permute-done.refs_1_), channel_id=1, source_target_pairs={{0,2},{1,3},{2,0},{3,1},{4,6},{5,7},{6,4},{7,5},{8,10},{9,11},{10,... | collective-permute-start | bytes 774152 | tf_op jit(solution)/shard_map/tokens/ppermute | solution.py:198
  30.4 0.1 collective-permute-start.8
  30.5 0.5 collective-permute-start.6
  31.0 0.1 collective-permute-start.7
  31.1 4.9 %collective-permute-done.2.refs_3_.refs_1_ = bf16[112,1152]{1,0:T(8,128)(2,1)S(1)} collective-permute-done((bf16[112,1152]{1,0:T(8,128)(2,1)S(1)}, bf16[112,1152]{1,0:T(8,128)(2,1)S(1)}, u32[]{:S(2)}, u32[]{:S(2)}) %collective-permute-start.2) | collective-permute-done | bytes 258080 | tf_op jit(solution)/shard_map/tokens/ppermute | solution.py:198
  36.0 4.9 %collective-permute-done.3.refs_4_.came = bf16[1024,384]{1,0:T(8,128)(2,1)S(1)} collective-permute-done((bf16[1024,384]{1,0:T(8,128)(2,1)S(1)}, bf16[1024,384]{1,0:T(8,128)(2,1)S(1)}, u32[]{:S(2)}, u32[]{:S(2)}) %collective-permute-start.3) | collective-permute-done | bytes 786464 | tf_op jit(solution)/shard_map/swap/ppermute | solution.py:198
  40.9 1.6 %collective-permute-start.4 = (bf16[1024,384]{1,0:T(8,128)(2,1)S(1)}, bf16[1024,384]{1,0:T(8,128)(2,1)S(1)}, u32[]{:S(2)}, u32[]{:S(2)}) collective-permute-start(bf16[1024,384]{1,0:T(8,128)(2,1)S(1)} %collective-permute-done.3.refs_4_.came), channel_id=1, source_target_pairs={{0,16},{16,0},{1,17},{17,1},{2,18},{18,2},{3,19},{19,3},{4,20},{20... | collective-permute-start | bytes 2359304 | tf_op jit(solution)/shard_map/trade/ppermute | solution.py:202
  42.5 2.3 %shard_map.113 = (f32[112,1024]{1,0:T(8,128)S(1)}, f32[112,1024]{1,0:T(8,128)S(1)}) custom-call(s32[16]{0:T(128)S(1)} %copy-done.3, bf16[112,1152]{1,0:T(8,128)(2,1)S(1)} %collective-permute-done.1.refs_2_.refs_0_, bf16[112,1152]{1,0:T(8,128)(2,1)S(1)} %collective-permute-done.2.refs_3_.refs_1_, bf16[1024,384]{1,0:T(8,128)(2,1)S(1)} %bitcast.24, ...), custom_call_target="tpu_custom_call" | custom-call | tf_op jit(solution)/shard_map/pallas_call | solution.py:122
  44.9 2.3 %shard_map.112 = (f32[112,1024]{1,0:T(8,128)S(1)}, f32[112,1024]{1,0:T(8,128)S(1)}) custom-call(s32[16]{0:T(128)S(1)} %copy-done.3, bf16[112,1152]{1,0:T(8,128)(2,1)S(1)} %fusion.1.refs_0_, bf16[112,1152]{1,0:T(8,128)(2,1)S(1)} %collective-permute-done.refs_1_, bf16[1024,384]{1,0:T(8,128)(2,1)S(1)} %bitcast.25, bf16[1024,384]{1,0:T(8,128)(2,1)S(1)} %bitcast.21, ...), custom_call_target="tpu_custom_call" | custom-call | tf_op jit(solution)/shard_map/pallas_call | solution.py:122
  47.2 0.1 collective-permute-start.9
  47.3 14.3 %collective-permute-done.5.refs_3_.came = bf16[384,512]{1,0:T(8,128)(2,1)S(1)} collective-permute-done((bf16[384,512]{1,0:T(8,128)(2,1)S(1)}, bf16[384,512]{1,0:T(8,128)(2,1)S(1)}, u32[]{:S(2)}, u32[]{:S(2)}) %collective-permute-start.5) | collective-permute-done | bytes 393248 | tf_op jit(solution)/shard_map/swap/ppermute | solution.py:198
  61.5 0.5 collective-permute-start.11
  62.1 0.8 collective-permute-start.15
  62.8 1.2 %shard_map.111.refs_2_.refs_4_ = bf16[448,384]{1,0:T(8,128)(2,1)S(1)} custom-call(bf16[112,1152]{1,0:T(8,128)(2,1)S(1)} %fusion.1.refs_0_, bf16[112,1152]{1,0:T(8,128)(2,1)S(1)} %collective-permute-done.refs_1_, bf16[112,1152]{1,0:T(8,128)(2,1)S(1)} %collective-permute-done.1.refs_2_.refs_0_, bf16[112,1152]{1,0:T(8,128)(2,1)S(1)} %collective-permute-done.2.refs_3_.refs_1_, ...), custom_call_target="tpu_custom_call" | custom-call | tf_op jit(solution)/shard_map/pallas_call | solution.py:122
  64.0 1.2 %shard_map.114.refs_4_.refs_2_ = bf16[448,384]{1,0:T(8,128)(2,1)S(1)} custom-call(bf16[112,1152]{1,0:T(8,128)(2,1)S(1)} %fusion.1.refs_0_, bf16[112,1152]{1,0:T(8,128)(2,1)S(1)} %collective-permute-done.refs_1_, bf16[112,1152]{1,0:T(8,128)(2,1)S(1)} %collective-permute-done.1.refs_2_.refs_0_, bf16[112,1152]{1,0:T(8,128)(2,1)S(1)} %collective-permute-done.2.refs_3_.refs_1_, ...), custom_call_target="tpu_custom_call" | custom-call | tf_op jit(solution)/shard_map/pallas_call | solution.py:122
  65.2 1.0 %shard_map.116 = (bf16[112,512]{1,0:T(8,128)(2,1)S(1)}, bf16[112,512]{1,0:T(8,128)(2,1)S(1)}) custom-call(s32[16]{0:T(128)S(1)} %copy-done.3, bf16[112,1152]{1,0:T(8,128)(2,1)S(1)} %collective-permute-done.1.refs_2_.refs_0_, bf16[112,1152]{1,0:T(8,128)(2,1)S(1)} %collective-permute-done.2.refs_3_.refs_1_, bf16[448,384]{1,0:T(8,128)(2,1)S(1)} %shard_map.111.refs_2_.refs_4_, ...), custom_call_target="tpu_custom_call" | custom-call | tf_op jit(solution)/shard_map/pallas_call | solution.py:122
  66.2 0.0 copy-start.4
  66.2 1.3 %collective-permute-start.12 = (bf16[112,512]{1,0:T(8,128)(2,1)S(1)}, bf16[112,512]{1,0:T(8,128)(2,1)S(1)}, u32[]{:S(2)}, u32[]{:S(2)}) collective-permute-start(bf16[112,512]{1,0:T(8,128)(2,1)S(1)} %get-tuple-element.42), channel_id=1, source_target_pairs={{0,6},{1,7},{2,4},{3,5},{4,2},{5,3},{6,0},{7,1},{8,14},{9,15},{10,... | collective-permute-start | bytes 344072 | tf_op jit(solution)/shard_map/sums/ppermute | solution.py:198
  67.5 0.9 %shard_map.115 = (f32[112,512]{1,0:T(8,128)S(1)}, bf16[112,512]{1,0:T(8,128)(2,1)S(1)}) custom-call(s32[16]{0:T(128)S(1)} %copy-done.3, bf16[112,1152]{1,0:T(8,128)(2,1)S(1)} %fusion.1.refs_0_, bf16[112,1152]{1,0:T(8,128)(2,1)S(1)} %collective-permute-done.refs_1_, bf16[448,384]{1,0:T(8,128)(2,1)S(1)} %shard_map.111.refs_2_.refs_4_, ...), custom_call_target="tpu_custom_call" | custom-call | tf_op jit(solution)/shard_map/pallas_call | solution.py:122
  68.5 1.4 %shard_map.118 = bf16[1024,384]{1,0:T(8,128)(2,1)} custom-call(s32[16]{0:T(128)S(1)} %copy-done.4, bf16[1024,384]{1,0:T(8,128)(2,1)S(1)} %bitcast.22, bf16[1024,384]{1,0:T(8,128)(2,1)S(1)} %collective-permute-done.3.refs_4_.came, bf16[1024,384]{1,0:T(8,128)(2,1)S(1)} %collective-permute-done.4.refs_5_.other), custom_call_target="tpu_custom_call" | custom-call | tf_op jit(solution)/shard_map/pallas_call | solution.py:172
  70.0 1.4 %shard_map.117 = bf16[1024,384]{1,0:T(8,128)(2,1)} custom-call(s32[16]{0:T(128)S(1)} %copy-done.4, bf16[1024,384]{1,0:T(8,128)(2,1)S(1)} %bitcast.26, bf16[1024,384]{1,0:T(8,128)(2,1)S(1)} %collective-permute-done.3.refs_4_.came, bf16[1024,384]{1,0:T(8,128)(2,1)S(1)} %collective-permute-done.4.refs_5_.other), custom_call_target="tpu_custom_call" | custom-call | tf_op jit(solution)/shard_map/pallas_call | solution.py:172
  71.4 1.7 %collective-permute-done.15.refs_5_.other = bf16[384,512]{1,0:T(8,128)(2,1)S(1)} collective-permute-done((bf16[384,512]{1,0:T(8,128)(2,1)S(1)}, bf16[384,512]{1,0:T(8,128)(2,1)S(1)}, u32[]{:S(2)}, u32[]{:S(2)}) %collective-permute-start.15) | collective-permute-done | bytes 393248 | tf_op jit(solution)/shard_map/trade/ppermute | solution.py:202
  73.1 1.5 %collective-permute-start.13 = (bf16[112,512]{1,0:T(8,128)(2,1)S(1)}, bf16[112,512]{1,0:T(8,128)(2,1)S(1)}, u32[]{:S(2)}, u32[]{:S(2)}) collective-permute-start(bf16[112,512]{1,0:T(8,128)(2,1)S(1)} %get-tuple-element.43), channel_id=1, source_target_pairs={{0,2},{1,3},{2,0},{3,1},{4,6},{5,7},{6,4},{7,5},{8,10},{9,11},{10,... | collective-permute-start | bytes 344072 | tf_op jit(solution)/shard_map/sums/ppermute | solution.py:198
  74.6 1.0 %shard_map.119 = (f32[112,512]{1,0:T(8,128)S(1)}, f32[112,512]{1,0:T(8,128)S(1)}, f32[112,512]{1,0:T(8,128)S(1)}, f32[112,512]{1,0:T(8,128)S(1)}) custom-call(s32[16]{0:T(128)S(1)} %copy-done.3, bf16[112,1152]{1,0:T(8,128)(2,1)S(1)} %fusion.1.refs_0_, bf16[112,1152]{1,0:T(8,128)(2,1)S(1)} %collective-permute-done.refs_1_, ...), custom_call_target="tpu_custom_call" | custom-call | tf_op jit(solution)/shard_map/pallas_call | solution.py:122
  75.6 0.8 shard_map.121
  76.4 2.1 %collective-permute-start.17 = (bf16[112,512]{1,0:T(8,128)(2,1)S(1)}, bf16[112,512]{1,0:T(8,128)(2,1)S(1)}, u32[]{:S(2)}, u32[]{:S(2)}) collective-permute-start(bf16[112,512]{1,0:T(8,128)(2,1)S(1)} %get-tuple-element.52), channel_id=1, source_target_pairs={{0,6},{1,7},{2,4},{3,5},{4,2},{5,3},{6,0},{7,1},{8,14},{9,15},{10,... | collective-permute-start | bytes 344072 | tf_op jit(solution)/shard_map/sums/ppermute | solution.py:198
  78.5 1.5 %collective-permute-start.18 = (bf16[112,512]{1,0:T(8,128)(2,1)S(1)}, bf16[112,512]{1,0:T(8,128)(2,1)S(1)}, u32[]{:S(2)}, u32[]{:S(2)}) collective-permute-start(bf16[112,512]{1,0:T(8,128)(2,1)S(1)} %get-tuple-element.53), channel_id=1, source_target_pairs={{0,2},{1,3},{2,0},{3,1},{4,6},{5,7},{6,4},{7,5},{8,10},{9,11},{10,... | collective-permute-start | bytes 344072 | tf_op jit(solution)/shard_map/sums/ppermute | solution.py:198
  79.9 0.8 shard_map.120
  80.8 0.1 collective-permute-start.19
  80.9 1.4 %shard_map.123 = bf16[384,1024]{1,0:T(8,128)(2,1)} custom-call(s32[16]{0:T(128)S(1)} %copy-done.4, bf16[384,1024]{1,0:T(8,128)(2,1)S(1)} %bitcast.18, bf16[384,512]{1,0:T(8,128)(2,1)S(1)} %collective-permute-done.5.refs_3_.came, bf16[384,512]{1,0:T(8,128)(2,1)S(1)} %collective-permute-done.15.refs_5_.other), custom_call_target="tpu_custom_call" | custom-call | tf_op jit(solution)/shard_map/pallas_call | solution.py:172
  82.3 0.4 collective-permute-done.17.refs_5_
  82.7 2.4 %collective-permute-done.18.refs_6_ = bf16[112,512]{1,0:T(8,128)(2,1)S(1)} collective-permute-done((bf16[112,512]{1,0:T(8,128)(2,1)S(1)}, bf16[112,512]{1,0:T(8,128)(2,1)S(1)}, u32[]{:S(2)}, u32[]{:S(2)}) %collective-permute-start.18) | collective-permute-done | bytes 114720 | tf_op jit(solution)/shard_map/sums/ppermute | solution.py:198
  85.1 0.5 collective-permute-done.19.refs_7_
  85.6 0.8 shard_map.122
  (29 shorter events, 0.2 us)
Async XLA Ops:
  2.2 4.4 %copy-start.6 = (f32[112,8]{0,1:T(8,128)S(1)}, f32[112,8]{0,1:T(8,128)}, u32[]{:S(2)}) copy-start(f32[112,8]{0,1:T(8,128)} %param.10) | copy-start | bytes 10756
  2.2 4.4 %copy-start.7 = (s32[112,8]{0,1:T(8,128)S(1)}, s32[112,8]{0,1:T(8,128)}, u32[]{:S(2)}) copy-start(s32[112,8]{0,1:T(8,128)} %param.9) | copy-start | bytes 10756
  2.2 4.5 %copy-start.5 = (bf16[112,1024]{1,0:T(8,128)(2,1)S(1)}, bf16[112,1024]{1,0:T(8,128)(2,1)}, u32[]{:S(2)}) copy-start(bf16[112,1024]{1,0:T(8,128)(2,1)} %param.8) | copy-start | bytes 688132
  2.2 28.2 %copy-start = (bf16[1,384,1024]{2,1,0:T(8,128)(2,1)S(1)}, bf16[1,384,1024]{2,1,0:T(8,128)(2,1)}, u32[]{:S(2)}) copy-start(bf16[1,384,1024]{2,1,0:T(8,128)(2,1)} %param.13) | copy-start | bytes 2359300
  2.4 38.5 %collective-permute-start.3 = (bf16[1024,384]{1,0:T(8,128)(2,1)S(1)}, bf16[1024,384]{1,0:T(8,128)(2,1)S(1)}, u32[]{:S(2)}, u32[]{:S(2)}) collective-permute-start(bf16[1024,384]{1,0:T(8,128)(2,1)S(1)} %maximum_select_fusion), channel_id=1, source_target_pairs={{0,8},{1,9},{2,10},{3,11},{4,12},{5,13},{6,14},{7,15},{8,0},{9,1},... | collective-permute-start | bytes 2359304 | tf_op jit(solution)/shard_map/swap/ppermute | solution.py:198
  6.7 23.8 %copy-start.2 = (bf16[1,1024,384]{2,1,0:T(8,128)(2,1)S(1)}, bf16[1,1024,384]{2,1,0:T(8,128)(2,1)}, u32[]{:S(2)}) copy-start(bf16[1,1024,384]{2,1,0:T(8,128)(2,1)} %param.11) | copy-start | bytes 2359300
  6.7 24.3 %copy-start.1 = (bf16[1,1024,384]{2,1,0:T(8,128)(2,1)S(1)}, bf16[1,1024,384]{2,1,0:T(8,128)(2,1)}, u32[]{:S(2)}) copy-start(bf16[1,1024,384]{2,1,0:T(8,128)(2,1)} %param.12) | copy-start | bytes 2359300
  6.7 35.8 %copy-start.3 = (s32[16]{0:T(128)S(1)}, s32[16]{0:T(128)}, u32[]{:S(2)}) copy-start(s32[16]{0:T(128)} %placement.13) | copy-start | bytes 196
  6.8 22.1 %collective-permute-start = (bf16[112,1152]{1,0:T(8,128)(2,1)S(1)}, bf16[112,1152]{1,0:T(8,128)(2,1)S(1)}, u32[]{:S(2)}, u32[]{:S(2)}) collective-permute-start(bf16[112,1152]{1,0:T(8,128)(2,1)S(1)} %fusion.1.refs_0_), channel_id=1, source_target_pairs={{0,4},{1,5},{2,6},{3,7},{4,0},{5,1},{6,2},{7,3},{8,12},{9,13},{10,... | collective-permute-start | bytes 774152 | tf_op jit(solution)/shard_map/tokens/ppermute | solution.py:198
  8.4 22.6 %collective-permute-start.1 = (bf16[112,1152]{1,0:T(8,128)(2,1)S(1)}, bf16[112,1152]{1,0:T(8,128)(2,1)S(1)}, u32[]{:S(2)}, u32[]{:S(2)}) collective-permute-start(bf16[112,1152]{1,0:T(8,128)(2,1)S(1)} %fusion.1.refs_0_), channel_id=1, source_target_pairs={{0,2},{1,3},{2,0},{3,1},{4,6},{5,7},{6,4},{7,5},{8,10},{9,11},{10,... | collective-permute-start | bytes 774152 | tf_op jit(solution)/shard_map/tokens/ppermute | solution.py:198
  28.9 7.1 %collective-permute-start.2 = (bf16[112,1152]{1,0:T(8,128)(2,1)S(1)}, bf16[112,1152]{1,0:T(8,128)(2,1)S(1)}, u32[]{:S(2)}, u32[]{:S(2)}) collective-permute-start(bf16[112,1152]{1,0:T(8,128)(2,1)S(1)} %collective-permute-done.refs_1_), channel_id=1, source_target_pairs={{0,2},{1,3},{2,0},{3,1},{4,6},{5,7},{6,4},{7,5},{8,10},{9,11},{10,... | collective-permute-start | bytes 774152 | tf_op jit(solution)/shard_map/tokens/ppermute | solution.py:198
  30.4 12.1 %collective-permute-start.8 = (bf16[384,1024]{1,0:T(8,128)(2,1)S(1)}, bf16[384,1024]{1,0:T(8,128)(2,1)S(1)}, u32[]{:S(2)}, u32[]{:S(2)}) collective-permute-start(bf16[384,1024]{1,0:T(8,128)(2,1)S(1)} %bitcast.15), channel_id=1, source_target_pairs={{0,1},{1,0},{2,3},{3,2},{4,5},{5,4},{6,7},{7,6},{8,9},{9,8},{10,11... | collective-permute-start | bytes 2359304 | tf_op jit(solution)/shard_map/near/ppermute | solution.py:198
  30.5 12.0 %collective-permute-start.6 = (bf16[1024,384]{1,0:T(8,128)(2,1)S(1)}, bf16[1024,384]{1,0:T(8,128)(2,1)S(1)}, u32[]{:S(2)}, u32[]{:S(2)}) collective-permute-start(bf16[1024,384]{1,0:T(8,128)(2,1)S(1)} %bitcast.23), channel_id=1, source_target_pairs={{0,1},{1,0},{2,3},{3,2},{4,5},{5,4},{6,7},{7,6},{8,9},{9,8},{10,11... | collective-permute-start | bytes 2359304 | tf_op jit(solution)/shard_map/near/ppermute | solution.py:198
  31.0 11.5 %collective-permute-start.7 = (bf16[1024,384]{1,0:T(8,128)(2,1)S(1)}, bf16[1024,384]{1,0:T(8,128)(2,1)S(1)}, u32[]{:S(2)}, u32[]{:S(2)}) collective-permute-start(bf16[1024,384]{1,0:T(8,128)(2,1)S(1)} %bitcast.19), channel_id=1, source_target_pairs={{0,1},{1,0},{2,3},{3,2},{4,5},{5,4},{6,7},{7,6},{8,9},{9,8},{10,11... | collective-permute-start | bytes 2359304 | tf_op jit(solution)/shard_map/near/ppermute | solution.py:198
  40.9 20.6 %collective-permute-start.4 = (bf16[1024,384]{1,0:T(8,128)(2,1)S(1)}, bf16[1024,384]{1,0:T(8,128)(2,1)S(1)}, u32[]{:S(2)}, u32[]{:S(2)}) collective-permute-start(bf16[1024,384]{1,0:T(8,128)(2,1)S(1)} %collective-permute-done.3.refs_4_.came), channel_id=1, source_target_pairs={{0,16},{16,0},{1,17},{17,1},{2,18},{18,2},{3,19},{19,3},{4,20},{20... | collective-permute-start | bytes 2359304 | tf_op jit(solution)/shard_map/trade/ppermute | solution.py:202
  42.5 19.1 %collective-permute-start.5 = (bf16[384,512]{1,0:T(8,128)(2,1)S(1)}, bf16[384,512]{1,0:T(8,128)(2,1)S(1)}, u32[]{:S(2)}, u32[]{:S(2)}) collective-permute-start(bf16[384,512]{1,0:T(8,128)(2,1)S(1)} %slice_select_fusion), channel_id=1, source_target_pairs={{0,8},{1,9},{2,10},{3,11},{4,12},{5,13},{6,14},{7,15},{8,0},{9,1},... | collective-permute-start | bytes 1179656 | tf_op jit(solution)/shard_map/swap/ppermute | solution.py:198
  47.2 16.8 %collective-permute-start.9 = (bf16[1024,384]{1,0:T(8,128)(2,1)S(1)}, bf16[1024,384]{1,0:T(8,128)(2,1)S(1)}, u32[]{:S(2)}, u32[]{:S(2)}) collective-permute-start(bf16[1024,384]{1,0:T(8,128)(2,1)S(1)} %collective-permute-done.3.refs_4_.came), channel_id=1, source_target_pairs={{0,1},{1,0},{2,3},{3,2},{4,5},{5,4},{6,7},{7,6},{8,9},{9,8},{10,11... | collective-permute-start | bytes 2359304 | tf_op jit(solution)/shard_map/z_near/ppermute | solution.py:198
  61.5 2.5 %collective-permute-start.10 = (bf16[1024,384]{1,0:T(8,128)(2,1)S(1)}, bf16[1024,384]{1,0:T(8,128)(2,1)S(1)}, u32[]{:S(2)}, u32[]{:S(2)}) collective-permute-start(bf16[1024,384]{1,0:T(8,128)(2,1)S(1)} %collective-permute-done.4.refs_5_.other), channel_id=1, source_target_pairs={{0,1},{1,0},{2,3},{3,2},{4,5},{5,4},{6,7},{7,6},{8,9},{9,8},{10,11... | collective-permute-start | bytes 2359304 | tf_op jit(solution)/shard_map/y_near/ppermute | solution.py:198
  61.5 3.7 %collective-permute-start.11 = (bf16[384,512]{1,0:T(8,128)(2,1)S(1)}, bf16[384,512]{1,0:T(8,128)(2,1)S(1)}, u32[]{:S(2)}, u32[]{:S(2)}) collective-permute-start(bf16[384,512]{1,0:T(8,128)(2,1)S(1)} %collective-permute-done.5.refs_3_.came), channel_id=1, source_target_pairs={{0,1},{1,0},{2,3},{3,2},{4,5},{5,4},{6,7},{7,6},{8,9},{9,8},{10,11... | collective-permute-start | bytes 1179656 | tf_op jit(solution)/shard_map/z_near/ppermute | solution.py:198
  62.1 11.0 %collective-permute-start.15 = (bf16[384,512]{1,0:T(8,128)(2,1)S(1)}, bf16[384,512]{1,0:T(8,128)(2,1)S(1)}, u32[]{:S(2)}, u32[]{:S(2)}) collective-permute-start(bf16[384,512]{1,0:T(8,128)(2,1)S(1)} %collective-permute-done.5.refs_3_.came), channel_id=1, source_target_pairs={{0,16},{16,0},{1,17},{17,1},{2,18},{18,2},{3,19},{19,3},{4,20},{20... | collective-permute-start | bytes 1179656 | tf_op jit(solution)/shard_map/trade/ppermute | solution.py:202
  66.2 2.3 %copy-start.4 = (s32[16]{0:T(128)S(1)}, s32[16]{0:T(128)}, u32[]{:S(2)}) copy-start(s32[16]{0:T(128)} %flags.2) | copy-start | bytes 196
  66.2 6.9 %collective-permute-start.12 = (bf16[112,512]{1,0:T(8,128)(2,1)S(1)}, bf16[112,512]{1,0:T(8,128)(2,1)S(1)}, u32[]{:S(2)}, u32[]{:S(2)}) collective-permute-start(bf16[112,512]{1,0:T(8,128)(2,1)S(1)} %get-tuple-element.42), channel_id=1, source_target_pairs={{0,6},{1,7},{2,4},{3,5},{4,2},{5,3},{6,0},{7,1},{8,14},{9,15},{10,... | collective-permute-start | bytes 344072 | tf_op jit(solution)/shard_map/sums/ppermute | solution.py:198
  73.1 2.5 %collective-permute-start.16 = (bf16[384,512]{1,0:T(8,128)(2,1)S(1)}, bf16[384,512]{1,0:T(8,128)(2,1)S(1)}, u32[]{:S(2)}, u32[]{:S(2)}) collective-permute-start(bf16[384,512]{1,0:T(8,128)(2,1)S(1)} %collective-permute-done.15.refs_5_.other), channel_id=1, source_target_pairs={{0,1},{1,0},{2,3},{3,2},{4,5},{5,4},{6,7},{7,6},{8,9},{9,8},{10,11... | collective-permute-start | bytes 1179656 | tf_op jit(solution)/shard_map/y_near/ppermute | solution.py:198
  73.1 9.2 %collective-permute-start.13 = (bf16[112,512]{1,0:T(8,128)(2,1)S(1)}, bf16[112,512]{1,0:T(8,128)(2,1)S(1)}, u32[]{:S(2)}, u32[]{:S(2)}) collective-permute-start(bf16[112,512]{1,0:T(8,128)(2,1)S(1)} %get-tuple-element.43), channel_id=1, source_target_pairs={{0,2},{1,3},{2,0},{3,1},{4,6},{5,7},{6,4},{7,5},{8,10},{9,11},{10,... | collective-permute-start | bytes 344072 | tf_op jit(solution)/shard_map/sums/ppermute | solution.py:198
  74.6 7.7 %collective-permute-start.14 = (bf16[112,512]{1,0:T(8,128)(2,1)S(1)}, bf16[112,512]{1,0:T(8,128)(2,1)S(1)}, u32[]{:S(2)}, u32[]{:S(2)}) collective-permute-start(bf16[112,512]{1,0:T(8,128)(2,1)S(1)} %get-tuple-element.44), channel_id=1, source_target_pairs={{0,4},{1,5},{2,6},{3,7},{4,0},{5,1},{6,2},{7,3},{8,12},{9,13},{10,... | collective-permute-start | bytes 344072 | tf_op jit(solution)/shard_map/sums/ppermute | solution.py:198
  76.4 6.4 %collective-permute-start.17 = (bf16[112,512]{1,0:T(8,128)(2,1)S(1)}, bf16[112,512]{1,0:T(8,128)(2,1)S(1)}, u32[]{:S(2)}, u32[]{:S(2)}) collective-permute-start(bf16[112,512]{1,0:T(8,128)(2,1)S(1)} %get-tuple-element.52), channel_id=1, source_target_pairs={{0,6},{1,7},{2,4},{3,5},{4,2},{5,3},{6,0},{7,1},{8,14},{9,15},{10,... | collective-permute-start | bytes 344072 | tf_op jit(solution)/shard_map/sums/ppermute | solution.py:198
  78.5 6.6 %collective-permute-start.18 = (bf16[112,512]{1,0:T(8,128)(2,1)S(1)}, bf16[112,512]{1,0:T(8,128)(2,1)S(1)}, u32[]{:S(2)}, u32[]{:S(2)}) collective-permute-start(bf16[112,512]{1,0:T(8,128)(2,1)S(1)} %get-tuple-element.53), channel_id=1, source_target_pairs={{0,2},{1,3},{2,0},{3,1},{4,6},{5,7},{6,4},{7,5},{8,10},{9,11},{10,... | collective-permute-start | bytes 344072 | tf_op jit(solution)/shard_map/sums/ppermute | solution.py:198
  80.8 4.9 %collective-permute-start.19 = (bf16[112,512]{1,0:T(8,128)(2,1)S(1)}, bf16[112,512]{1,0:T(8,128)(2,1)S(1)}, u32[]{:S(2)}, u32[]{:S(2)}) collective-permute-start(bf16[112,512]{1,0:T(8,128)(2,1)S(1)} %get-tuple-element.54), channel_id=1, source_target_pairs={{0,4},{1,5},{2,6},{3,7},{4,0},{5,1},{6,2},{7,3},{8,12},{9,13},{10,... | collective-permute-start | bytes 344072 | tf_op jit(solution)/shard_map/sums/ppermute | solution.py:198

commit v10 on v5

--- a/solution.py
+++ b/solution.py
@@ -242,19 +242,20 @@
             scalars=1,
         )
 
-    arrived = after(z_lower, base)
+    def hidden_units(*halves):
+        return call(
+            functools.partial(hidden_kernel, len(rows), width),
+            jax.ShapeDtypeStruct((len(rows) * height, ff), jnp.bfloat16),
+            [*rows, *halves],
+            scratch,
+        )
+
+    hidden = [hidden_units(z_upper, y_upper)]
+    arrived = after(z_lower, base, hidden[0])
     y_lower = trade(arrived)
     z_near = [send(z_upper, 1, "z_near"), send(arrived, 1, "z_near")]
     y_near = [send(after(y_upper, arrived), 1, "y_near")]
-    hidden = [
-        call(
-            functools.partial(hidden_kernel, len(rows), width),
-            jax.ShapeDtypeStruct((len(rows) * height, ff), jnp.bfloat16),
-            [*rows, own_part, other_part],
-            scratch,
-        )
-        for own_part, other_part in ((z_upper, y_upper), (z_near[0], y_near[0]))
-    ]
+    hidden.append(hidden_units(z_near[0], y_near[0]))
 
     def far_sums(flips, downs, half_flip, blocks, sums, last):
         kinds = [jnp.bfloat16 if last and i > 0 else jnp.float32 for i in blocks]

time: 86.6 us -> 87 us (level)
  starting transfers between devices: 18.2 us -> 19.1 us
    ppermute x18, waiting for transfers between devices: 47.5 us -> 34.9 us  [send(): return lax.ppermute(value, 'expert', [(d, d ^ bit) for d in range(count)])]
    ppermute x2, waiting for transfers between devices: 1.15 us -> 13.2 us  [trade(): return lax.ppermute(value, 'dp', trades)]
    ppermute x18, starting transfers between devices: 15.9 us -> 16.8 us  [send(): return lax.ppermute(value, 'expert', [(d, d ^ bit) for d in range(count)])]
  transfers between devices with their start and end apart: 20 -> 20, of which waited for: 9 -> 10; matrix products, arithmetic and copies ran while one was open for 0% -> 0% of each run, Pallas kernels for 18% -> 18%
where the time goes in v10:
time: 87 us; the launch traced here: 86.8 us
  waiting for transfers between devices  48 us (55%)
  starting transfers between devices  19.1 us (22%)
  Pallas kernels  16.7 us (19%)
  local copies, waits for them, and re-layouts  1.67 us (2%)
  between operations  0.92 us (1%)
    ppermute x18, waiting for transfers between devices, send(): return lax.ppermute(value, 'expert', [(d, d ^ bit) for d in range(count)])  34.9 us
    ppermute x18, starting transfers between devices, send(): return lax.ppermute(value, 'expert', [(d, d ^ bit) for d in range(count)])  16.8 us
    ppermute x2, waiting for transfers between devices, trade(): return lax.ppermute(value, 'dp', trades)  13.2 us
    pallas_call x10, Pallas kernels, call(): pl.pallas_call(kernel, out_shape=out_shape, in_specs=[smem] * scalars + [...  12.4 us
    pallas_call x3, Pallas kernels, store(): pl.pallas_call(functools.partial(store_kernel, axis, first), out_shape=ja...  4.34 us
    ppermute x2, starting transfers between devices, trade(): return lax.ppermute(value, 'dp', trades)  2.32 us
  transfers between devices with their start and end apart: 20, of which 10 were waited for; matrix products, arithmetic and copies ran while one was open for 0% of the time, Pallas kernels for 18%

profile of v10, /device:TPU:0, one launch (start us, length us, event | category | flops | bytes accessed | tf_op | source)
XLA Modules:
  0.0 86.8 jit_solution(6005470301545489320)
XLA Ops:
  0.6 1.5 %slice_bitcast_fusion = (bf16[512,384]{1,0:T(8,128)(2,1)S(1)}, bf16[512,384]{1,0:T(8,128)(2,1)S(1)}, bf16[512,384]{1,0:T(8,128)(2,1)S(1)}, bf16[512,384]{1,0:T(8,128)(2,1)S(1)}) fusion(bf16[1,1024,384]{2,1,0:T(8,128)(2,1)} %param.12, bf16[1,1024,384]{2,1,0:T(8,128)(2,1)} %param.11), kind=kLoop, calls=%fused_computation.4 | loop fusion | bytes 3145728 | tf_op jit(solution)/shard_map/slice | solution.py:211
  2.2 0.0 copy-start.5
  2.2 0.0 copy-start
  2.2 0.2 maximum_select_fusion
  2.4 4.1 %collective-permute-start.3 = (bf16[1024,384]{1,0:T(8,128)(2,1)S(1)}, bf16[1024,384]{1,0:T(8,128)(2,1)S(1)}, u32[]{:S(2)}, u32[]{:S(2)}) collective-permute-start(bf16[1024,384]{1,0:T(8,128)(2,1)S(1)} %maximum_select_fusion), channel_id=1, source_target_pairs={{0,8},{1,9},{2,10},{3,11},{4,12},{5,13},{6,14},{7,15},{8,0},{9,1},... | collective-permute-start | bytes 2359304 | tf_op jit(solution)/shard_map/swap/ppermute | solution.py:198
  6.6 0.1 copy.17
  6.7 0.0 copy-start.1
  6.8 1.6 %collective-permute-start = (bf16[112,1152]{1,0:T(8,128)(2,1)S(1)}, bf16[112,1152]{1,0:T(8,128)(2,1)S(1)}, u32[]{:S(2)}, u32[]{:S(2)}) collective-permute-start(bf16[112,1152]{1,0:T(8,128)(2,1)S(1)} %fusion.1.refs_0_), channel_id=1, source_target_pairs={{0,4},{1,5},{2,6},{3,7},{4,0},{5,1},{6,2},{7,3},{8,12},{9,13},{10,... | collective-permute-start | bytes 774152 | tf_op jit(solution)/shard_map/tokens/ppermute | solution.py:198
  8.4 1.5 %collective-permute-start.1 = (bf16[112,1152]{1,0:T(8,128)(2,1)S(1)}, bf16[112,1152]{1,0:T(8,128)(2,1)S(1)}, u32[]{:S(2)}, u32[]{:S(2)}) collective-permute-start(bf16[112,1152]{1,0:T(8,128)(2,1)S(1)} %fusion.1.refs_0_), channel_id=1, source_target_pairs={{0,2},{1,3},{2,0},{3,1},{4,6},{5,7},{6,4},{7,5},{8,10},{9,11},{10,... | collective-permute-start | bytes 774152 | tf_op jit(solution)/shard_map/tokens/ppermute | solution.py:198
  9.9 19.0 %collective-permute-done.refs_1_ = bf16[112,1152]{1,0:T(8,128)(2,1)S(1)} collective-permute-done((bf16[112,1152]{1,0:T(8,128)(2,1)S(1)}, bf16[112,1152]{1,0:T(8,128)(2,1)S(1)}, u32[]{:S(2)}, u32[]{:S(2)}) %collective-permute-start) | collective-permute-done | bytes 258080 | tf_op jit(solution)/shard_map/tokens/ppermute | solution.py:198
  28.9 1.5 %collective-permute-start.2 = (bf16[112,1152]{1,0:T(8,128)(2,1)S(1)}, bf16[112,1152]{1,0:T(8,128)(2,1)S(1)}, u32[]{:S(2)}, u32[]{:S(2)}) collective-permute-start(bf16[112,1152]{1,0:T(8,128)(2,1)S(1)} %collective-permute-done.refs_1_), channel_id=1, source_target_pairs={{0,2},{1,3},{2,0},{3,1},{4,6},{5,7},{6,4},{7,5},{8,10},{9,11},{10,... | collective-permute-start | bytes 774152 | tf_op jit(solution)/shard_map/tokens/ppermute | solution.py:198
  30.4 0.1 collective-permute-start.8
  30.5 0.5 collective-permute-start.6
  31.0 0.1 collective-permute-start.7
  31.1 4.9 %collective-permute-done.2.refs_3_.refs_1_ = bf16[112,1152]{1,0:T(8,128)(2,1)S(1)} collective-permute-done((bf16[112,1152]{1,0:T(8,128)(2,1)S(1)}, bf16[112,1152]{1,0:T(8,128)(2,1)S(1)}, u32[]{:S(2)}, u32[]{:S(2)}) %collective-permute-start.2) | collective-permute-done | bytes 258080 | tf_op jit(solution)/shard_map/tokens/ppermute | solution.py:198
  36.0 4.9 %collective-permute-done.3.refs_4_.came = bf16[1024,384]{1,0:T(8,128)(2,1)S(1)} collective-permute-done((bf16[1024,384]{1,0:T(8,128)(2,1)S(1)}, bf16[1024,384]{1,0:T(8,128)(2,1)S(1)}, u32[]{:S(2)}, u32[]{:S(2)}) %collective-permute-start.3) | collective-permute-done | bytes 786464 | tf_op jit(solution)/shard_map/swap/ppermute | solution.py:198
  40.9 1.6 %collective-permute-start.4 = (bf16[1024,384]{1,0:T(8,128)(2,1)S(1)}, bf16[1024,384]{1,0:T(8,128)(2,1)S(1)}, u32[]{:S(2)}, u32[]{:S(2)}) collective-permute-start(bf16[1024,384]{1,0:T(8,128)(2,1)S(1)} %collective-permute-done.3.refs_4_.came), channel_id=1, source_target_pairs={{0,16},{16,0},{1,17},{17,1},{2,18},{18,2},{3,19},{19,3},{4,20},{20... | collective-permute-start | bytes 2359304 | tf_op jit(solution)/shard_map/trade/ppermute | solution.py:202
  42.5 2.3 %shard_map.113 = (f32[112,1024]{1,0:T(8,128)S(1)}, f32[112,1024]{1,0:T(8,128)S(1)}) custom-call(s32[16]{0:T(128)S(1)} %copy-done.3, bf16[112,1152]{1,0:T(8,128)(2,1)S(1)} %collective-permute-done.1.refs_2_.refs_0_, bf16[112,1152]{1,0:T(8,128)(2,1)S(1)} %collective-permute-done.2.refs_3_.refs_1_, bf16[1024,384]{1,0:T(8,128)(2,1)S(1)} %bitcast.24, ...), custom_call_target="tpu_custom_call" | custom-call | tf_op jit(solution)/shard_map/pallas_call | solution.py:122
  44.9 2.3 %shard_map.112 = (f32[112,1024]{1,0:T(8,128)S(1)}, f32[112,1024]{1,0:T(8,128)S(1)}) custom-call(s32[16]{0:T(128)S(1)} %copy-done.3, bf16[112,1152]{1,0:T(8,128)(2,1)S(1)} %fusion.1.refs_0_, bf16[112,1152]{1,0:T(8,128)(2,1)S(1)} %collective-permute-done.refs_1_, bf16[1024,384]{1,0:T(8,128)(2,1)S(1)} %bitcast.25, bf16[1024,384]{1,0:T(8,128)(2,1)S(1)} %bitcast.21, ...), custom_call_target="tpu_custom_call" | custom-call | tf_op jit(solution)/shard_map/pallas_call | solution.py:122
  47.2 0.1 collective-permute-start.9
  47.3 12.4 %collective-permute-done.4.refs_5_.other = bf16[1024,384]{1,0:T(8,128)(2,1)S(1)} collective-permute-done((bf16[1024,384]{1,0:T(8,128)(2,1)S(1)}, bf16[1024,384]{1,0:T(8,128)(2,1)S(1)}, u32[]{:S(2)}, u32[]{:S(2)}) %collective-permute-start.4) | collective-permute-done | bytes 786464 | tf_op jit(solution)/shard_map/trade/ppermute | solution.py:202
  59.6 1.2 %shard_map.111.refs_2_.refs_4_ = bf16[448,384]{1,0:T(8,128)(2,1)S(1)} custom-call(bf16[112,1152]{1,0:T(8,128)(2,1)S(1)} %fusion.1.refs_0_, bf16[112,1152]{1,0:T(8,128)(2,1)S(1)} %collective-permute-done.refs_1_, bf16[112,1152]{1,0:T(8,128)(2,1)S(1)} %collective-permute-done.1.refs_2_.refs_0_, bf16[112,1152]{1,0:T(8,128)(2,1)S(1)} %collective-permute-done.2.refs_3_.refs_1_, ...), custom_call_target="tpu_custom_call" | custom-call | tf_op jit(solution)/shard_map/pallas_call | solution.py:122
  60.8 0.7 collective-permute-done.5.refs_3_.came
  61.5 0.5 collective-permute-start.11
  62.1 0.8 collective-permute-start.15
  62.8 1.0 %collective-permute-done.10.refs_5_ = bf16[1024,384]{1,0:T(8,128)(2,1)S(1)} collective-permute-done((bf16[1024,384]{1,0:T(8,128)(2,1)S(1)}, bf16[1024,384]{1,0:T(8,128)(2,1)S(1)}, u32[]{:S(2)}, u32[]{:S(2)}) %collective-permute-start.10) | collective-permute-done | bytes 786464 | tf_op jit(solution)/shard_map/y_near/ppermute | solution.py:198
  63.8 1.2 %shard_map.114.refs_4_.refs_2_ = bf16[448,384]{1,0:T(8,128)(2,1)S(1)} custom-call(bf16[112,1152]{1,0:T(8,128)(2,1)S(1)} %fusion.1.refs_0_, bf16[112,1152]{1,0:T(8,128)(2,1)S(1)} %collective-permute-done.refs_1_, bf16[112,1152]{1,0:T(8,128)(2,1)S(1)} %collective-permute-done.1.refs_2_.refs_0_, bf16[112,1152]{1,0:T(8,128)(2,1)S(1)} %collective-permute-done.2.refs_3_.refs_1_, ...), custom_call_target="tpu_custom_call" | custom-call | tf_op jit(solution)/shard_map/pallas_call | solution.py:122
  65.0 1.0 %shard_map.116 = (bf16[112,512]{1,0:T(8,128)(2,1)S(1)}, bf16[112,512]{1,0:T(8,128)(2,1)S(1)}) custom-call(s32[16]{0:T(128)S(1)} %copy-done.3, bf16[112,1152]{1,0:T(8,128)(2,1)S(1)} %collective-permute-done.1.refs_2_.refs_0_, bf16[112,1152]{1,0:T(8,128)(2,1)S(1)} %collective-permute-done.2.refs_3_.refs_1_, bf16[448,384]{1,0:T(8,128)(2,1)S(1)} %shard_map.111.refs_2_.refs_4_, ...), custom_call_target="tpu_custom_call" | custom-call | tf_op jit(solution)/shard_map/pallas_call | solution.py:122
  66.0 1.8 %collective-permute-start.12 = (bf16[112,512]{1,0:T(8,128)(2,1)S(1)}, bf16[112,512]{1,0:T(8,128)(2,1)S(1)}, u32[]{:S(2)}, u32[]{:S(2)}) collective-permute-start(bf16[112,512]{1,0:T(8,128)(2,1)S(1)} %get-tuple-element.42), channel_id=1, source_target_pairs={{0,6},{1,7},{2,4},{3,5},{4,2},{5,3},{6,0},{7,1},{8,14},{9,15},{10,... | collective-permute-start | bytes 344072 | tf_op jit(solution)/shard_map/sums/ppermute | solution.py:198
  67.8 0.6 collective-permute-start.13
  68.4 0.9 %shard_map.115 = (f32[112,512]{1,0:T(8,128)S(1)}, bf16[112,512]{1,0:T(8,128)(2,1)S(1)}) custom-call(s32[16]{0:T(128)S(1)} %copy-done.3, bf16[112,1152]{1,0:T(8,128)(2,1)S(1)} %fusion.1.refs_0_, bf16[112,1152]{1,0:T(8,128)(2,1)S(1)} %collective-permute-done.refs_1_, bf16[448,384]{1,0:T(8,128)(2,1)S(1)} %shard_map.111.refs_2_.refs_4_, ...), custom_call_target="tpu_custom_call" | custom-call | tf_op jit(solution)/shard_map/pallas_call | solution.py:122
  69.3 1.4 %shard_map.118 = bf16[1024,384]{1,0:T(8,128)(2,1)} custom-call(s32[16]{0:T(128)S(1)} %copy-done.4, bf16[1024,384]{1,0:T(8,128)(2,1)S(1)} %bitcast.22, bf16[1024,384]{1,0:T(8,128)(2,1)S(1)} %collective-permute-done.3.refs_4_.came, bf16[1024,384]{1,0:T(8,128)(2,1)S(1)} %collective-permute-done.4.refs_5_.other), custom_call_target="tpu_custom_call" | custom-call | tf_op jit(solution)/shard_map/pallas_call | solution.py:172
  70.8 1.4 %shard_map.117 = bf16[1024,384]{1,0:T(8,128)(2,1)} custom-call(s32[16]{0:T(128)S(1)} %copy-done.4, bf16[1024,384]{1,0:T(8,128)(2,1)S(1)} %bitcast.26, bf16[1024,384]{1,0:T(8,128)(2,1)S(1)} %collective-permute-done.3.refs_4_.came, bf16[1024,384]{1,0:T(8,128)(2,1)S(1)} %collective-permute-done.4.refs_5_.other), custom_call_target="tpu_custom_call" | custom-call | tf_op jit(solution)/shard_map/pallas_call | solution.py:172
  72.3 0.8 collective-permute-done.15.refs_5_.other
  73.1 1.5 %collective-permute-done.13.refs_2_ = bf16[112,512]{1,0:T(8,128)(2,1)S(1)} collective-permute-done((bf16[112,512]{1,0:T(8,128)(2,1)S(1)}, bf16[112,512]{1,0:T(8,128)(2,1)S(1)}, u32[]{:S(2)}, u32[]{:S(2)}) %collective-permute-start.13) | collective-permute-done | bytes 114720 | tf_op jit(solution)/shard_map/sums/ppermute | solution.py:198
  74.6 0.0 collective-permute-start.16
  74.6 0.9 collective-permute-start.14
  75.5 0.9 %shard_map.119 = (f32[112,512]{1,0:T(8,128)S(1)}, f32[112,512]{1,0:T(8,128)S(1)}, f32[112,512]{1,0:T(8,128)S(1)}, f32[112,512]{1,0:T(8,128)S(1)}) custom-call(s32[16]{0:T(128)S(1)} %copy-done.3, bf16[112,1152]{1,0:T(8,128)(2,1)S(1)} %fusion.1.refs_0_, bf16[112,1152]{1,0:T(8,128)(2,1)S(1)} %collective-permute-done.refs_1_, ...), custom_call_target="tpu_custom_call" | custom-call | tf_op jit(solution)/shard_map/pallas_call | solution.py:122
  76.4 0.8 shard_map.121
  77.3 1.8 %collective-permute-start.17 = (bf16[112,512]{1,0:T(8,128)(2,1)S(1)}, bf16[112,512]{1,0:T(8,128)(2,1)S(1)}, u32[]{:S(2)}, u32[]{:S(2)}) collective-permute-start(bf16[112,512]{1,0:T(8,128)(2,1)S(1)} %get-tuple-element.52), channel_id=1, source_target_pairs={{0,6},{1,7},{2,4},{3,5},{4,2},{5,3},{6,0},{7,1},{8,14},{9,15},{10,... | collective-permute-start | bytes 344072 | tf_op jit(solution)/shard_map/sums/ppermute | solution.py:198
  79.1 0.9 %collective-permute-start.18 = (bf16[112,512]{1,0:T(8,128)(2,1)S(1)}, bf16[112,512]{1,0:T(8,128)(2,1)S(1)}, u32[]{:S(2)}, u32[]{:S(2)}) collective-permute-start(bf16[112,512]{1,0:T(8,128)(2,1)S(1)} %get-tuple-element.53), channel_id=1, source_target_pairs={{0,2},{1,3},{2,0},{3,1},{4,6},{5,7},{6,4},{7,5},{8,10},{9,11},{10,... | collective-permute-start | bytes 344072 | tf_op jit(solution)/shard_map/sums/ppermute | solution.py:198
  80.0 0.8 shard_map.120
  80.8 0.9 %collective-permute-start.19 = (bf16[112,512]{1,0:T(8,128)(2,1)S(1)}, bf16[112,512]{1,0:T(8,128)(2,1)S(1)}, u32[]{:S(2)}, u32[]{:S(2)}) collective-permute-start(bf16[112,512]{1,0:T(8,128)(2,1)S(1)} %get-tuple-element.54), channel_id=1, source_target_pairs={{0,4},{1,5},{2,6},{3,7},{4,0},{5,1},{6,2},{7,3},{8,12},{9,13},{10,... | collective-permute-start | bytes 344072 | tf_op jit(solution)/shard_map/sums/ppermute | solution.py:198
  81.7 1.4 %shard_map.123 = bf16[384,1024]{1,0:T(8,128)(2,1)} custom-call(s32[16]{0:T(128)S(1)} %copy-done.4, bf16[384,1024]{1,0:T(8,128)(2,1)S(1)} %bitcast.18, bf16[384,512]{1,0:T(8,128)(2,1)S(1)} %collective-permute-done.5.refs_3_.came, bf16[384,512]{1,0:T(8,128)(2,1)S(1)} %collective-permute-done.15.refs_5_.other), custom_call_target="tpu_custom_call" | custom-call | tf_op jit(solution)/shard_map/pallas_call | solution.py:172
  83.2 0.4 collective-permute-done.17.refs_5_
  83.6 2.4 %collective-permute-done.18.refs_6_ = bf16[112,512]{1,0:T(8,128)(2,1)S(1)} collective-permute-done((bf16[112,512]{1,0:T(8,128)(2,1)S(1)}, bf16[112,512]{1,0:T(8,128)(2,1)S(1)}, u32[]{:S(2)}, u32[]{:S(2)}) %collective-permute-start.18) | collective-permute-done | bytes 114720 | tf_op jit(solution)/shard_map/sums/ppermute | solution.py:198
  86.0 0.0 collective-permute-done.19.refs_7_
  86.0 0.8 shard_map.122
  (29 shorter events, 0.2 us)
Async XLA Ops:
  2.2 4.4 %copy-start.6 = (f32[112,8]{0,1:T(8,128)S(1)}, f32[112,8]{0,1:T(8,128)}, u32[]{:S(2)}) copy-start(f32[112,8]{0,1:T(8,128)} %param.10) | copy-start | bytes 10756
  2.2 4.4 %copy-start.7 = (s32[112,8]{0,1:T(8,128)S(1)}, s32[112,8]{0,1:T(8,128)}, u32[]{:S(2)}) copy-start(s32[112,8]{0,1:T(8,128)} %param.9) | copy-start | bytes 10756
  2.2 4.5 %copy-start.5 = (bf16[112,1024]{1,0:T(8,128)(2,1)S(1)}, bf16[112,1024]{1,0:T(8,128)(2,1)}, u32[]{:S(2)}) copy-start(bf16[112,1024]{1,0:T(8,128)(2,1)} %param.8) | copy-start | bytes 688132
  2.2 28.2 %copy-start = (bf16[1,384,1024]{2,1,0:T(8,128)(2,1)S(1)}, bf16[1,384,1024]{2,1,0:T(8,128)(2,1)}, u32[]{:S(2)}) copy-start(bf16[1,384,1024]{2,1,0:T(8,128)(2,1)} %param.13) | copy-start | bytes 2359300
  2.4 38.5 %collective-permute-start.3 = (bf16[1024,384]{1,0:T(8,128)(2,1)S(1)}, bf16[1024,384]{1,0:T(8,128)(2,1)S(1)}, u32[]{:S(2)}, u32[]{:S(2)}) collective-permute-start(bf16[1024,384]{1,0:T(8,128)(2,1)S(1)} %maximum_select_fusion), channel_id=1, source_target_pairs={{0,8},{1,9},{2,10},{3,11},{4,12},{5,13},{6,14},{7,15},{8,0},{9,1},... | collective-permute-start | bytes 2359304 | tf_op jit(solution)/shard_map/swap/ppermute | solution.py:198
  6.7 23.8 %copy-start.2 = (bf16[1,1024,384]{2,1,0:T(8,128)(2,1)S(1)}, bf16[1,1024,384]{2,1,0:T(8,128)(2,1)}, u32[]{:S(2)}) copy-start(bf16[1,1024,384]{2,1,0:T(8,128)(2,1)} %param.11) | copy-start | bytes 2359300
  6.7 24.3 %copy-start.1 = (bf16[1,1024,384]{2,1,0:T(8,128)(2,1)S(1)}, bf16[1,1024,384]{2,1,0:T(8,128)(2,1)}, u32[]{:S(2)}) copy-start(bf16[1,1024,384]{2,1,0:T(8,128)(2,1)} %param.12) | copy-start | bytes 2359300
  6.7 35.8 %copy-start.3 = (s32[16]{0:T(128)S(1)}, s32[16]{0:T(128)}, u32[]{:S(2)}) copy-start(s32[16]{0:T(128)} %placement.13) | copy-start | bytes 196
  6.8 22.1 %collective-permute-start = (bf16[112,1152]{1,0:T(8,128)(2,1)S(1)}, bf16[112,1152]{1,0:T(8,128)(2,1)S(1)}, u32[]{:S(2)}, u32[]{:S(2)}) collective-permute-start(bf16[112,1152]{1,0:T(8,128)(2,1)S(1)} %fusion.1.refs_0_), channel_id=1, source_target_pairs={{0,4},{1,5},{2,6},{3,7},{4,0},{5,1},{6,2},{7,3},{8,12},{9,13},{10,... | collective-permute-start | bytes 774152 | tf_op jit(solution)/shard_map/tokens/ppermute | solution.py:198
  8.4 22.6 %collective-permute-start.1 = (bf16[112,1152]{1,0:T(8,128)(2,1)S(1)}, bf16[112,1152]{1,0:T(8,128)(2,1)S(1)}, u32[]{:S(2)}, u32[]{:S(2)}) collective-permute-start(bf16[112,1152]{1,0:T(8,128)(2,1)S(1)} %fusion.1.refs_0_), channel_id=1, source_target_pairs={{0,2},{1,3},{2,0},{3,1},{4,6},{5,7},{6,4},{7,5},{8,10},{9,11},{10,... | collective-permute-start | bytes 774152 | tf_op jit(solution)/shard_map/tokens/ppermute | solution.py:198
  28.9 7.1 %collective-permute-start.2 = (bf16[112,1152]{1,0:T(8,128)(2,1)S(1)}, bf16[112,1152]{1,0:T(8,128)(2,1)S(1)}, u32[]{:S(2)}, u32[]{:S(2)}) collective-permute-start(bf16[112,1152]{1,0:T(8,128)(2,1)S(1)} %collective-permute-done.refs_1_), channel_id=1, source_target_pairs={{0,2},{1,3},{2,0},{3,1},{4,6},{5,7},{6,4},{7,5},{8,10},{9,11},{10,... | collective-permute-start | bytes 774152 | tf_op jit(solution)/shard_map/tokens/ppermute | solution.py:198
  30.4 12.1 %collective-permute-start.8 = (bf16[384,1024]{1,0:T(8,128)(2,1)S(1)}, bf16[384,1024]{1,0:T(8,128)(2,1)S(1)}, u32[]{:S(2)}, u32[]{:S(2)}) collective-permute-start(bf16[384,1024]{1,0:T(8,128)(2,1)S(1)} %bitcast.15), channel_id=1, source_target_pairs={{0,1},{1,0},{2,3},{3,2},{4,5},{5,4},{6,7},{7,6},{8,9},{9,8},{10,11... | collective-permute-start | bytes 2359304 | tf_op jit(solution)/shard_map/near/ppermute | solution.py:198
  30.5 12.0 %collective-permute-start.6 = (bf16[1024,384]{1,0:T(8,128)(2,1)S(1)}, bf16[1024,384]{1,0:T(8,128)(2,1)S(1)}, u32[]{:S(2)}, u32[]{:S(2)}) collective-permute-start(bf16[1024,384]{1,0:T(8,128)(2,1)S(1)} %bitcast.23), channel_id=1, source_target_pairs={{0,1},{1,0},{2,3},{3,2},{4,5},{5,4},{6,7},{7,6},{8,9},{9,8},{10,11... | collective-permute-start | bytes 2359304 | tf_op jit(solution)/shard_map/near/ppermute | solution.py:198
  31.0 11.5 %collective-permute-start.7 = (bf16[1024,384]{1,0:T(8,128)(2,1)S(1)}, bf16[1024,384]{1,0:T(8,128)(2,1)S(1)}, u32[]{:S(2)}, u32[]{:S(2)}) collective-permute-start(bf16[1024,384]{1,0:T(8,128)(2,1)S(1)} %bitcast.19), channel_id=1, source_target_pairs={{0,1},{1,0},{2,3},{3,2},{4,5},{5,4},{6,7},{7,6},{8,9},{9,8},{10,11... | collective-permute-start | bytes 2359304 | tf_op jit(solution)/shard_map/near/ppermute | solution.py:198
  40.9 18.7 %collective-permute-start.4 = (bf16[1024,384]{1,0:T(8,128)(2,1)S(1)}, bf16[1024,384]{1,0:T(8,128)(2,1)S(1)}, u32[]{:S(2)}, u32[]{:S(2)}) collective-permute-start(bf16[1024,384]{1,0:T(8,128)(2,1)S(1)} %collective-permute-done.3.refs_4_.came), channel_id=1, source_target_pairs={{0,16},{16,0},{1,17},{17,1},{2,18},{18,2},{3,19},{19,3},{4,20},{20... | collective-permute-start | bytes 2359304 | tf_op jit(solution)/shard_map/trade/ppermute | solution.py:202
  42.5 19.1 %collective-permute-start.5 = (bf16[384,512]{1,0:T(8,128)(2,1)S(1)}, bf16[384,512]{1,0:T(8,128)(2,1)S(1)}, u32[]{:S(2)}, u32[]{:S(2)}) collective-permute-start(bf16[384,512]{1,0:T(8,128)(2,1)S(1)} %slice_select_fusion), channel_id=1, source_target_pairs={{0,8},{1,9},{2,10},{3,11},{4,12},{5,13},{6,14},{7,15},{8,0},{9,1},... | collective-permute-start | bytes 1179656 | tf_op jit(solution)/shard_map/swap/ppermute | solution.py:198
  47.2 15.6 %collective-permute-start.9 = (bf16[1024,384]{1,0:T(8,128)(2,1)S(1)}, bf16[1024,384]{1,0:T(8,128)(2,1)S(1)}, u32[]{:S(2)}, u32[]{:S(2)}) collective-permute-start(bf16[1024,384]{1,0:T(8,128)(2,1)S(1)} %collective-permute-done.3.refs_4_.came), channel_id=1, source_target_pairs={{0,1},{1,0},{2,3},{3,2},{4,5},{5,4},{6,7},{7,6},{8,9},{9,8},{10,11... | collective-permute-start | bytes 2359304 | tf_op jit(solution)/shard_map/z_near/ppermute | solution.py:198
  61.5 2.3 %collective-permute-start.10 = (bf16[1024,384]{1,0:T(8,128)(2,1)S(1)}, bf16[1024,384]{1,0:T(8,128)(2,1)S(1)}, u32[]{:S(2)}, u32[]{:S(2)}) collective-permute-start(bf16[1024,384]{1,0:T(8,128)(2,1)S(1)} %collective-permute-done.4.refs_5_.other), channel_id=1, source_target_pairs={{0,1},{1,0},{2,3},{3,2},{4,5},{5,4},{6,7},{7,6},{8,9},{9,8},{10,11... | collective-permute-start | bytes 2359304 | tf_op jit(solution)/shard_map/y_near/ppermute | solution.py:198
  61.5 3.5 %collective-permute-start.11 = (bf16[384,512]{1,0:T(8,128)(2,1)S(1)}, bf16[384,512]{1,0:T(8,128)(2,1)S(1)}, u32[]{:S(2)}, u32[]{:S(2)}) collective-permute-start(bf16[384,512]{1,0:T(8,128)(2,1)S(1)} %collective-permute-done.5.refs_3_.came), channel_id=1, source_target_pairs={{0,1},{1,0},{2,3},{3,2},{4,5},{5,4},{6,7},{7,6},{8,9},{9,8},{10,11... | collective-permute-start | bytes 1179656 | tf_op jit(solution)/shard_map/z_near/ppermute | solution.py:198
  62.1 11.0 %collective-permute-start.15 = (bf16[384,512]{1,0:T(8,128)(2,1)S(1)}, bf16[384,512]{1,0:T(8,128)(2,1)S(1)}, u32[]{:S(2)}, u32[]{:S(2)}) collective-permute-start(bf16[384,512]{1,0:T(8,128)(2,1)S(1)} %collective-permute-done.5.refs_3_.came), channel_id=1, source_target_pairs={{0,16},{16,0},{1,17},{17,1},{2,18},{18,2},{3,19},{19,3},{4,20},{20... | collective-permute-start | bytes 1179656 | tf_op jit(solution)/shard_map/trade/ppermute | solution.py:202
  66.0 7.1 %collective-permute-start.12 = (bf16[112,512]{1,0:T(8,128)(2,1)S(1)}, bf16[112,512]{1,0:T(8,128)(2,1)S(1)}, u32[]{:S(2)}, u32[]{:S(2)}) collective-permute-start(bf16[112,512]{1,0:T(8,128)(2,1)S(1)} %get-tuple-element.42), channel_id=1, source_target_pairs={{0,6},{1,7},{2,4},{3,5},{4,2},{5,3},{6,0},{7,1},{8,14},{9,15},{10,... | collective-permute-start | bytes 344072 | tf_op jit(solution)/shard_map/sums/ppermute | solution.py:198
  67.8 1.5 %copy-start.4 = (s32[16]{0:T(128)S(1)}, s32[16]{0:T(128)}, u32[]{:S(2)}) copy-start(s32[16]{0:T(128)} %flags.2) | copy-start | bytes 196
  67.8 6.8 %collective-permute-start.13 = (bf16[112,512]{1,0:T(8,128)(2,1)S(1)}, bf16[112,512]{1,0:T(8,128)(2,1)S(1)}, u32[]{:S(2)}, u32[]{:S(2)}) collective-permute-start(bf16[112,512]{1,0:T(8,128)(2,1)S(1)} %get-tuple-element.43), channel_id=1, source_target_pairs={{0,2},{1,3},{2,0},{3,1},{4,6},{5,7},{6,4},{7,5},{8,10},{9,11},{10,... | collective-permute-start | bytes 344072 | tf_op jit(solution)/shard_map/sums/ppermute | solution.py:198
  74.6 1.8 %collective-permute-start.16 = (bf16[384,512]{1,0:T(8,128)(2,1)S(1)}, bf16[384,512]{1,0:T(8,128)(2,1)S(1)}, u32[]{:S(2)}, u32[]{:S(2)}) collective-permute-start(bf16[384,512]{1,0:T(8,128)(2,1)S(1)} %collective-permute-done.15.refs_5_.other), channel_id=1, source_target_pairs={{0,1},{1,0},{2,3},{3,2},{4,5},{5,4},{6,7},{7,6},{8,9},{9,8},{10,11... | collective-permute-start | bytes 1179656 | tf_op jit(solution)/shard_map/y_near/ppermute | solution.py:198
  74.6 8.6 %collective-permute-start.14 = (bf16[112,512]{1,0:T(8,128)(2,1)S(1)}, bf16[112,512]{1,0:T(8,128)(2,1)S(1)}, u32[]{:S(2)}, u32[]{:S(2)}) collective-permute-start(bf16[112,512]{1,0:T(8,128)(2,1)S(1)} %get-tuple-element.44), channel_id=1, source_target_pairs={{0,4},{1,5},{2,6},{3,7},{4,0},{5,1},{6,2},{7,3},{8,12},{9,13},{10,... | collective-permute-start | bytes 344072 | tf_op jit(solution)/shard_map/sums/ppermute | solution.py:198
  77.3 6.3 %collective-permute-start.17 = (bf16[112,512]{1,0:T(8,128)(2,1)S(1)}, bf16[112,512]{1,0:T(8,128)(2,1)S(1)}, u32[]{:S(2)}, u32[]{:S(2)}) collective-permute-start(bf16[112,512]{1,0:T(8,128)(2,1)S(1)} %get-tuple-element.52), channel_id=1, source_target_pairs={{0,6},{1,7},{2,4},{3,5},{4,2},{5,3},{6,0},{7,1},{8,14},{9,15},{10,... | collective-permute-start | bytes 344072 | tf_op jit(solution)/shard_map/sums/ppermute | solution.py:198
  79.1 6.9 %collective-permute-start.18 = (bf16[112,512]{1,0:T(8,128)(2,1)S(1)}, bf16[112,512]{1,0:T(8,128)(2,1)S(1)}, u32[]{:S(2)}, u32[]{:S(2)}) collective-permute-start(bf16[112,512]{1,0:T(8,128)(2,1)S(1)} %get-tuple-element.53), channel_id=1, source_target_pairs={{0,2},{1,3},{2,0},{3,1},{4,6},{5,7},{6,4},{7,5},{8,10},{9,11},{10,... | collective-permute-start | bytes 344072 | tf_op jit(solution)/shard_map/sums/ppermute | solution.py:198
  80.8 5.2 %collective-permute-start.19 = (bf16[112,512]{1,0:T(8,128)(2,1)S(1)}, bf16[112,512]{1,0:T(8,128)(2,1)S(1)}, u32[]{:S(2)}, u32[]{:S(2)}) collective-permute-start(bf16[112,512]{1,0:T(8,128)(2,1)S(1)} %get-tuple-element.54), channel_id=1, source_target_pairs={{0,4},{1,5},{2,6},{3,7},{4,0},{5,1},{6,2},{7,3},{8,12},{9,13},{10,... | collective-permute-start | bytes 344072 | tf_op jit(solution)/shard_map/sums/ppermute | solution.py:198

commit v11 on v10

--- a/solution.py
+++ b/solution.py
@@ -65,19 +65,20 @@
 
 
 def hidden_kernel(blocks, width, *refs):
-    rows, own, other, out, x = refs[:blocks], refs[blocks], refs[blocks + 1], refs[blocks + 2], refs[blocks + 3]
+    rows, mats, out, x = refs[:blocks], refs[blocks : blocks + 4], refs[blocks + 4], refs[blocks + 5]
+    came_gate, came_up, traded_gate, traded_up = mats
     height = rows[0].shape[0]
     half = lax.axis_index("dp") % 2
-    depth = own.shape[0] // 2
-    at = pl.multiple_of(half * depth, depth)
-    off = pl.multiple_of(depth - at, depth)
-    for first in range(0, blocks, 2):
-        for i in range(2):
-            x[i * height : (i + 1) * height, :] = rows[first + i][:, :width]
-        xa, xb = x[:, pl.ds(at, depth)], x[:, pl.ds(off, depth)]
-        gate = dot(xa, own[:depth, :]) + dot(xb, other[:depth, :])
-        up = dot(xa, own[depth:, :]) + dot(xb, other[depth:, :])
-        out[first * height : (first + 2) * height, :] = activate(gate, up)
+
+    def run(g, u):
+        for first in range(0, blocks, 2):
+            for i in range(2):
+                x[i * height : (i + 1) * height, :] = rows[first + i][:, :width]
+            units = activate(dot(x[...], g[...]), dot(x[...], u[...]))
+            out[first * height : (first + 2) * height, :] = units
+
+    pl.when(half == 0)(lambda: run(came_gate, traded_up))
+    pl.when(half == 1)(lambda: run(traded_gate, came_up))
 
 
 def down_kernel(count, flips, blocks, half_flip, placement, *refs):
@@ -143,34 +144,34 @@
     return ref.at[span, :] if axis == 0 else ref.at[:, span]
 
 
-def store_kernel(axis, first, flags, own, came, other, out, sems):
+def store_kernel(turn, flags, own, came, other, out, sems):
     half = lax.axis_index("dp") % 2
-    size = out.shape[axis] // 2
     taken = flags[lax.axis_index("expert")] == 1
 
     @pl.when(taken)
     def _():
-        if axis == 0:
-            parts = [ref.at[pl.ds(first, size), :] for ref in (came, other)]
+        if turn is None:
+            size = came.shape[1]
+            run_copies(
+                [
+                    (came, part_of(out, 1, half, size)),
+                    (other, part_of(out, 1, 1 - half, size)),
+                ],
+                sems,
+            )
         else:
-            parts = [came, other]
-        run_copies(
-            [
-                (parts[0], part_of(out, axis, half, size)),
-                (parts[1], part_of(out, axis, 1 - half, size)),
-            ],
-            sems,
-        )
+            pl.when(half == turn)(lambda: run_copies([(came, out)], sems))
+            pl.when(half != turn)(lambda: run_copies([(other, out)], sems))
 
     @pl.when(jnp.logical_not(taken))
     def _():
         run_copies([(own, out)], sems)
 
 
-def store(axis, first, flags, own, came, other):
+def store(turn, flags, own, came, other):
     vmem = pl.BlockSpec(memory_space=pltpu.VMEM)
     return pl.pallas_call(
-        functools.partial(store_kernel, axis, first),
+        functools.partial(store_kernel, turn),
         out_shape=jax.ShapeDtypeStruct(own.shape, own.dtype),
         in_specs=[pl.BlockSpec(memory_space=pltpu.SMEM)] + [vmem] * 3,
         out_specs=pl.BlockSpec(memory_space=pl.ANY),
@@ -197,19 +198,28 @@
         with jax.named_scope(name):
             return lax.ppermute(value, "expert", [(d, d ^ bit) for d in range(count)])
 
+    def send_in(value, bit, turn, name):
+        pairs = [
+            (d * count + e, d * count + (e ^ bit))
+            for d in range(turn, lax.axis_size("dp"), 2)
+            for e in range(count)
+        ]
+        with jax.named_scope(name):
+            return lax.ppermute(value, ("dp", "expert"), pairs)
+
+    def hand_over(value, turn):
+        with jax.named_scope("trade"):
+            return lax.ppermute(value, "dp", trades[turn::2])
+
     def trade(value):
         with jax.named_scope("trade"):
             return lax.ppermute(value, "dp", trades)
 
-    depth, part = own[0].shape[0] // 2, width // 2
+    part = width // 2
 
     def half_of(first, second):
         return jnp.where(couple == 0, first, second)
 
-    upper = half_of(
-        jnp.concatenate([own[0][:depth], own[1][:depth]], axis=0),
-        jnp.concatenate([own[0][depth:], own[1][depth:]], axis=0),
-    )
     lower = half_of(own[2][:, :part], own[2][:, part:])
 
     bits = []
@@ -225,9 +235,9 @@
             masks[i | 1 << stage] = masks[i] ^ bit
     rows = [blocks[i] for i in range(len(blocks))]
 
-    z_upper = send(upper, half_axis, "swap")
+    z_upper = [send_in(own[turn], half_axis, turn, "swap") for turn in (0, 1)]
     z_lower = send(after(lower, z_upper, *rows), half_axis, "swap")
-    y_upper = trade(after(z_upper, *rows))
+    y_upper = [hand_over(after(z_upper[turn], *rows), turn) for turn in (0, 1)]
     near = [send(after(w, lower), 1, "near") for w in own]
 
     firsts = list(reversed(range(0, len(rows), 2)))
@@ -250,12 +260,13 @@
             scratch,
         )
 
-    hidden = [hidden_units(z_upper, y_upper)]
+    hidden = [hidden_units(*z_upper, *y_upper)]
     arrived = after(z_lower, base, hidden[0])
     y_lower = trade(arrived)
-    z_near = [send(z_upper, 1, "z_near"), send(arrived, 1, "z_near")]
-    y_near = [send(after(y_upper, arrived), 1, "y_near")]
-    hidden.append(hidden_units(z_near[0], y_near[0]))
+    z_across = [send_in(z_upper[turn], 1, turn, "z_near") for turn in (0, 1)]
+    y_across = [send_in(after(y_upper[turn], arrived), 1, 1 - turn, "y_near") for turn in (0, 1)]
+    z_near, y_near = [send(arrived, 1, "z_near")], []
+    hidden.append(hidden_units(*z_across, *y_across))
 
     def far_sums(flips, downs, half_flip, blocks, sums, last):
         kinds = [jnp.bfloat16 if last and i > 0 else jnp.float32 for i in blocks]
@@ -274,11 +285,11 @@
     near_sums = [x for first in reversed(firsts) for x in base[first]]
     parts = {}
     for first in firsts:
-        parts |= far_sums((0, 1), [arrived, z_near[1]], 0, (first, first + 1), near_sums, True)
+        parts |= far_sums((0, 1), [arrived, z_near[0]], 0, (first, first + 1), near_sums, True)
     flags = after(swap_flags, parts)
     stored = [
-        store(0, 0, flags, own[0], z_upper, y_upper),
-        store(0, depth, flags, own[1], z_upper, y_upper),
+        store(0, flags, own[0], z_upper[0], y_upper[0]),
+        store(1, flags, own[1], z_upper[1], y_upper[1]),
     ]
     ours = collect(parts)
     landed = after(y_lower, stored, ours[1:-1])
@@ -287,8 +298,8 @@
     last_sums = far_sums((0,), [landed], 1, everyone, near_sums, False)
     last_parts = {}
     for first in firsts:
-        last_parts |= far_sums((1,), [y_near[1]], 1, (first, first + 1), last_sums, True)
-    stored.append(store(1, 0, after(swap_flags, last_parts), own[2], z_lower, y_lower))
+        last_parts |= far_sums((1,), [y_near[0]], 1, (first, first + 1), last_sums, True)
+    stored.append(store(None, after(swap_flags, last_parts), own[2], z_lower, y_lower))
     others = collect(last_parts)
     mixed = call(
         functools.partial(finish_kernel, len(ours)),

time: 87 us -> 94.6 us (1.087)
  starting transfers between devices: 19.1 us -> 35 us
  waiting for transfers between devices: 48 us -> 34.9 us
  other arithmetic: 0.32 us -> 2.99 us
  Pallas kernels: 16.7 us -> 18.5 us
    ppermute x0 -> x8, starting transfers between devices: none -> 19.7 us  [the longest x6 12.8 us: send_in(): return lax.ppermute(value, ('dp', 'expert'), pairs)]
    ppermute x2 -> x1, waiting for transfers between devices: 13.2 us -> 0.01 us  [trade(): return lax.ppermute(value, 'dp', trades)]
    ppermute x0 -> x8, waiting for transfers between devices: none -> 9.37 us  [the longest x2 7.28 us: hand_over(): return lax.ppermute(value, 'dp', trades[turn::2])]
    ppermute x18 -> x15, waiting for transfers between devices: 34.9 us -> 25.5 us  [send(): return lax.ppermute(value, 'expert', [(d, d ^ bit) for d in range(count)])]
    ppermute x18 -> x15, starting transfers between devices: 16.8 us -> 13.7 us  [send(): return lax.ppermute(value, 'expert', [(d, d ^ bit) for d in range(count)])]
    unnamed x16 -> x12, local copies, waits for them, and re-layouts: 0.05 us -> 1.8 us
    slice x1 -> x0, local copies, waits for them, and re-layouts: 1.52 us -> none  [per_device(): own[1][depth:]]
    pallas_call x10, Pallas kernels: 12.4 us -> 13.5 us  [call(): pl.pallas_call(kernel, out_shape=out_shape, in_specs=[smem] * scalars + [...]
  transfers between devices with their start and end apart: 20 -> 24, of which waited for: 10 -> 8; matrix products, arithmetic and copies ran while one was open for 0% -> 3% of each run, Pallas kernels for 18% -> 19%
where the time goes in v11:
time: 94.6 us; the launch traced here: 94.2 us
  starting transfers between devices  35 us (37%)
  waiting for transfers between devices  34.9 us (37%)
  Pallas kernels  18.5 us (20%)
  other arithmetic  2.99 us (3%)
  local copies, waits for them, and re-layouts  1.91 us (2%)
  between operations  0.98 us (1%)
    ppermute x15, waiting for transfers between devices, send(): return lax.ppermute(value, 'expert', [(d, d ^ bit) for d in range(count)])  25.5 us
    ppermute x15, starting transfers between devices, send(): return lax.ppermute(value, 'expert', [(d, d ^ bit) for d in range(count)])  13.7 us
    pallas_call x10, Pallas kernels, call(): pl.pallas_call(kernel, out_shape=out_shape, in_specs=[smem] * scalars + [...  13.5 us
    ppermute x6, starting transfers between devices, send_in(): return lax.ppermute(value, ('dp', 'expert'), pairs)  12.8 us
    ppermute x2, waiting for transfers between devices, hand_over(): return lax.ppermute(value, 'dp', trades[turn::2])  7.28 us
    ppermute x2, starting transfers between devices, hand_over(): return lax.ppermute(value, 'dp', trades[turn::2])  6.98 us
    pallas_call x3, Pallas kernels, store(): pl.pallas_call(functools.partial(store_kernel, turn), out_shape=jax.Shape...  5.03 us
    ppermute x6, waiting for transfers between devices, send_in(): return lax.ppermute(value, ('dp', 'expert'), pairs)  2.09 us
  transfers between devices with their start and end apart: 24, of which 8 were waited for; matrix products, arithmetic and copies ran while one was open for 3% of the time, Pallas kernels for 19%

profile of v11, /device:TPU:0, one launch (start us, length us, event | category | flops | bytes accessed | tf_op | source)
XLA Modules:
  0.0 94.2 jit_solution(16907347908849472038)
XLA Ops:
  0.6 5.9 %collective-permute-start.3 = (bf16[1024,384]{1,0:T(8,128)(2,1)}, bf16[1024,384]{1,0:T(8,128)(2,1)S(1)}, u32[]{:S(2)}, u32[]{:S(2)}) collective-permute-start(bf16[1024,384]{1,0:T(8,128)(2,1)} %bitcast.16), channel_id=1, source_target_pairs={{0,8},{1,9},{2,10},{3,11},{4,12},{5,13},{6,14},{7,15},{8,0},{9,1},... | collective-permute-start | bytes 2359304 | tf_op jit(solution)/shard_map/swap/ppermute | solution.py:208
  6.6 1.6 %collective-permute-start.4 = (bf16[1024,384]{1,0:T(8,128)(2,1)}, bf16[1024,384]{1,0:T(8,128)(2,1)}, u32[]{:S(2)}, u32[]{:S(2)}) collective-permute-start(bf16[1024,384]{1,0:T(8,128)(2,1)} %bitcast.11), channel_id=1, source_target_pairs={{16,24},{17,25},{18,26},{19,27},{20,28},{21,29},{22,30},{23,31},{2... | collective-permute-start | bytes 2359304 | tf_op jit(solution)/shard_map/swap/ppermute | solution.py:208
  8.1 0.7 select_reduce_fusion
  8.9 0.1 copy.17
  9.0 1.1 %fusion.1.refs_0_ = bf16[112,1152]{1,0:T(8,128)(2,1)S(1)} fusion(bf16[112,48]{1,0:T(8,128)(2,1)S(1)} %copy.17, bf16[112,1024]{1,0:T(8,128)(2,1)} %param.8), kind=kLoop, calls=%fused_computation.3 | loop fusion | flops 774144 | bytes 498176 | tf_op jit(solution)/shard_map/concatenate | solution.py:29
  10.1 1.6 %collective-permute-start = (bf16[112,1152]{1,0:T(8,128)(2,1)S(1)}, bf16[112,1152]{1,0:T(8,128)(2,1)S(1)}, u32[]{:S(2)}, u32[]{:S(2)}) collective-permute-start(bf16[112,1152]{1,0:T(8,128)(2,1)S(1)} %fusion.1.refs_0_), channel_id=1, source_target_pairs={{0,4},{1,5},{2,6},{3,7},{4,0},{5,1},{6,2},{7,3},{8,12},{9,13},{10,... | collective-permute-start | bytes 774152 | tf_op jit(solution)/shard_map/tokens/ppermute | solution.py:199
  11.8 1.5 %collective-permute-start.1 = (bf16[112,1152]{1,0:T(8,128)(2,1)S(1)}, bf16[112,1152]{1,0:T(8,128)(2,1)S(1)}, u32[]{:S(2)}, u32[]{:S(2)}) collective-permute-start(bf16[112,1152]{1,0:T(8,128)(2,1)S(1)} %fusion.1.refs_0_), channel_id=1, source_target_pairs={{0,2},{1,3},{2,0},{3,1},{4,6},{5,7},{6,4},{7,5},{8,10},{9,11},{10,... | collective-permute-start | bytes 774152 | tf_op jit(solution)/shard_map/tokens/ppermute | solution.py:199
  13.3 1.2 %slice_select_fusion = bf16[384,512]{1,0:T(8,128)(2,1)S(1)} fusion(bf16[384,1024]{1,0:T(8,128)(2,1)} %bitcast.6, pred[]{:T(512)S(6)} %eq.21), kind=kLoop, calls=%fused_computation.2 | loop fusion | flops 196608 | bytes 1179649 | tf_op jit(solution)/shard_map/jit(_where)/select_n | solution.py:221
  14.4 0.1 collective-permute-start.10
  14.5 14.6 %collective-permute-done.refs_1_ = bf16[112,1152]{1,0:T(8,128)(2,1)S(1)} collective-permute-done((bf16[112,1152]{1,0:T(8,128)(2,1)S(1)}, bf16[112,1152]{1,0:T(8,128)(2,1)S(1)}, u32[]{:S(2)}, u32[]{:S(2)}) %collective-permute-start) | collective-permute-done | bytes 258080 | tf_op jit(solution)/shard_map/tokens/ppermute | solution.py:199
  29.2 1.5 %collective-permute-start.2 = (bf16[112,1152]{1,0:T(8,128)(2,1)S(1)}, bf16[112,1152]{1,0:T(8,128)(2,1)S(1)}, u32[]{:S(2)}, u32[]{:S(2)}) collective-permute-start(bf16[112,1152]{1,0:T(8,128)(2,1)S(1)} %collective-permute-done.refs_1_), channel_id=1, source_target_pairs={{0,2},{1,3},{2,0},{3,1},{4,6},{5,7},{6,4},{7,5},{8,10},{9,11},{10,... | collective-permute-start | bytes 774152 | tf_op jit(solution)/shard_map/tokens/ppermute | solution.py:199
  30.6 7.1 %collective-permute-done.2.refs_3_.refs_1_ = bf16[112,1152]{1,0:T(8,128)(2,1)S(1)} collective-permute-done((bf16[112,1152]{1,0:T(8,128)(2,1)S(1)}, bf16[112,1152]{1,0:T(8,128)(2,1)S(1)}, u32[]{:S(2)}, u32[]{:S(2)}) %collective-permute-start.2) | collective-permute-done | bytes 258080 | tf_op jit(solution)/shard_map/tokens/ppermute | solution.py:199
  37.8 1.3 %collective-permute-start.6 = (bf16[1024,384]{1,0:T(8,128)(2,1)}, bf16[1024,384]{1,0:T(8,128)(2,1)S(1)}, u32[]{:S(2)}, u32[]{:S(2)}) collective-permute-start(bf16[1024,384]{1,0:T(8,128)(2,1)} %collective-permute-done.4.refs_5_.came), channel_id=1, source_target_pairs={{16,0},{17,1},{18,2},{19,3},{20,4},{21,5},{22,6},{23,7},{24,8},{25... | collective-permute-start | bytes 2359304 | tf_op jit(solution)/shard_map/trade/ppermute | solution.py:212
  39.1 2.1 %collective-permute-done.3.refs_4_.came = bf16[1024,384]{1,0:T(8,128)(2,1)S(1)} collective-permute-done((bf16[1024,384]{1,0:T(8,128)(2,1)}, bf16[1024,384]{1,0:T(8,128)(2,1)S(1)}, u32[]{:S(2)}, u32[]{:S(2)}) %collective-permute-start.3) | collective-permute-done | bytes 786464 | tf_op jit(solution)/shard_map/swap/ppermute | solution.py:208
  41.2 5.7 %collective-permute-start.5 = (bf16[1024,384]{1,0:T(8,128)(2,1)S(1)}, bf16[1024,384]{1,0:T(8,128)(2,1)S(1)}, u32[]{:S(2)}, u32[]{:S(2)}) collective-permute-start(bf16[1024,384]{1,0:T(8,128)(2,1)S(1)} %collective-permute-done.3.refs_4_.came), channel_id=1, source_target_pairs={{0,16},{1,17},{2,18},{3,19},{4,20},{5,21},{6,22},{7,23},{8,24},{9,... | collective-permute-start | bytes 2359304 | tf_op jit(solution)/shard_map/trade/ppermute | solution.py:212
  46.9 0.1 collective-permute-start.7
  47.0 1.9 %collective-permute-start.11 = (bf16[1024,384]{1,0:T(8,128)(2,1)S(1)}, bf16[1024,384]{1,0:T(8,128)(2,1)S(1)}, u32[]{:S(2)}, u32[]{:S(2)}) collective-permute-start(bf16[1024,384]{1,0:T(8,128)(2,1)S(1)} %collective-permute-done.3.refs_4_.came), channel_id=1, source_target_pairs={{0,1},{1,0},{2,3},{3,2},{4,5},{5,4},{6,7},{7,6},{8,9},{9,8},{10,11... | collective-permute-start | bytes 2359304 | tf_op jit(solution)/shard_map/z_near/ppermute | solution.py:208
  48.9 1.1 %copy-done.2 = bf16[1,1024,384]{2,1,0:T(8,128)(2,1)S(1)} copy-done((bf16[1,1024,384]{2,1,0:T(8,128)(2,1)S(1)}, bf16[1,1024,384]{2,1,0:T(8,128)(2,1)}, u32[]{:S(2)}) %copy-start.2) | copy-done | bytes 786456
  50.1 2.3 %shard_map.113 = (f32[112,1024]{1,0:T(8,128)S(1)}, f32[112,1024]{1,0:T(8,128)S(1)}) custom-call(s32[16]{0:T(128)S(1)} %copy-done.4, bf16[112,1152]{1,0:T(8,128)(2,1)S(1)} %collective-permute-done.1.refs_2_.refs_0_, bf16[112,1152]{1,0:T(8,128)(2,1)S(1)} %collective-permute-done.2.refs_3_.refs_1_, bf16[1024,384]{1,0:T(8,128)(2,1)S(1)} %bitcast.18, ...), custom_call_target="tpu_custom_call" | custom-call | tf_op jit(solution)/shard_map/pallas_call | solution.py:123
  52.4 2.3 %shard_map.112 = (f32[112,1024]{1,0:T(8,128)S(1)}, f32[112,1024]{1,0:T(8,128)S(1)}) custom-call(s32[16]{0:T(128)S(1)} %copy-done.4, bf16[112,1152]{1,0:T(8,128)(2,1)S(1)} %fusion.1.refs_0_, bf16[112,1152]{1,0:T(8,128)(2,1)S(1)} %collective-permute-done.refs_1_, bf16[1024,384]{1,0:T(8,128)(2,1)S(1)} %bitcast.19, bf16[1024,384]{1,0:T(8,128)(2,1)S(1)} %bitcast.14, ...), custom_call_target="tpu_custom_call" | custom-call | tf_op jit(solution)/shard_map/pallas_call | solution.py:123
  54.8 0.7 collective-permute-start.12
  55.5 6.3 %collective-permute-done.6.refs_7_.other = bf16[1024,384]{1,0:T(8,128)(2,1)S(1)} collective-permute-done((bf16[1024,384]{1,0:T(8,128)(2,1)}, bf16[1024,384]{1,0:T(8,128)(2,1)S(1)}, u32[]{:S(2)}, u32[]{:S(2)}) %collective-permute-start.6) | collective-permute-done | bytes 786464 | tf_op jit(solution)/shard_map/trade/ppermute | solution.py:212
  61.7 1.0 %collective-permute-done.5.refs_6_.other = bf16[1024,384]{1,0:T(8,128)(2,1)S(1)} collective-permute-done((bf16[1024,384]{1,0:T(8,128)(2,1)S(1)}, bf16[1024,384]{1,0:T(8,128)(2,1)S(1)}, u32[]{:S(2)}, u32[]{:S(2)}) %collective-permute-start.5) | collective-permute-done | bytes 786464 | tf_op jit(solution)/shard_map/trade/ppermute | solution.py:212
  62.8 2.3 %shard_map.111.refs_2_.refs_4_ = bf16[448,384]{1,0:T(8,128)(2,1)S(1)} custom-call(bf16[112,1152]{1,0:T(8,128)(2,1)S(1)} %fusion.1.refs_0_, bf16[112,1152]{1,0:T(8,128)(2,1)S(1)} %collective-permute-done.refs_1_, bf16[112,1152]{1,0:T(8,128)(2,1)S(1)} %collective-permute-done.1.refs_2_.refs_0_, bf16[112,1152]{1,0:T(8,128)(2,1)S(1)} %collective-permute-done.2.refs_3_.refs_1_, ...), custom_call_target="tpu_custom_call" | custom-call | tf_op jit(solution)/shard_map/pallas_call | solution.py:123
  65.1 0.9 %collective-permute-done.7.refs_3_.came = bf16[384,512]{1,0:T(8,128)(2,1)S(1)} collective-permute-done((bf16[384,512]{1,0:T(8,128)(2,1)S(1)}, bf16[384,512]{1,0:T(8,128)(2,1)S(1)}, u32[]{:S(2)}, u32[]{:S(2)}) %collective-permute-start.7) | collective-permute-done | bytes 393248 | tf_op jit(solution)/shard_map/swap/ppermute | solution.py:199
  66.0 1.9 %collective-permute-start.14 = (bf16[1024,384]{1,0:T(8,128)(2,1)S(1)}, bf16[1024,384]{1,0:T(8,128)(2,1)S(1)}, u32[]{:S(2)}, u32[]{:S(2)}) collective-permute-start(bf16[1024,384]{1,0:T(8,128)(2,1)S(1)} %collective-permute-done.6.refs_7_.other), channel_id=1, source_target_pairs={{0,1},{1,0},{2,3},{3,2},{4,5},{5,4},{6,7},{7,6},{8,9},{9,8},{10,11... | collective-permute-start | bytes 2359304 | tf_op jit(solution)/shard_map/y_near/ppermute | solution.py:208
  67.9 0.7 collective-permute-start.13
  68.6 0.6 collective-permute-start.15
  69.2 1.5 %collective-permute-start.19 = (bf16[384,512]{1,0:T(8,128)(2,1)S(1)}, bf16[384,512]{1,0:T(8,128)(2,1)S(1)}, u32[]{:S(2)}, u32[]{:S(2)}) collective-permute-start(bf16[384,512]{1,0:T(8,128)(2,1)S(1)} %collective-permute-done.7.refs_3_.came), channel_id=1, source_target_pairs={{0,16},{16,0},{1,17},{17,1},{2,18},{18,2},{3,19},{19,3},{4,20},{20... | collective-permute-start | bytes 1179656 | tf_op jit(solution)/shard_map/trade/ppermute | solution.py:216
  70.8 1.2 %shard_map.114.refs_4_.refs_2_ = bf16[448,384]{1,0:T(8,128)(2,1)S(1)} custom-call(bf16[112,1152]{1,0:T(8,128)(2,1)S(1)} %fusion.1.refs_0_, bf16[112,1152]{1,0:T(8,128)(2,1)S(1)} %collective-permute-done.refs_1_, bf16[112,1152]{1,0:T(8,128)(2,1)S(1)} %collective-permute-done.1.refs_2_.refs_0_, bf16[112,1152]{1,0:T(8,128)(2,1)S(1)} %collective-permute-done.2.refs_3_.refs_1_, ...), custom_call_target="tpu_custom_call" | custom-call | tf_op jit(solution)/shard_map/pallas_call | solution.py:123
  72.0 0.9 %shard_map.116 = (bf16[112,512]{1,0:T(8,128)(2,1)S(1)}, bf16[112,512]{1,0:T(8,128)(2,1)S(1)}) custom-call(s32[16]{0:T(128)S(1)} %copy-done.4, bf16[112,1152]{1,0:T(8,128)(2,1)S(1)} %collective-permute-done.1.refs_2_.refs_0_, bf16[112,1152]{1,0:T(8,128)(2,1)S(1)} %collective-permute-done.2.refs_3_.refs_1_, bf16[448,384]{1,0:T(8,128)(2,1)S(1)} %shard_map.111.refs_2_.refs_4_, ...), custom_call_target="tpu_custom_call" | custom-call | tf_op jit(solution)/shard_map/pallas_call | solution.py:123
  72.9 2.7 %collective-permute-start.16 = (bf16[112,512]{1,0:T(8,128)(2,1)S(1)}, bf16[112,512]{1,0:T(8,128)(2,1)S(1)}, u32[]{:S(2)}, u32[]{:S(2)}) collective-permute-start(bf16[112,512]{1,0:T(8,128)(2,1)S(1)} %get-tuple-element.46), channel_id=1, source_target_pairs={{0,6},{1,7},{2,4},{3,5},{4,2},{5,3},{6,0},{7,1},{8,14},{9,15},{10,... | collective-permute-start | bytes 344072 | tf_op jit(solution)/shard_map/sums/ppermute | solution.py:199
  75.6 0.5 collective-permute-start.17
  76.1 0.9 %shard_map.115 = (f32[112,512]{1,0:T(8,128)S(1)}, bf16[112,512]{1,0:T(8,128)(2,1)S(1)}) custom-call(s32[16]{0:T(128)S(1)} %copy-done.4, bf16[112,1152]{1,0:T(8,128)(2,1)S(1)} %fusion.1.refs_0_, bf16[112,1152]{1,0:T(8,128)(2,1)S(1)} %collective-permute-done.refs_1_, bf16[448,384]{1,0:T(8,128)(2,1)S(1)} %shard_map.111.refs_2_.refs_4_, ...), custom_call_target="tpu_custom_call" | custom-call | tf_op jit(solution)/shard_map/pallas_call | solution.py:123
  77.1 0.6 copy-done.5
  77.8 2.1 %shard_map.118 = bf16[1024,384]{1,0:T(8,128)(2,1)} custom-call(s32[16]{0:T(128)S(1)} %copy-done.5, bf16[1024,384]{1,0:T(8,128)(2,1)S(1)} %bitcast.15, bf16[1024,384]{1,0:T(8,128)(2,1)} %collective-permute-done.4.refs_5_.came, bf16[1024,384]{1,0:T(8,128)(2,1)S(1)} %collective-permute-done.6.refs_7_.other), custom_call_target="tpu_custom_call" | custom-call | tf_op jit(solution)/shard_map/pallas_call | solution.py:173
  79.9 1.5 %shard_map.117 = bf16[1024,384]{1,0:T(8,128)(2,1)} custom-call(s32[16]{0:T(128)S(1)} %copy-done.5, bf16[1024,384]{1,0:T(8,128)(2,1)S(1)} %bitcast.20, bf16[1024,384]{1,0:T(8,128)(2,1)S(1)} %collective-permute-done.3.refs_4_.came, bf16[1024,384]{1,0:T(8,128)(2,1)S(1)} %collective-permute-done.5.refs_6_.other), custom_call_target="tpu_custom_call" | custom-call | tf_op jit(solution)/shard_map/pallas_call | solution.py:173
  81.5 1.4 %collective-permute-start.18 = (bf16[112,512]{1,0:T(8,128)(2,1)S(1)}, bf16[112,512]{1,0:T(8,128)(2,1)S(1)}, u32[]{:S(2)}, u32[]{:S(2)}) collective-permute-start(bf16[112,512]{1,0:T(8,128)(2,1)S(1)} %get-tuple-element.48), channel_id=1, source_target_pairs={{0,4},{1,5},{2,6},{3,7},{4,0},{5,1},{6,2},{7,3},{8,12},{9,13},{10,... | collective-permute-start | bytes 344072 | tf_op jit(solution)/shard_map/sums/ppermute | solution.py:199
  82.9 1.0 %shard_map.119 = (f32[112,512]{1,0:T(8,128)S(1)}, f32[112,512]{1,0:T(8,128)S(1)}, f32[112,512]{1,0:T(8,128)S(1)}, f32[112,512]{1,0:T(8,128)S(1)}) custom-call(s32[16]{0:T(128)S(1)} %copy-done.4, bf16[112,1152]{1,0:T(8,128)(2,1)S(1)} %fusion.1.refs_0_, bf16[112,1152]{1,0:T(8,128)(2,1)S(1)} %collective-permute-done.refs_1_, ...), custom_call_target="tpu_custom_call" | custom-call | tf_op jit(solution)/shard_map/pallas_call | solution.py:123
  83.9 0.8 shard_map.121
  84.7 1.7 %collective-permute-start.21 = (bf16[112,512]{1,0:T(8,128)(2,1)S(1)}, bf16[112,512]{1,0:T(8,128)(2,1)S(1)}, u32[]{:S(2)}, u32[]{:S(2)}) collective-permute-start(bf16[112,512]{1,0:T(8,128)(2,1)S(1)} %get-tuple-element.56), channel_id=1, source_target_pairs={{0,6},{1,7},{2,4},{3,5},{4,2},{5,3},{6,0},{7,1},{8,14},{9,15},{10,... | collective-permute-start | bytes 344072 | tf_op jit(solution)/shard_map/sums/ppermute | solution.py:199
  86.4 0.6 collective-permute-start.22
  87.0 0.8 shard_map.120
  87.8 1.4 %collective-permute-start.23 = (bf16[112,512]{1,0:T(8,128)(2,1)S(1)}, bf16[112,512]{1,0:T(8,128)(2,1)S(1)}, u32[]{:S(2)}, u32[]{:S(2)}) collective-permute-start(bf16[112,512]{1,0:T(8,128)(2,1)S(1)} %get-tuple-element.58), channel_id=1, source_target_pairs={{0,4},{1,5},{2,6},{3,7},{4,0},{5,1},{6,2},{7,3},{8,12},{9,13},{10,... | collective-permute-start | bytes 344072 | tf_op jit(solution)/shard_map/sums/ppermute | solution.py:199
  89.2 1.4 %shard_map.123 = bf16[384,1024]{1,0:T(8,128)(2,1)} custom-call(s32[16]{0:T(128)S(1)} %copy-done.5, bf16[384,1024]{1,0:T(8,128)(2,1)S(1)} %bitcast.10, bf16[384,512]{1,0:T(8,128)(2,1)S(1)} %collective-permute-done.7.refs_3_.came, bf16[384,512]{1,0:T(8,128)(2,1)S(1)} %collective-permute-done.19.refs_5_.other), custom_call_target="tpu_custom_call" | custom-call | tf_op jit(solution)/shard_map/pallas_call | solution.py:173
  90.6 0.4 collective-permute-done.21.refs_5_
  91.0 2.4 %collective-permute-done.22.refs_6_ = bf16[112,512]{1,0:T(8,128)(2,1)S(1)} collective-permute-done((bf16[112,512]{1,0:T(8,128)(2,1)S(1)}, bf16[112,512]{1,0:T(8,128)(2,1)S(1)}, u32[]{:S(2)}, u32[]{:S(2)}) %collective-permute-start.22) | collective-permute-done | bytes 114720 | tf_op jit(solution)/shard_map/sums/ppermute | solution.py:199
  93.4 0.8 shard_map.122
  (31 shorter events, 0.2 us)
Async XLA Ops:
  0.6 40.5 %collective-permute-start.3 = (bf16[1024,384]{1,0:T(8,128)(2,1)}, bf16[1024,384]{1,0:T(8,128)(2,1)S(1)}, u32[]{:S(2)}, u32[]{:S(2)}) collective-permute-start(bf16[1024,384]{1,0:T(8,128)(2,1)} %bitcast.16), channel_id=1, source_target_pairs={{0,8},{1,9},{2,10},{3,11},{4,12},{5,13},{6,14},{7,15},{8,0},{9,1},... | collective-permute-start | bytes 2359304 | tf_op jit(solution)/shard_map/swap/ppermute | solution.py:208
  6.6 31.2 %collective-permute-start.4 = (bf16[1024,384]{1,0:T(8,128)(2,1)}, bf16[1024,384]{1,0:T(8,128)(2,1)}, u32[]{:S(2)}, u32[]{:S(2)}) collective-permute-start(bf16[1024,384]{1,0:T(8,128)(2,1)} %bitcast.11), channel_id=1, source_target_pairs={{16,24},{17,25},{18,26},{19,27},{20,28},{21,29},{22,30},{23,31},{2... | collective-permute-start | bytes 2359304 | tf_op jit(solution)/shard_map/swap/ppermute | solution.py:208
  9.0 5.4 %copy-start = (bf16[1,384,1024]{2,1,0:T(8,128)(2,1)S(1)}, bf16[1,384,1024]{2,1,0:T(8,128)(2,1)}, u32[]{:S(2)}) copy-start(bf16[1,384,1024]{2,1,0:T(8,128)(2,1)} %param.13) | copy-start | bytes 2359300
  9.0 28.8 %copy-start.1 = (bf16[1,1024,384]{2,1,0:T(8,128)(2,1)S(1)}, bf16[1,1024,384]{2,1,0:T(8,128)(2,1)}, u32[]{:S(2)}) copy-start(bf16[1,1024,384]{2,1,0:T(8,128)(2,1)} %param.12) | copy-start | bytes 2359300
  10.1 19.0 %collective-permute-start = (bf16[112,1152]{1,0:T(8,128)(2,1)S(1)}, bf16[112,1152]{1,0:T(8,128)(2,1)S(1)}, u32[]{:S(2)}, u32[]{:S(2)}) collective-permute-start(bf16[112,1152]{1,0:T(8,128)(2,1)S(1)} %fusion.1.refs_0_), channel_id=1, source_target_pairs={{0,4},{1,5},{2,6},{3,7},{4,0},{5,1},{6,2},{7,3},{8,12},{9,13},{10,... | collective-permute-start | bytes 774152 | tf_op jit(solution)/shard_map/tokens/ppermute | solution.py:199
  11.8 17.4 %collective-permute-start.1 = (bf16[112,1152]{1,0:T(8,128)(2,1)S(1)}, bf16[112,1152]{1,0:T(8,128)(2,1)S(1)}, u32[]{:S(2)}, u32[]{:S(2)}) collective-permute-start(bf16[112,1152]{1,0:T(8,128)(2,1)S(1)} %fusion.1.refs_0_), channel_id=1, source_target_pairs={{0,2},{1,3},{2,0},{3,1},{4,6},{5,7},{6,4},{7,5},{8,10},{9,11},{10,... | collective-permute-start | bytes 774152 | tf_op jit(solution)/shard_map/tokens/ppermute | solution.py:199
  13.3 35.7 %copy-start.4 = (s32[16]{0:T(128)S(1)}, s32[16]{0:T(128)}, u32[]{:S(2)}) copy-start(s32[16]{0:T(128)} %placement.13) | copy-start | bytes 196
  14.4 32.4 %collective-permute-start.10 = (bf16[384,1024]{1,0:T(8,128)(2,1)S(1)}, bf16[384,1024]{1,0:T(8,128)(2,1)S(1)}, u32[]{:S(2)}, u32[]{:S(2)}) collective-permute-start(bf16[384,1024]{1,0:T(8,128)(2,1)S(1)} %bitcast.7), channel_id=1, source_target_pairs={{0,1},{1,0},{2,3},{3,2},{4,5},{5,4},{6,7},{7,6},{8,9},{9,8},{10,11... | collective-permute-start | bytes 2359304 | tf_op jit(solution)/shard_map/near/ppermute | solution.py:199
  29.1 17.8 %collective-permute-start.8 = (bf16[1024,384]{1,0:T(8,128)(2,1)}, bf16[1024,384]{1,0:T(8,128)(2,1)S(1)}, u32[]{:S(2)}, u32[]{:S(2)}) collective-permute-start(bf16[1024,384]{1,0:T(8,128)(2,1)} %bitcast.17), channel_id=1, source_target_pairs={{0,1},{1,0},{2,3},{3,2},{4,5},{5,4},{6,7},{7,6},{8,9},{9,8},{10,11... | collective-permute-start | bytes 2359304 | tf_op jit(solution)/shard_map/near/ppermute | solution.py:199
  29.2 8.6 %collective-permute-start.2 = (bf16[112,1152]{1,0:T(8,128)(2,1)S(1)}, bf16[112,1152]{1,0:T(8,128)(2,1)S(1)}, u32[]{:S(2)}, u32[]{:S(2)}) collective-permute-start(bf16[112,1152]{1,0:T(8,128)(2,1)S(1)} %collective-permute-done.refs_1_), channel_id=1, source_target_pairs={{0,2},{1,3},{2,0},{3,1},{4,6},{5,7},{6,4},{7,5},{8,10},{9,11},{10,... | collective-permute-start | bytes 774152 | tf_op jit(solution)/shard_map/tokens/ppermute | solution.py:199
  37.8 11.1 %collective-permute-start.9 = (bf16[1024,384]{1,0:T(8,128)(2,1)S(1)}, bf16[1024,384]{1,0:T(8,128)(2,1)S(1)}, u32[]{:S(2)}, u32[]{:S(2)}) collective-permute-start(bf16[1024,384]{1,0:T(8,128)(2,1)S(1)} %bitcast.12), channel_id=1, source_target_pairs={{0,1},{1,0},{2,3},{3,2},{4,5},{5,4},{6,7},{7,6},{8,9},{9,8},{10,11... | collective-permute-start | bytes 2359304 | tf_op jit(solution)/shard_map/near/ppermute | solution.py:199
  37.8 23.9 %collective-permute-start.6 = (bf16[1024,384]{1,0:T(8,128)(2,1)}, bf16[1024,384]{1,0:T(8,128)(2,1)S(1)}, u32[]{:S(2)}, u32[]{:S(2)}) collective-permute-start(bf16[1024,384]{1,0:T(8,128)(2,1)} %collective-permute-done.4.refs_5_.came), channel_id=1, source_target_pairs={{16,0},{17,1},{18,2},{19,3},{20,4},{21,5},{22,6},{23,7},{24,8},{25... | collective-permute-start | bytes 2359304 | tf_op jit(solution)/shard_map/trade/ppermute | solution.py:212
  41.2 21.6 %collective-permute-start.5 = (bf16[1024,384]{1,0:T(8,128)(2,1)S(1)}, bf16[1024,384]{1,0:T(8,128)(2,1)S(1)}, u32[]{:S(2)}, u32[]{:S(2)}) collective-permute-start(bf16[1024,384]{1,0:T(8,128)(2,1)S(1)} %collective-permute-done.3.refs_4_.came), channel_id=1, source_target_pairs={{0,16},{1,17},{2,18},{3,19},{4,20},{5,21},{6,22},{7,23},{8,24},{9,... | collective-permute-start | bytes 2359304 | tf_op jit(solution)/shard_map/trade/ppermute | solution.py:212
  46.9 19.1 %collective-permute-start.7 = (bf16[384,512]{1,0:T(8,128)(2,1)S(1)}, bf16[384,512]{1,0:T(8,128)(2,1)S(1)}, u32[]{:S(2)}, u32[]{:S(2)}) collective-permute-start(bf16[384,512]{1,0:T(8,128)(2,1)S(1)} %slice_select_fusion), channel_id=1, source_target_pairs={{0,8},{1,9},{2,10},{3,11},{4,12},{5,13},{6,14},{7,15},{8,0},{9,1},... | collective-permute-start | bytes 1179656 | tf_op jit(solution)/shard_map/swap/ppermute | solution.py:199
  47.0 22.2 %collective-permute-start.11 = (bf16[1024,384]{1,0:T(8,128)(2,1)S(1)}, bf16[1024,384]{1,0:T(8,128)(2,1)S(1)}, u32[]{:S(2)}, u32[]{:S(2)}) collective-permute-start(bf16[1024,384]{1,0:T(8,128)(2,1)S(1)} %collective-permute-done.3.refs_4_.came), channel_id=1, source_target_pairs={{0,1},{1,0},{2,3},{3,2},{4,5},{5,4},{6,7},{7,6},{8,9},{9,8},{10,11... | collective-permute-start | bytes 2359304 | tf_op jit(solution)/shard_map/z_near/ppermute | solution.py:208
  48.9 1.1 %copy-start.2 = (bf16[1,1024,384]{2,1,0:T(8,128)(2,1)S(1)}, bf16[1,1024,384]{2,1,0:T(8,128)(2,1)}, u32[]{:S(2)}) copy-start(bf16[1,1024,384]{2,1,0:T(8,128)(2,1)} %param.11) | copy-start | bytes 2359300
  54.8 16.0 %collective-permute-start.12 = (bf16[1024,384]{1,0:T(8,128)(2,1)}, bf16[1024,384]{1,0:T(8,128)(2,1)S(1)}, u32[]{:S(2)}, u32[]{:S(2)}) collective-permute-start(bf16[1024,384]{1,0:T(8,128)(2,1)} %collective-permute-done.4.refs_5_.came), channel_id=1, source_target_pairs={{16,17},{17,16},{18,19},{19,18},{20,21},{21,20},{22,23},{23,22},{2... | collective-permute-start | bytes 2359304 | tf_op jit(solution)/shard_map/z_near/ppermute | solution.py:208
  66.0 4.8 %collective-permute-start.14 = (bf16[1024,384]{1,0:T(8,128)(2,1)S(1)}, bf16[1024,384]{1,0:T(8,128)(2,1)S(1)}, u32[]{:S(2)}, u32[]{:S(2)}) collective-permute-start(bf16[1024,384]{1,0:T(8,128)(2,1)S(1)} %collective-permute-done.6.refs_7_.other), channel_id=1, source_target_pairs={{0,1},{1,0},{2,3},{3,2},{4,5},{5,4},{6,7},{7,6},{8,9},{9,8},{10,11... | collective-permute-start | bytes 2359304 | tf_op jit(solution)/shard_map/y_near/ppermute | solution.py:208
  67.9 2.8 %collective-permute-start.13 = (bf16[1024,384]{1,0:T(8,128)(2,1)S(1)}, bf16[1024,384]{1,0:T(8,128)(2,1)S(1)}, u32[]{:S(2)}, u32[]{:S(2)}) collective-permute-start(bf16[1024,384]{1,0:T(8,128)(2,1)S(1)} %collective-permute-done.5.refs_6_.other), channel_id=1, source_target_pairs={{16,17},{17,16},{18,19},{19,18},{20,21},{21,20},{22,23},{23,22},{2... | collective-permute-start | bytes 2359304 | tf_op jit(solution)/shard_map/y_near/ppermute | solution.py:208
  68.6 3.3 %collective-permute-start.15 = (bf16[384,512]{1,0:T(8,128)(2,1)S(1)}, bf16[384,512]{1,0:T(8,128)(2,1)S(1)}, u32[]{:S(2)}, u32[]{:S(2)}) collective-permute-start(bf16[384,512]{1,0:T(8,128)(2,1)S(1)} %collective-permute-done.7.refs_3_.came), channel_id=1, source_target_pairs={{0,1},{1,0},{2,3},{3,2},{4,5},{5,4},{6,7},{7,6},{8,9},{9,8},{10,11... | collective-permute-start | bytes 1179656 | tf_op jit(solution)/shard_map/z_near/ppermute | solution.py:199
  69.2 12.2 %collective-permute-start.19 = (bf16[384,512]{1,0:T(8,128)(2,1)S(1)}, bf16[384,512]{1,0:T(8,128)(2,1)S(1)}, u32[]{:S(2)}, u32[]{:S(2)}) collective-permute-start(bf16[384,512]{1,0:T(8,128)(2,1)S(1)} %collective-permute-done.7.refs_3_.came), channel_id=1, source_target_pairs={{0,16},{16,0},{1,17},{17,1},{2,18},{18,2},{3,19},{19,3},{4,20},{20... | collective-permute-start | bytes 1179656 | tf_op jit(solution)/shard_map/trade/ppermute | solution.py:216
  72.9 8.5 %collective-permute-start.16 = (bf16[112,512]{1,0:T(8,128)(2,1)S(1)}, bf16[112,512]{1,0:T(8,128)(2,1)S(1)}, u32[]{:S(2)}, u32[]{:S(2)}) collective-permute-start(bf16[112,512]{1,0:T(8,128)(2,1)S(1)} %get-tuple-element.46), channel_id=1, source_target_pairs={{0,6},{1,7},{2,4},{3,5},{4,2},{5,3},{6,0},{7,1},{8,14},{9,15},{10,... | collective-permute-start | bytes 344072 | tf_op jit(solution)/shard_map/sums/ppermute | solution.py:199
  75.6 5.8 %collective-permute-start.17 = (bf16[112,512]{1,0:T(8,128)(2,1)S(1)}, bf16[112,512]{1,0:T(8,128)(2,1)S(1)}, u32[]{:S(2)}, u32[]{:S(2)}) collective-permute-start(bf16[112,512]{1,0:T(8,128)(2,1)S(1)} %get-tuple-element.47), channel_id=1, source_target_pairs={{0,2},{1,3},{2,0},{3,1},{4,6},{5,7},{6,4},{7,5},{8,10},{9,11},{10,... | collective-permute-start | bytes 344072 | tf_op jit(solution)/shard_map/sums/ppermute | solution.py:199
  77.1 0.7 copy-start.5
  77.8 2.1 %copy-start.3 = (bf16[1,1024,384]{2,1,0:T(8,128)(2,1)S(1)}, bf16[1,1024,384]{2,1,0:T(8,128)(2,1)}, u32[]{:S(2)}) copy-start(bf16[1,1024,384]{2,1,0:T(8,128)(2,1)} %param.11) | copy-start | bytes 2359300
  81.4 2.5 %collective-permute-start.20 = (bf16[384,512]{1,0:T(8,128)(2,1)S(1)}, bf16[384,512]{1,0:T(8,128)(2,1)S(1)}, u32[]{:S(2)}, u32[]{:S(2)}) collective-permute-start(bf16[384,512]{1,0:T(8,128)(2,1)S(1)} %collective-permute-done.19.refs_5_.other), channel_id=1, source_target_pairs={{0,1},{1,0},{2,3},{3,2},{4,5},{5,4},{6,7},{7,6},{8,9},{9,8},{10,11... | collective-permute-start | bytes 1179656 | tf_op jit(solution)/shard_map/y_near/ppermute | solution.py:199
  81.5 9.1 %collective-permute-start.18 = (bf16[112,512]{1,0:T(8,128)(2,1)S(1)}, bf16[112,512]{1,0:T(8,128)(2,1)S(1)}, u32[]{:S(2)}, u32[]{:S(2)}) collective-permute-start(bf16[112,512]{1,0:T(8,128)(2,1)S(1)} %get-tuple-element.48), channel_id=1, source_target_pairs={{0,4},{1,5},{2,6},{3,7},{4,0},{5,1},{6,2},{7,3},{8,12},{9,13},{10,... | collective-permute-start | bytes 344072 | tf_op jit(solution)/shard_map/sums/ppermute | solution.py:199
  84.7 6.3 %collective-permute-start.21 = (bf16[112,512]{1,0:T(8,128)(2,1)S(1)}, bf16[112,512]{1,0:T(8,128)(2,1)S(1)}, u32[]{:S(2)}, u32[]{:S(2)}) collective-permute-start(bf16[112,512]{1,0:T(8,128)(2,1)S(1)} %get-tuple-element.56), channel_id=1, source_target_pairs={{0,6},{1,7},{2,4},{3,5},{4,2},{5,3},{6,0},{7,1},{8,14},{9,15},{10,... | collective-permute-start | bytes 344072 | tf_op jit(solution)/shard_map/sums/ppermute | solution.py:199
  86.4 7.0 %collective-permute-start.22 = (bf16[112,512]{1,0:T(8,128)(2,1)S(1)}, bf16[112,512]{1,0:T(8,128)(2,1)S(1)}, u32[]{:S(2)}, u32[]{:S(2)}) collective-permute-start(bf16[112,512]{1,0:T(8,128)(2,1)S(1)} %get-tuple-element.57), channel_id=1, source_target_pairs={{0,2},{1,3},{2,0},{3,1},{4,6},{5,7},{6,4},{7,5},{8,10},{9,11},{10,... | collective-permute-start | bytes 344072 | tf_op jit(solution)/shard_map/sums/ppermute | solution.py:199
  87.8 5.6 %collective-permute-start.23 = (bf16[112,512]{1,0:T(8,128)(2,1)S(1)}, bf16[112,512]{1,0:T(8,128)(2,1)S(1)}, u32[]{:S(2)}, u32[]{:S(2)}) collective-permute-start(bf16[112,512]{1,0:T(8,128)(2,1)S(1)} %get-tuple-element.58), channel_id=1, source_target_pairs={{0,4},{1,5},{2,6},{3,7},{4,0},{5,1},{6,2},{7,3},{8,12},{9,13},{10,... | collective-permute-start | bytes 344072 | tf_op jit(solution)/shard_map/sums/ppermute | solution.py:199

commit v12 on v10

--- a/solution.py
+++ b/solution.py
@@ -281,7 +281,7 @@
         store(0, depth, flags, own[1], z_upper, y_upper),
     ]
     ours = collect(parts)
-    landed = after(y_lower, stored, ours[1:-1])
+    landed = after(y_lower, stored, ours[1 : len(ours) // 2])
     y_near.append(send(landed, 1, "y_near"))
     everyone = tuple(range(len(rows)))
     last_sums = far_sums((0,), [landed], 1, everyone, near_sums, False)

time: 87 us -> 86.6 us (level)
  waiting for transfers between devices: 48 us -> 46.7 us
  starting transfers between devices: 19.1 us -> 20.1 us
    ppermute x18, waiting for transfers between devices: 34.9 us -> 32.9 us  [send(): return lax.ppermute(value, 'expert', [(d, d ^ bit) for d in range(count)])]
    ppermute x18, starting transfers between devices: 16.8 us -> 17.8 us  [send(): return lax.ppermute(value, 'expert', [(d, d ^ bit) for d in range(count)])]
  transfers between devices with their start and end apart: 20 -> 20, of which waited for: 10 -> 9; matrix products, arithmetic and copies ran while one was open for 0% -> 0% of each run, Pallas kernels for 18% -> 18%
where the time goes in v12:
time: 86.6 us; the launch traced here: 86.4 us
  waiting for transfers between devices  46.7 us (54%)
  starting transfers between devices  20.1 us (23%)
  Pallas kernels  16.7 us (19%)
  local copies, waits for them, and re-layouts  1.68 us (2%)
  between operations  0.94 us (1%)
    ppermute x18, waiting for transfers between devices, send(): return lax.ppermute(value, 'expert', [(d, d ^ bit) for d in range(count)])  32.9 us
    ppermute x18, starting transfers between devices, send(): return lax.ppermute(value, 'expert', [(d, d ^ bit) for d in range(count)])  17.8 us
    ppermute x2, waiting for transfers between devices, trade(): return lax.ppermute(value, 'dp', trades)  13.7 us
    pallas_call x10, Pallas kernels, call(): pl.pallas_call(kernel, out_shape=out_shape, in_specs=[smem] * scalars + [...  12.4 us
    pallas_call x3, Pallas kernels, store(): pl.pallas_call(functools.partial(store_kernel, axis, first), out_shape=ja...  4.34 us
    ppermute x2, starting transfers between devices, trade(): return lax.ppermute(value, 'dp', trades)  2.32 us
  transfers between devices with their start and end apart: 20, of which 9 were waited for; matrix products, arithmetic and copies ran while one was open for 0% of the time, Pallas kernels for 18%

profile of v12, /device:TPU:0, one launch (start us, length us, event | category | flops | bytes accessed | tf_op | source)
XLA Modules:
  0.0 86.4 jit_solution(15307077162140073496)
XLA Ops:
  0.6 1.5 %slice_bitcast_fusion = (bf16[512,384]{1,0:T(8,128)(2,1)S(1)}, bf16[512,384]{1,0:T(8,128)(2,1)S(1)}, bf16[512,384]{1,0:T(8,128)(2,1)S(1)}, bf16[512,384]{1,0:T(8,128)(2,1)S(1)}) fusion(bf16[1,1024,384]{2,1,0:T(8,128)(2,1)} %param.12, bf16[1,1024,384]{2,1,0:T(8,128)(2,1)} %param.11), kind=kLoop, calls=%fused_computation.4 | loop fusion | bytes 3145728 | tf_op jit(solution)/shard_map/slice | solution.py:211
  2.2 0.0 copy-start.6
  2.2 0.0 copy-start.7
  2.2 0.0 copy-start.5
  2.2 0.2 maximum_select_fusion
  2.4 4.1 %collective-permute-start.3 = (bf16[1024,384]{1,0:T(8,128)(2,1)S(1)}, bf16[1024,384]{1,0:T(8,128)(2,1)S(1)}, u32[]{:S(2)}, u32[]{:S(2)}) collective-permute-start(bf16[1024,384]{1,0:T(8,128)(2,1)S(1)} %maximum_select_fusion), channel_id=1, source_target_pairs={{0,8},{1,9},{2,10},{3,11},{4,12},{5,13},{6,14},{7,15},{8,0},{9,1},... | collective-permute-start | bytes 2359304 | tf_op jit(solution)/shard_map/swap/ppermute | solution.py:198
  6.6 0.1 copy.17
  6.7 0.0 copy-start.2
  6.8 1.6 %collective-permute-start = (bf16[112,1152]{1,0:T(8,128)(2,1)S(1)}, bf16[112,1152]{1,0:T(8,128)(2,1)S(1)}, u32[]{:S(2)}, u32[]{:S(2)}) collective-permute-start(bf16[112,1152]{1,0:T(8,128)(2,1)S(1)} %fusion.1.refs_0_), channel_id=1, source_target_pairs={{0,4},{1,5},{2,6},{3,7},{4,0},{5,1},{6,2},{7,3},{8,12},{9,13},{10,... | collective-permute-start | bytes 774152 | tf_op jit(solution)/shard_map/tokens/ppermute | solution.py:198
  8.4 1.5 %collective-permute-start.1 = (bf16[112,1152]{1,0:T(8,128)(2,1)S(1)}, bf16[112,1152]{1,0:T(8,128)(2,1)S(1)}, u32[]{:S(2)}, u32[]{:S(2)}) collective-permute-start(bf16[112,1152]{1,0:T(8,128)(2,1)S(1)} %fusion.1.refs_0_), channel_id=1, source_target_pairs={{0,2},{1,3},{2,0},{3,1},{4,6},{5,7},{6,4},{7,5},{8,10},{9,11},{10,... | collective-permute-start | bytes 774152 | tf_op jit(solution)/shard_map/tokens/ppermute | solution.py:198
  9.9 19.0 %collective-permute-done.refs_1_ = bf16[112,1152]{1,0:T(8,128)(2,1)S(1)} collective-permute-done((bf16[112,1152]{1,0:T(8,128)(2,1)S(1)}, bf16[112,1152]{1,0:T(8,128)(2,1)S(1)}, u32[]{:S(2)}, u32[]{:S(2)}) %collective-permute-start) | collective-permute-done | bytes 258080 | tf_op jit(solution)/shard_map/tokens/ppermute | solution.py:198
  28.9 1.5 %collective-permute-start.2 = (bf16[112,1152]{1,0:T(8,128)(2,1)S(1)}, bf16[112,1152]{1,0:T(8,128)(2,1)S(1)}, u32[]{:S(2)}, u32[]{:S(2)}) collective-permute-start(bf16[112,1152]{1,0:T(8,128)(2,1)S(1)} %collective-permute-done.refs_1_), channel_id=1, source_target_pairs={{0,2},{1,3},{2,0},{3,1},{4,6},{5,7},{6,4},{7,5},{8,10},{9,11},{10,... | collective-permute-start | bytes 774152 | tf_op jit(solution)/shard_map/tokens/ppermute | solution.py:198
  30.4 0.1 collective-permute-start.8
  30.5 0.5 collective-permute-start.6
  31.0 0.1 collective-permute-start.7
  31.1 4.9 %collective-permute-done.2.refs_3_.refs_1_ = bf16[112,1152]{1,0:T(8,128)(2,1)S(1)} collective-permute-done((bf16[112,1152]{1,0:T(8,128)(2,1)S(1)}, bf16[112,1152]{1,0:T(8,128)(2,1)S(1)}, u32[]{:S(2)}, u32[]{:S(2)}) %collective-permute-start.2) | collective-permute-done | bytes 258080 | tf_op jit(solution)/shard_map/tokens/ppermute | solution.py:198
  36.0 4.9 %collective-permute-done.3.refs_4_.came = bf16[1024,384]{1,0:T(8,128)(2,1)S(1)} collective-permute-done((bf16[1024,384]{1,0:T(8,128)(2,1)S(1)}, bf16[1024,384]{1,0:T(8,128)(2,1)S(1)}, u32[]{:S(2)}, u32[]{:S(2)}) %collective-permute-start.3) | collective-permute-done | bytes 786464 | tf_op jit(solution)/shard_map/swap/ppermute | solution.py:198
  40.9 1.6 %collective-permute-start.4 = (bf16[1024,384]{1,0:T(8,128)(2,1)S(1)}, bf16[1024,384]{1,0:T(8,128)(2,1)S(1)}, u32[]{:S(2)}, u32[]{:S(2)}) collective-permute-start(bf16[1024,384]{1,0:T(8,128)(2,1)S(1)} %collective-permute-done.3.refs_4_.came), channel_id=1, source_target_pairs={{0,16},{16,0},{1,17},{17,1},{2,18},{18,2},{3,19},{19,3},{4,20},{20... | collective-permute-start | bytes 2359304 | tf_op jit(solution)/shard_map/trade/ppermute | solution.py:202
  42.5 2.3 %shard_map.113 = (f32[112,1024]{1,0:T(8,128)S(1)}, f32[112,1024]{1,0:T(8,128)S(1)}) custom-call(s32[16]{0:T(128)S(1)} %copy-done.3, bf16[112,1152]{1,0:T(8,128)(2,1)S(1)} %collective-permute-done.1.refs_2_.refs_0_, bf16[112,1152]{1,0:T(8,128)(2,1)S(1)} %collective-permute-done.2.refs_3_.refs_1_, bf16[1024,384]{1,0:T(8,128)(2,1)S(1)} %bitcast.24, ...), custom_call_target="tpu_custom_call" | custom-call | tf_op jit(solution)/shard_map/pallas_call | solution.py:122
  44.9 2.3 %shard_map.112 = (f32[112,1024]{1,0:T(8,128)S(1)}, f32[112,1024]{1,0:T(8,128)S(1)}) custom-call(s32[16]{0:T(128)S(1)} %copy-done.3, bf16[112,1152]{1,0:T(8,128)(2,1)S(1)} %fusion.1.refs_0_, bf16[112,1152]{1,0:T(8,128)(2,1)S(1)} %collective-permute-done.refs_1_, bf16[1024,384]{1,0:T(8,128)(2,1)S(1)} %bitcast.25, bf16[1024,384]{1,0:T(8,128)(2,1)S(1)} %bitcast.21, ...), custom_call_target="tpu_custom_call" | custom-call | tf_op jit(solution)/shard_map/pallas_call | solution.py:122
  47.2 0.1 collective-permute-start.9
  47.3 12.4 %collective-permute-done.4.refs_5_.other = bf16[1024,384]{1,0:T(8,128)(2,1)S(1)} collective-permute-done((bf16[1024,384]{1,0:T(8,128)(2,1)S(1)}, bf16[1024,384]{1,0:T(8,128)(2,1)S(1)}, u32[]{:S(2)}, u32[]{:S(2)}) %collective-permute-start.4) | collective-permute-done | bytes 786464 | tf_op jit(solution)/shard_map/trade/ppermute | solution.py:202
  59.6 1.2 %shard_map.111.refs_2_.refs_4_ = bf16[448,384]{1,0:T(8,128)(2,1)S(1)} custom-call(bf16[112,1152]{1,0:T(8,128)(2,1)S(1)} %fusion.1.refs_0_, bf16[112,1152]{1,0:T(8,128)(2,1)S(1)} %collective-permute-done.refs_1_, bf16[112,1152]{1,0:T(8,128)(2,1)S(1)} %collective-permute-done.1.refs_2_.refs_0_, bf16[112,1152]{1,0:T(8,128)(2,1)S(1)} %collective-permute-done.2.refs_3_.refs_1_, ...), custom_call_target="tpu_custom_call" | custom-call | tf_op jit(solution)/shard_map/pallas_call | solution.py:122
  60.8 0.7 collective-permute-done.5.refs_3_.came
  61.5 0.5 collective-permute-start.11
  62.1 0.8 collective-permute-start.15
  62.8 1.0 %collective-permute-done.10.refs_5_ = bf16[1024,384]{1,0:T(8,128)(2,1)S(1)} collective-permute-done((bf16[1024,384]{1,0:T(8,128)(2,1)S(1)}, bf16[1024,384]{1,0:T(8,128)(2,1)S(1)}, u32[]{:S(2)}, u32[]{:S(2)}) %collective-permute-start.10) | collective-permute-done | bytes 786464 | tf_op jit(solution)/shard_map/y_near/ppermute | solution.py:198
  63.8 1.2 %shard_map.114.refs_4_.refs_2_ = bf16[448,384]{1,0:T(8,128)(2,1)S(1)} custom-call(bf16[112,1152]{1,0:T(8,128)(2,1)S(1)} %fusion.1.refs_0_, bf16[112,1152]{1,0:T(8,128)(2,1)S(1)} %collective-permute-done.refs_1_, bf16[112,1152]{1,0:T(8,128)(2,1)S(1)} %collective-permute-done.1.refs_2_.refs_0_, bf16[112,1152]{1,0:T(8,128)(2,1)S(1)} %collective-permute-done.2.refs_3_.refs_1_, ...), custom_call_target="tpu_custom_call" | custom-call | tf_op jit(solution)/shard_map/pallas_call | solution.py:122
  65.0 1.0 %shard_map.116 = (bf16[112,512]{1,0:T(8,128)(2,1)S(1)}, bf16[112,512]{1,0:T(8,128)(2,1)S(1)}) custom-call(s32[16]{0:T(128)S(1)} %copy-done.3, bf16[112,1152]{1,0:T(8,128)(2,1)S(1)} %collective-permute-done.1.refs_2_.refs_0_, bf16[112,1152]{1,0:T(8,128)(2,1)S(1)} %collective-permute-done.2.refs_3_.refs_1_, bf16[448,384]{1,0:T(8,128)(2,1)S(1)} %shard_map.111.refs_2_.refs_4_, ...), custom_call_target="tpu_custom_call" | custom-call | tf_op jit(solution)/shard_map/pallas_call | solution.py:122
  66.0 0.0 copy-start.4
  66.0 1.8 %collective-permute-start.12 = (bf16[112,512]{1,0:T(8,128)(2,1)S(1)}, bf16[112,512]{1,0:T(8,128)(2,1)S(1)}, u32[]{:S(2)}, u32[]{:S(2)}) collective-permute-start(bf16[112,512]{1,0:T(8,128)(2,1)S(1)} %get-tuple-element.42), channel_id=1, source_target_pairs={{0,6},{1,7},{2,4},{3,5},{4,2},{5,3},{6,0},{7,1},{8,14},{9,15},{10,... | collective-permute-start | bytes 344072 | tf_op jit(solution)/shard_map/sums/ppermute | solution.py:198
  67.8 0.9 %shard_map.115 = (f32[112,512]{1,0:T(8,128)S(1)}, bf16[112,512]{1,0:T(8,128)(2,1)S(1)}) custom-call(s32[16]{0:T(128)S(1)} %copy-done.3, bf16[112,1152]{1,0:T(8,128)(2,1)S(1)} %fusion.1.refs_0_, bf16[112,1152]{1,0:T(8,128)(2,1)S(1)} %collective-permute-done.refs_1_, bf16[448,384]{1,0:T(8,128)(2,1)S(1)} %shard_map.111.refs_2_.refs_4_, ...), custom_call_target="tpu_custom_call" | custom-call | tf_op jit(solution)/shard_map/pallas_call | solution.py:122
  68.8 1.4 %shard_map.118 = bf16[1024,384]{1,0:T(8,128)(2,1)} custom-call(s32[16]{0:T(128)S(1)} %copy-done.4, bf16[1024,384]{1,0:T(8,128)(2,1)S(1)} %bitcast.22, bf16[1024,384]{1,0:T(8,128)(2,1)S(1)} %collective-permute-done.3.refs_4_.came, bf16[1024,384]{1,0:T(8,128)(2,1)S(1)} %collective-permute-done.4.refs_5_.other), custom_call_target="tpu_custom_call" | custom-call | tf_op jit(solution)/shard_map/pallas_call | solution.py:172
  70.3 1.4 %shard_map.117 = bf16[1024,384]{1,0:T(8,128)(2,1)} custom-call(s32[16]{0:T(128)S(1)} %copy-done.4, bf16[1024,384]{1,0:T(8,128)(2,1)S(1)} %bitcast.26, bf16[1024,384]{1,0:T(8,128)(2,1)S(1)} %collective-permute-done.3.refs_4_.came, bf16[1024,384]{1,0:T(8,128)(2,1)S(1)} %collective-permute-done.4.refs_5_.other), custom_call_target="tpu_custom_call" | custom-call | tf_op jit(solution)/shard_map/pallas_call | solution.py:172
  71.7 1.4 %collective-permute-done.15.refs_5_.other = bf16[384,512]{1,0:T(8,128)(2,1)S(1)} collective-permute-done((bf16[384,512]{1,0:T(8,128)(2,1)S(1)}, bf16[384,512]{1,0:T(8,128)(2,1)S(1)}, u32[]{:S(2)}, u32[]{:S(2)}) %collective-permute-start.15) | collective-permute-done | bytes 393248 | tf_op jit(solution)/shard_map/trade/ppermute | solution.py:202
  73.1 1.5 %collective-permute-start.13 = (bf16[112,512]{1,0:T(8,128)(2,1)S(1)}, bf16[112,512]{1,0:T(8,128)(2,1)S(1)}, u32[]{:S(2)}, u32[]{:S(2)}) collective-permute-start(bf16[112,512]{1,0:T(8,128)(2,1)S(1)} %get-tuple-element.43), channel_id=1, source_target_pairs={{0,2},{1,3},{2,0},{3,1},{4,6},{5,7},{6,4},{7,5},{8,10},{9,11},{10,... | collective-permute-start | bytes 344072 | tf_op jit(solution)/shard_map/sums/ppermute | solution.py:198
  74.6 0.9 %collective-permute-start.14 = (bf16[112,512]{1,0:T(8,128)(2,1)S(1)}, bf16[112,512]{1,0:T(8,128)(2,1)S(1)}, u32[]{:S(2)}, u32[]{:S(2)}) collective-permute-start(bf16[112,512]{1,0:T(8,128)(2,1)S(1)} %get-tuple-element.44), channel_id=1, source_target_pairs={{0,4},{1,5},{2,6},{3,7},{4,0},{5,1},{6,2},{7,3},{8,12},{9,13},{10,... | collective-permute-start | bytes 344072 | tf_op jit(solution)/shard_map/sums/ppermute | solution.py:198
  75.5 0.9 %shard_map.119 = (f32[112,512]{1,0:T(8,128)S(1)}, f32[112,512]{1,0:T(8,128)S(1)}, f32[112,512]{1,0:T(8,128)S(1)}, f32[112,512]{1,0:T(8,128)S(1)}) custom-call(s32[16]{0:T(128)S(1)} %copy-done.3, bf16[112,1152]{1,0:T(8,128)(2,1)S(1)} %fusion.1.refs_0_, bf16[112,1152]{1,0:T(8,128)(2,1)S(1)} %collective-permute-done.refs_1_, ...), custom_call_target="tpu_custom_call" | custom-call | tf_op jit(solution)/shard_map/pallas_call | solution.py:122
  76.5 0.8 shard_map.121
  77.3 1.1 %collective-permute-start.17 = (bf16[112,512]{1,0:T(8,128)(2,1)S(1)}, bf16[112,512]{1,0:T(8,128)(2,1)S(1)}, u32[]{:S(2)}, u32[]{:S(2)}) collective-permute-start(bf16[112,512]{1,0:T(8,128)(2,1)S(1)} %get-tuple-element.52), channel_id=1, source_target_pairs={{0,6},{1,7},{2,4},{3,5},{4,2},{5,3},{6,0},{7,1},{8,14},{9,15},{10,... | collective-permute-start | bytes 344072 | tf_op jit(solution)/shard_map/sums/ppermute | solution.py:198
  78.4 1.5 %collective-permute-start.18 = (bf16[112,512]{1,0:T(8,128)(2,1)S(1)}, bf16[112,512]{1,0:T(8,128)(2,1)S(1)}, u32[]{:S(2)}, u32[]{:S(2)}) collective-permute-start(bf16[112,512]{1,0:T(8,128)(2,1)S(1)} %get-tuple-element.53), channel_id=1, source_target_pairs={{0,2},{1,3},{2,0},{3,1},{4,6},{5,7},{6,4},{7,5},{8,10},{9,11},{10,... | collective-permute-start | bytes 344072 | tf_op jit(solution)/shard_map/sums/ppermute | solution.py:198
  79.9 0.8 shard_map.120
  80.8 1.0 %collective-permute-start.19 = (bf16[112,512]{1,0:T(8,128)(2,1)S(1)}, bf16[112,512]{1,0:T(8,128)(2,1)S(1)}, u32[]{:S(2)}, u32[]{:S(2)}) collective-permute-start(bf16[112,512]{1,0:T(8,128)(2,1)S(1)} %get-tuple-element.54), channel_id=1, source_target_pairs={{0,4},{1,5},{2,6},{3,7},{4,0},{5,1},{6,2},{7,3},{8,12},{9,13},{10,... | collective-permute-start | bytes 344072 | tf_op jit(solution)/shard_map/sums/ppermute | solution.py:198
  81.8 1.4 %shard_map.123 = bf16[384,1024]{1,0:T(8,128)(2,1)} custom-call(s32[16]{0:T(128)S(1)} %copy-done.4, bf16[384,1024]{1,0:T(8,128)(2,1)S(1)} %bitcast.18, bf16[384,512]{1,0:T(8,128)(2,1)S(1)} %collective-permute-done.5.refs_3_.came, bf16[384,512]{1,0:T(8,128)(2,1)S(1)} %collective-permute-done.15.refs_5_.other), custom_call_target="tpu_custom_call" | custom-call | tf_op jit(solution)/shard_map/pallas_call | solution.py:172
  83.2 0.6 collective-permute-done.17.refs_5_
  83.8 1.8 %collective-permute-done.18.refs_6_ = bf16[112,512]{1,0:T(8,128)(2,1)S(1)} collective-permute-done((bf16[112,512]{1,0:T(8,128)(2,1)S(1)}, bf16[112,512]{1,0:T(8,128)(2,1)S(1)}, u32[]{:S(2)}, u32[]{:S(2)}) %collective-permute-start.18) | collective-permute-done | bytes 114720 | tf_op jit(solution)/shard_map/sums/ppermute | solution.py:198
  85.6 0.0 collective-permute-done.19.refs_7_
  85.6 0.8 shard_map.122
  (29 shorter events, 0.2 us)
Async XLA Ops:
  2.2 4.4 %copy-start.6 = (f32[112,8]{0,1:T(8,128)S(1)}, f32[112,8]{0,1:T(8,128)}, u32[]{:S(2)}) copy-start(f32[112,8]{0,1:T(8,128)} %param.10) | copy-start | bytes 10756
  2.2 4.4 %copy-start.7 = (s32[112,8]{0,1:T(8,128)S(1)}, s32[112,8]{0,1:T(8,128)}, u32[]{:S(2)}) copy-start(s32[112,8]{0,1:T(8,128)} %param.9) | copy-start | bytes 10756
  2.2 4.5 %copy-start.5 = (bf16[112,1024]{1,0:T(8,128)(2,1)S(1)}, bf16[112,1024]{1,0:T(8,128)(2,1)}, u32[]{:S(2)}) copy-start(bf16[112,1024]{1,0:T(8,128)(2,1)} %param.8) | copy-start | bytes 688132
  2.2 28.2 %copy-start = (bf16[1,384,1024]{2,1,0:T(8,128)(2,1)S(1)}, bf16[1,384,1024]{2,1,0:T(8,128)(2,1)}, u32[]{:S(2)}) copy-start(bf16[1,384,1024]{2,1,0:T(8,128)(2,1)} %param.13) | copy-start | bytes 2359300
  2.4 38.5 %collective-permute-start.3 = (bf16[1024,384]{1,0:T(8,128)(2,1)S(1)}, bf16[1024,384]{1,0:T(8,128)(2,1)S(1)}, u32[]{:S(2)}, u32[]{:S(2)}) collective-permute-start(bf16[1024,384]{1,0:T(8,128)(2,1)S(1)} %maximum_select_fusion), channel_id=1, source_target_pairs={{0,8},{1,9},{2,10},{3,11},{4,12},{5,13},{6,14},{7,15},{8,0},{9,1},... | collective-permute-start | bytes 2359304 | tf_op jit(solution)/shard_map/swap/ppermute | solution.py:198
  6.7 23.8 %copy-start.2 = (bf16[1,1024,384]{2,1,0:T(8,128)(2,1)S(1)}, bf16[1,1024,384]{2,1,0:T(8,128)(2,1)}, u32[]{:S(2)}) copy-start(bf16[1,1024,384]{2,1,0:T(8,128)(2,1)} %param.11) | copy-start | bytes 2359300
  6.7 24.3 %copy-start.1 = (bf16[1,1024,384]{2,1,0:T(8,128)(2,1)S(1)}, bf16[1,1024,384]{2,1,0:T(8,128)(2,1)}, u32[]{:S(2)}) copy-start(bf16[1,1024,384]{2,1,0:T(8,128)(2,1)} %param.12) | copy-start | bytes 2359300
  6.7 35.8 %copy-start.3 = (s32[16]{0:T(128)S(1)}, s32[16]{0:T(128)}, u32[]{:S(2)}) copy-start(s32[16]{0:T(128)} %placement.13) | copy-start | bytes 196
  6.8 22.1 %collective-permute-start = (bf16[112,1152]{1,0:T(8,128)(2,1)S(1)}, bf16[112,1152]{1,0:T(8,128)(2,1)S(1)}, u32[]{:S(2)}, u32[]{:S(2)}) collective-permute-start(bf16[112,1152]{1,0:T(8,128)(2,1)S(1)} %fusion.1.refs_0_), channel_id=1, source_target_pairs={{0,4},{1,5},{2,6},{3,7},{4,0},{5,1},{6,2},{7,3},{8,12},{9,13},{10,... | collective-permute-start | bytes 774152 | tf_op jit(solution)/shard_map/tokens/ppermute | solution.py:198
  8.4 22.6 %collective-permute-start.1 = (bf16[112,1152]{1,0:T(8,128)(2,1)S(1)}, bf16[112,1152]{1,0:T(8,128)(2,1)S(1)}, u32[]{:S(2)}, u32[]{:S(2)}) collective-permute-start(bf16[112,1152]{1,0:T(8,128)(2,1)S(1)} %fusion.1.refs_0_), channel_id=1, source_target_pairs={{0,2},{1,3},{2,0},{3,1},{4,6},{5,7},{6,4},{7,5},{8,10},{9,11},{10,... | collective-permute-start | bytes 774152 | tf_op jit(solution)/shard_map/tokens/ppermute | solution.py:198
  28.9 7.1 %collective-permute-start.2 = (bf16[112,1152]{1,0:T(8,128)(2,1)S(1)}, bf16[112,1152]{1,0:T(8,128)(2,1)S(1)}, u32[]{:S(2)}, u32[]{:S(2)}) collective-permute-start(bf16[112,1152]{1,0:T(8,128)(2,1)S(1)} %collective-permute-done.refs_1_), channel_id=1, source_target_pairs={{0,2},{1,3},{2,0},{3,1},{4,6},{5,7},{6,4},{7,5},{8,10},{9,11},{10,... | collective-permute-start | bytes 774152 | tf_op jit(solution)/shard_map/tokens/ppermute | solution.py:198
  30.4 12.1 %collective-permute-start.8 = (bf16[384,1024]{1,0:T(8,128)(2,1)S(1)}, bf16[384,1024]{1,0:T(8,128)(2,1)S(1)}, u32[]{:S(2)}, u32[]{:S(2)}) collective-permute-start(bf16[384,1024]{1,0:T(8,128)(2,1)S(1)} %bitcast.15), channel_id=1, source_target_pairs={{0,1},{1,0},{2,3},{3,2},{4,5},{5,4},{6,7},{7,6},{8,9},{9,8},{10,11... | collective-permute-start | bytes 2359304 | tf_op jit(solution)/shard_map/near/ppermute | solution.py:198
  30.5 12.0 %collective-permute-start.6 = (bf16[1024,384]{1,0:T(8,128)(2,1)S(1)}, bf16[1024,384]{1,0:T(8,128)(2,1)S(1)}, u32[]{:S(2)}, u32[]{:S(2)}) collective-permute-start(bf16[1024,384]{1,0:T(8,128)(2,1)S(1)} %bitcast.23), channel_id=1, source_target_pairs={{0,1},{1,0},{2,3},{3,2},{4,5},{5,4},{6,7},{7,6},{8,9},{9,8},{10,11... | collective-permute-start | bytes 2359304 | tf_op jit(solution)/shard_map/near/ppermute | solution.py:198
  31.0 11.5 %collective-permute-start.7 = (bf16[1024,384]{1,0:T(8,128)(2,1)S(1)}, bf16[1024,384]{1,0:T(8,128)(2,1)S(1)}, u32[]{:S(2)}, u32[]{:S(2)}) collective-permute-start(bf16[1024,384]{1,0:T(8,128)(2,1)S(1)} %bitcast.19), channel_id=1, source_target_pairs={{0,1},{1,0},{2,3},{3,2},{4,5},{5,4},{6,7},{7,6},{8,9},{9,8},{10,11... | collective-permute-start | bytes 2359304 | tf_op jit(solution)/shard_map/near/ppermute | solution.py:198
  40.9 18.7 %collective-permute-start.4 = (bf16[1024,384]{1,0:T(8,128)(2,1)S(1)}, bf16[1024,384]{1,0:T(8,128)(2,1)S(1)}, u32[]{:S(2)}, u32[]{:S(2)}) collective-permute-start(bf16[1024,384]{1,0:T(8,128)(2,1)S(1)} %collective-permute-done.3.refs_4_.came), channel_id=1, source_target_pairs={{0,16},{16,0},{1,17},{17,1},{2,18},{18,2},{3,19},{19,3},{4,20},{20... | collective-permute-start | bytes 2359304 | tf_op jit(solution)/shard_map/trade/ppermute | solution.py:202
  42.5 19.1 %collective-permute-start.5 = (bf16[384,512]{1,0:T(8,128)(2,1)S(1)}, bf16[384,512]{1,0:T(8,128)(2,1)S(1)}, u32[]{:S(2)}, u32[]{:S(2)}) collective-permute-start(bf16[384,512]{1,0:T(8,128)(2,1)S(1)} %slice_select_fusion), channel_id=1, source_target_pairs={{0,8},{1,9},{2,10},{3,11},{4,12},{5,13},{6,14},{7,15},{8,0},{9,1},... | collective-permute-start | bytes 1179656 | tf_op jit(solution)/shard_map/swap/ppermute | solution.py:198
  47.2 15.6 %collective-permute-start.9 = (bf16[1024,384]{1,0:T(8,128)(2,1)S(1)}, bf16[1024,384]{1,0:T(8,128)(2,1)S(1)}, u32[]{:S(2)}, u32[]{:S(2)}) collective-permute-start(bf16[1024,384]{1,0:T(8,128)(2,1)S(1)} %collective-permute-done.3.refs_4_.came), channel_id=1, source_target_pairs={{0,1},{1,0},{2,3},{3,2},{4,5},{5,4},{6,7},{7,6},{8,9},{9,8},{10,11... | collective-permute-start | bytes 2359304 | tf_op jit(solution)/shard_map/z_near/ppermute | solution.py:198
  61.5 2.3 %collective-permute-start.10 = (bf16[1024,384]{1,0:T(8,128)(2,1)S(1)}, bf16[1024,384]{1,0:T(8,128)(2,1)S(1)}, u32[]{:S(2)}, u32[]{:S(2)}) collective-permute-start(bf16[1024,384]{1,0:T(8,128)(2,1)S(1)} %collective-permute-done.4.refs_5_.other), channel_id=1, source_target_pairs={{0,1},{1,0},{2,3},{3,2},{4,5},{5,4},{6,7},{7,6},{8,9},{9,8},{10,11... | collective-permute-start | bytes 2359304 | tf_op jit(solution)/shard_map/y_near/ppermute | solution.py:198
  61.5 3.5 %collective-permute-start.11 = (bf16[384,512]{1,0:T(8,128)(2,1)S(1)}, bf16[384,512]{1,0:T(8,128)(2,1)S(1)}, u32[]{:S(2)}, u32[]{:S(2)}) collective-permute-start(bf16[384,512]{1,0:T(8,128)(2,1)S(1)} %collective-permute-done.5.refs_3_.came), channel_id=1, source_target_pairs={{0,1},{1,0},{2,3},{3,2},{4,5},{5,4},{6,7},{7,6},{8,9},{9,8},{10,11... | collective-permute-start | bytes 1179656 | tf_op jit(solution)/shard_map/z_near/ppermute | solution.py:198
  62.1 11.0 %collective-permute-start.15 = (bf16[384,512]{1,0:T(8,128)(2,1)S(1)}, bf16[384,512]{1,0:T(8,128)(2,1)S(1)}, u32[]{:S(2)}, u32[]{:S(2)}) collective-permute-start(bf16[384,512]{1,0:T(8,128)(2,1)S(1)} %collective-permute-done.5.refs_3_.came), channel_id=1, source_target_pairs={{0,16},{16,0},{1,17},{17,1},{2,18},{18,2},{3,19},{19,3},{4,20},{20... | collective-permute-start | bytes 1179656 | tf_op jit(solution)/shard_map/trade/ppermute | solution.py:202
  66.0 2.8 %copy-start.4 = (s32[16]{0:T(128)S(1)}, s32[16]{0:T(128)}, u32[]{:S(2)}) copy-start(s32[16]{0:T(128)} %flags.2) | copy-start | bytes 196
  66.0 7.1 %collective-permute-start.12 = (bf16[112,512]{1,0:T(8,128)(2,1)S(1)}, bf16[112,512]{1,0:T(8,128)(2,1)S(1)}, u32[]{:S(2)}, u32[]{:S(2)}) collective-permute-start(bf16[112,512]{1,0:T(8,128)(2,1)S(1)} %get-tuple-element.42), channel_id=1, source_target_pairs={{0,6},{1,7},{2,4},{3,5},{4,2},{5,3},{6,0},{7,1},{8,14},{9,15},{10,... | collective-permute-start | bytes 344072 | tf_op jit(solution)/shard_map/sums/ppermute | solution.py:198
  73.1 3.4 %collective-permute-start.16 = (bf16[384,512]{1,0:T(8,128)(2,1)S(1)}, bf16[384,512]{1,0:T(8,128)(2,1)S(1)}, u32[]{:S(2)}, u32[]{:S(2)}) collective-permute-start(bf16[384,512]{1,0:T(8,128)(2,1)S(1)} %collective-permute-done.15.refs_5_.other), channel_id=1, source_target_pairs={{0,1},{1,0},{2,3},{3,2},{4,5},{5,4},{6,7},{7,6},{8,9},{9,8},{10,11... | collective-permute-start | bytes 1179656 | tf_op jit(solution)/shard_map/y_near/ppermute | solution.py:198
  73.1 10.1 %collective-permute-start.13 = (bf16[112,512]{1,0:T(8,128)(2,1)S(1)}, bf16[112,512]{1,0:T(8,128)(2,1)S(1)}, u32[]{:S(2)}, u32[]{:S(2)}) collective-permute-start(bf16[112,512]{1,0:T(8,128)(2,1)S(1)} %get-tuple-element.43), channel_id=1, source_target_pairs={{0,2},{1,3},{2,0},{3,1},{4,6},{5,7},{6,4},{7,5},{8,10},{9,11},{10,... | collective-permute-start | bytes 344072 | tf_op jit(solution)/shard_map/sums/ppermute | solution.py:198
  74.6 8.6 %collective-permute-start.14 = (bf16[112,512]{1,0:T(8,128)(2,1)S(1)}, bf16[112,512]{1,0:T(8,128)(2,1)S(1)}, u32[]{:S(2)}, u32[]{:S(2)}) collective-permute-start(bf16[112,512]{1,0:T(8,128)(2,1)S(1)} %get-tuple-element.44), channel_id=1, source_target_pairs={{0,4},{1,5},{2,6},{3,7},{4,0},{5,1},{6,2},{7,3},{8,12},{9,13},{10,... | collective-permute-start | bytes 344072 | tf_op jit(solution)/shard_map/sums/ppermute | solution.py:198
  77.3 6.5 %collective-permute-start.17 = (bf16[112,512]{1,0:T(8,128)(2,1)S(1)}, bf16[112,512]{1,0:T(8,128)(2,1)S(1)}, u32[]{:S(2)}, u32[]{:S(2)}) collective-permute-start(bf16[112,512]{1,0:T(8,128)(2,1)S(1)} %get-tuple-element.52), channel_id=1, source_target_pairs={{0,6},{1,7},{2,4},{3,5},{4,2},{5,3},{6,0},{7,1},{8,14},{9,15},{10,... | collective-permute-start | bytes 344072 | tf_op jit(solution)/shard_map/sums/ppermute | solution.py:198
  78.4 7.2 %collective-permute-start.18 = (bf16[112,512]{1,0:T(8,128)(2,1)S(1)}, bf16[112,512]{1,0:T(8,128)(2,1)S(1)}, u32[]{:S(2)}, u32[]{:S(2)}) collective-permute-start(bf16[112,512]{1,0:T(8,128)(2,1)S(1)} %get-tuple-element.53), channel_id=1, source_target_pairs={{0,2},{1,3},{2,0},{3,1},{4,6},{5,7},{6,4},{7,5},{8,10},{9,11},{10,... | collective-permute-start | bytes 344072 | tf_op jit(solution)/shard_map/sums/ppermute | solution.py:198
  80.8 4.9 %collective-permute-start.19 = (bf16[112,512]{1,0:T(8,128)(2,1)S(1)}, bf16[112,512]{1,0:T(8,128)(2,1)S(1)}, u32[]{:S(2)}, u32[]{:S(2)}) collective-permute-start(bf16[112,512]{1,0:T(8,128)(2,1)S(1)} %get-tuple-element.54), channel_id=1, source_target_pairs={{0,4},{1,5},{2,6},{3,7},{4,0},{5,1},{6,2},{7,3},{8,12},{9,13},{10,... | collective-permute-start | bytes 344072 | tf_op jit(solution)/shard_map/sums/ppermute | solution.py:198

commit v13 on v5

--- a/solution.py
+++ b/solution.py
@@ -65,7 +65,7 @@
 
 
 def hidden_kernel(blocks, width, *refs):
-    rows, own, other, out, x = refs[:blocks], refs[blocks], refs[blocks + 1], refs[blocks + 2], refs[blocks + 3]
+    rows, (own, other_gate, other_up), out, x = refs[:blocks], refs[blocks : blocks + 3], refs[-2], refs[-1]
     height = rows[0].shape[0]
     half = lax.axis_index("dp") % 2
     depth = own.shape[0] // 2
@@ -75,8 +75,8 @@
         for i in range(2):
             x[i * height : (i + 1) * height, :] = rows[first + i][:, :width]
         xa, xb = x[:, pl.ds(at, depth)], x[:, pl.ds(off, depth)]
-        gate = dot(xa, own[:depth, :]) + dot(xb, other[:depth, :])
-        up = dot(xa, own[depth:, :]) + dot(xb, other[depth:, :])
+        gate = dot(xa, own[:depth, :]) + dot(xb, other_gate[...])
+        up = dot(xa, own[depth:, :]) + dot(xb, other_up[...])
         out[first * height : (first + 2) * height, :] = activate(gate, up)
 
 
@@ -151,7 +151,7 @@
     @pl.when(taken)
     def _():
         if axis == 0:
-            parts = [ref.at[pl.ds(first, size), :] for ref in (came, other)]
+            parts = [came.at[pl.ds(first, size), :], other]
         else:
             parts = [came, other]
         run_copies(
@@ -227,7 +227,7 @@
 
     z_upper = send(upper, half_axis, "swap")
     z_lower = send(after(lower, z_upper, *rows), half_axis, "swap")
-    y_upper = trade(after(z_upper, *rows))
+    y_upper = [trade(after(w, *rows)) for w in (z_upper[:depth], z_upper[depth:])]
     near = [send(after(w, lower), 1, "near") for w in own]
 
     firsts = list(reversed(range(0, len(rows), 2)))
@@ -245,12 +245,12 @@
     arrived = after(z_lower, base)
     y_lower = trade(arrived)
     z_near = [send(z_upper, 1, "z_near"), send(arrived, 1, "z_near")]
-    y_near = [send(after(y_upper, arrived), 1, "y_near")]
+    y_near = [[send(after(w, arrived), 1, "y_near") for w in y_upper]]
     hidden = [
         call(
             functools.partial(hidden_kernel, len(rows), width),
             jax.ShapeDtypeStruct((len(rows) * height, ff), jnp.bfloat16),
-            [*rows, own_part, other_part],
+            [*rows, own_part, *other_part],
             scratch,
         )
         for own_part, other_part in ((z_upper, y_upper), (z_near[0], y_near[0]))
@@ -276,8 +276,8 @@
         parts |= far_sums((0, 1), [arrived, z_near[1]], 0, (first, first + 1), near_sums, True)
     flags = after(swap_flags, parts)
     stored = [
-        store(0, 0, flags, own[0], z_upper, y_upper),
-        store(0, depth, flags, own[1], z_upper, y_upper),
+        store(0, 0, flags, own[0], z_upper, y_upper[0]),
+        store(0, depth, flags, own[1], z_upper, y_upper[1]),
     ]
     ours = collect(parts)
     landed = after(y_lower, stored, ours[1:-1])

time: 86.6 us -> 89.8 us (1.037)
  waiting for transfers between devices: 48.6 us -> 42.5 us
  starting transfers between devices: 18.2 us -> 23.3 us
  other arithmetic: 0.32 us -> 2.15 us
  Pallas kernels: 16.7 us -> 18.4 us
    ppermute x18 -> x19, waiting for transfers between devices: 47.5 us -> 42.5 us  [send(): return lax.ppermute(value, 'expert', [(d, d ^ bit) for d in range(count)])]
    ppermute x18 -> x19, starting transfers between devices: 15.9 us -> 19.9 us  [send(): return lax.ppermute(value, 'expert', [(d, d ^ bit) for d in range(count)])]
    pallas_call x10, Pallas kernels: 12.4 us -> 14 us  [call(): pl.pallas_call(kernel, out_shape=out_shape, in_specs=[smem] * scalars + [...]
    ppermute x2 -> x3, waiting for transfers between devices: 1.15 us -> 0.01 us  [trade(): return lax.ppermute(value, 'dp', trades)]
    ppermute x2 -> x3, starting transfers between devices: 2.32 us -> 3.37 us  [trade(): return lax.ppermute(value, 'dp', trades)]
    concatenate x1, other arithmetic: 0.02 us -> 0.98 us  [pack_gates(): return jnp.concatenate([tokens, parts], axis=1)]
  transfers between devices with their start and end apart: 20 -> 22, of which waited for: 9 -> 8; matrix products, arithmetic and copies ran while one was open for 0% -> 2% of each run, Pallas kernels for 18% -> 20%
where the time goes in v13:
time: 89.8 us; the launch traced here: 89.5 us
  waiting for transfers between devices  42.5 us (47%)
  starting transfers between devices  23.3 us (26%)
  Pallas kernels  18.4 us (20%)
  local copies, waits for them, and re-layouts  2.34 us (3%)
  other arithmetic  2.15 us (2%)
  between operations  0.9 us (1%)
    ppermute x19, waiting for transfers between devices, send(): return lax.ppermute(value, 'expert', [(d, d ^ bit) for d in range(count)])  42.5 us
    ppermute x19, starting transfers between devices, send(): return lax.ppermute(value, 'expert', [(d, d ^ bit) for d in range(count)])  19.9 us
    pallas_call x10, Pallas kernels, call(): pl.pallas_call(kernel, out_shape=out_shape, in_specs=[smem] * scalars + [...  14 us
    pallas_call x3, Pallas kernels, store(): pl.pallas_call(functools.partial(store_kernel, axis, first), out_shape=ja...  4.34 us
    ppermute x3, starting transfers between devices, trade(): return lax.ppermute(value, 'dp', trades)  3.37 us
  transfers between devices with their start and end apart: 22, of which 8 were waited for; matrix products, arithmetic and copies ran while one was open for 2% of the time, Pallas kernels for 20%

profile of v13, /device:TPU:0, one launch (start us, length us, event | category | flops | bytes accessed | tf_op | source)
XLA Modules:
  0.0 89.5 jit_solution(215312126226619518)
XLA Ops:
  0.6 1.5 %slice_bitcast_fusion = (bf16[512,384]{1,0:T(8,128)(2,1)S(1)}, bf16[512,384]{1,0:T(8,128)(2,1)S(1)}, bf16[512,384]{1,0:T(8,128)(2,1)S(1)}, bf16[512,384]{1,0:T(8,128)(2,1)S(1)}) fusion(bf16[1,1024,384]{2,1,0:T(8,128)(2,1)} %param.12, bf16[1,1024,384]{2,1,0:T(8,128)(2,1)} %param.11), kind=kLoop, calls=%fused_computation.4 | loop fusion | bytes 3145728 | tf_op jit(solution)/shard_map/slice | solution.py:211
  2.2 0.0 copy-start
  2.2 1.1 %maximum_select_fusion = bf16[1024,384]{1,0:T(8,128)(2,1)} fusion(bf16[512,384]{1,0:T(8,128)(2,1)S(1)} %get-tuple-element.65, bf16[512,384]{1,0:T(8,128)(2,1)S(1)} %get-tuple-element.69, bf16[512,384]{1,0:T(8,128)(2,1)S(1)} %get-tuple-element.64, bf16[512,384]{1,0:T(8,128)(2,1)S(1)} %get-tuple-element.70, pred[]{:T(512)S(6)} %eq.22), kind=kLoop, calls=%fused_computation | loop fusion | flops 3538944 | bytes 2359297 | tf_op jit(solution)/shard_map/jit(_where)/select_n | solution.py:207
  3.3 4.0 %collective-permute-start.3 = (bf16[1024,384]{1,0:T(8,128)(2,1)}, bf16[1024,384]{1,0:T(8,128)(2,1)S(1)}, u32[]{:S(2)}, u32[]{:S(2)}) collective-permute-start(bf16[1024,384]{1,0:T(8,128)(2,1)} %maximum_select_fusion), channel_id=1, source_target_pairs={{0,8},{1,9},{2,10},{3,11},{4,12},{5,13},{6,14},{7,15},{8,0},{9,1},... | collective-permute-start | bytes 2359304 | tf_op jit(solution)/shard_map/swap/ppermute | solution.py:198
  7.4 0.1 collective-permute-start.9
  7.4 0.5 collective-permute-start.7
  8.0 0.7 copy.17
  8.7 1.0 %fusion.1.refs_0_ = bf16[112,1152]{1,0:T(8,128)(2,1)S(1)} fusion(bf16[112,48]{1,0:T(8,128)(2,1)} %copy.17, bf16[112,1024]{1,0:T(8,128)(2,1)} %param.8), kind=kLoop, calls=%fused_computation.8 | loop fusion | flops 774144 | bytes 498176 | tf_op jit(solution)/shard_map/concatenate | solution.py:29
  9.7 1.6 %collective-permute-start = (bf16[112,1152]{1,0:T(8,128)(2,1)S(1)}, bf16[112,1152]{1,0:T(8,128)(2,1)S(1)}, u32[]{:S(2)}, u32[]{:S(2)}) collective-permute-start(bf16[112,1152]{1,0:T(8,128)(2,1)S(1)} %fusion.1.refs_0_), channel_id=1, source_target_pairs={{0,4},{1,5},{2,6},{3,7},{4,0},{5,1},{6,2},{7,3},{8,12},{9,13},{10,... | collective-permute-start | bytes 774152 | tf_op jit(solution)/shard_map/tokens/ppermute | solution.py:198
  11.3 1.5 %collective-permute-start.1 = (bf16[112,1152]{1,0:T(8,128)(2,1)S(1)}, bf16[112,1152]{1,0:T(8,128)(2,1)S(1)}, u32[]{:S(2)}, u32[]{:S(2)}) collective-permute-start(bf16[112,1152]{1,0:T(8,128)(2,1)S(1)} %fusion.1.refs_0_), channel_id=1, source_target_pairs={{0,2},{1,3},{2,0},{3,1},{4,6},{5,7},{6,4},{7,5},{8,10},{9,11},{10,... | collective-permute-start | bytes 774152 | tf_op jit(solution)/shard_map/tokens/ppermute | solution.py:198
  12.8 17.1 %collective-permute-done.refs_1_ = bf16[112,1152]{1,0:T(8,128)(2,1)S(1)} collective-permute-done((bf16[112,1152]{1,0:T(8,128)(2,1)S(1)}, bf16[112,1152]{1,0:T(8,128)(2,1)S(1)}, u32[]{:S(2)}, u32[]{:S(2)}) %collective-permute-start) | collective-permute-done | bytes 258080 | tf_op jit(solution)/shard_map/tokens/ppermute | solution.py:198
  29.9 1.5 %collective-permute-start.2 = (bf16[112,1152]{1,0:T(8,128)(2,1)S(1)}, bf16[112,1152]{1,0:T(8,128)(2,1)S(1)}, u32[]{:S(2)}, u32[]{:S(2)}) collective-permute-start(bf16[112,1152]{1,0:T(8,128)(2,1)S(1)} %collective-permute-done.refs_1_), channel_id=1, source_target_pairs={{0,2},{1,3},{2,0},{3,1},{4,6},{5,7},{6,4},{7,5},{8,10},{9,11},{10,... | collective-permute-start | bytes 774152 | tf_op jit(solution)/shard_map/tokens/ppermute | solution.py:198
  31.4 0.0 collective-permute-done.1.refs_2_.refs_0_
  31.4 0.1 collective-permute-start.8
  31.5 5.5 %collective-permute-done.2.refs_3_.refs_1_ = bf16[112,1152]{1,0:T(8,128)(2,1)S(1)} collective-permute-done((bf16[112,1152]{1,0:T(8,128)(2,1)S(1)}, bf16[112,1152]{1,0:T(8,128)(2,1)S(1)}, u32[]{:S(2)}, u32[]{:S(2)}) %collective-permute-start.2) | collective-permute-done | bytes 258080 | tf_op jit(solution)/shard_map/tokens/ppermute | solution.py:198
  37.0 4.9 %collective-permute-done.3.refs_4_.came = bf16[1024,384]{1,0:T(8,128)(2,1)S(1)} collective-permute-done((bf16[1024,384]{1,0:T(8,128)(2,1)}, bf16[1024,384]{1,0:T(8,128)(2,1)S(1)}, u32[]{:S(2)}, u32[]{:S(2)}) %collective-permute-start.3) | collective-permute-done | bytes 786464 | tf_op jit(solution)/shard_map/swap/ppermute | solution.py:198
  41.9 0.1 fusion.4
  42.0 1.6 %collective-permute-start.5 = (bf16[512,384]{1,0:T(8,128)(2,1)S(1)}, bf16[512,384]{1,0:T(8,128)(2,1)S(1)}, u32[]{:S(2)}, u32[]{:S(2)}) collective-permute-start(bf16[512,384]{1,0:T(8,128)(2,1)S(1)} %get-tuple-element.33), channel_id=1, source_target_pairs={{0,16},{16,0},{1,17},{17,1},{2,18},{18,2},{3,19},{19,3},{4,20},{20... | collective-permute-start | bytes 1179656 | tf_op jit(solution)/shard_map/trade/ppermute | solution.py:202
  43.6 0.5 collective-permute-start.4
  44.1 0.0 collective-permute-done.7.refs_5_
  44.1 0.0 collective-permute-start.10
  44.1 3.2 %shard_map.113 = (f32[112,1024]{1,0:T(8,128)S(1)}, f32[112,1024]{1,0:T(8,128)S(1)}) custom-call(s32[16]{0:T(128)S(1)} %copy-done.3, bf16[112,1152]{1,0:T(8,128)(2,1)S(1)} %collective-permute-done.1.refs_2_.refs_0_, bf16[112,1152]{1,0:T(8,128)(2,1)S(1)} %collective-permute-done.2.refs_3_.refs_1_, bf16[1024,384]{1,0:T(8,128)(2,1)S(1)} %bitcast.24, ...), custom_call_target="tpu_custom_call" | custom-call | tf_op jit(solution)/shard_map/pallas_call | solution.py:122
  47.3 3.2 %shard_map.112 = (f32[112,1024]{1,0:T(8,128)S(1)}, f32[112,1024]{1,0:T(8,128)S(1)}) custom-call(s32[16]{0:T(128)S(1)} %copy-done.3, bf16[112,1152]{1,0:T(8,128)(2,1)S(1)} %fusion.1.refs_0_, bf16[112,1152]{1,0:T(8,128)(2,1)S(1)} %collective-permute-done.refs_1_, bf16[1024,384]{1,0:T(8,128)(2,1)S(1)} %bitcast.25, bf16[1024,384]{1,0:T(8,128)(2,1)S(1)} %bitcast.21, ...), custom_call_target="tpu_custom_call" | custom-call | tf_op jit(solution)/shard_map/pallas_call | solution.py:122
  50.5 11.1 %collective-permute-done.6.refs_3_.came = bf16[384,512]{1,0:T(8,128)(2,1)S(1)} collective-permute-done((bf16[384,512]{1,0:T(8,128)(2,1)S(1)}, bf16[384,512]{1,0:T(8,128)(2,1)S(1)}, u32[]{:S(2)}, u32[]{:S(2)}) %collective-permute-start.6) | collective-permute-done | bytes 393248 | tf_op jit(solution)/shard_map/swap/ppermute | solution.py:198
  61.5 0.5 collective-permute-start.11
  62.1 0.1 collective-permute-start.13
  62.1 1.3 %collective-permute-start.17 = (bf16[384,512]{1,0:T(8,128)(2,1)S(1)}, bf16[384,512]{1,0:T(8,128)(2,1)S(1)}, u32[]{:S(2)}, u32[]{:S(2)}) collective-permute-start(bf16[384,512]{1,0:T(8,128)(2,1)S(1)} %collective-permute-done.6.refs_3_.came), channel_id=1, source_target_pairs={{0,16},{16,0},{1,17},{17,1},{2,18},{18,2},{3,19},{19,3},{4,20},{20... | collective-permute-start | bytes 1179656 | tf_op jit(solution)/shard_map/trade/ppermute | solution.py:202
  63.4 1.2 %shard_map.111.refs_2_.refs_4_ = bf16[448,384]{1,0:T(8,128)(2,1)S(1)} custom-call(bf16[112,1152]{1,0:T(8,128)(2,1)S(1)} %fusion.1.refs_0_, bf16[112,1152]{1,0:T(8,128)(2,1)S(1)} %collective-permute-done.refs_1_, bf16[112,1152]{1,0:T(8,128)(2,1)S(1)} %collective-permute-done.1.refs_2_.refs_0_, bf16[112,1152]{1,0:T(8,128)(2,1)S(1)} %collective-permute-done.2.refs_3_.refs_1_, ...), custom_call_target="tpu_custom_call" | custom-call | tf_op jit(solution)/shard_map/pallas_call | solution.py:122
  64.6 1.2 %shard_map.114.refs_4_.refs_2_ = bf16[448,384]{1,0:T(8,128)(2,1)S(1)} custom-call(bf16[112,1152]{1,0:T(8,128)(2,1)S(1)} %fusion.1.refs_0_, bf16[112,1152]{1,0:T(8,128)(2,1)S(1)} %collective-permute-done.refs_1_, bf16[112,1152]{1,0:T(8,128)(2,1)S(1)} %collective-permute-done.1.refs_2_.refs_0_, bf16[112,1152]{1,0:T(8,128)(2,1)S(1)} %collective-permute-done.2.refs_3_.refs_1_, ...), custom_call_target="tpu_custom_call" | custom-call | tf_op jit(solution)/shard_map/pallas_call | solution.py:122
  65.8 1.0 %shard_map.116 = (bf16[112,512]{1,0:T(8,128)(2,1)S(1)}, bf16[112,512]{1,0:T(8,128)(2,1)S(1)}) custom-call(s32[16]{0:T(128)S(1)} %copy-done.3, bf16[112,1152]{1,0:T(8,128)(2,1)S(1)} %collective-permute-done.1.refs_2_.refs_0_, bf16[112,1152]{1,0:T(8,128)(2,1)S(1)} %collective-permute-done.2.refs_3_.refs_1_, bf16[448,384]{1,0:T(8,128)(2,1)S(1)} %shard_map.111.refs_2_.refs_4_, ...), custom_call_target="tpu_custom_call" | custom-call | tf_op jit(solution)/shard_map/pallas_call | solution.py:122
  66.8 5.0 %collective-permute-start.14 = (bf16[112,512]{1,0:T(8,128)(2,1)S(1)}, bf16[112,512]{1,0:T(8,128)(2,1)S(1)}, u32[]{:S(2)}, u32[]{:S(2)}) collective-permute-start(bf16[112,512]{1,0:T(8,128)(2,1)S(1)} %get-tuple-element.46), channel_id=1, source_target_pairs={{0,6},{1,7},{2,4},{3,5},{4,2},{5,3},{6,0},{7,1},{8,14},{9,15},{10,... | collective-permute-start | bytes 344072 | tf_op jit(solution)/shard_map/sums/ppermute | solution.py:198
  71.8 0.5 collective-permute-start.15
  72.3 0.9 %shard_map.115 = (f32[112,512]{1,0:T(8,128)S(1)}, bf16[112,512]{1,0:T(8,128)(2,1)S(1)}) custom-call(s32[16]{0:T(128)S(1)} %copy-done.3, bf16[112,1152]{1,0:T(8,128)(2,1)S(1)} %fusion.1.refs_0_, bf16[112,1152]{1,0:T(8,128)(2,1)S(1)} %collective-permute-done.refs_1_, bf16[448,384]{1,0:T(8,128)(2,1)S(1)} %shard_map.111.refs_2_.refs_4_, ...), custom_call_target="tpu_custom_call" | custom-call | tf_op jit(solution)/shard_map/pallas_call | solution.py:122
  73.3 1.4 %shard_map.118 = bf16[1024,384]{1,0:T(8,128)(2,1)} custom-call(s32[16]{0:T(128)S(1)} %copy-done.4, bf16[1024,384]{1,0:T(8,128)(2,1)S(1)} %bitcast.22, bf16[1024,384]{1,0:T(8,128)(2,1)S(1)} %collective-permute-done.3.refs_4_.came, bf16[512,384]{1,0:T(8,128)(2,1)S(1)} %collective-permute-done.5.refs_6_.other), custom_call_target="tpu_custom_call" | custom-call | tf_op jit(solution)/shard_map/pallas_call | solution.py:172
  74.7 1.4 %shard_map.117 = bf16[1024,384]{1,0:T(8,128)(2,1)} custom-call(s32[16]{0:T(128)S(1)} %copy-done.4, bf16[1024,384]{1,0:T(8,128)(2,1)S(1)} %bitcast.26, bf16[1024,384]{1,0:T(8,128)(2,1)S(1)} %collective-permute-done.3.refs_4_.came, bf16[512,384]{1,0:T(8,128)(2,1)S(1)} %collective-permute-done.4.refs_5_.other), custom_call_target="tpu_custom_call" | custom-call | tf_op jit(solution)/shard_map/pallas_call | solution.py:172
  76.2 1.0 %collective-permute-done.15.refs_2_ = bf16[112,512]{1,0:T(8,128)(2,1)S(1)} collective-permute-done((bf16[112,512]{1,0:T(8,128)(2,1)S(1)}, bf16[112,512]{1,0:T(8,128)(2,1)S(1)}, u32[]{:S(2)}, u32[]{:S(2)}) %collective-permute-start.15) | collective-permute-done | bytes 114720 | tf_op jit(solution)/shard_map/sums/ppermute | solution.py:198
  77.3 0.9 %collective-permute-start.16 = (bf16[112,512]{1,0:T(8,128)(2,1)S(1)}, bf16[112,512]{1,0:T(8,128)(2,1)S(1)}, u32[]{:S(2)}, u32[]{:S(2)}) collective-permute-start(bf16[112,512]{1,0:T(8,128)(2,1)S(1)} %get-tuple-element.48), channel_id=1, source_target_pairs={{0,4},{1,5},{2,6},{3,7},{4,0},{5,1},{6,2},{7,3},{8,12},{9,13},{10,... | collective-permute-start | bytes 344072 | tf_op jit(solution)/shard_map/sums/ppermute | solution.py:198
  78.2 0.9 %shard_map.119 = (f32[112,512]{1,0:T(8,128)S(1)}, f32[112,512]{1,0:T(8,128)S(1)}, f32[112,512]{1,0:T(8,128)S(1)}, f32[112,512]{1,0:T(8,128)S(1)}) custom-call(s32[16]{0:T(128)S(1)} %copy-done.3, bf16[112,1152]{1,0:T(8,128)(2,1)S(1)} %fusion.1.refs_0_, bf16[112,1152]{1,0:T(8,128)(2,1)S(1)} %collective-permute-done.refs_1_, ...), custom_call_target="tpu_custom_call" | custom-call | tf_op jit(solution)/shard_map/pallas_call | solution.py:122
  79.1 0.8 shard_map.121
  80.0 1.7 %collective-permute-start.19 = (bf16[112,512]{1,0:T(8,128)(2,1)S(1)}, bf16[112,512]{1,0:T(8,128)(2,1)S(1)}, u32[]{:S(2)}, u32[]{:S(2)}) collective-permute-start(bf16[112,512]{1,0:T(8,128)(2,1)S(1)} %get-tuple-element.56), channel_id=1, source_target_pairs={{0,6},{1,7},{2,4},{3,5},{4,2},{5,3},{6,0},{7,1},{8,14},{9,15},{10,... | collective-permute-start | bytes 344072 | tf_op jit(solution)/shard_map/sums/ppermute | solution.py:198
  81.7 0.9 %collective-permute-start.20 = (bf16[112,512]{1,0:T(8,128)(2,1)S(1)}, bf16[112,512]{1,0:T(8,128)(2,1)S(1)}, u32[]{:S(2)}, u32[]{:S(2)}) collective-permute-start(bf16[112,512]{1,0:T(8,128)(2,1)S(1)} %get-tuple-element.57), channel_id=1, source_target_pairs={{0,2},{1,3},{2,0},{3,1},{4,6},{5,7},{6,4},{7,5},{8,10},{9,11},{10,... | collective-permute-start | bytes 344072 | tf_op jit(solution)/shard_map/sums/ppermute | solution.py:198
  82.6 0.8 shard_map.120
  83.5 1.0 %collective-permute-start.21 = (bf16[112,512]{1,0:T(8,128)(2,1)S(1)}, bf16[112,512]{1,0:T(8,128)(2,1)S(1)}, u32[]{:S(2)}, u32[]{:S(2)}) collective-permute-start(bf16[112,512]{1,0:T(8,128)(2,1)S(1)} %get-tuple-element.58), channel_id=1, source_target_pairs={{0,4},{1,5},{2,6},{3,7},{4,0},{5,1},{6,2},{7,3},{8,12},{9,13},{10,... | collective-permute-start | bytes 344072 | tf_op jit(solution)/shard_map/sums/ppermute | solution.py:198
  84.4 1.4 %shard_map.123 = bf16[384,1024]{1,0:T(8,128)(2,1)} custom-call(s32[16]{0:T(128)S(1)} %copy-done.4, bf16[384,1024]{1,0:T(8,128)(2,1)S(1)} %bitcast.18, bf16[384,512]{1,0:T(8,128)(2,1)S(1)} %collective-permute-done.6.refs_3_.came, bf16[384,512]{1,0:T(8,128)(2,1)S(1)} %collective-permute-done.17.refs_5_.other), custom_call_target="tpu_custom_call" | custom-call | tf_op jit(solution)/shard_map/pallas_call | solution.py:172
  85.9 0.4 collective-permute-done.19.refs_5_
  86.3 2.4 %collective-permute-done.20.refs_6_ = bf16[112,512]{1,0:T(8,128)(2,1)S(1)} collective-permute-done((bf16[112,512]{1,0:T(8,128)(2,1)S(1)}, bf16[112,512]{1,0:T(8,128)(2,1)S(1)}, u32[]{:S(2)}, u32[]{:S(2)}) %collective-permute-start.20) | collective-permute-done | bytes 114720 | tf_op jit(solution)/shard_map/sums/ppermute | solution.py:198
  88.7 0.1 collective-permute-done.21.refs_7_
  88.7 0.8 shard_map.122
  (32 shorter events, 0.1 us)
Async XLA Ops:
  2.2 5.1 %copy-start = (bf16[1,384,1024]{2,1,0:T(8,128)(2,1)S(1)}, bf16[1,384,1024]{2,1,0:T(8,128)(2,1)}, u32[]{:S(2)}) copy-start(bf16[1,384,1024]{2,1,0:T(8,128)(2,1)} %param.13) | copy-start | bytes 2359300
  3.3 4.2 %copy-start.2 = (bf16[1,1024,384]{2,1,0:T(8,128)(2,1)S(1)}, bf16[1,1024,384]{2,1,0:T(8,128)(2,1)}, u32[]{:S(2)}) copy-start(bf16[1,1024,384]{2,1,0:T(8,128)(2,1)} %param.11) | copy-start | bytes 2359300
  3.3 4.7 %copy-start.5 = (f32[112,8]{0,1:T(8,128)S(1)}, f32[112,8]{0,1:T(8,128)}, u32[]{:S(2)}) copy-start(f32[112,8]{0,1:T(8,128)} %param.10) | copy-start | bytes 10756
  3.3 4.7 %copy-start.6 = (s32[112,8]{0,1:T(8,128)S(1)}, s32[112,8]{0,1:T(8,128)}, u32[]{:S(2)}) copy-start(s32[112,8]{0,1:T(8,128)} %param.9) | copy-start | bytes 10756
  3.3 38.6 %collective-permute-start.3 = (bf16[1024,384]{1,0:T(8,128)(2,1)}, bf16[1024,384]{1,0:T(8,128)(2,1)S(1)}, u32[]{:S(2)}, u32[]{:S(2)}) collective-permute-start(bf16[1024,384]{1,0:T(8,128)(2,1)} %maximum_select_fusion), channel_id=1, source_target_pairs={{0,8},{1,9},{2,10},{3,11},{4,12},{5,13},{6,14},{7,15},{8,0},{9,1},... | collective-permute-start | bytes 2359304 | tf_op jit(solution)/shard_map/swap/ppermute | solution.py:198
  7.3 24.1 %copy-start.1 = (bf16[1,1024,384]{2,1,0:T(8,128)(2,1)S(1)}, bf16[1,1024,384]{2,1,0:T(8,128)(2,1)}, u32[]{:S(2)}) copy-start(bf16[1,1024,384]{2,1,0:T(8,128)(2,1)} %param.12) | copy-start | bytes 2359300
  7.4 36.3 %collective-permute-start.9 = (bf16[384,1024]{1,0:T(8,128)(2,1)S(1)}, bf16[384,1024]{1,0:T(8,128)(2,1)}, u32[]{:S(2)}, u32[]{:S(2)}) collective-permute-start(bf16[384,1024]{1,0:T(8,128)(2,1)S(1)} %bitcast.15), channel_id=1, source_target_pairs={{0,1},{1,0},{2,3},{3,2},{4,5},{5,4},{6,7},{7,6},{8,9},{9,8},{10,11... | collective-permute-start | bytes 2359304 | tf_op jit(solution)/shard_map/near/ppermute | solution.py:198
  7.4 36.6 %collective-permute-start.7 = (bf16[1024,384]{1,0:T(8,128)(2,1)S(1)}, bf16[1024,384]{1,0:T(8,128)(2,1)}, u32[]{:S(2)}, u32[]{:S(2)}) collective-permute-start(bf16[1024,384]{1,0:T(8,128)(2,1)S(1)} %bitcast.23), channel_id=1, source_target_pairs={{0,1},{1,0},{2,3},{3,2},{4,5},{5,4},{6,7},{7,6},{8,9},{9,8},{10,11... | collective-permute-start | bytes 2359304 | tf_op jit(solution)/shard_map/near/ppermute | solution.py:198
  9.7 20.2 %collective-permute-start = (bf16[112,1152]{1,0:T(8,128)(2,1)S(1)}, bf16[112,1152]{1,0:T(8,128)(2,1)S(1)}, u32[]{:S(2)}, u32[]{:S(2)}) collective-permute-start(bf16[112,1152]{1,0:T(8,128)(2,1)S(1)} %fusion.1.refs_0_), channel_id=1, source_target_pairs={{0,4},{1,5},{2,6},{3,7},{4,0},{5,1},{6,2},{7,3},{8,12},{9,13},{10,... | collective-permute-start | bytes 774152 | tf_op jit(solution)/shard_map/tokens/ppermute | solution.py:198
  11.3 20.0 %collective-permute-start.1 = (bf16[112,1152]{1,0:T(8,128)(2,1)S(1)}, bf16[112,1152]{1,0:T(8,128)(2,1)S(1)}, u32[]{:S(2)}, u32[]{:S(2)}) collective-permute-start(bf16[112,1152]{1,0:T(8,128)(2,1)S(1)} %fusion.1.refs_0_), channel_id=1, source_target_pairs={{0,2},{1,3},{2,0},{3,1},{4,6},{5,7},{6,4},{7,5},{8,10},{9,11},{10,... | collective-permute-start | bytes 774152 | tf_op jit(solution)/shard_map/tokens/ppermute | solution.py:198
  29.9 7.1 %collective-permute-start.2 = (bf16[112,1152]{1,0:T(8,128)(2,1)S(1)}, bf16[112,1152]{1,0:T(8,128)(2,1)S(1)}, u32[]{:S(2)}, u32[]{:S(2)}) collective-permute-start(bf16[112,1152]{1,0:T(8,128)(2,1)S(1)} %collective-permute-done.refs_1_), channel_id=1, source_target_pairs={{0,2},{1,3},{2,0},{3,1},{4,6},{5,7},{6,4},{7,5},{8,10},{9,11},{10,... | collective-permute-start | bytes 774152 | tf_op jit(solution)/shard_map/tokens/ppermute | solution.py:198
  31.4 12.7 %copy-start.3 = (s32[16]{0:T(128)S(1)}, s32[16]{0:T(128)}, u32[]{:S(2)}) copy-start(s32[16]{0:T(128)} %placement.13) | copy-start | bytes 196
  31.4 12.7 %collective-permute-start.8 = (bf16[1024,384]{1,0:T(8,128)(2,1)S(1)}, bf16[1024,384]{1,0:T(8,128)(2,1)S(1)}, u32[]{:S(2)}, u32[]{:S(2)}) collective-permute-start(bf16[1024,384]{1,0:T(8,128)(2,1)S(1)} %bitcast.19), channel_id=1, source_target_pairs={{0,1},{1,0},{2,3},{3,2},{4,5},{5,4},{6,7},{7,6},{8,9},{9,8},{10,11... | collective-permute-start | bytes 2359304 | tf_op jit(solution)/shard_map/near/ppermute | solution.py:198
  41.9 19.6 %collective-permute-start.6 = (bf16[384,512]{1,0:T(8,128)(2,1)S(1)}, bf16[384,512]{1,0:T(8,128)(2,1)S(1)}, u32[]{:S(2)}, u32[]{:S(2)}) collective-permute-start(bf16[384,512]{1,0:T(8,128)(2,1)S(1)} %slice_select_fusion), channel_id=1, source_target_pairs={{0,8},{1,9},{2,10},{3,11},{4,12},{5,13},{6,14},{7,15},{8,0},{9,1},... | collective-permute-start | bytes 1179656 | tf_op jit(solution)/shard_map/swap/ppermute | solution.py:198
  42.0 19.5 %collective-permute-start.5 = (bf16[512,384]{1,0:T(8,128)(2,1)S(1)}, bf16[512,384]{1,0:T(8,128)(2,1)S(1)}, u32[]{:S(2)}, u32[]{:S(2)}) collective-permute-start(bf16[512,384]{1,0:T(8,128)(2,1)S(1)} %get-tuple-element.33), channel_id=1, source_target_pairs={{0,16},{16,0},{1,17},{17,1},{2,18},{18,2},{3,19},{19,3},{4,20},{20... | collective-permute-start | bytes 1179656 | tf_op jit(solution)/shard_map/trade/ppermute | solution.py:202
  43.6 17.9 %collective-permute-start.4 = (bf16[512,384]{1,0:T(8,128)(2,1)S(1)}, bf16[512,384]{1,0:T(8,128)(2,1)S(1)}, u32[]{:S(2)}, u32[]{:S(2)}) collective-permute-start(bf16[512,384]{1,0:T(8,128)(2,1)S(1)} %get-tuple-element.32), channel_id=1, source_target_pairs={{0,16},{16,0},{1,17},{17,1},{2,18},{18,2},{3,19},{19,3},{4,20},{20... | collective-permute-start | bytes 1179656 | tf_op jit(solution)/shard_map/trade/ppermute | solution.py:202
  44.1 20.5 %collective-permute-start.10 = (bf16[1024,384]{1,0:T(8,128)(2,1)S(1)}, bf16[1024,384]{1,0:T(8,128)(2,1)S(1)}, u32[]{:S(2)}, u32[]{:S(2)}) collective-permute-start(bf16[1024,384]{1,0:T(8,128)(2,1)S(1)} %collective-permute-done.3.refs_4_.came), channel_id=1, source_target_pairs={{0,1},{1,0},{2,3},{3,2},{4,5},{5,4},{6,7},{7,6},{8,9},{9,8},{10,11... | collective-permute-start | bytes 2359304 | tf_op jit(solution)/shard_map/z_near/ppermute | solution.py:198
  61.5 3.1 %collective-permute-start.12 = (bf16[512,384]{1,0:T(8,128)(2,1)S(1)}, bf16[512,384]{1,0:T(8,128)(2,1)S(1)}, u32[]{:S(2)}, u32[]{:S(2)}) collective-permute-start(bf16[512,384]{1,0:T(8,128)(2,1)S(1)} %collective-permute-done.5.refs_6_.other), channel_id=1, source_target_pairs={{0,1},{1,0},{2,3},{3,2},{4,5},{5,4},{6,7},{7,6},{8,9},{9,8},{10,11... | collective-permute-start | bytes 1179656 | tf_op jit(solution)/shard_map/y_near/ppermute | solution.py:198
  61.5 3.1 %collective-permute-start.11 = (bf16[512,384]{1,0:T(8,128)(2,1)S(1)}, bf16[512,384]{1,0:T(8,128)(2,1)S(1)}, u32[]{:S(2)}, u32[]{:S(2)}) collective-permute-start(bf16[512,384]{1,0:T(8,128)(2,1)S(1)} %collective-permute-done.4.refs_5_.other), channel_id=1, source_target_pairs={{0,1},{1,0},{2,3},{3,2},{4,5},{5,4},{6,7},{7,6},{8,9},{9,8},{10,11... | collective-permute-start | bytes 1179656 | tf_op jit(solution)/shard_map/y_near/ppermute | solution.py:198
  62.1 3.8 %collective-permute-start.13 = (bf16[384,512]{1,0:T(8,128)(2,1)S(1)}, bf16[384,512]{1,0:T(8,128)(2,1)S(1)}, u32[]{:S(2)}, u32[]{:S(2)}) collective-permute-start(bf16[384,512]{1,0:T(8,128)(2,1)S(1)} %collective-permute-done.6.refs_3_.came), channel_id=1, source_target_pairs={{0,1},{1,0},{2,3},{3,2},{4,5},{5,4},{6,7},{7,6},{8,9},{9,8},{10,11... | collective-permute-start | bytes 1179656 | tf_op jit(solution)/shard_map/z_near/ppermute | solution.py:198
  62.1 14.1 %collective-permute-start.17 = (bf16[384,512]{1,0:T(8,128)(2,1)S(1)}, bf16[384,512]{1,0:T(8,128)(2,1)S(1)}, u32[]{:S(2)}, u32[]{:S(2)}) collective-permute-start(bf16[384,512]{1,0:T(8,128)(2,1)S(1)} %collective-permute-done.6.refs_3_.came), channel_id=1, source_target_pairs={{0,16},{16,0},{1,17},{17,1},{2,18},{18,2},{3,19},{19,3},{4,20},{20... | collective-permute-start | bytes 1179656 | tf_op jit(solution)/shard_map/trade/ppermute | solution.py:202
  66.8 9.4 %collective-permute-start.14 = (bf16[112,512]{1,0:T(8,128)(2,1)S(1)}, bf16[112,512]{1,0:T(8,128)(2,1)S(1)}, u32[]{:S(2)}, u32[]{:S(2)}) collective-permute-start(bf16[112,512]{1,0:T(8,128)(2,1)S(1)} %get-tuple-element.46), channel_id=1, source_target_pairs={{0,6},{1,7},{2,4},{3,5},{4,2},{5,3},{6,0},{7,1},{8,14},{9,15},{10,... | collective-permute-start | bytes 344072 | tf_op jit(solution)/shard_map/sums/ppermute | solution.py:198
  71.8 1.5 %copy-start.4 = (s32[16]{0:T(128)S(1)}, s32[16]{0:T(128)}, u32[]{:S(2)}) copy-start(s32[16]{0:T(128)} %flags.2) | copy-start | bytes 196
  71.8 5.5 %collective-permute-start.15 = (bf16[112,512]{1,0:T(8,128)(2,1)S(1)}, bf16[112,512]{1,0:T(8,128)(2,1)S(1)}, u32[]{:S(2)}, u32[]{:S(2)}) collective-permute-start(bf16[112,512]{1,0:T(8,128)(2,1)S(1)} %get-tuple-element.47), channel_id=1, source_target_pairs={{0,2},{1,3},{2,0},{3,1},{4,6},{5,7},{6,4},{7,5},{8,10},{9,11},{10,... | collective-permute-start | bytes 344072 | tf_op jit(solution)/shard_map/sums/ppermute | solution.py:198
  77.3 1.9 %collective-permute-start.18 = (bf16[384,512]{1,0:T(8,128)(2,1)S(1)}, bf16[384,512]{1,0:T(8,128)(2,1)S(1)}, u32[]{:S(2)}, u32[]{:S(2)}) collective-permute-start(bf16[384,512]{1,0:T(8,128)(2,1)S(1)} %collective-permute-done.17.refs_5_.other), channel_id=1, source_target_pairs={{0,1},{1,0},{2,3},{3,2},{4,5},{5,4},{6,7},{7,6},{8,9},{9,8},{10,11... | collective-permute-start | bytes 1179656 | tf_op jit(solution)/shard_map/y_near/ppermute | solution.py:198
  77.3 8.6 %collective-permute-start.16 = (bf16[112,512]{1,0:T(8,128)(2,1)S(1)}, bf16[112,512]{1,0:T(8,128)(2,1)S(1)}, u32[]{:S(2)}, u32[]{:S(2)}) collective-permute-start(bf16[112,512]{1,0:T(8,128)(2,1)S(1)} %get-tuple-element.48), channel_id=1, source_target_pairs={{0,4},{1,5},{2,6},{3,7},{4,0},{5,1},{6,2},{7,3},{8,12},{9,13},{10,... | collective-permute-start | bytes 344072 | tf_op jit(solution)/shard_map/sums/ppermute | solution.py:198
  80.0 6.4 %collective-permute-start.19 = (bf16[112,512]{1,0:T(8,128)(2,1)S(1)}, bf16[112,512]{1,0:T(8,128)(2,1)S(1)}, u32[]{:S(2)}, u32[]{:S(2)}) collective-permute-start(bf16[112,512]{1,0:T(8,128)(2,1)S(1)} %get-tuple-element.56), channel_id=1, source_target_pairs={{0,6},{1,7},{2,4},{3,5},{4,2},{5,3},{6,0},{7,1},{8,14},{9,15},{10,... | collective-permute-start | bytes 344072 | tf_op jit(solution)/shard_map/sums/ppermute | solution.py:198
  81.7 7.0 %collective-permute-start.20 = (bf16[112,512]{1,0:T(8,128)(2,1)S(1)}, bf16[112,512]{1,0:T(8,128)(2,1)S(1)}, u32[]{:S(2)}, u32[]{:S(2)}) collective-permute-start(bf16[112,512]{1,0:T(8,128)(2,1)S(1)} %get-tuple-element.57), channel_id=1, source_target_pairs={{0,2},{1,3},{2,0},{3,1},{4,6},{5,7},{6,4},{7,5},{8,10},{9,11},{10,... | collective-permute-start | bytes 344072 | tf_op jit(solution)/shard_map/sums/ppermute | solution.py:198
  83.5 5.3 %collective-permute-start.21 = (bf16[112,512]{1,0:T(8,128)(2,1)S(1)}, bf16[112,512]{1,0:T(8,128)(2,1)S(1)}, u32[]{:S(2)}, u32[]{:S(2)}) collective-permute-start(bf16[112,512]{1,0:T(8,128)(2,1)S(1)} %get-tuple-element.58), channel_id=1, source_target_pairs={{0,4},{1,5},{2,6},{3,7},{4,0},{5,1},{6,2},{7,3},{8,12},{9,13},{10,... | collective-permute-start | bytes 344072 | tf_op jit(solution)/shard_map/sums/ppermute | solution.py:198

commit v14 on v5

--- a/solution.py
+++ b/solution.py
@@ -95,8 +95,9 @@
         pair = range(first, first + 2)
         totals = {i: base[i][...] if base[i].shape[1] == part else base[i][:, columns] for i in pair}
         for flip, hidden, down in zip(flips, experts[::2], experts[1::2]):
-            span = slice(blocks[first] * height, (blocks[first] + 2) * height)
-            value = rounded(dot(hidden[span, :], down[...]))
+            spans = [slice(blocks[i] * height, (blocks[i] + 1) * height) for i in pair]
+            units = jnp.concatenate([hidden[span, :] for span in spans], axis=0)
+            value = rounded(dot(units, down[...]))
             for i in pair:
                 weight = token_weight(rows[i][:, width:], placement[me ^ far ^ flip], count)
                 at = (i - first) * height
@@ -267,13 +268,16 @@
         )
         return dict(zip(blocks, out))
 
+    pairs = [(i, i + len(rows) // 2) for i in reversed(range(len(rows) // 2))]
+    order = [i for pair in pairs for i in reversed(pair) if i > 0]
+
     def collect(parts):
-        return [parts[0]] + [send(parts[i], masks[i], "sums") for i in reversed(range(1, len(parts)))]
+        return [parts[0]] + [send(parts[i], masks[i], "sums") for i in order]
 
     near_sums = [x for first in reversed(firsts) for x in base[first]]
     parts = {}
-    for first in firsts:
-        parts |= far_sums((0, 1), [arrived, z_near[1]], 0, (first, first + 1), near_sums, True)
+    for pair in pairs:
+        parts |= far_sums((0, 1), [arrived, z_near[1]], 0, pair, near_sums, True)
     flags = after(swap_flags, parts)
     stored = [
         store(0, 0, flags, own[0], z_upper, y_upper),
@@ -285,8 +289,8 @@
     everyone = tuple(range(len(rows)))
     last_sums = far_sums((0,), [landed], 1, everyone, near_sums, False)
     last_parts = {}
-    for first in firsts:
-        last_parts |= far_sums((1,), [y_near[1]], 1, (first, first + 1), last_sums, True)
+    for pair in pairs:
+        last_parts |= far_sums((1,), [y_near[1]], 1, pair, last_sums, True)
     stored.append(store(1, 0, after(swap_flags, last_parts), own[2], z_lower, y_lower))
     others = collect(last_parts)
     mixed = call(

time: 86.6 us -> 87.1 us (level)
  starting transfers between devices: 18.2 us -> 19.2 us
    ppermute x18, starting transfers between devices: 15.9 us -> 16.9 us  [send(): return lax.ppermute(value, 'expert', [(d, d ^ bit) for d in range(count)])]
    ppermute x2, waiting for transfers between devices: 1.15 us -> 0.17 us  [trade(): return lax.ppermute(value, 'dp', trades)]
  transfers between devices with their start and end apart: 20 -> 20, of which waited for: 9 -> 11; matrix products, arithmetic and copies ran while one was open for 0% -> 0% of each run, Pallas kernels for 18% -> 18%
where the time goes in v14:
time: 87.1 us; the launch traced here: 86.9 us
  waiting for transfers between devices  48 us (55%)
  starting transfers between devices  19.2 us (22%)
  Pallas kernels  16.7 us (19%)
  local copies, waits for them, and re-layouts  1.67 us (2%)
  between operations  0.93 us (1%)
    ppermute x18, waiting for transfers between devices, send(): return lax.ppermute(value, 'expert', [(d, d ^ bit) for d in range(count)])  47.9 us
    ppermute x18, starting transfers between devices, send(): return lax.ppermute(value, 'expert', [(d, d ^ bit) for d in range(count)])  16.9 us
    pallas_call x10, Pallas kernels, call(): pl.pallas_call(kernel, out_shape=out_shape, in_specs=[smem] * scalars + [...  12.4 us
    pallas_call x3, Pallas kernels, store(): pl.pallas_call(functools.partial(store_kernel, axis, first), out_shape=ja...  4.34 us
    ppermute x2, starting transfers between devices, trade(): return lax.ppermute(value, 'dp', trades)  2.32 us
  transfers between devices with their start and end apart: 20, of which 11 were waited for; matrix products, arithmetic and copies ran while one was open for 0% of the time, Pallas kernels for 18%

profile of v14, /device:TPU:0, one launch (start us, length us, event | category | flops | bytes accessed | tf_op | source)
XLA Modules:
  0.0 86.9 jit_solution(11188947156120257887)
XLA Ops:
  0.6 1.5 %slice_bitcast_fusion = (bf16[512,384]{1,0:T(8,128)(2,1)S(1)}, bf16[512,384]{1,0:T(8,128)(2,1)S(1)}, bf16[512,384]{1,0:T(8,128)(2,1)S(1)}, bf16[512,384]{1,0:T(8,128)(2,1)S(1)}) fusion(bf16[1,1024,384]{2,1,0:T(8,128)(2,1)} %param.12, bf16[1,1024,384]{2,1,0:T(8,128)(2,1)} %param.11), kind=kLoop, calls=%fused_computation.4 | loop fusion | bytes 3145728 | tf_op jit(solution)/shard_map/slice | solution.py:212
  2.2 0.0 copy-start.5
  2.2 0.0 copy-start
  2.2 0.2 maximum_select_fusion
  2.4 4.1 %collective-permute-start.3 = (bf16[1024,384]{1,0:T(8,128)(2,1)S(1)}, bf16[1024,384]{1,0:T(8,128)(2,1)S(1)}, u32[]{:S(2)}, u32[]{:S(2)}) collective-permute-start(bf16[1024,384]{1,0:T(8,128)(2,1)S(1)} %maximum_select_fusion), channel_id=1, source_target_pairs={{0,8},{1,9},{2,10},{3,11},{4,12},{5,13},{6,14},{7,15},{8,0},{9,1},... | collective-permute-start | bytes 2359304 | tf_op jit(solution)/shard_map/swap/ppermute | solution.py:199
  6.6 0.1 copy.17
  6.7 0.0 copy-start.1
  6.7 0.0 copy-start.3
  6.8 1.6 %collective-permute-start.1 = (bf16[112,1152]{1,0:T(8,128)(2,1)S(1)}, bf16[112,1152]{1,0:T(8,128)(2,1)S(1)}, u32[]{:S(2)}, u32[]{:S(2)}) collective-permute-start(bf16[112,1152]{1,0:T(8,128)(2,1)S(1)} %fusion.1.refs_0_), channel_id=1, source_target_pairs={{0,4},{1,5},{2,6},{3,7},{4,0},{5,1},{6,2},{7,3},{8,12},{9,13},{10,... | collective-permute-start | bytes 774152 | tf_op jit(solution)/shard_map/tokens/ppermute | solution.py:199
  8.4 1.5 %collective-permute-start = (bf16[112,1152]{1,0:T(8,128)(2,1)S(1)}, bf16[112,1152]{1,0:T(8,128)(2,1)S(1)}, u32[]{:S(2)}, u32[]{:S(2)}) collective-permute-start(bf16[112,1152]{1,0:T(8,128)(2,1)S(1)} %fusion.1.refs_0_), channel_id=1, source_target_pairs={{0,2},{1,3},{2,0},{3,1},{4,6},{5,7},{6,4},{7,5},{8,10},{9,11},{10,... | collective-permute-start | bytes 774152 | tf_op jit(solution)/shard_map/tokens/ppermute | solution.py:199
  9.9 19.0 %collective-permute-done.1.refs_1_.refs_0_ = bf16[112,1152]{1,0:T(8,128)(2,1)S(1)} collective-permute-done((bf16[112,1152]{1,0:T(8,128)(2,1)S(1)}, bf16[112,1152]{1,0:T(8,128)(2,1)S(1)}, u32[]{:S(2)}, u32[]{:S(2)}) %collective-permute-start.1) | collective-permute-done | bytes 258080 | tf_op jit(solution)/shard_map/tokens/ppermute | solution.py:199
  28.9 1.5 %collective-permute-start.2 = (bf16[112,1152]{1,0:T(8,128)(2,1)S(1)}, bf16[112,1152]{1,0:T(8,128)(2,1)S(1)}, u32[]{:S(2)}, u32[]{:S(2)}) collective-permute-start(bf16[112,1152]{1,0:T(8,128)(2,1)S(1)} %collective-permute-done.1.refs_1_.refs_0_), channel_id=1, source_target_pairs={{0,2},{1,3},{2,0},{3,1},{4,6},{5,7},{6,4},{7,5},{8,10},{9,11},{10,... | collective-permute-start | bytes 774152 | tf_op jit(solution)/shard_map/tokens/ppermute | solution.py:199
  30.4 0.1 collective-permute-start.8
  30.5 0.5 collective-permute-start.6
  31.0 0.1 collective-permute-start.7
  31.1 4.9 %collective-permute-done.2.refs_3_.refs_1_ = bf16[112,1152]{1,0:T(8,128)(2,1)S(1)} collective-permute-done((bf16[112,1152]{1,0:T(8,128)(2,1)S(1)}, bf16[112,1152]{1,0:T(8,128)(2,1)S(1)}, u32[]{:S(2)}, u32[]{:S(2)}) %collective-permute-start.2) | collective-permute-done | bytes 258080 | tf_op jit(solution)/shard_map/tokens/ppermute | solution.py:199
  36.0 4.9 %collective-permute-done.3.refs_4_.came = bf16[1024,384]{1,0:T(8,128)(2,1)S(1)} collective-permute-done((bf16[1024,384]{1,0:T(8,128)(2,1)S(1)}, bf16[1024,384]{1,0:T(8,128)(2,1)S(1)}, u32[]{:S(2)}, u32[]{:S(2)}) %collective-permute-start.3) | collective-permute-done | bytes 786464 | tf_op jit(solution)/shard_map/swap/ppermute | solution.py:199
  40.9 1.6 %collective-permute-start.4 = (bf16[1024,384]{1,0:T(8,128)(2,1)S(1)}, bf16[1024,384]{1,0:T(8,128)(2,1)S(1)}, u32[]{:S(2)}, u32[]{:S(2)}) collective-permute-start(bf16[1024,384]{1,0:T(8,128)(2,1)S(1)} %collective-permute-done.3.refs_4_.came), channel_id=1, source_target_pairs={{0,16},{16,0},{1,17},{17,1},{2,18},{18,2},{3,19},{19,3},{4,20},{20... | collective-permute-start | bytes 2359304 | tf_op jit(solution)/shard_map/trade/ppermute | solution.py:203
  42.5 2.3 %shard_map.113 = (f32[112,1024]{1,0:T(8,128)S(1)}, f32[112,1024]{1,0:T(8,128)S(1)}) custom-call(s32[16]{0:T(128)S(1)} %copy-done.3, bf16[112,1152]{1,0:T(8,128)(2,1)S(1)} %collective-permute-done.refs_2_.refs_0_.refs_1_, bf16[112,1152]{1,0:T(8,128)(2,1)S(1)} %collective-permute-done.2.refs_3_.refs_1_, bf16[1024,384]{1,0:T(8,128)(2,1)S(1)} %bitcast.24, ...), custom_call_target="tpu_custom_call" | custom-call | tf_op jit(solution)/shard_map/pallas_call | solution.py:123
  44.9 2.3 %shard_map.112 = (f32[112,1024]{1,0:T(8,128)S(1)}, f32[112,1024]{1,0:T(8,128)S(1)}) custom-call(s32[16]{0:T(128)S(1)} %copy-done.3, bf16[112,1152]{1,0:T(8,128)(2,1)S(1)} %fusion.1.refs_0_, bf16[112,1152]{1,0:T(8,128)(2,1)S(1)} %collective-permute-done.1.refs_1_.refs_0_, bf16[1024,384]{1,0:T(8,128)(2,1)S(1)} %bitcast.25, bf16[1024,384]{1,0:T(8,128)(2,1)S(1)} %bitcast.21, ...), custom_call_target="tpu_custom_call" | custom-call | tf_op jit(solution)/shard_map/pallas_call | solution.py:123
  47.2 0.1 collective-permute-start.9
  47.3 14.3 %collective-permute-done.5.refs_3_.came = bf16[384,512]{1,0:T(8,128)(2,1)S(1)} collective-permute-done((bf16[384,512]{1,0:T(8,128)(2,1)S(1)}, bf16[384,512]{1,0:T(8,128)(2,1)S(1)}, u32[]{:S(2)}, u32[]{:S(2)}) %collective-permute-start.5) | collective-permute-done | bytes 393248 | tf_op jit(solution)/shard_map/swap/ppermute | solution.py:199
  61.5 0.5 collective-permute-start.11
  62.1 0.8 collective-permute-start.15
  62.8 1.2 %shard_map.111.refs_2_.refs_4_ = bf16[448,384]{1,0:T(8,128)(2,1)S(1)} custom-call(bf16[112,1152]{1,0:T(8,128)(2,1)S(1)} %fusion.1.refs_0_, bf16[112,1152]{1,0:T(8,128)(2,1)S(1)} %collective-permute-done.1.refs_1_.refs_0_, bf16[112,1152]{1,0:T(8,128)(2,1)S(1)} %collective-permute-done.refs_2_.refs_0_.refs_1_, ...), custom_call_target="tpu_custom_call" | custom-call | tf_op jit(solution)/shard_map/pallas_call | solution.py:123
  64.0 1.2 %shard_map.114.refs_4_.refs_2_ = bf16[448,384]{1,0:T(8,128)(2,1)S(1)} custom-call(bf16[112,1152]{1,0:T(8,128)(2,1)S(1)} %fusion.1.refs_0_, bf16[112,1152]{1,0:T(8,128)(2,1)S(1)} %collective-permute-done.1.refs_1_.refs_0_, bf16[112,1152]{1,0:T(8,128)(2,1)S(1)} %collective-permute-done.refs_2_.refs_0_.refs_1_, ...), custom_call_target="tpu_custom_call" | custom-call | tf_op jit(solution)/shard_map/pallas_call | solution.py:123
  65.3 1.0 %shard_map.116 = (bf16[112,512]{1,0:T(8,128)(2,1)S(1)}, bf16[112,512]{1,0:T(8,128)(2,1)S(1)}) custom-call(s32[16]{0:T(128)S(1)} %copy-done.3, bf16[112,1152]{1,0:T(8,128)(2,1)S(1)} %collective-permute-done.1.refs_1_.refs_0_, bf16[112,1152]{1,0:T(8,128)(2,1)S(1)} %collective-permute-done.2.refs_3_.refs_1_, bf16[448,384]{1,0:T(8,128)(2,1)S(1)} %shard_map.111.refs_2_.refs_4_, ...), custom_call_target="tpu_custom_call" | custom-call | tf_op jit(solution)/shard_map/pallas_call | solution.py:123
  66.2 1.3 %collective-permute-start.12 = (bf16[112,512]{1,0:T(8,128)(2,1)S(1)}, bf16[112,512]{1,0:T(8,128)(2,1)S(1)}, u32[]{:S(2)}, u32[]{:S(2)}) collective-permute-start(bf16[112,512]{1,0:T(8,128)(2,1)S(1)} %get-tuple-element.42), channel_id=1, source_target_pairs={{0,6},{1,7},{2,4},{3,5},{4,2},{5,3},{6,0},{7,1},{8,14},{9,15},{10,... | collective-permute-start | bytes 344072 | tf_op jit(solution)/shard_map/sums/ppermute | solution.py:199
  67.5 1.5 %collective-permute-start.13 = (bf16[112,512]{1,0:T(8,128)(2,1)S(1)}, bf16[112,512]{1,0:T(8,128)(2,1)S(1)}, u32[]{:S(2)}, u32[]{:S(2)}) collective-permute-start(bf16[112,512]{1,0:T(8,128)(2,1)S(1)} %get-tuple-element.43), channel_id=1, source_target_pairs={{0,4},{1,5},{2,6},{3,7},{4,0},{5,1},{6,2},{7,3},{8,12},{9,13},{10,... | collective-permute-start | bytes 344072 | tf_op jit(solution)/shard_map/sums/ppermute | solution.py:199
  69.0 0.9 %shard_map.115 = (f32[112,512]{1,0:T(8,128)S(1)}, bf16[112,512]{1,0:T(8,128)(2,1)S(1)}) custom-call(s32[16]{0:T(128)S(1)} %copy-done.3, bf16[112,1152]{1,0:T(8,128)(2,1)S(1)} %fusion.1.refs_0_, bf16[112,1152]{1,0:T(8,128)(2,1)S(1)} %collective-permute-done.refs_2_.refs_0_.refs_1_, bf16[448,384]{1,0:T(8,128)(2,1)S(1)} %shard_map.111.refs_2_.refs_4_, ...), custom_call_target="tpu_custom_call" | custom-call | tf_op jit(solution)/shard_map/pallas_call | solution.py:123
  70.0 1.4 %shard_map.118 = bf16[1024,384]{1,0:T(8,128)(2,1)} custom-call(s32[16]{0:T(128)S(1)} %copy-done.4, bf16[1024,384]{1,0:T(8,128)(2,1)S(1)} %bitcast.22, bf16[1024,384]{1,0:T(8,128)(2,1)S(1)} %collective-permute-done.3.refs_4_.came, bf16[1024,384]{1,0:T(8,128)(2,1)S(1)} %collective-permute-done.4.refs_5_.other), custom_call_target="tpu_custom_call" | custom-call | tf_op jit(solution)/shard_map/pallas_call | solution.py:173
  71.5 1.4 %shard_map.117 = bf16[1024,384]{1,0:T(8,128)(2,1)} custom-call(s32[16]{0:T(128)S(1)} %copy-done.4, bf16[1024,384]{1,0:T(8,128)(2,1)S(1)} %bitcast.26, bf16[1024,384]{1,0:T(8,128)(2,1)S(1)} %collective-permute-done.3.refs_4_.came, bf16[1024,384]{1,0:T(8,128)(2,1)S(1)} %collective-permute-done.4.refs_5_.other), custom_call_target="tpu_custom_call" | custom-call | tf_op jit(solution)/shard_map/pallas_call | solution.py:173
  72.9 0.2 collective-permute-done.15.refs_5_.other
  73.1 0.1 collective-permute-done.12.refs_1_
  73.2 1.4 %collective-permute-done.13.refs_2_ = bf16[112,512]{1,0:T(8,128)(2,1)S(1)} collective-permute-done((bf16[112,512]{1,0:T(8,128)(2,1)S(1)}, bf16[112,512]{1,0:T(8,128)(2,1)S(1)}, u32[]{:S(2)}, u32[]{:S(2)}) %collective-permute-start.13) | collective-permute-done | bytes 114720 | tf_op jit(solution)/shard_map/sums/ppermute | solution.py:199
  74.7 0.5 collective-permute-start.14
  75.2 1.0 %shard_map.119 = (f32[112,512]{1,0:T(8,128)S(1)}, f32[112,512]{1,0:T(8,128)S(1)}, f32[112,512]{1,0:T(8,128)S(1)}, f32[112,512]{1,0:T(8,128)S(1)}) custom-call(s32[16]{0:T(128)S(1)} %copy-done.3, bf16[112,1152]{1,0:T(8,128)(2,1)S(1)} %fusion.1.refs_0_, bf16[112,1152]{1,0:T(8,128)(2,1)S(1)} %collective-permute-done.1.refs_1_.refs_0_, ...), custom_call_target="tpu_custom_call" | custom-call | tf_op jit(solution)/shard_map/pallas_call | solution.py:123
  76.1 0.2 collective-permute-done.16.refs_3_
  76.4 0.8 shard_map.121
  77.2 0.9 %collective-permute-start.17 = (bf16[112,512]{1,0:T(8,128)(2,1)S(1)}, bf16[112,512]{1,0:T(8,128)(2,1)S(1)}, u32[]{:S(2)}, u32[]{:S(2)}) collective-permute-start(bf16[112,512]{1,0:T(8,128)(2,1)S(1)} %get-tuple-element.52), channel_id=1, source_target_pairs={{0,6},{1,7},{2,4},{3,5},{4,2},{5,3},{6,0},{7,1},{8,14},{9,15},{10,... | collective-permute-start | bytes 344072 | tf_op jit(solution)/shard_map/sums/ppermute | solution.py:199
  78.1 1.9 %collective-permute-start.18 = (bf16[112,512]{1,0:T(8,128)(2,1)S(1)}, bf16[112,512]{1,0:T(8,128)(2,1)S(1)}, u32[]{:S(2)}, u32[]{:S(2)}) collective-permute-start(bf16[112,512]{1,0:T(8,128)(2,1)S(1)} %get-tuple-element.53), channel_id=1, source_target_pairs={{0,4},{1,5},{2,6},{3,7},{4,0},{5,1},{6,2},{7,3},{8,12},{9,13},{10,... | collective-permute-start | bytes 344072 | tf_op jit(solution)/shard_map/sums/ppermute | solution.py:199
  80.0 0.8 shard_map.120
  80.8 0.8 collective-permute-start.19
  81.7 1.4 %shard_map.123 = bf16[384,1024]{1,0:T(8,128)(2,1)} custom-call(s32[16]{0:T(128)S(1)} %copy-done.4, bf16[384,1024]{1,0:T(8,128)(2,1)S(1)} %bitcast.18, bf16[384,512]{1,0:T(8,128)(2,1)S(1)} %collective-permute-done.5.refs_3_.came, bf16[384,512]{1,0:T(8,128)(2,1)S(1)} %collective-permute-done.15.refs_5_.other), custom_call_target="tpu_custom_call" | custom-call | tf_op jit(solution)/shard_map/pallas_call | solution.py:173
  83.1 1.0 %collective-permute-done.17.refs_5_ = bf16[112,512]{1,0:T(8,128)(2,1)S(1)} collective-permute-done((bf16[112,512]{1,0:T(8,128)(2,1)S(1)}, bf16[112,512]{1,0:T(8,128)(2,1)S(1)}, u32[]{:S(2)}, u32[]{:S(2)}) %collective-permute-start.17) | collective-permute-done | bytes 114720 | tf_op jit(solution)/shard_map/sums/ppermute | solution.py:199
  84.2 1.6 %collective-permute-done.18.refs_6_ = bf16[112,512]{1,0:T(8,128)(2,1)S(1)} collective-permute-done((bf16[112,512]{1,0:T(8,128)(2,1)S(1)}, bf16[112,512]{1,0:T(8,128)(2,1)S(1)}, u32[]{:S(2)}, u32[]{:S(2)}) %collective-permute-start.18) | collective-permute-done | bytes 114720 | tf_op jit(solution)/shard_map/sums/ppermute | solution.py:199
  85.7 0.4 collective-permute-done.19.refs_7_
  86.1 0.8 shard_map.122
  (29 shorter events, 0.2 us)
Async XLA Ops:
  2.2 4.4 %copy-start.6 = (f32[112,8]{0,1:T(8,128)S(1)}, f32[112,8]{0,1:T(8,128)}, u32[]{:S(2)}) copy-start(f32[112,8]{0,1:T(8,128)} %param.10) | copy-start | bytes 10756
  2.2 4.4 %copy-start.7 = (s32[112,8]{0,1:T(8,128)S(1)}, s32[112,8]{0,1:T(8,128)}, u32[]{:S(2)}) copy-start(s32[112,8]{0,1:T(8,128)} %param.9) | copy-start | bytes 10756
  2.2 4.5 %copy-start.5 = (bf16[112,1024]{1,0:T(8,128)(2,1)S(1)}, bf16[112,1024]{1,0:T(8,128)(2,1)}, u32[]{:S(2)}) copy-start(bf16[112,1024]{1,0:T(8,128)(2,1)} %param.8) | copy-start | bytes 688132
  2.2 28.2 %copy-start = (bf16[1,384,1024]{2,1,0:T(8,128)(2,1)S(1)}, bf16[1,384,1024]{2,1,0:T(8,128)(2,1)}, u32[]{:S(2)}) copy-start(bf16[1,384,1024]{2,1,0:T(8,128)(2,1)} %param.13) | copy-start | bytes 2359300
  2.4 38.5 %collective-permute-start.3 = (bf16[1024,384]{1,0:T(8,128)(2,1)S(1)}, bf16[1024,384]{1,0:T(8,128)(2,1)S(1)}, u32[]{:S(2)}, u32[]{:S(2)}) collective-permute-start(bf16[1024,384]{1,0:T(8,128)(2,1)S(1)} %maximum_select_fusion), channel_id=1, source_target_pairs={{0,8},{1,9},{2,10},{3,11},{4,12},{5,13},{6,14},{7,15},{8,0},{9,1},... | collective-permute-start | bytes 2359304 | tf_op jit(solution)/shard_map/swap/ppermute | solution.py:199
  6.7 23.8 %copy-start.2 = (bf16[1,1024,384]{2,1,0:T(8,128)(2,1)S(1)}, bf16[1,1024,384]{2,1,0:T(8,128)(2,1)}, u32[]{:S(2)}) copy-start(bf16[1,1024,384]{2,1,0:T(8,128)(2,1)} %param.11) | copy-start | bytes 2359300
  6.7 24.3 %copy-start.1 = (bf16[1,1024,384]{2,1,0:T(8,128)(2,1)S(1)}, bf16[1,1024,384]{2,1,0:T(8,128)(2,1)}, u32[]{:S(2)}) copy-start(bf16[1,1024,384]{2,1,0:T(8,128)(2,1)} %param.12) | copy-start | bytes 2359300
  6.7 35.8 %copy-start.3 = (s32[16]{0:T(128)S(1)}, s32[16]{0:T(128)}, u32[]{:S(2)}) copy-start(s32[16]{0:T(128)} %placement.13) | copy-start | bytes 196
  6.8 22.1 %collective-permute-start.1 = (bf16[112,1152]{1,0:T(8,128)(2,1)S(1)}, bf16[112,1152]{1,0:T(8,128)(2,1)S(1)}, u32[]{:S(2)}, u32[]{:S(2)}) collective-permute-start(bf16[112,1152]{1,0:T(8,128)(2,1)S(1)} %fusion.1.refs_0_), channel_id=1, source_target_pairs={{0,4},{1,5},{2,6},{3,7},{4,0},{5,1},{6,2},{7,3},{8,12},{9,13},{10,... | collective-permute-start | bytes 774152 | tf_op jit(solution)/shard_map/tokens/ppermute | solution.py:199
  8.4 22.6 %collective-permute-start = (bf16[112,1152]{1,0:T(8,128)(2,1)S(1)}, bf16[112,1152]{1,0:T(8,128)(2,1)S(1)}, u32[]{:S(2)}, u32[]{:S(2)}) collective-permute-start(bf16[112,1152]{1,0:T(8,128)(2,1)S(1)} %fusion.1.refs_0_), channel_id=1, source_target_pairs={{0,2},{1,3},{2,0},{3,1},{4,6},{5,7},{6,4},{7,5},{8,10},{9,11},{10,... | collective-permute-start | bytes 774152 | tf_op jit(solution)/shard_map/tokens/ppermute | solution.py:199
  28.9 7.1 %collective-permute-start.2 = (bf16[112,1152]{1,0:T(8,128)(2,1)S(1)}, bf16[112,1152]{1,0:T(8,128)(2,1)S(1)}, u32[]{:S(2)}, u32[]{:S(2)}) collective-permute-start(bf16[112,1152]{1,0:T(8,128)(2,1)S(1)} %collective-permute-done.1.refs_1_.refs_0_), channel_id=1, source_target_pairs={{0,2},{1,3},{2,0},{3,1},{4,6},{5,7},{6,4},{7,5},{8,10},{9,11},{10,... | collective-permute-start | bytes 774152 | tf_op jit(solution)/shard_map/tokens/ppermute | solution.py:199
  30.4 12.1 %collective-permute-start.8 = (bf16[384,1024]{1,0:T(8,128)(2,1)S(1)}, bf16[384,1024]{1,0:T(8,128)(2,1)S(1)}, u32[]{:S(2)}, u32[]{:S(2)}) collective-permute-start(bf16[384,1024]{1,0:T(8,128)(2,1)S(1)} %bitcast.15), channel_id=1, source_target_pairs={{0,1},{1,0},{2,3},{3,2},{4,5},{5,4},{6,7},{7,6},{8,9},{9,8},{10,11... | collective-permute-start | bytes 2359304 | tf_op jit(solution)/shard_map/near/ppermute | solution.py:199
  30.5 12.0 %collective-permute-start.6 = (bf16[1024,384]{1,0:T(8,128)(2,1)S(1)}, bf16[1024,384]{1,0:T(8,128)(2,1)S(1)}, u32[]{:S(2)}, u32[]{:S(2)}) collective-permute-start(bf16[1024,384]{1,0:T(8,128)(2,1)S(1)} %bitcast.23), channel_id=1, source_target_pairs={{0,1},{1,0},{2,3},{3,2},{4,5},{5,4},{6,7},{7,6},{8,9},{9,8},{10,11... | collective-permute-start | bytes 2359304 | tf_op jit(solution)/shard_map/near/ppermute | solution.py:199
  31.0 11.5 %collective-permute-start.7 = (bf16[1024,384]{1,0:T(8,128)(2,1)S(1)}, bf16[1024,384]{1,0:T(8,128)(2,1)S(1)}, u32[]{:S(2)}, u32[]{:S(2)}) collective-permute-start(bf16[1024,384]{1,0:T(8,128)(2,1)S(1)} %bitcast.19), channel_id=1, source_target_pairs={{0,1},{1,0},{2,3},{3,2},{4,5},{5,4},{6,7},{7,6},{8,9},{9,8},{10,11... | collective-permute-start | bytes 2359304 | tf_op jit(solution)/shard_map/near/ppermute | solution.py:199
  40.9 20.6 %collective-permute-start.4 = (bf16[1024,384]{1,0:T(8,128)(2,1)S(1)}, bf16[1024,384]{1,0:T(8,128)(2,1)S(1)}, u32[]{:S(2)}, u32[]{:S(2)}) collective-permute-start(bf16[1024,384]{1,0:T(8,128)(2,1)S(1)} %collective-permute-done.3.refs_4_.came), channel_id=1, source_target_pairs={{0,16},{16,0},{1,17},{17,1},{2,18},{18,2},{3,19},{19,3},{4,20},{20... | collective-permute-start | bytes 2359304 | tf_op jit(solution)/shard_map/trade/ppermute | solution.py:203
  42.5 19.1 %collective-permute-start.5 = (bf16[384,512]{1,0:T(8,128)(2,1)S(1)}, bf16[384,512]{1,0:T(8,128)(2,1)S(1)}, u32[]{:S(2)}, u32[]{:S(2)}) collective-permute-start(bf16[384,512]{1,0:T(8,128)(2,1)S(1)} %slice_select_fusion), channel_id=1, source_target_pairs={{0,8},{1,9},{2,10},{3,11},{4,12},{5,13},{6,14},{7,15},{8,0},{9,1},... | collective-permute-start | bytes 1179656 | tf_op jit(solution)/shard_map/swap/ppermute | solution.py:199
  47.2 16.8 %collective-permute-start.9 = (bf16[1024,384]{1,0:T(8,128)(2,1)S(1)}, bf16[1024,384]{1,0:T(8,128)(2,1)S(1)}, u32[]{:S(2)}, u32[]{:S(2)}) collective-permute-start(bf16[1024,384]{1,0:T(8,128)(2,1)S(1)} %collective-permute-done.3.refs_4_.came), channel_id=1, source_target_pairs={{0,1},{1,0},{2,3},{3,2},{4,5},{5,4},{6,7},{7,6},{8,9},{9,8},{10,11... | collective-permute-start | bytes 2359304 | tf_op jit(solution)/shard_map/z_near/ppermute | solution.py:199
  61.5 2.5 %collective-permute-start.10 = (bf16[1024,384]{1,0:T(8,128)(2,1)S(1)}, bf16[1024,384]{1,0:T(8,128)(2,1)S(1)}, u32[]{:S(2)}, u32[]{:S(2)}) collective-permute-start(bf16[1024,384]{1,0:T(8,128)(2,1)S(1)} %collective-permute-done.4.refs_5_.other), channel_id=1, source_target_pairs={{0,1},{1,0},{2,3},{3,2},{4,5},{5,4},{6,7},{7,6},{8,9},{9,8},{10,11... | collective-permute-start | bytes 2359304 | tf_op jit(solution)/shard_map/y_near/ppermute | solution.py:199
  61.5 3.7 %collective-permute-start.11 = (bf16[384,512]{1,0:T(8,128)(2,1)S(1)}, bf16[384,512]{1,0:T(8,128)(2,1)S(1)}, u32[]{:S(2)}, u32[]{:S(2)}) collective-permute-start(bf16[384,512]{1,0:T(8,128)(2,1)S(1)} %collective-permute-done.5.refs_3_.came), channel_id=1, source_target_pairs={{0,1},{1,0},{2,3},{3,2},{4,5},{5,4},{6,7},{7,6},{8,9},{9,8},{10,11... | collective-permute-start | bytes 1179656 | tf_op jit(solution)/shard_map/z_near/ppermute | solution.py:199
  62.1 11.0 %collective-permute-start.15 = (bf16[384,512]{1,0:T(8,128)(2,1)S(1)}, bf16[384,512]{1,0:T(8,128)(2,1)S(1)}, u32[]{:S(2)}, u32[]{:S(2)}) collective-permute-start(bf16[384,512]{1,0:T(8,128)(2,1)S(1)} %collective-permute-done.5.refs_3_.came), channel_id=1, source_target_pairs={{0,16},{16,0},{1,17},{17,1},{2,18},{18,2},{3,19},{19,3},{4,20},{20... | collective-permute-start | bytes 1179656 | tf_op jit(solution)/shard_map/trade/ppermute | solution.py:203
  66.2 7.0 %collective-permute-start.12 = (bf16[112,512]{1,0:T(8,128)(2,1)S(1)}, bf16[112,512]{1,0:T(8,128)(2,1)S(1)}, u32[]{:S(2)}, u32[]{:S(2)}) collective-permute-start(bf16[112,512]{1,0:T(8,128)(2,1)S(1)} %get-tuple-element.42), channel_id=1, source_target_pairs={{0,6},{1,7},{2,4},{3,5},{4,2},{5,3},{6,0},{7,1},{8,14},{9,15},{10,... | collective-permute-start | bytes 344072 | tf_op jit(solution)/shard_map/sums/ppermute | solution.py:199
  67.5 2.4 %copy-start.4 = (s32[16]{0:T(128)S(1)}, s32[16]{0:T(128)}, u32[]{:S(2)}) copy-start(s32[16]{0:T(128)} %flags.2) | copy-start | bytes 196
  67.5 7.1 %collective-permute-start.13 = (bf16[112,512]{1,0:T(8,128)(2,1)S(1)}, bf16[112,512]{1,0:T(8,128)(2,1)S(1)}, u32[]{:S(2)}, u32[]{:S(2)}) collective-permute-start(bf16[112,512]{1,0:T(8,128)(2,1)S(1)} %get-tuple-element.43), channel_id=1, source_target_pairs={{0,4},{1,5},{2,6},{3,7},{4,0},{5,1},{6,2},{7,3},{8,12},{9,13},{10,... | collective-permute-start | bytes 344072 | tf_op jit(solution)/shard_map/sums/ppermute | solution.py:199
  74.6 1.7 %collective-permute-start.16 = (bf16[384,512]{1,0:T(8,128)(2,1)S(1)}, bf16[384,512]{1,0:T(8,128)(2,1)S(1)}, u32[]{:S(2)}, u32[]{:S(2)}) collective-permute-start(bf16[384,512]{1,0:T(8,128)(2,1)S(1)} %collective-permute-done.15.refs_5_.other), channel_id=1, source_target_pairs={{0,1},{1,0},{2,3},{3,2},{4,5},{5,4},{6,7},{7,6},{8,9},{9,8},{10,11... | collective-permute-start | bytes 1179656 | tf_op jit(solution)/shard_map/y_near/ppermute | solution.py:199
  74.7 8.5 %collective-permute-start.14 = (bf16[112,512]{1,0:T(8,128)(2,1)S(1)}, bf16[112,512]{1,0:T(8,128)(2,1)S(1)}, u32[]{:S(2)}, u32[]{:S(2)}) collective-permute-start(bf16[112,512]{1,0:T(8,128)(2,1)S(1)} %get-tuple-element.44), channel_id=1, source_target_pairs={{0,2},{1,3},{2,0},{3,1},{4,6},{5,7},{6,4},{7,5},{8,10},{9,11},{10,... | collective-permute-start | bytes 344072 | tf_op jit(solution)/shard_map/sums/ppermute | solution.py:199
  77.2 7.0 %collective-permute-start.17 = (bf16[112,512]{1,0:T(8,128)(2,1)S(1)}, bf16[112,512]{1,0:T(8,128)(2,1)S(1)}, u32[]{:S(2)}, u32[]{:S(2)}) collective-permute-start(bf16[112,512]{1,0:T(8,128)(2,1)S(1)} %get-tuple-element.52), channel_id=1, source_target_pairs={{0,6},{1,7},{2,4},{3,5},{4,2},{5,3},{6,0},{7,1},{8,14},{9,15},{10,... | collective-permute-start | bytes 344072 | tf_op jit(solution)/shard_map/sums/ppermute | solution.py:199
  78.1 7.6 %collective-permute-start.18 = (bf16[112,512]{1,0:T(8,128)(2,1)S(1)}, bf16[112,512]{1,0:T(8,128)(2,1)S(1)}, u32[]{:S(2)}, u32[]{:S(2)}) collective-permute-start(bf16[112,512]{1,0:T(8,128)(2,1)S(1)} %get-tuple-element.53), channel_id=1, source_target_pairs={{0,4},{1,5},{2,6},{3,7},{4,0},{5,1},{6,2},{7,3},{8,12},{9,13},{10,... | collective-permute-start | bytes 344072 | tf_op jit(solution)/shard_map/sums/ppermute | solution.py:199
  80.8 5.3 %collective-permute-start.19 = (bf16[112,512]{1,0:T(8,128)(2,1)S(1)}, bf16[112,512]{1,0:T(8,128)(2,1)S(1)}, u32[]{:S(2)}, u32[]{:S(2)}) collective-permute-start(bf16[112,512]{1,0:T(8,128)(2,1)S(1)} %get-tuple-element.54), channel_id=1, source_target_pairs={{0,2},{1,3},{2,0},{3,1},{4,6},{5,7},{6,4},{7,5},{8,10},{9,11},{10,... | collective-permute-start | bytes 344072 | tf_op jit(solution)/shard_map/sums/ppermute | solution.py:199

commit v15 on v10

--- a/solution.py
+++ b/solution.py
@@ -95,8 +95,9 @@
         pair = range(first, first + 2)
         totals = {i: base[i][...] if base[i].shape[1] == part else base[i][:, columns] for i in pair}
         for flip, hidden, down in zip(flips, experts[::2], experts[1::2]):
-            span = slice(blocks[first] * height, (blocks[first] + 2) * height)
-            value = rounded(dot(hidden[span, :], down[...]))
+            spans = [slice(blocks[i] * height, (blocks[i] + 1) * height) for i in pair]
+            units = jnp.concatenate([hidden[span, :] for span in spans], axis=0)
+            value = rounded(dot(units, down[...]))
             for i in pair:
                 weight = token_weight(rows[i][:, width:], placement[me ^ far ^ flip], count)
                 at = (i - first) * height
@@ -268,13 +269,16 @@
         )
         return dict(zip(blocks, out))
 
+    pairs = [(i, i + len(rows) // 2) for i in reversed(range(len(rows) // 2))]
+    order = [i for pair in pairs for i in reversed(pair) if i > 0]
+
     def collect(parts):
-        return [parts[0]] + [send(parts[i], masks[i], "sums") for i in reversed(range(1, len(parts)))]
+        return [parts[0]] + [send(parts[i], masks[i], "sums") for i in order]
 
     near_sums = [x for first in reversed(firsts) for x in base[first]]
     parts = {}
-    for first in firsts:
-        parts |= far_sums((0, 1), [arrived, z_near[1]], 0, (first, first + 1), near_sums, True)
+    for pair in pairs:
+        parts |= far_sums((0, 1), [arrived, z_near[1]], 0, pair, near_sums, True)
     flags = after(swap_flags, parts)
     stored = [
         store(0, 0, flags, own[0], z_upper, y_upper),
@@ -286,8 +290,8 @@
     everyone = tuple(range(len(rows)))
     last_sums = far_sums((0,), [landed], 1, everyone, near_sums, False)
     last_parts = {}
-    for first in firsts:
-        last_parts |= far_sums((1,), [y_near[1]], 1, (first, first + 1), last_sums, True)
+    for pair in pairs:
+        last_parts |= far_sums((1,), [y_near[1]], 1, pair, last_sums, True)
     stored.append(store(1, 0, after(swap_flags, last_parts), own[2], z_lower, y_lower))
     others = collect(last_parts)
     mixed = call(

time: 87 us -> 87.1 us (level)
  transfers between devices with their start and end apart: 20 -> 20, of which waited for: 10 -> 12; matrix products, arithmetic and copies ran while one was open for 0% -> 0% of each run, Pallas kernels for 18% -> 18%
where the time goes in v15:
time: 87.1 us; the launch traced here: 86.9 us
  waiting for transfers between devices  47.8 us (55%)
  starting transfers between devices  19.5 us (22%)
  Pallas kernels  16.7 us (19%)
  local copies, waits for them, and re-layouts  1.67 us (2%)
  between operations  0.92 us (1%)
    ppermute x18, waiting for transfers between devices, send(): return lax.ppermute(value, 'expert', [(d, d ^ bit) for d in range(count)])  35.3 us
    ppermute x18, starting transfers between devices, send(): return lax.ppermute(value, 'expert', [(d, d ^ bit) for d in range(count)])  17.1 us
    ppermute x2, waiting for transfers between devices, trade(): return lax.ppermute(value, 'dp', trades)  12.5 us
    pallas_call x10, Pallas kernels, call(): pl.pallas_call(kernel, out_shape=out_shape, in_specs=[smem] * scalars + [...  12.4 us
    pallas_call x3, Pallas kernels, store(): pl.pallas_call(functools.partial(store_kernel, axis, first), out_shape=ja...  4.34 us
    ppermute x2, starting transfers between devices, trade(): return lax.ppermute(value, 'dp', trades)  2.32 us
  transfers between devices with their start and end apart: 20, of which 12 were waited for; matrix products, arithmetic and copies ran while one was open for 0% of the time, Pallas kernels for 18%

profile of v15, /device:TPU:0, one launch (start us, length us, event | category | flops | bytes accessed | tf_op | source)
XLA Modules:
  0.0 86.9 jit_solution(16266061339640176980)
XLA Ops:
  0.6 1.5 %slice_bitcast_fusion = (bf16[512,384]{1,0:T(8,128)(2,1)S(1)}, bf16[512,384]{1,0:T(8,128)(2,1)S(1)}, bf16[512,384]{1,0:T(8,128)(2,1)S(1)}, bf16[512,384]{1,0:T(8,128)(2,1)S(1)}) fusion(bf16[1,1024,384]{2,1,0:T(8,128)(2,1)} %param.12, bf16[1,1024,384]{2,1,0:T(8,128)(2,1)} %param.11), kind=kLoop, calls=%fused_computation.4 | loop fusion | bytes 3145728 | tf_op jit(solution)/shard_map/slice | solution.py:212
  2.2 0.0 copy-start.7
  2.2 0.0 copy-start.5
  2.2 0.2 maximum_select_fusion
  2.4 4.1 %collective-permute-start.3 = (bf16[1024,384]{1,0:T(8,128)(2,1)S(1)}, bf16[1024,384]{1,0:T(8,128)(2,1)S(1)}, u32[]{:S(2)}, u32[]{:S(2)}) collective-permute-start(bf16[1024,384]{1,0:T(8,128)(2,1)S(1)} %maximum_select_fusion), channel_id=1, source_target_pairs={{0,8},{1,9},{2,10},{3,11},{4,12},{5,13},{6,14},{7,15},{8,0},{9,1},... | collective-permute-start | bytes 2359304 | tf_op jit(solution)/shard_map/swap/ppermute | solution.py:199
  6.6 0.1 copy.17
  6.7 0.0 copy-start.2
  6.8 1.6 %collective-permute-start.1 = (bf16[112,1152]{1,0:T(8,128)(2,1)S(1)}, bf16[112,1152]{1,0:T(8,128)(2,1)S(1)}, u32[]{:S(2)}, u32[]{:S(2)}) collective-permute-start(bf16[112,1152]{1,0:T(8,128)(2,1)S(1)} %fusion.1.refs_0_), channel_id=1, source_target_pairs={{0,4},{1,5},{2,6},{3,7},{4,0},{5,1},{6,2},{7,3},{8,12},{9,13},{10,... | collective-permute-start | bytes 774152 | tf_op jit(solution)/shard_map/tokens/ppermute | solution.py:199
  8.4 1.5 %collective-permute-start = (bf16[112,1152]{1,0:T(8,128)(2,1)S(1)}, bf16[112,1152]{1,0:T(8,128)(2,1)S(1)}, u32[]{:S(2)}, u32[]{:S(2)}) collective-permute-start(bf16[112,1152]{1,0:T(8,128)(2,1)S(1)} %fusion.1.refs_0_), channel_id=1, source_target_pairs={{0,2},{1,3},{2,0},{3,1},{4,6},{5,7},{6,4},{7,5},{8,10},{9,11},{10,... | collective-permute-start | bytes 774152 | tf_op jit(solution)/shard_map/tokens/ppermute | solution.py:199
  9.9 19.0 %collective-permute-done.1.refs_1_.refs_0_ = bf16[112,1152]{1,0:T(8,128)(2,1)S(1)} collective-permute-done((bf16[112,1152]{1,0:T(8,128)(2,1)S(1)}, bf16[112,1152]{1,0:T(8,128)(2,1)S(1)}, u32[]{:S(2)}, u32[]{:S(2)}) %collective-permute-start.1) | collective-permute-done | bytes 258080 | tf_op jit(solution)/shard_map/tokens/ppermute | solution.py:199
  28.9 1.5 %collective-permute-start.2 = (bf16[112,1152]{1,0:T(8,128)(2,1)S(1)}, bf16[112,1152]{1,0:T(8,128)(2,1)S(1)}, u32[]{:S(2)}, u32[]{:S(2)}) collective-permute-start(bf16[112,1152]{1,0:T(8,128)(2,1)S(1)} %collective-permute-done.1.refs_1_.refs_0_), channel_id=1, source_target_pairs={{0,2},{1,3},{2,0},{3,1},{4,6},{5,7},{6,4},{7,5},{8,10},{9,11},{10,... | collective-permute-start | bytes 774152 | tf_op jit(solution)/shard_map/tokens/ppermute | solution.py:199
  30.4 0.1 collective-permute-start.8
  30.5 0.5 collective-permute-start.6
  31.0 0.1 collective-permute-start.7
  31.1 4.9 %collective-permute-done.2.refs_3_.refs_1_ = bf16[112,1152]{1,0:T(8,128)(2,1)S(1)} collective-permute-done((bf16[112,1152]{1,0:T(8,128)(2,1)S(1)}, bf16[112,1152]{1,0:T(8,128)(2,1)S(1)}, u32[]{:S(2)}, u32[]{:S(2)}) %collective-permute-start.2) | collective-permute-done | bytes 258080 | tf_op jit(solution)/shard_map/tokens/ppermute | solution.py:199
  36.0 4.9 %collective-permute-done.3.refs_4_.came = bf16[1024,384]{1,0:T(8,128)(2,1)S(1)} collective-permute-done((bf16[1024,384]{1,0:T(8,128)(2,1)S(1)}, bf16[1024,384]{1,0:T(8,128)(2,1)S(1)}, u32[]{:S(2)}, u32[]{:S(2)}) %collective-permute-start.3) | collective-permute-done | bytes 786464 | tf_op jit(solution)/shard_map/swap/ppermute | solution.py:199
  40.9 1.6 %collective-permute-start.4 = (bf16[1024,384]{1,0:T(8,128)(2,1)S(1)}, bf16[1024,384]{1,0:T(8,128)(2,1)S(1)}, u32[]{:S(2)}, u32[]{:S(2)}) collective-permute-start(bf16[1024,384]{1,0:T(8,128)(2,1)S(1)} %collective-permute-done.3.refs_4_.came), channel_id=1, source_target_pairs={{0,16},{16,0},{1,17},{17,1},{2,18},{18,2},{3,19},{19,3},{4,20},{20... | collective-permute-start | bytes 2359304 | tf_op jit(solution)/shard_map/trade/ppermute | solution.py:203
  42.5 2.3 %shard_map.113 = (f32[112,1024]{1,0:T(8,128)S(1)}, f32[112,1024]{1,0:T(8,128)S(1)}) custom-call(s32[16]{0:T(128)S(1)} %copy-done.3, bf16[112,1152]{1,0:T(8,128)(2,1)S(1)} %collective-permute-done.refs_2_.refs_0_.refs_1_, bf16[112,1152]{1,0:T(8,128)(2,1)S(1)} %collective-permute-done.2.refs_3_.refs_1_, bf16[1024,384]{1,0:T(8,128)(2,1)S(1)} %bitcast.24, ...), custom_call_target="tpu_custom_call" | custom-call | tf_op jit(solution)/shard_map/pallas_call | solution.py:123
  44.9 2.3 %shard_map.112 = (f32[112,1024]{1,0:T(8,128)S(1)}, f32[112,1024]{1,0:T(8,128)S(1)}) custom-call(s32[16]{0:T(128)S(1)} %copy-done.3, bf16[112,1152]{1,0:T(8,128)(2,1)S(1)} %fusion.1.refs_0_, bf16[112,1152]{1,0:T(8,128)(2,1)S(1)} %collective-permute-done.1.refs_1_.refs_0_, bf16[1024,384]{1,0:T(8,128)(2,1)S(1)} %bitcast.25, bf16[1024,384]{1,0:T(8,128)(2,1)S(1)} %bitcast.21, ...), custom_call_target="tpu_custom_call" | custom-call | tf_op jit(solution)/shard_map/pallas_call | solution.py:123
  47.2 0.1 collective-permute-start.9
  47.3 12.4 %collective-permute-done.4.refs_5_.other = bf16[1024,384]{1,0:T(8,128)(2,1)S(1)} collective-permute-done((bf16[1024,384]{1,0:T(8,128)(2,1)S(1)}, bf16[1024,384]{1,0:T(8,128)(2,1)S(1)}, u32[]{:S(2)}, u32[]{:S(2)}) %collective-permute-start.4) | collective-permute-done | bytes 786464 | tf_op jit(solution)/shard_map/trade/ppermute | solution.py:203
  59.6 1.2 %shard_map.111.refs_2_.refs_4_ = bf16[448,384]{1,0:T(8,128)(2,1)S(1)} custom-call(bf16[112,1152]{1,0:T(8,128)(2,1)S(1)} %fusion.1.refs_0_, bf16[112,1152]{1,0:T(8,128)(2,1)S(1)} %collective-permute-done.1.refs_1_.refs_0_, bf16[112,1152]{1,0:T(8,128)(2,1)S(1)} %collective-permute-done.refs_2_.refs_0_.refs_1_, ...), custom_call_target="tpu_custom_call" | custom-call | tf_op jit(solution)/shard_map/pallas_call | solution.py:123
  60.9 0.7 collective-permute-done.5.refs_3_.came
  61.5 0.5 collective-permute-start.11
  62.1 0.8 collective-permute-start.15
  62.8 1.0 %collective-permute-done.10.refs_5_ = bf16[1024,384]{1,0:T(8,128)(2,1)S(1)} collective-permute-done((bf16[1024,384]{1,0:T(8,128)(2,1)S(1)}, bf16[1024,384]{1,0:T(8,128)(2,1)S(1)}, u32[]{:S(2)}, u32[]{:S(2)}) %collective-permute-start.10) | collective-permute-done | bytes 786464 | tf_op jit(solution)/shard_map/y_near/ppermute | solution.py:199
  63.8 1.2 %shard_map.114.refs_4_.refs_2_ = bf16[448,384]{1,0:T(8,128)(2,1)S(1)} custom-call(bf16[112,1152]{1,0:T(8,128)(2,1)S(1)} %fusion.1.refs_0_, bf16[112,1152]{1,0:T(8,128)(2,1)S(1)} %collective-permute-done.1.refs_1_.refs_0_, bf16[112,1152]{1,0:T(8,128)(2,1)S(1)} %collective-permute-done.refs_2_.refs_0_.refs_1_, ...), custom_call_target="tpu_custom_call" | custom-call | tf_op jit(solution)/shard_map/pallas_call | solution.py:123
  65.1 0.9 %shard_map.116 = (bf16[112,512]{1,0:T(8,128)(2,1)S(1)}, bf16[112,512]{1,0:T(8,128)(2,1)S(1)}) custom-call(s32[16]{0:T(128)S(1)} %copy-done.3, bf16[112,1152]{1,0:T(8,128)(2,1)S(1)} %collective-permute-done.1.refs_1_.refs_0_, bf16[112,1152]{1,0:T(8,128)(2,1)S(1)} %collective-permute-done.2.refs_3_.refs_1_, bf16[448,384]{1,0:T(8,128)(2,1)S(1)} %shard_map.111.refs_2_.refs_4_, ...), custom_call_target="tpu_custom_call" | custom-call | tf_op jit(solution)/shard_map/pallas_call | solution.py:123
  66.0 1.8 %collective-permute-start.12 = (bf16[112,512]{1,0:T(8,128)(2,1)S(1)}, bf16[112,512]{1,0:T(8,128)(2,1)S(1)}, u32[]{:S(2)}, u32[]{:S(2)}) collective-permute-start(bf16[112,512]{1,0:T(8,128)(2,1)S(1)} %get-tuple-element.42), channel_id=1, source_target_pairs={{0,6},{1,7},{2,4},{3,5},{4,2},{5,3},{6,0},{7,1},{8,14},{9,15},{10,... | collective-permute-start | bytes 344072 | tf_op jit(solution)/shard_map/sums/ppermute | solution.py:199
  67.8 1.2 %collective-permute-start.13 = (bf16[112,512]{1,0:T(8,128)(2,1)S(1)}, bf16[112,512]{1,0:T(8,128)(2,1)S(1)}, u32[]{:S(2)}, u32[]{:S(2)}) collective-permute-start(bf16[112,512]{1,0:T(8,128)(2,1)S(1)} %get-tuple-element.43), channel_id=1, source_target_pairs={{0,4},{1,5},{2,6},{3,7},{4,0},{5,1},{6,2},{7,3},{8,12},{9,13},{10,... | collective-permute-start | bytes 344072 | tf_op jit(solution)/shard_map/sums/ppermute | solution.py:199
  69.0 1.0 %shard_map.115 = (f32[112,512]{1,0:T(8,128)S(1)}, bf16[112,512]{1,0:T(8,128)(2,1)S(1)}) custom-call(s32[16]{0:T(128)S(1)} %copy-done.3, bf16[112,1152]{1,0:T(8,128)(2,1)S(1)} %fusion.1.refs_0_, bf16[112,1152]{1,0:T(8,128)(2,1)S(1)} %collective-permute-done.refs_2_.refs_0_.refs_1_, bf16[448,384]{1,0:T(8,128)(2,1)S(1)} %shard_map.111.refs_2_.refs_4_, ...), custom_call_target="tpu_custom_call" | custom-call | tf_op jit(solution)/shard_map/pallas_call | solution.py:123
  70.0 1.4 %shard_map.118 = bf16[1024,384]{1,0:T(8,128)(2,1)} custom-call(s32[16]{0:T(128)S(1)} %copy-done.4, bf16[1024,384]{1,0:T(8,128)(2,1)S(1)} %bitcast.22, bf16[1024,384]{1,0:T(8,128)(2,1)S(1)} %collective-permute-done.3.refs_4_.came, bf16[1024,384]{1,0:T(8,128)(2,1)S(1)} %collective-permute-done.4.refs_5_.other), custom_call_target="tpu_custom_call" | custom-call | tf_op jit(solution)/shard_map/pallas_call | solution.py:173
  71.4 1.4 %shard_map.117 = bf16[1024,384]{1,0:T(8,128)(2,1)} custom-call(s32[16]{0:T(128)S(1)} %copy-done.4, bf16[1024,384]{1,0:T(8,128)(2,1)S(1)} %bitcast.26, bf16[1024,384]{1,0:T(8,128)(2,1)S(1)} %collective-permute-done.3.refs_4_.came, bf16[1024,384]{1,0:T(8,128)(2,1)S(1)} %collective-permute-done.4.refs_5_.other), custom_call_target="tpu_custom_call" | custom-call | tf_op jit(solution)/shard_map/pallas_call | solution.py:173
  72.9 0.2 collective-permute-done.15.refs_5_.other
  73.1 1.6 %collective-permute-done.13.refs_2_ = bf16[112,512]{1,0:T(8,128)(2,1)S(1)} collective-permute-done((bf16[112,512]{1,0:T(8,128)(2,1)S(1)}, bf16[112,512]{1,0:T(8,128)(2,1)S(1)}, u32[]{:S(2)}, u32[]{:S(2)}) %collective-permute-start.13) | collective-permute-done | bytes 114720 | tf_op jit(solution)/shard_map/sums/ppermute | solution.py:199
  74.6 0.5 collective-permute-start.14
  75.2 1.0 %shard_map.119 = (f32[112,512]{1,0:T(8,128)S(1)}, f32[112,512]{1,0:T(8,128)S(1)}, f32[112,512]{1,0:T(8,128)S(1)}, f32[112,512]{1,0:T(8,128)S(1)}) custom-call(s32[16]{0:T(128)S(1)} %copy-done.3, bf16[112,1152]{1,0:T(8,128)(2,1)S(1)} %fusion.1.refs_0_, bf16[112,1152]{1,0:T(8,128)(2,1)S(1)} %collective-permute-done.1.refs_1_.refs_0_, ...), custom_call_target="tpu_custom_call" | custom-call | tf_op jit(solution)/shard_map/pallas_call | solution.py:123
  76.1 0.2 collective-permute-done.16.refs_3_
  76.4 0.8 shard_map.121
  77.2 1.6 %collective-permute-start.17 = (bf16[112,512]{1,0:T(8,128)(2,1)S(1)}, bf16[112,512]{1,0:T(8,128)(2,1)S(1)}, u32[]{:S(2)}, u32[]{:S(2)}) collective-permute-start(bf16[112,512]{1,0:T(8,128)(2,1)S(1)} %get-tuple-element.52), channel_id=1, source_target_pairs={{0,6},{1,7},{2,4},{3,5},{4,2},{5,3},{6,0},{7,1},{8,14},{9,15},{10,... | collective-permute-start | bytes 344072 | tf_op jit(solution)/shard_map/sums/ppermute | solution.py:199
  78.8 1.2 %collective-permute-start.18 = (bf16[112,512]{1,0:T(8,128)(2,1)S(1)}, bf16[112,512]{1,0:T(8,128)(2,1)S(1)}, u32[]{:S(2)}, u32[]{:S(2)}) collective-permute-start(bf16[112,512]{1,0:T(8,128)(2,1)S(1)} %get-tuple-element.53), channel_id=1, source_target_pairs={{0,4},{1,5},{2,6},{3,7},{4,0},{5,1},{6,2},{7,3},{8,12},{9,13},{10,... | collective-permute-start | bytes 344072 | tf_op jit(solution)/shard_map/sums/ppermute | solution.py:199
  80.0 0.8 shard_map.120
  80.8 0.8 collective-permute-start.19
  81.7 1.4 %shard_map.123 = bf16[384,1024]{1,0:T(8,128)(2,1)} custom-call(s32[16]{0:T(128)S(1)} %copy-done.4, bf16[384,1024]{1,0:T(8,128)(2,1)S(1)} %bitcast.18, bf16[384,512]{1,0:T(8,128)(2,1)S(1)} %collective-permute-done.5.refs_3_.came, bf16[384,512]{1,0:T(8,128)(2,1)S(1)} %collective-permute-done.15.refs_5_.other), custom_call_target="tpu_custom_call" | custom-call | tf_op jit(solution)/shard_map/pallas_call | solution.py:173
  83.1 1.0 %collective-permute-done.17.refs_5_ = bf16[112,512]{1,0:T(8,128)(2,1)S(1)} collective-permute-done((bf16[112,512]{1,0:T(8,128)(2,1)S(1)}, bf16[112,512]{1,0:T(8,128)(2,1)S(1)}, u32[]{:S(2)}, u32[]{:S(2)}) %collective-permute-start.17) | collective-permute-done | bytes 114720 | tf_op jit(solution)/shard_map/sums/ppermute | solution.py:199
  84.2 1.6 %collective-permute-done.18.refs_6_ = bf16[112,512]{1,0:T(8,128)(2,1)S(1)} collective-permute-done((bf16[112,512]{1,0:T(8,128)(2,1)S(1)}, bf16[112,512]{1,0:T(8,128)(2,1)S(1)}, u32[]{:S(2)}, u32[]{:S(2)}) %collective-permute-start.18) | collective-permute-done | bytes 114720 | tf_op jit(solution)/shard_map/sums/ppermute | solution.py:199
  85.7 0.4 collective-permute-done.19.refs_7_
  86.1 0.8 shard_map.122
  (29 shorter events, 0.2 us)
Async XLA Ops:
  2.2 4.4 %copy-start.6 = (f32[112,8]{0,1:T(8,128)S(1)}, f32[112,8]{0,1:T(8,128)}, u32[]{:S(2)}) copy-start(f32[112,8]{0,1:T(8,128)} %param.10) | copy-start | bytes 10756
  2.2 4.4 %copy-start.7 = (s32[112,8]{0,1:T(8,128)S(1)}, s32[112,8]{0,1:T(8,128)}, u32[]{:S(2)}) copy-start(s32[112,8]{0,1:T(8,128)} %param.9) | copy-start | bytes 10756
  2.2 4.5 %copy-start.5 = (bf16[112,1024]{1,0:T(8,128)(2,1)S(1)}, bf16[112,1024]{1,0:T(8,128)(2,1)}, u32[]{:S(2)}) copy-start(bf16[112,1024]{1,0:T(8,128)(2,1)} %param.8) | copy-start | bytes 688132
  2.2 28.2 %copy-start = (bf16[1,384,1024]{2,1,0:T(8,128)(2,1)S(1)}, bf16[1,384,1024]{2,1,0:T(8,128)(2,1)}, u32[]{:S(2)}) copy-start(bf16[1,384,1024]{2,1,0:T(8,128)(2,1)} %param.13) | copy-start | bytes 2359300
  2.4 38.5 %collective-permute-start.3 = (bf16[1024,384]{1,0:T(8,128)(2,1)S(1)}, bf16[1024,384]{1,0:T(8,128)(2,1)S(1)}, u32[]{:S(2)}, u32[]{:S(2)}) collective-permute-start(bf16[1024,384]{1,0:T(8,128)(2,1)S(1)} %maximum_select_fusion), channel_id=1, source_target_pairs={{0,8},{1,9},{2,10},{3,11},{4,12},{5,13},{6,14},{7,15},{8,0},{9,1},... | collective-permute-start | bytes 2359304 | tf_op jit(solution)/shard_map/swap/ppermute | solution.py:199
  6.7 23.8 %copy-start.2 = (bf16[1,1024,384]{2,1,0:T(8,128)(2,1)S(1)}, bf16[1,1024,384]{2,1,0:T(8,128)(2,1)}, u32[]{:S(2)}) copy-start(bf16[1,1024,384]{2,1,0:T(8,128)(2,1)} %param.11) | copy-start | bytes 2359300
  6.7 24.3 %copy-start.1 = (bf16[1,1024,384]{2,1,0:T(8,128)(2,1)S(1)}, bf16[1,1024,384]{2,1,0:T(8,128)(2,1)}, u32[]{:S(2)}) copy-start(bf16[1,1024,384]{2,1,0:T(8,128)(2,1)} %param.12) | copy-start | bytes 2359300
  6.7 35.8 %copy-start.3 = (s32[16]{0:T(128)S(1)}, s32[16]{0:T(128)}, u32[]{:S(2)}) copy-start(s32[16]{0:T(128)} %placement.13) | copy-start | bytes 196
  6.8 22.1 %collective-permute-start.1 = (bf16[112,1152]{1,0:T(8,128)(2,1)S(1)}, bf16[112,1152]{1,0:T(8,128)(2,1)S(1)}, u32[]{:S(2)}, u32[]{:S(2)}) collective-permute-start(bf16[112,1152]{1,0:T(8,128)(2,1)S(1)} %fusion.1.refs_0_), channel_id=1, source_target_pairs={{0,4},{1,5},{2,6},{3,7},{4,0},{5,1},{6,2},{7,3},{8,12},{9,13},{10,... | collective-permute-start | bytes 774152 | tf_op jit(solution)/shard_map/tokens/ppermute | solution.py:199
  8.4 22.6 %collective-permute-start = (bf16[112,1152]{1,0:T(8,128)(2,1)S(1)}, bf16[112,1152]{1,0:T(8,128)(2,1)S(1)}, u32[]{:S(2)}, u32[]{:S(2)}) collective-permute-start(bf16[112,1152]{1,0:T(8,128)(2,1)S(1)} %fusion.1.refs_0_), channel_id=1, source_target_pairs={{0,2},{1,3},{2,0},{3,1},{4,6},{5,7},{6,4},{7,5},{8,10},{9,11},{10,... | collective-permute-start | bytes 774152 | tf_op jit(solution)/shard_map/tokens/ppermute | solution.py:199
  28.9 7.1 %collective-permute-start.2 = (bf16[112,1152]{1,0:T(8,128)(2,1)S(1)}, bf16[112,1152]{1,0:T(8,128)(2,1)S(1)}, u32[]{:S(2)}, u32[]{:S(2)}) collective-permute-start(bf16[112,1152]{1,0:T(8,128)(2,1)S(1)} %collective-permute-done.1.refs_1_.refs_0_), channel_id=1, source_target_pairs={{0,2},{1,3},{2,0},{3,1},{4,6},{5,7},{6,4},{7,5},{8,10},{9,11},{10,... | collective-permute-start | bytes 774152 | tf_op jit(solution)/shard_map/tokens/ppermute | solution.py:199
  30.4 12.1 %collective-permute-start.8 = (bf16[384,1024]{1,0:T(8,128)(2,1)S(1)}, bf16[384,1024]{1,0:T(8,128)(2,1)S(1)}, u32[]{:S(2)}, u32[]{:S(2)}) collective-permute-start(bf16[384,1024]{1,0:T(8,128)(2,1)S(1)} %bitcast.15), channel_id=1, source_target_pairs={{0,1},{1,0},{2,3},{3,2},{4,5},{5,4},{6,7},{7,6},{8,9},{9,8},{10,11... | collective-permute-start | bytes 2359304 | tf_op jit(solution)/shard_map/near/ppermute | solution.py:199
  30.5 12.0 %collective-permute-start.6 = (bf16[1024,384]{1,0:T(8,128)(2,1)S(1)}, bf16[1024,384]{1,0:T(8,128)(2,1)S(1)}, u32[]{:S(2)}, u32[]{:S(2)}) collective-permute-start(bf16[1024,384]{1,0:T(8,128)(2,1)S(1)} %bitcast.23), channel_id=1, source_target_pairs={{0,1},{1,0},{2,3},{3,2},{4,5},{5,4},{6,7},{7,6},{8,9},{9,8},{10,11... | collective-permute-start | bytes 2359304 | tf_op jit(solution)/shard_map/near/ppermute | solution.py:199
  31.0 11.5 %collective-permute-start.7 = (bf16[1024,384]{1,0:T(8,128)(2,1)S(1)}, bf16[1024,384]{1,0:T(8,128)(2,1)S(1)}, u32[]{:S(2)}, u32[]{:S(2)}) collective-permute-start(bf16[1024,384]{1,0:T(8,128)(2,1)S(1)} %bitcast.19), channel_id=1, source_target_pairs={{0,1},{1,0},{2,3},{3,2},{4,5},{5,4},{6,7},{7,6},{8,9},{9,8},{10,11... | collective-permute-start | bytes 2359304 | tf_op jit(solution)/shard_map/near/ppermute | solution.py:199
  40.9 18.7 %collective-permute-start.4 = (bf16[1024,384]{1,0:T(8,128)(2,1)S(1)}, bf16[1024,384]{1,0:T(8,128)(2,1)S(1)}, u32[]{:S(2)}, u32[]{:S(2)}) collective-permute-start(bf16[1024,384]{1,0:T(8,128)(2,1)S(1)} %collective-permute-done.3.refs_4_.came), channel_id=1, source_target_pairs={{0,16},{16,0},{1,17},{17,1},{2,18},{18,2},{3,19},{19,3},{4,20},{20... | collective-permute-start | bytes 2359304 | tf_op jit(solution)/shard_map/trade/ppermute | solution.py:203
  42.5 19.1 %collective-permute-start.5 = (bf16[384,512]{1,0:T(8,128)(2,1)S(1)}, bf16[384,512]{1,0:T(8,128)(2,1)S(1)}, u32[]{:S(2)}, u32[]{:S(2)}) collective-permute-start(bf16[384,512]{1,0:T(8,128)(2,1)S(1)} %slice_select_fusion), channel_id=1, source_target_pairs={{0,8},{1,9},{2,10},{3,11},{4,12},{5,13},{6,14},{7,15},{8,0},{9,1},... | collective-permute-start | bytes 1179656 | tf_op jit(solution)/shard_map/swap/ppermute | solution.py:199
  47.2 15.6 %collective-permute-start.9 = (bf16[1024,384]{1,0:T(8,128)(2,1)S(1)}, bf16[1024,384]{1,0:T(8,128)(2,1)S(1)}, u32[]{:S(2)}, u32[]{:S(2)}) collective-permute-start(bf16[1024,384]{1,0:T(8,128)(2,1)S(1)} %collective-permute-done.3.refs_4_.came), channel_id=1, source_target_pairs={{0,1},{1,0},{2,3},{3,2},{4,5},{5,4},{6,7},{7,6},{8,9},{9,8},{10,11... | collective-permute-start | bytes 2359304 | tf_op jit(solution)/shard_map/z_near/ppermute | solution.py:199
  61.5 2.3 %collective-permute-start.10 = (bf16[1024,384]{1,0:T(8,128)(2,1)S(1)}, bf16[1024,384]{1,0:T(8,128)(2,1)S(1)}, u32[]{:S(2)}, u32[]{:S(2)}) collective-permute-start(bf16[1024,384]{1,0:T(8,128)(2,1)S(1)} %collective-permute-done.4.refs_5_.other), channel_id=1, source_target_pairs={{0,1},{1,0},{2,3},{3,2},{4,5},{5,4},{6,7},{7,6},{8,9},{9,8},{10,11... | collective-permute-start | bytes 2359304 | tf_op jit(solution)/shard_map/y_near/ppermute | solution.py:199
  61.5 3.5 %collective-permute-start.11 = (bf16[384,512]{1,0:T(8,128)(2,1)S(1)}, bf16[384,512]{1,0:T(8,128)(2,1)S(1)}, u32[]{:S(2)}, u32[]{:S(2)}) collective-permute-start(bf16[384,512]{1,0:T(8,128)(2,1)S(1)} %collective-permute-done.5.refs_3_.came), channel_id=1, source_target_pairs={{0,1},{1,0},{2,3},{3,2},{4,5},{5,4},{6,7},{7,6},{8,9},{9,8},{10,11... | collective-permute-start | bytes 1179656 | tf_op jit(solution)/shard_map/z_near/ppermute | solution.py:199
  62.1 11.0 %collective-permute-start.15 = (bf16[384,512]{1,0:T(8,128)(2,1)S(1)}, bf16[384,512]{1,0:T(8,128)(2,1)S(1)}, u32[]{:S(2)}, u32[]{:S(2)}) collective-permute-start(bf16[384,512]{1,0:T(8,128)(2,1)S(1)} %collective-permute-done.5.refs_3_.came), channel_id=1, source_target_pairs={{0,16},{16,0},{1,17},{17,1},{2,18},{18,2},{3,19},{19,3},{4,20},{20... | collective-permute-start | bytes 1179656 | tf_op jit(solution)/shard_map/trade/ppermute | solution.py:203
  66.0 7.1 %collective-permute-start.12 = (bf16[112,512]{1,0:T(8,128)(2,1)S(1)}, bf16[112,512]{1,0:T(8,128)(2,1)S(1)}, u32[]{:S(2)}, u32[]{:S(2)}) collective-permute-start(bf16[112,512]{1,0:T(8,128)(2,1)S(1)} %get-tuple-element.42), channel_id=1, source_target_pairs={{0,6},{1,7},{2,4},{3,5},{4,2},{5,3},{6,0},{7,1},{8,14},{9,15},{10,... | collective-permute-start | bytes 344072 | tf_op jit(solution)/shard_map/sums/ppermute | solution.py:199
  67.8 2.1 %copy-start.4 = (s32[16]{0:T(128)S(1)}, s32[16]{0:T(128)}, u32[]{:S(2)}) copy-start(s32[16]{0:T(128)} %flags.2) | copy-start | bytes 196
  67.8 6.8 %collective-permute-start.13 = (bf16[112,512]{1,0:T(8,128)(2,1)S(1)}, bf16[112,512]{1,0:T(8,128)(2,1)S(1)}, u32[]{:S(2)}, u32[]{:S(2)}) collective-permute-start(bf16[112,512]{1,0:T(8,128)(2,1)S(1)} %get-tuple-element.43), channel_id=1, source_target_pairs={{0,4},{1,5},{2,6},{3,7},{4,0},{5,1},{6,2},{7,3},{8,12},{9,13},{10,... | collective-permute-start | bytes 344072 | tf_op jit(solution)/shard_map/sums/ppermute | solution.py:199
  74.6 1.7 %collective-permute-start.16 = (bf16[384,512]{1,0:T(8,128)(2,1)S(1)}, bf16[384,512]{1,0:T(8,128)(2,1)S(1)}, u32[]{:S(2)}, u32[]{:S(2)}) collective-permute-start(bf16[384,512]{1,0:T(8,128)(2,1)S(1)} %collective-permute-done.15.refs_5_.other), channel_id=1, source_target_pairs={{0,1},{1,0},{2,3},{3,2},{4,5},{5,4},{6,7},{7,6},{8,9},{9,8},{10,11... | collective-permute-start | bytes 1179656 | tf_op jit(solution)/shard_map/y_near/ppermute | solution.py:199
  74.6 8.5 %collective-permute-start.14 = (bf16[112,512]{1,0:T(8,128)(2,1)S(1)}, bf16[112,512]{1,0:T(8,128)(2,1)S(1)}, u32[]{:S(2)}, u32[]{:S(2)}) collective-permute-start(bf16[112,512]{1,0:T(8,128)(2,1)S(1)} %get-tuple-element.44), channel_id=1, source_target_pairs={{0,2},{1,3},{2,0},{3,1},{4,6},{5,7},{6,4},{7,5},{8,10},{9,11},{10,... | collective-permute-start | bytes 344072 | tf_op jit(solution)/shard_map/sums/ppermute | solution.py:199
  77.2 7.0 %collective-permute-start.17 = (bf16[112,512]{1,0:T(8,128)(2,1)S(1)}, bf16[112,512]{1,0:T(8,128)(2,1)S(1)}, u32[]{:S(2)}, u32[]{:S(2)}) collective-permute-start(bf16[112,512]{1,0:T(8,128)(2,1)S(1)} %get-tuple-element.52), channel_id=1, source_target_pairs={{0,6},{1,7},{2,4},{3,5},{4,2},{5,3},{6,0},{7,1},{8,14},{9,15},{10,... | collective-permute-start | bytes 344072 | tf_op jit(solution)/shard_map/sums/ppermute | solution.py:199
  78.8 6.9 %collective-permute-start.18 = (bf16[112,512]{1,0:T(8,128)(2,1)S(1)}, bf16[112,512]{1,0:T(8,128)(2,1)S(1)}, u32[]{:S(2)}, u32[]{:S(2)}) collective-permute-start(bf16[112,512]{1,0:T(8,128)(2,1)S(1)} %get-tuple-element.53), channel_id=1, source_target_pairs={{0,4},{1,5},{2,6},{3,7},{4,0},{5,1},{6,2},{7,3},{8,12},{9,13},{10,... | collective-permute-start | bytes 344072 | tf_op jit(solution)/shard_map/sums/ppermute | solution.py:199
  80.8 5.3 %collective-permute-start.19 = (bf16[112,512]{1,0:T(8,128)(2,1)S(1)}, bf16[112,512]{1,0:T(8,128)(2,1)S(1)}, u32[]{:S(2)}, u32[]{:S(2)}) collective-permute-start(bf16[112,512]{1,0:T(8,128)(2,1)S(1)} %get-tuple-element.54), channel_id=1, source_target_pairs={{0,2},{1,3},{2,0},{3,1},{4,6},{5,7},{6,4},{7,5},{8,10},{9,11},{10,... | collective-permute-start | bytes 344072 | tf_op jit(solution)/shard_map/sums/ppermute | solution.py:199

commit v16 on v14

--- a/solution.py
+++ b/solution.py
@@ -284,7 +284,7 @@
         store(0, depth, flags, own[1], z_upper, y_upper),
     ]
     ours = collect(parts)
-    landed = after(y_lower, stored, ours[1:-1])
+    landed = after(y_lower, stored, ours[1 : len(ours) // 2])
     y_near.append(send(landed, 1, "y_near"))
     everyone = tuple(range(len(rows)))
     last_sums = far_sums((0,), [landed], 1, everyone, near_sums, False)

time: 87.1 us -> 86 us (0.987)
    ppermute x18, waiting for transfers between devices: 47.9 us -> 45.8 us  [send(): return lax.ppermute(value, 'expert', [(d, d ^ bit) for d in range(count)])]
    ppermute x2, waiting for transfers between devices: 0.17 us -> 1.65 us  [trade(): return lax.ppermute(value, 'dp', trades)]
  transfers between devices with their start and end apart: 20 -> 20, of which waited for: 11 -> 8; matrix products, arithmetic and copies ran while one was open for 0% -> 0% of each run, Pallas kernels for 18% -> 19%
where the time goes in v16:
time: 86 us; the launch traced here: 85.9 us
  waiting for transfers between devices  47.4 us (55%)
  starting transfers between devices  18.8 us (22%)
  Pallas kernels  16.7 us (19%)
  local copies, waits for them, and re-layouts  1.68 us (2%)
  between operations  0.95 us (1%)
    ppermute x18, waiting for transfers between devices, send(): return lax.ppermute(value, 'expert', [(d, d ^ bit) for d in range(count)])  45.8 us
    ppermute x18, starting transfers between devices, send(): return lax.ppermute(value, 'expert', [(d, d ^ bit) for d in range(count)])  16.5 us
    pallas_call x10, Pallas kernels, call(): pl.pallas_call(kernel, out_shape=out_shape, in_specs=[smem] * scalars + [...  12.4 us
    pallas_call x3, Pallas kernels, store(): pl.pallas_call(functools.partial(store_kernel, axis, first), out_shape=ja...  4.34 us
    ppermute x2, starting transfers between devices, trade(): return lax.ppermute(value, 'dp', trades)  2.32 us
  transfers between devices with their start and end apart: 20, of which 8 were waited for; matrix products, arithmetic and copies ran while one was open for 0% of the time, Pallas kernels for 19%

profile of v16, /device:TPU:0, one launch (start us, length us, event | category | flops | bytes accessed | tf_op | source)
XLA Modules:
  0.0 85.9 jit_solution(8589982623442850876)
XLA Ops:
  0.6 1.5 %slice_bitcast_fusion = (bf16[512,384]{1,0:T(8,128)(2,1)S(1)}, bf16[512,384]{1,0:T(8,128)(2,1)S(1)}, bf16[512,384]{1,0:T(8,128)(2,1)S(1)}, bf16[512,384]{1,0:T(8,128)(2,1)S(1)}) fusion(bf16[1,1024,384]{2,1,0:T(8,128)(2,1)} %param.12, bf16[1,1024,384]{2,1,0:T(8,128)(2,1)} %param.11), kind=kLoop, calls=%fused_computation.4 | loop fusion | bytes 3145728 | tf_op jit(solution)/shard_map/slice | solution.py:212
  2.2 0.0 copy-start.6
  2.2 0.0 copy-start.7
  2.2 0.0 copy-start.5
  2.2 0.0 copy-start
  2.2 0.2 maximum_select_fusion
  2.4 4.1 %collective-permute-start.3 = (bf16[1024,384]{1,0:T(8,128)(2,1)S(1)}, bf16[1024,384]{1,0:T(8,128)(2,1)S(1)}, u32[]{:S(2)}, u32[]{:S(2)}) collective-permute-start(bf16[1024,384]{1,0:T(8,128)(2,1)S(1)} %maximum_select_fusion), channel_id=1, source_target_pairs={{0,8},{1,9},{2,10},{3,11},{4,12},{5,13},{6,14},{7,15},{8,0},{9,1},... | collective-permute-start | bytes 2359304 | tf_op jit(solution)/shard_map/swap/ppermute | solution.py:199
  6.6 0.1 copy.17
  6.7 0.0 copy-start.2
  6.7 0.0 copy-start.1
  6.7 0.0 copy-start.3
  6.8 1.6 %collective-permute-start.1 = (bf16[112,1152]{1,0:T(8,128)(2,1)S(1)}, bf16[112,1152]{1,0:T(8,128)(2,1)S(1)}, u32[]{:S(2)}, u32[]{:S(2)}) collective-permute-start(bf16[112,1152]{1,0:T(8,128)(2,1)S(1)} %fusion.1.refs_0_), channel_id=1, source_target_pairs={{0,4},{1,5},{2,6},{3,7},{4,0},{5,1},{6,2},{7,3},{8,12},{9,13},{10,... | collective-permute-start | bytes 774152 | tf_op jit(solution)/shard_map/tokens/ppermute | solution.py:199
  8.4 1.5 %collective-permute-start = (bf16[112,1152]{1,0:T(8,128)(2,1)S(1)}, bf16[112,1152]{1,0:T(8,128)(2,1)S(1)}, u32[]{:S(2)}, u32[]{:S(2)}) collective-permute-start(bf16[112,1152]{1,0:T(8,128)(2,1)S(1)} %fusion.1.refs_0_), channel_id=1, source_target_pairs={{0,2},{1,3},{2,0},{3,1},{4,6},{5,7},{6,4},{7,5},{8,10},{9,11},{10,... | collective-permute-start | bytes 774152 | tf_op jit(solution)/shard_map/tokens/ppermute | solution.py:199
  9.9 19.0 %collective-permute-done.1.refs_1_.refs_0_ = bf16[112,1152]{1,0:T(8,128)(2,1)S(1)} collective-permute-done((bf16[112,1152]{1,0:T(8,128)(2,1)S(1)}, bf16[112,1152]{1,0:T(8,128)(2,1)S(1)}, u32[]{:S(2)}, u32[]{:S(2)}) %collective-permute-start.1) | collective-permute-done | bytes 258080 | tf_op jit(solution)/shard_map/tokens/ppermute | solution.py:199
  28.9 1.5 %collective-permute-start.2 = (bf16[112,1152]{1,0:T(8,128)(2,1)S(1)}, bf16[112,1152]{1,0:T(8,128)(2,1)S(1)}, u32[]{:S(2)}, u32[]{:S(2)}) collective-permute-start(bf16[112,1152]{1,0:T(8,128)(2,1)S(1)} %collective-permute-done.1.refs_1_.refs_0_), channel_id=1, source_target_pairs={{0,2},{1,3},{2,0},{3,1},{4,6},{5,7},{6,4},{7,5},{8,10},{9,11},{10,... | collective-permute-start | bytes 774152 | tf_op jit(solution)/shard_map/tokens/ppermute | solution.py:199
  30.4 0.1 collective-permute-start.8
  30.5 0.5 collective-permute-start.6
  31.0 0.1 collective-permute-start.7
  31.1 4.9 %collective-permute-done.2.refs_3_.refs_1_ = bf16[112,1152]{1,0:T(8,128)(2,1)S(1)} collective-permute-done((bf16[112,1152]{1,0:T(8,128)(2,1)S(1)}, bf16[112,1152]{1,0:T(8,128)(2,1)S(1)}, u32[]{:S(2)}, u32[]{:S(2)}) %collective-permute-start.2) | collective-permute-done | bytes 258080 | tf_op jit(solution)/shard_map/tokens/ppermute | solution.py:199
  36.0 4.9 %collective-permute-done.3.refs_4_.came = bf16[1024,384]{1,0:T(8,128)(2,1)S(1)} collective-permute-done((bf16[1024,384]{1,0:T(8,128)(2,1)S(1)}, bf16[1024,384]{1,0:T(8,128)(2,1)S(1)}, u32[]{:S(2)}, u32[]{:S(2)}) %collective-permute-start.3) | collective-permute-done | bytes 786464 | tf_op jit(solution)/shard_map/swap/ppermute | solution.py:199
  40.9 1.6 %collective-permute-start.4 = (bf16[1024,384]{1,0:T(8,128)(2,1)S(1)}, bf16[1024,384]{1,0:T(8,128)(2,1)S(1)}, u32[]{:S(2)}, u32[]{:S(2)}) collective-permute-start(bf16[1024,384]{1,0:T(8,128)(2,1)S(1)} %collective-permute-done.3.refs_4_.came), channel_id=1, source_target_pairs={{0,16},{16,0},{1,17},{17,1},{2,18},{18,2},{3,19},{19,3},{4,20},{20... | collective-permute-start | bytes 2359304 | tf_op jit(solution)/shard_map/trade/ppermute | solution.py:203
  42.5 2.3 %shard_map.113 = (f32[112,1024]{1,0:T(8,128)S(1)}, f32[112,1024]{1,0:T(8,128)S(1)}) custom-call(s32[16]{0:T(128)S(1)} %copy-done.3, bf16[112,1152]{1,0:T(8,128)(2,1)S(1)} %collective-permute-done.refs_2_.refs_0_.refs_1_, bf16[112,1152]{1,0:T(8,128)(2,1)S(1)} %collective-permute-done.2.refs_3_.refs_1_, bf16[1024,384]{1,0:T(8,128)(2,1)S(1)} %bitcast.24, ...), custom_call_target="tpu_custom_call" | custom-call | tf_op jit(solution)/shard_map/pallas_call | solution.py:123
  44.9 2.3 %shard_map.112 = (f32[112,1024]{1,0:T(8,128)S(1)}, f32[112,1024]{1,0:T(8,128)S(1)}) custom-call(s32[16]{0:T(128)S(1)} %copy-done.3, bf16[112,1152]{1,0:T(8,128)(2,1)S(1)} %fusion.1.refs_0_, bf16[112,1152]{1,0:T(8,128)(2,1)S(1)} %collective-permute-done.1.refs_1_.refs_0_, bf16[1024,384]{1,0:T(8,128)(2,1)S(1)} %bitcast.25, bf16[1024,384]{1,0:T(8,128)(2,1)S(1)} %bitcast.21, ...), custom_call_target="tpu_custom_call" | custom-call | tf_op jit(solution)/shard_map/pallas_call | solution.py:123
  47.2 0.1 collective-permute-start.9
  47.3 14.3 %collective-permute-done.5.refs_3_.came = bf16[384,512]{1,0:T(8,128)(2,1)S(1)} collective-permute-done((bf16[384,512]{1,0:T(8,128)(2,1)S(1)}, bf16[384,512]{1,0:T(8,128)(2,1)S(1)}, u32[]{:S(2)}, u32[]{:S(2)}) %collective-permute-start.5) | collective-permute-done | bytes 393248 | tf_op jit(solution)/shard_map/swap/ppermute | solution.py:199
  61.5 0.5 collective-permute-start.11
  62.1 0.8 collective-permute-start.15
  62.8 1.2 %shard_map.111.refs_2_.refs_4_ = bf16[448,384]{1,0:T(8,128)(2,1)S(1)} custom-call(bf16[112,1152]{1,0:T(8,128)(2,1)S(1)} %fusion.1.refs_0_, bf16[112,1152]{1,0:T(8,128)(2,1)S(1)} %collective-permute-done.1.refs_1_.refs_0_, bf16[112,1152]{1,0:T(8,128)(2,1)S(1)} %collective-permute-done.refs_2_.refs_0_.refs_1_, ...), custom_call_target="tpu_custom_call" | custom-call | tf_op jit(solution)/shard_map/pallas_call | solution.py:123
  64.0 1.2 %shard_map.114.refs_4_.refs_2_ = bf16[448,384]{1,0:T(8,128)(2,1)S(1)} custom-call(bf16[112,1152]{1,0:T(8,128)(2,1)S(1)} %fusion.1.refs_0_, bf16[112,1152]{1,0:T(8,128)(2,1)S(1)} %collective-permute-done.1.refs_1_.refs_0_, bf16[112,1152]{1,0:T(8,128)(2,1)S(1)} %collective-permute-done.refs_2_.refs_0_.refs_1_, ...), custom_call_target="tpu_custom_call" | custom-call | tf_op jit(solution)/shard_map/pallas_call | solution.py:123
  65.3 1.0 %shard_map.116 = (bf16[112,512]{1,0:T(8,128)(2,1)S(1)}, bf16[112,512]{1,0:T(8,128)(2,1)S(1)}) custom-call(s32[16]{0:T(128)S(1)} %copy-done.3, bf16[112,1152]{1,0:T(8,128)(2,1)S(1)} %collective-permute-done.1.refs_1_.refs_0_, bf16[112,1152]{1,0:T(8,128)(2,1)S(1)} %collective-permute-done.2.refs_3_.refs_1_, bf16[448,384]{1,0:T(8,128)(2,1)S(1)} %shard_map.111.refs_2_.refs_4_, ...), custom_call_target="tpu_custom_call" | custom-call | tf_op jit(solution)/shard_map/pallas_call | solution.py:123
  66.2 1.3 %collective-permute-start.12 = (bf16[112,512]{1,0:T(8,128)(2,1)S(1)}, bf16[112,512]{1,0:T(8,128)(2,1)S(1)}, u32[]{:S(2)}, u32[]{:S(2)}) collective-permute-start(bf16[112,512]{1,0:T(8,128)(2,1)S(1)} %get-tuple-element.42), channel_id=1, source_target_pairs={{0,6},{1,7},{2,4},{3,5},{4,2},{5,3},{6,0},{7,1},{8,14},{9,15},{10,... | collective-permute-start | bytes 344072 | tf_op jit(solution)/shard_map/sums/ppermute | solution.py:199
  67.6 0.9 %shard_map.115 = (f32[112,512]{1,0:T(8,128)S(1)}, bf16[112,512]{1,0:T(8,128)(2,1)S(1)}) custom-call(s32[16]{0:T(128)S(1)} %copy-done.3, bf16[112,1152]{1,0:T(8,128)(2,1)S(1)} %fusion.1.refs_0_, bf16[112,1152]{1,0:T(8,128)(2,1)S(1)} %collective-permute-done.refs_2_.refs_0_.refs_1_, bf16[448,384]{1,0:T(8,128)(2,1)S(1)} %shard_map.111.refs_2_.refs_4_, ...), custom_call_target="tpu_custom_call" | custom-call | tf_op jit(solution)/shard_map/pallas_call | solution.py:123
  68.5 1.4 %shard_map.118 = bf16[1024,384]{1,0:T(8,128)(2,1)} custom-call(s32[16]{0:T(128)S(1)} %copy-done.4, bf16[1024,384]{1,0:T(8,128)(2,1)S(1)} %bitcast.22, bf16[1024,384]{1,0:T(8,128)(2,1)S(1)} %collective-permute-done.3.refs_4_.came, bf16[1024,384]{1,0:T(8,128)(2,1)S(1)} %collective-permute-done.4.refs_5_.other), custom_call_target="tpu_custom_call" | custom-call | tf_op jit(solution)/shard_map/pallas_call | solution.py:173
  70.0 1.4 %shard_map.117 = bf16[1024,384]{1,0:T(8,128)(2,1)} custom-call(s32[16]{0:T(128)S(1)} %copy-done.4, bf16[1024,384]{1,0:T(8,128)(2,1)S(1)} %bitcast.26, bf16[1024,384]{1,0:T(8,128)(2,1)S(1)} %collective-permute-done.3.refs_4_.came, bf16[1024,384]{1,0:T(8,128)(2,1)S(1)} %collective-permute-done.4.refs_5_.other), custom_call_target="tpu_custom_call" | custom-call | tf_op jit(solution)/shard_map/pallas_call | solution.py:173
  71.4 1.6 %collective-permute-done.15.refs_5_.other = bf16[384,512]{1,0:T(8,128)(2,1)S(1)} collective-permute-done((bf16[384,512]{1,0:T(8,128)(2,1)S(1)}, bf16[384,512]{1,0:T(8,128)(2,1)S(1)}, u32[]{:S(2)}, u32[]{:S(2)}) %collective-permute-start.15) | collective-permute-done | bytes 393248 | tf_op jit(solution)/shard_map/trade/ppermute | solution.py:203
  73.1 0.0 collective-permute-start.13
  73.1 1.5 %collective-permute-start.14 = (bf16[112,512]{1,0:T(8,128)(2,1)S(1)}, bf16[112,512]{1,0:T(8,128)(2,1)S(1)}, u32[]{:S(2)}, u32[]{:S(2)}) collective-permute-start(bf16[112,512]{1,0:T(8,128)(2,1)S(1)} %get-tuple-element.44), channel_id=1, source_target_pairs={{0,2},{1,3},{2,0},{3,1},{4,6},{5,7},{6,4},{7,5},{8,10},{9,11},{10,... | collective-permute-start | bytes 344072 | tf_op jit(solution)/shard_map/sums/ppermute | solution.py:199
  74.7 1.0 %shard_map.119 = (f32[112,512]{1,0:T(8,128)S(1)}, f32[112,512]{1,0:T(8,128)S(1)}, f32[112,512]{1,0:T(8,128)S(1)}, f32[112,512]{1,0:T(8,128)S(1)}) custom-call(s32[16]{0:T(128)S(1)} %copy-done.3, bf16[112,1152]{1,0:T(8,128)(2,1)S(1)} %fusion.1.refs_0_, bf16[112,1152]{1,0:T(8,128)(2,1)S(1)} %collective-permute-done.1.refs_1_.refs_0_, ...), custom_call_target="tpu_custom_call" | custom-call | tf_op jit(solution)/shard_map/pallas_call | solution.py:123
  75.6 0.8 shard_map.121
  76.5 2.0 %collective-permute-start.17 = (bf16[112,512]{1,0:T(8,128)(2,1)S(1)}, bf16[112,512]{1,0:T(8,128)(2,1)S(1)}, u32[]{:S(2)}, u32[]{:S(2)}) collective-permute-start(bf16[112,512]{1,0:T(8,128)(2,1)S(1)} %get-tuple-element.52), channel_id=1, source_target_pairs={{0,6},{1,7},{2,4},{3,5},{4,2},{5,3},{6,0},{7,1},{8,14},{9,15},{10,... | collective-permute-start | bytes 344072 | tf_op jit(solution)/shard_map/sums/ppermute | solution.py:199
  78.5 0.2 collective-permute-start.18
  78.7 0.8 shard_map.120
  79.5 1.4 %collective-permute-start.19 = (bf16[112,512]{1,0:T(8,128)(2,1)S(1)}, bf16[112,512]{1,0:T(8,128)(2,1)S(1)}, u32[]{:S(2)}, u32[]{:S(2)}) collective-permute-start(bf16[112,512]{1,0:T(8,128)(2,1)S(1)} %get-tuple-element.54), channel_id=1, source_target_pairs={{0,2},{1,3},{2,0},{3,1},{4,6},{5,7},{6,4},{7,5},{8,10},{9,11},{10,... | collective-permute-start | bytes 344072 | tf_op jit(solution)/shard_map/sums/ppermute | solution.py:199
  80.9 1.4 %shard_map.123 = bf16[384,1024]{1,0:T(8,128)(2,1)} custom-call(s32[16]{0:T(128)S(1)} %copy-done.4, bf16[384,1024]{1,0:T(8,128)(2,1)S(1)} %bitcast.18, bf16[384,512]{1,0:T(8,128)(2,1)S(1)} %collective-permute-done.5.refs_3_.came, bf16[384,512]{1,0:T(8,128)(2,1)S(1)} %collective-permute-done.15.refs_5_.other), custom_call_target="tpu_custom_call" | custom-call | tf_op jit(solution)/shard_map/pallas_call | solution.py:173
  82.4 1.0 %collective-permute-done.17.refs_5_ = bf16[112,512]{1,0:T(8,128)(2,1)S(1)} collective-permute-done((bf16[112,512]{1,0:T(8,128)(2,1)S(1)}, bf16[112,512]{1,0:T(8,128)(2,1)S(1)}, u32[]{:S(2)}, u32[]{:S(2)}) %collective-permute-start.17) | collective-permute-done | bytes 114720 | tf_op jit(solution)/shard_map/sums/ppermute | solution.py:199
  83.4 0.9 collective-permute-done.18.refs_6_
  84.3 0.8 collective-permute-done.19.refs_7_
  85.1 0.8 shard_map.122
  (29 shorter events, 0.2 us)
Async XLA Ops:
  2.2 4.4 %copy-start.6 = (f32[112,8]{0,1:T(8,128)S(1)}, f32[112,8]{0,1:T(8,128)}, u32[]{:S(2)}) copy-start(f32[112,8]{0,1:T(8,128)} %param.10) | copy-start | bytes 10756
  2.2 4.4 %copy-start.7 = (s32[112,8]{0,1:T(8,128)S(1)}, s32[112,8]{0,1:T(8,128)}, u32[]{:S(2)}) copy-start(s32[112,8]{0,1:T(8,128)} %param.9) | copy-start | bytes 10756
  2.2 4.5 %copy-start.5 = (bf16[112,1024]{1,0:T(8,128)(2,1)S(1)}, bf16[112,1024]{1,0:T(8,128)(2,1)}, u32[]{:S(2)}) copy-start(bf16[112,1024]{1,0:T(8,128)(2,1)} %param.8) | copy-start | bytes 688132
  2.2 28.2 %copy-start = (bf16[1,384,1024]{2,1,0:T(8,128)(2,1)S(1)}, bf16[1,384,1024]{2,1,0:T(8,128)(2,1)}, u32[]{:S(2)}) copy-start(bf16[1,384,1024]{2,1,0:T(8,128)(2,1)} %param.13) | copy-start | bytes 2359300
  2.4 38.5 %collective-permute-start.3 = (bf16[1024,384]{1,0:T(8,128)(2,1)S(1)}, bf16[1024,384]{1,0:T(8,128)(2,1)S(1)}, u32[]{:S(2)}, u32[]{:S(2)}) collective-permute-start(bf16[1024,384]{1,0:T(8,128)(2,1)S(1)} %maximum_select_fusion), channel_id=1, source_target_pairs={{0,8},{1,9},{2,10},{3,11},{4,12},{5,13},{6,14},{7,15},{8,0},{9,1},... | collective-permute-start | bytes 2359304 | tf_op jit(solution)/shard_map/swap/ppermute | solution.py:199
  6.7 23.8 %copy-start.2 = (bf16[1,1024,384]{2,1,0:T(8,128)(2,1)S(1)}, bf16[1,1024,384]{2,1,0:T(8,128)(2,1)}, u32[]{:S(2)}) copy-start(bf16[1,1024,384]{2,1,0:T(8,128)(2,1)} %param.11) | copy-start | bytes 2359300
  6.7 24.3 %copy-start.1 = (bf16[1,1024,384]{2,1,0:T(8,128)(2,1)S(1)}, bf16[1,1024,384]{2,1,0:T(8,128)(2,1)}, u32[]{:S(2)}) copy-start(bf16[1,1024,384]{2,1,0:T(8,128)(2,1)} %param.12) | copy-start | bytes 2359300
  6.7 35.8 %copy-start.3 = (s32[16]{0:T(128)S(1)}, s32[16]{0:T(128)}, u32[]{:S(2)}) copy-start(s32[16]{0:T(128)} %placement.13) | copy-start | bytes 196
  6.8 22.1 %collective-permute-start.1 = (bf16[112,1152]{1,0:T(8,128)(2,1)S(1)}, bf16[112,1152]{1,0:T(8,128)(2,1)S(1)}, u32[]{:S(2)}, u32[]{:S(2)}) collective-permute-start(bf16[112,1152]{1,0:T(8,128)(2,1)S(1)} %fusion.1.refs_0_), channel_id=1, source_target_pairs={{0,4},{1,5},{2,6},{3,7},{4,0},{5,1},{6,2},{7,3},{8,12},{9,13},{10,... | collective-permute-start | bytes 774152 | tf_op jit(solution)/shard_map/tokens/ppermute | solution.py:199
  8.4 22.6 %collective-permute-start = (bf16[112,1152]{1,0:T(8,128)(2,1)S(1)}, bf16[112,1152]{1,0:T(8,128)(2,1)S(1)}, u32[]{:S(2)}, u32[]{:S(2)}) collective-permute-start(bf16[112,1152]{1,0:T(8,128)(2,1)S(1)} %fusion.1.refs_0_), channel_id=1, source_target_pairs={{0,2},{1,3},{2,0},{3,1},{4,6},{5,7},{6,4},{7,5},{8,10},{9,11},{10,... | collective-permute-start | bytes 774152 | tf_op jit(solution)/shard_map/tokens/ppermute | solution.py:199
  28.9 7.1 %collective-permute-start.2 = (bf16[112,1152]{1,0:T(8,128)(2,1)S(1)}, bf16[112,1152]{1,0:T(8,128)(2,1)S(1)}, u32[]{:S(2)}, u32[]{:S(2)}) collective-permute-start(bf16[112,1152]{1,0:T(8,128)(2,1)S(1)} %collective-permute-done.1.refs_1_.refs_0_), channel_id=1, source_target_pairs={{0,2},{1,3},{2,0},{3,1},{4,6},{5,7},{6,4},{7,5},{8,10},{9,11},{10,... | collective-permute-start | bytes 774152 | tf_op jit(solution)/shard_map/tokens/ppermute | solution.py:199
  30.4 12.1 %collective-permute-start.8 = (bf16[384,1024]{1,0:T(8,128)(2,1)S(1)}, bf16[384,1024]{1,0:T(8,128)(2,1)S(1)}, u32[]{:S(2)}, u32[]{:S(2)}) collective-permute-start(bf16[384,1024]{1,0:T(8,128)(2,1)S(1)} %bitcast.15), channel_id=1, source_target_pairs={{0,1},{1,0},{2,3},{3,2},{4,5},{5,4},{6,7},{7,6},{8,9},{9,8},{10,11... | collective-permute-start | bytes 2359304 | tf_op jit(solution)/shard_map/near/ppermute | solution.py:199
  30.5 12.0 %collective-permute-start.6 = (bf16[1024,384]{1,0:T(8,128)(2,1)S(1)}, bf16[1024,384]{1,0:T(8,128)(2,1)S(1)}, u32[]{:S(2)}, u32[]{:S(2)}) collective-permute-start(bf16[1024,384]{1,0:T(8,128)(2,1)S(1)} %bitcast.23), channel_id=1, source_target_pairs={{0,1},{1,0},{2,3},{3,2},{4,5},{5,4},{6,7},{7,6},{8,9},{9,8},{10,11... | collective-permute-start | bytes 2359304 | tf_op jit(solution)/shard_map/near/ppermute | solution.py:199
  31.0 11.5 %collective-permute-start.7 = (bf16[1024,384]{1,0:T(8,128)(2,1)S(1)}, bf16[1024,384]{1,0:T(8,128)(2,1)S(1)}, u32[]{:S(2)}, u32[]{:S(2)}) collective-permute-start(bf16[1024,384]{1,0:T(8,128)(2,1)S(1)} %bitcast.19), channel_id=1, source_target_pairs={{0,1},{1,0},{2,3},{3,2},{4,5},{5,4},{6,7},{7,6},{8,9},{9,8},{10,11... | collective-permute-start | bytes 2359304 | tf_op jit(solution)/shard_map/near/ppermute | solution.py:199
  40.9 20.6 %collective-permute-start.4 = (bf16[1024,384]{1,0:T(8,128)(2,1)S(1)}, bf16[1024,384]{1,0:T(8,128)(2,1)S(1)}, u32[]{:S(2)}, u32[]{:S(2)}) collective-permute-start(bf16[1024,384]{1,0:T(8,128)(2,1)S(1)} %collective-permute-done.3.refs_4_.came), channel_id=1, source_target_pairs={{0,16},{16,0},{1,17},{17,1},{2,18},{18,2},{3,19},{19,3},{4,20},{20... | collective-permute-start | bytes 2359304 | tf_op jit(solution)/shard_map/trade/ppermute | solution.py:203
  42.5 19.1 %collective-permute-start.5 = (bf16[384,512]{1,0:T(8,128)(2,1)S(1)}, bf16[384,512]{1,0:T(8,128)(2,1)S(1)}, u32[]{:S(2)}, u32[]{:S(2)}) collective-permute-start(bf16[384,512]{1,0:T(8,128)(2,1)S(1)} %slice_select_fusion), channel_id=1, source_target_pairs={{0,8},{1,9},{2,10},{3,11},{4,12},{5,13},{6,14},{7,15},{8,0},{9,1},... | collective-permute-start | bytes 1179656 | tf_op jit(solution)/shard_map/swap/ppermute | solution.py:199
  47.2 16.8 %collective-permute-start.9 = (bf16[1024,384]{1,0:T(8,128)(2,1)S(1)}, bf16[1024,384]{1,0:T(8,128)(2,1)S(1)}, u32[]{:S(2)}, u32[]{:S(2)}) collective-permute-start(bf16[1024,384]{1,0:T(8,128)(2,1)S(1)} %collective-permute-done.3.refs_4_.came), channel_id=1, source_target_pairs={{0,1},{1,0},{2,3},{3,2},{4,5},{5,4},{6,7},{7,6},{8,9},{9,8},{10,11... | collective-permute-start | bytes 2359304 | tf_op jit(solution)/shard_map/z_near/ppermute | solution.py:199
  61.5 2.5 %collective-permute-start.10 = (bf16[1024,384]{1,0:T(8,128)(2,1)S(1)}, bf16[1024,384]{1,0:T(8,128)(2,1)S(1)}, u32[]{:S(2)}, u32[]{:S(2)}) collective-permute-start(bf16[1024,384]{1,0:T(8,128)(2,1)S(1)} %collective-permute-done.4.refs_5_.other), channel_id=1, source_target_pairs={{0,1},{1,0},{2,3},{3,2},{4,5},{5,4},{6,7},{7,6},{8,9},{9,8},{10,11... | collective-permute-start | bytes 2359304 | tf_op jit(solution)/shard_map/y_near/ppermute | solution.py:199
  61.5 3.7 %collective-permute-start.11 = (bf16[384,512]{1,0:T(8,128)(2,1)S(1)}, bf16[384,512]{1,0:T(8,128)(2,1)S(1)}, u32[]{:S(2)}, u32[]{:S(2)}) collective-permute-start(bf16[384,512]{1,0:T(8,128)(2,1)S(1)} %collective-permute-done.5.refs_3_.came), channel_id=1, source_target_pairs={{0,1},{1,0},{2,3},{3,2},{4,5},{5,4},{6,7},{7,6},{8,9},{9,8},{10,11... | collective-permute-start | bytes 1179656 | tf_op jit(solution)/shard_map/z_near/ppermute | solution.py:199
  62.1 11.0 %collective-permute-start.15 = (bf16[384,512]{1,0:T(8,128)(2,1)S(1)}, bf16[384,512]{1,0:T(8,128)(2,1)S(1)}, u32[]{:S(2)}, u32[]{:S(2)}) collective-permute-start(bf16[384,512]{1,0:T(8,128)(2,1)S(1)} %collective-permute-done.5.refs_3_.came), channel_id=1, source_target_pairs={{0,16},{16,0},{1,17},{17,1},{2,18},{18,2},{3,19},{19,3},{4,20},{20... | collective-permute-start | bytes 1179656 | tf_op jit(solution)/shard_map/trade/ppermute | solution.py:203
  66.2 2.3 %copy-start.4 = (s32[16]{0:T(128)S(1)}, s32[16]{0:T(128)}, u32[]{:S(2)}) copy-start(s32[16]{0:T(128)} %flags.2) | copy-start | bytes 196
  66.2 6.9 %collective-permute-start.12 = (bf16[112,512]{1,0:T(8,128)(2,1)S(1)}, bf16[112,512]{1,0:T(8,128)(2,1)S(1)}, u32[]{:S(2)}, u32[]{:S(2)}) collective-permute-start(bf16[112,512]{1,0:T(8,128)(2,1)S(1)} %get-tuple-element.42), channel_id=1, source_target_pairs={{0,6},{1,7},{2,4},{3,5},{4,2},{5,3},{6,0},{7,1},{8,14},{9,15},{10,... | collective-permute-start | bytes 344072 | tf_op jit(solution)/shard_map/sums/ppermute | solution.py:199
  73.1 2.5 %collective-permute-start.16 = (bf16[384,512]{1,0:T(8,128)(2,1)S(1)}, bf16[384,512]{1,0:T(8,128)(2,1)S(1)}, u32[]{:S(2)}, u32[]{:S(2)}) collective-permute-start(bf16[384,512]{1,0:T(8,128)(2,1)S(1)} %collective-permute-done.15.refs_5_.other), channel_id=1, source_target_pairs={{0,1},{1,0},{2,3},{3,2},{4,5},{5,4},{6,7},{7,6},{8,9},{9,8},{10,11... | collective-permute-start | bytes 1179656 | tf_op jit(solution)/shard_map/y_near/ppermute | solution.py:199
  73.1 9.3 %collective-permute-start.13 = (bf16[112,512]{1,0:T(8,128)(2,1)S(1)}, bf16[112,512]{1,0:T(8,128)(2,1)S(1)}, u32[]{:S(2)}, u32[]{:S(2)}) collective-permute-start(bf16[112,512]{1,0:T(8,128)(2,1)S(1)} %get-tuple-element.43), channel_id=1, source_target_pairs={{0,4},{1,5},{2,6},{3,7},{4,0},{5,1},{6,2},{7,3},{8,12},{9,13},{10,... | collective-permute-start | bytes 344072 | tf_op jit(solution)/shard_map/sums/ppermute | solution.py:199
  73.1 9.3 %collective-permute-start.14 = (bf16[112,512]{1,0:T(8,128)(2,1)S(1)}, bf16[112,512]{1,0:T(8,128)(2,1)S(1)}, u32[]{:S(2)}, u32[]{:S(2)}) collective-permute-start(bf16[112,512]{1,0:T(8,128)(2,1)S(1)} %get-tuple-element.44), channel_id=1, source_target_pairs={{0,2},{1,3},{2,0},{3,1},{4,6},{5,7},{6,4},{7,5},{8,10},{9,11},{10,... | collective-permute-start | bytes 344072 | tf_op jit(solution)/shard_map/sums/ppermute | solution.py:199
  76.5 7.0 %collective-permute-start.17 = (bf16[112,512]{1,0:T(8,128)(2,1)S(1)}, bf16[112,512]{1,0:T(8,128)(2,1)S(1)}, u32[]{:S(2)}, u32[]{:S(2)}) collective-permute-start(bf16[112,512]{1,0:T(8,128)(2,1)S(1)} %get-tuple-element.52), channel_id=1, source_target_pairs={{0,6},{1,7},{2,4},{3,5},{4,2},{5,3},{6,0},{7,1},{8,14},{9,15},{10,... | collective-permute-start | bytes 344072 | tf_op jit(solution)/shard_map/sums/ppermute | solution.py:199
  78.5 5.8 %collective-permute-start.18 = (bf16[112,512]{1,0:T(8,128)(2,1)S(1)}, bf16[112,512]{1,0:T(8,128)(2,1)S(1)}, u32[]{:S(2)}, u32[]{:S(2)}) collective-permute-start(bf16[112,512]{1,0:T(8,128)(2,1)S(1)} %get-tuple-element.53), channel_id=1, source_target_pairs={{0,4},{1,5},{2,6},{3,7},{4,0},{5,1},{6,2},{7,3},{8,12},{9,13},{10,... | collective-permute-start | bytes 344072 | tf_op jit(solution)/shard_map/sums/ppermute | solution.py:199
  79.5 5.6 %collective-permute-start.19 = (bf16[112,512]{1,0:T(8,128)(2,1)S(1)}, bf16[112,512]{1,0:T(8,128)(2,1)S(1)}, u32[]{:S(2)}, u32[]{:S(2)}) collective-permute-start(bf16[112,512]{1,0:T(8,128)(2,1)S(1)} %get-tuple-element.54), channel_id=1, source_target_pairs={{0,2},{1,3},{2,0},{3,1},{4,6},{5,7},{6,4},{7,5},{8,10},{9,11},{10,... | collective-permute-start | bytes 344072 | tf_op jit(solution)/shard_map/sums/ppermute | solution.py:199
